TPU v7x, 32 devices: a whole 2x2x4 slice. The times are simulated.
32 devices in a mesh: col: 8 (over z, y), row: 4 (over x, core).
Axes of the slice: x: 2, y: 2, z: 4, core: 2. Of those that a mesh axis runs over, the one named last changes fastest.
Arguments:
- r_slab: float32 [1024, 2048], P('row', 'col'), may hold values from -4 to 8, as said below
- arc_rows: float32 [4096, 2048], P('row', 'col'), may hold values from -6 to 6
- arc_blocks: int32 [32, 8], P('row', 'col'), may hold values 0 or 1
Outputs:
- r_updated: float32 [1024, 2048], P('row', 'col')
Inputs may be any that keep to these rules, and one draw needn't show every extreme that they name: r_slab is zero wherever an entry's global column index is below its row index, and its diagonal is positive.
All inputs are finite; a program needn't handle non-finite values. No bound on the sum of `arc_blocks` on one device may be relied on, other than what follows from the above.
Results may differ from a plain program's by a relative error of at most 0.000098.
Values sent between devices are 32-bit elements; how exact they have to be, the bound alone decides.
No kernel may reach another device: no remote copies, remote signals or barrier semaphores. Data moves between devices by JAX's collectives and lax.ppermute only.
A program may use at most 64 MiB of HBM per device.

v0:
```python
import functools

import jax
import jax.numpy as jnp
from jax import lax
from jax.experimental import pallas as pl
from jax.experimental.pallas import tpu as pltpu
from jax.sharding import Mesh
from jax.sharding import PartitionSpec as P

B = 256
P_SIZE = 4
ARC_ROWS = 128
NB = 128
SUB = 8
HIGHEST = lax.Precision.HIGHEST


def dot(left, right):
    return jnp.dot(left, right, precision=HIGHEST, preferred_element_type=jnp.float32)


def dot_t(left, right):
    return lax.dot_general(
        left, right, (((0,), (0,)), ((), ())), precision=HIGHEST, preferred_element_type=jnp.float32
    )


def inverse_factor(rows):
    n = NB // SUB
    tile = (SUB, NB)
    row_id = lax.broadcasted_iota(jnp.int32, tile, 0)
    col_id = lax.broadcasted_iota(jnp.int32, tile, 1)
    right = [jnp.where(row_id + r * SUB == col_id, 1.0, 0.0).astype(jnp.float32) for r in range(n)]
    for b in range(n):
        j = b * SUB
        head = rows[b]
        pivot = {}
        for k in range(SUB):
            for m in range(k, SUB):
                pivot[k, m] = jnp.broadcast_to(head[k : k + 1, j + m : j + m + 1], tile)
        scale = []
        for k in range(SUB):
            scale.append(lax.rsqrt(pivot[k, k]))
            for m in range(k + 1, SUB):
                pivot[k, m] = pivot[k, m] * scale[k]
            for m in range(k + 1, SUB):
                for q in range(m, SUB):
                    pivot[m, q] = pivot[m, q] - pivot[k, m] * pivot[k, q]
        top, top_right = [], []
        for k in range(SUB):
            here = jnp.broadcast_to(rows[b][k : k + 1, :], tile)
            there = jnp.broadcast_to(right[b][k : k + 1, :], tile)
            for m in range(k):
                here = here - pivot[m, k] * top[m]
                there = there - pivot[m, k] * top_right[m]
            top.append(here * scale[k])
            top_right.append(there * scale[k])
        strip = top_right[0]
        for k in range(1, SUB):
            strip = jnp.where(row_id == k, top_right[k], strip)
        for r in range(b + 1, n):
            left = []
            for k in range(SUB):
                part = jnp.broadcast_to(rows[r][:, j + k : j + k + 1], tile)
                for m in range(k):
                    part = part - pivot[m, k] * left[m]
                left.append(part * scale[k])
            body, body_right = rows[r], right[r]
            for k in range(SUB):
                body = body - left[k] * top[k]
                body_right = body_right - left[k] * top_right[k]
            rows[r], right[r] = body, body_right
        right[b] = strip
    return right


PAIRS = [(r, c) for r in range(P_SIZE) for c in range(r, P_SIZE)]
HALF = len(PAIRS) // 2
PIECES = 4 * P_SIZE


def split(value):
    high = value.astype(jnp.bfloat16)
    return high, (value - high.astype(jnp.float32)).astype(jnp.bfloat16)


def left_parts(value):
    high, low = split(value)
    return jnp.concatenate([high, high, low], axis=0)


def right_parts(value):
    high, low = split(value)
    return jnp.concatenate([high, low, high], axis=0)


def parts_dot(left, right):
    return lax.dot_general(
        left, right, (((0,), (0,)), ((), ())), preferred_element_type=jnp.float32
    )


def upper_products_kernel(place_ref, rows_ref, keep_ref, send_ref, work):
    side = place_ref[0]
    right = [right_parts(rows_ref[c]) for c in range(P_SIZE)]
    at = 0
    for r in range(P_SIZE):
        wide = jnp.concatenate(right[r:], axis=1)
        product = parts_dot(left_parts(rows_ref[r]), wide)
        for c in range(P_SIZE - r):
            work[at] = product[:, c * B : (c + 1) * B]
            at += 1
    for i in range(HALF):
        keep_ref[i] = work[side * HALF + i]
        send_ref[i] = work[(1 - side) * HALF + i]


def all_products_kernel(
    place_ref, left_ref, more_ref, right_ref, after_ref, keep_ref, send_ref, work
):
    del after_ref
    side = place_ref[0]
    right = jnp.concatenate([right_parts(right_ref[c]) for c in range(P_SIZE)], axis=1)
    for r in range(P_SIZE):
        left = left_ref[r] if r < P_SIZE // 2 else more_ref[r - P_SIZE // 2]
        product = parts_dot(left_parts(left), right)
        for b in range(P_SIZE):
            work[r, b] = product[:, b * B : (b + 1) * B]
    for a in range(2):
        keep_ref[a] = work[2 * a + side]
        send_ref[a] = work[2 * a + 1 - side]


def pass_kernel(value_ref, after_ref, out_ref):
    del after_ref
    out_ref[...] = value_ref[...]


def add_kernel(left_ref, right_ref, after_ref, out_ref):
    del after_ref
    out_ref[...] = left_ref[...] + right_ref[...]


def sum_kernel(parts_ref, after_ref, out_ref):
    del after_ref
    total = parts_ref[0]
    for i in range(1, parts_ref.shape[0]):
        total = total + parts_ref[i]
    out_ref[...] = total


def behind(value, after):
    (value,) = on_chip(pass_kernel, [value.shape], "behind", value, after=(after,))
    return value


def on_chip(kernel, shapes, name, *operands, scratch=(), scalars=0, after=()):
    return pl.pallas_call(
        kernel,
        out_shape=[jax.ShapeDtypeStruct(shape, jnp.float32) for shape in shapes],
        in_specs=[pl.BlockSpec(memory_space=pltpu.SMEM)] * scalars
        + [pl.BlockSpec(memory_space=pltpu.VMEM)] * (len(operands) - scalars)
        + [pl.BlockSpec(memory_space=pl.ANY)] * len(after),
        out_specs=[pl.BlockSpec(memory_space=pltpu.VMEM)] * len(shapes),
        scratch_shapes=list(scratch),
        compiler_params=pltpu.CompilerParams(vmem_limit_bytes=32 * 1024 * 1024),
        name=name,
    )(*operands, *after)


def collect_kernel(place_ref, mine_ref, other_ref, gram_ref):
    side, high, low = place_ref[0], place_ref[1], place_ref[2]
    at = high * P_SIZE + low
    rows = mine_ref.shape[1]
    for s in range(2):
        for p in range(PIECES // 2):
            start = ((s * PIECES) // 2 + p) * rows
            end = start + rows
            while start < end:
                block, first = start // B, start % B
                count = min(end - start, B - first)
                skip = rows - (end - start)

                @pl.when(side == s)
                def _(block=block, first=first, count=count, skip=skip, p=p):
                    gram_ref[block, first : first + count] = mine_ref[p ^ at, skip : skip + count]

                @pl.when(side != s)
                def _(block=block, first=first, count=count, skip=skip, p=p):
                    gram_ref[block, first : first + count] = other_ref[p ^ at, skip : skip + count]

                start += count


def factor_step_kernel(n, gram_ref, *rest):
    if n > 1:
        row_ref, inverse_ref, next_ref, work, inv = rest
    else:
        inverse_ref, work, inv = rest
    for c in range(n):
        work[:, c * B : (c + 1) * B] = gram_ref[c]
    width = n * B

    def step(b, carry):
        start = pl.multiple_of(b * NB, NB)
        rows = [
            work[pl.ds(pl.multiple_of(start + r * SUB, SUB), SUB), pl.ds(start, NB)]
            for r in range(NB // SUB)
        ]
        right = inverse_factor(rows)
        for r in range(NB // SUB):
            inv[pl.ds(pl.multiple_of(start + r * SUB, SUB), SUB), :] = right[r]

        @pl.when(b == 0)
        def _():
            panel = dot(inv[:NB, :], work[:NB, NB:])
            work[:NB, NB:] = panel
            work[NB:, NB:] = work[NB:, NB:] - dot_t(panel[:, :NB], panel)

        return carry

    lax.fori_loop(0, B // NB, step, 0)
    first, second = inv[:NB, :], inv[NB:, :]
    inverse_ref[:NB, :NB] = first
    inverse_ref[:NB, NB:] = jnp.zeros((NB, NB), jnp.float32)
    inverse_ref[NB:, :NB] = -dot(second, dot_t(work[:NB, NB:B], first))
    inverse_ref[NB:, NB:] = second
    if n > 1:
        work[NB:, B:] = dot(second, work[NB:, B:])
        row = work[:, B:]
        row_ref[...] = row
        at = n
        for r in range(1, n):
            left = row[:, (r - 1) * B : r * B]
            for c in range(r, n):
                next_ref[at - n] = gram_ref[at] - dot_t(left, row[:, (c - 1) * B : c * B])
                at += 1


def factor(gram):
    rows, inverses = [], []
    for n in range(P_SIZE, 0, -1):
        shapes = [(B, (n - 1) * B), (B, B), (n * (n - 1) // 2, B, B)] if n > 1 else [(B, B)]
        done = on_chip(
            functools.partial(factor_step_kernel, n),
            shapes,
            "factor_step",
            gram,
            scratch=[pltpu.VMEM((B, n * B), jnp.float32), pltpu.VMEM((B, NB), jnp.float32)],
        )
        if n > 1:
            row, inverse, gram = done
            rows.append(row)
        else:
            (inverse,) = done
        inverses.append(inverse)
    return rows, inverses


def solve_kernel(place_ref, *refs):
    rows, inverses = refs[: P_SIZE - 1], refs[P_SIZE - 1 : 2 * P_SIZE - 1]
    own_refs, out_ref, own_ref = refs[2 * P_SIZE - 1 : -2], refs[-2], refs[-1]
    row_index, col_index = 2 * place_ref[1] + place_ref[0], place_ref[3]
    for t in range(P_SIZE):
        own_ref[row_index ^ t] = own_refs[t][...]
    done = []
    for i in range(P_SIZE):
        block = own_ref[i]
        for k in range(i):
            off = (i - k - 1) * B
            block = block - dot_t(rows[k][:, off : off + B], done[k])
        block = dot(inverses[i][...], block)
        done.append(block)

        @pl.when(row_index == i)
        def _(block=block):
            rows_at = i * B + lax.broadcasted_iota(jnp.int32, block.shape, 0)
            cols_at = col_index * B + lax.broadcasted_iota(jnp.int32, block.shape, 1)
            out_ref[...] = jnp.where(cols_at >= rows_at, block, 0.0)


def from_first(value, n_hi):
    at = lax.axis_index("hi")
    have = 1
    while have < n_hi:
        more = min(have, n_hi - have)
        got = lax.ppermute(value, "hi", [(g, g + have) for g in range(more)])
        value = jnp.where(at < have, value, got)
        have += more
    return value


def exchange(value, high_bits, low_bits):
    bits = low_bits * 2 + high_bits
    return lax.ppermute(value, ("lo", "rh"), [(i, i ^ bits) for i in range(2 * P_SIZE)])


def swap(value):
    return lax.ppermute(value, "rl", [(0, 1), (1, 0)])


def spread(piece):
    y, z, x = (0, 1), (0, 2), (1, 0)
    by_z, by_y, by_x = exchange(piece, *z), exchange(piece, *y), exchange(piece, *x)
    by_zy, by_yx, by_xz = exchange(by_z, *y), exchange(by_y, *x), exchange(by_x, *z)
    by_zyx = exchange(by_zy, *x)
    return jnp.stack([piece, by_y, by_z, by_zy, by_x, by_yx, by_xz, by_zyx])


def on_device(r_slab, arc_rows, arc_blocks):
    n_hi = lax.axis_size("hi")
    low = lax.axis_index("lo")
    high_row, side = lax.axis_index("rh"), lax.axis_index("rl")
    col_index = lax.axis_index("hi") * P_SIZE + low
    row_index = high_row * 2 + side
    n_arcs, blocks_here = arc_blocks.shape
    columns = arc_rows.shape[1]
    live = arc_blocks.astype(jnp.float32)
    masked = (arc_rows.reshape(n_arcs, ARC_ROWS, blocks_here, B) * live[:, None, :, None]).reshape(
        arc_rows.shape
    )
    stacked = jnp.concatenate([r_slab, masked], axis=0)
    quarters = stacked.reshape(P_SIZE, stacked.shape[0] // P_SIZE, columns)
    quarters = lax.all_to_all(quarters, "lo", 0, 0)
    place = jnp.stack([side, high_row, low, col_index]).astype(jnp.int32)
    half_panels = P_SIZE // 2
    panels = from_first(quarters[:half_panels], n_hi)

    half = (HALF, B, B)
    keep, send = on_chip(
        upper_products_kernel,
        [half, half],
        "upper_products",
        place,
        quarters,
        scalars=1,
        scratch=[pltpu.VMEM((len(PAIRS), B, B), jnp.float32)],
    )
    gram = keep + swap(send)
    gram = lax.all_to_all(gram.reshape(2 * P_SIZE, -1, B), ("rh", "lo"), 0, 0).sum(axis=0)
    piece = from_first(gram, n_hi)
    more_panels = from_first(behind(quarters[half_panels:], piece), n_hi)
    pieces = spread(piece)
    (gram,) = on_chip(
        collect_kernel, [(len(PAIRS), B, B)], "collect", place, pieces, swap(pieces), scalars=1
    )

    half = (2, P_SIZE, B, B)
    keep, send = on_chip(
        all_products_kernel,
        [half, half],
        "all_products",
        place,
        panels,
        more_panels,
        quarters,
        scalars=1,
        scratch=[pltpu.VMEM((P_SIZE, P_SIZE, B, B), jnp.float32)],
        after=(pieces,),
    )
    (cross,) = on_chip(add_kernel, [half], "add_pair", keep, swap(send), after=(gram,))
    cross = lax.all_to_all(cross.reshape(2 * P_SIZE, B, B), ("rh", "lo"), 0, 0)
    rows, inverses = factor(gram)
    (mine,) = on_chip(sum_kernel, [(B, columns)], "sum_places", cross, after=(rows[1],))
    by_x = exchange(mine, 1, 0)
    own = [mine, swap(mine), by_x, swap(by_x)]

    (result,) = on_chip(
        solve_kernel,
        [(B, columns)],
        "solve",
        place,
        *rows,
        *inverses,
        *own,
        scalars=1,
        scratch=[pltpu.VMEM((P_SIZE, B, columns), jnp.float32)],
    )
    return result


def solution(mesh):
    n_col, n_row = mesh.shape["col"], mesh.shape["row"]
    split = Mesh(
        mesh.devices.reshape(n_col // P_SIZE, P_SIZE, n_row // 2, 2),
        ("hi", "lo", "rh", "rl"),
    )
    spec = P(("rh", "rl"), ("hi", "lo"))
    return jax.shard_map(
        on_device,
        mesh=split,
        in_specs=(spec, spec, spec),
        out_specs=spec,
        check_vma=False,
    )
```

profile of v0, /device:TPU:9, one launch (start us, length us, event | category | flops | bytes accessed | tf_op | source)
XLA Modules:
  0.0 189.3 jit_solution(8847597526033734172)
XLA Ops:
  0.0 0.7 convert_bitcast_fusion
  0.8 1.4 broadcast_multiply_fusion
  2.2 1.2 pad_maximum_fusion
  3.4 3.7 %all-to-all-start = ((f32[4,320,256]{2,1,0:T(8,128)}), f32[4,320,256]{2,1,0:T(8,128)S(1)}, u32[]{:S(2)}, u32[]{:S(2)}) async-start(f32[4,320,256]{2,1,0:T(8,128)} %bitcast.6), calls=%async_computation | async-start | bytes 2621440 | tf_op jit(solution)/shard_map/all_to_all | solution.py:325
  7.1 0.1 pad_add_fusion.place_ref
  7.2 16.5 %all-to-all-done.rows_ref.right_ref = f32[4,320,256]{2,1,0:T(8,128)S(1)} async-done(((f32[4,320,256]{2,1,0:T(8,128)}), f32[4,320,256]{2,1,0:T(8,128)S(1)}, u32[]{:S(2)}, u32[]{:S(2)}) %all-to-all-start) | async-done | bytes 1310752 | tf_op jit(solution)/shard_map/all_to_all | solution.py:325
  23.7 2.3 %upper_products.1 = (f32[5,256,256]{2,1,0:T(8,128)S(1)}, f32[5,256,256]{2,1,0:T(8,128)S(1)}) custom-call(s32[4]{0:T(128)S(1)} %pad_add_fusion.place_ref, f32[4,320,256]{2,1,0:T(8,128)S(1)} %all-to-all-done.rows_ref.right_ref), custom_call_target="tpu_custom_call" | custom-call | tf_op jit(solution)/shard_map/upper_products/pallas_call | solution.py:159
  25.9 0.6 collective-permute-start
  26.5 2.7 %collective-permute-done = f32[5,256,256]{2,1,0:T(8,128)S(1)} collective-permute-done((f32[5,256,256]{2,1,0:T(8,128)S(1)}, f32[5,256,256]{2,1,0:T(8,128)S(1)}, u32[]{:S(2)}, u32[]{:S(2)}) %collective-permute-start) | collective-permute-done | bytes 1310752 | tf_op jit(solution)/shard_map/ppermute | solution.py:300
  29.2 1.3 add.7
  30.4 3.8 %all-to-all-start.1 = ((f32[8,160,256]{2,1,0:T(8,128)}), f32[8,160,256]{2,1,0:T(8,128)S(1)}, u32[]{:S(2)}, u32[]{:S(2)}) async-start(f32[8,160,256]{2,1,0:T(8,128)} %bitcast.28), calls=%async_computation.1 | async-start | bytes 2621440 | tf_op jit(solution)/shard_map/all_to_all | solution.py:341
  34.3 5.1 %collective-permute-start.10 = (f32[2,320,256]{2,1,0:T(8,128)S(1)}, f32[2,320,256]{2,1,0:T(8,128)}, u32[]{:S(2)}, u32[]{:S(2)}) collective-permute-start(f32[2,320,256]{2,1,0:T(8,128)S(1)} %slice.8), channel_id=1, source_target_pairs={{0,16},{1,17},{2,18},{3,19},{4,20},{5,21},{6,22},{7,23},{8,24},{9,... | collective-permute-start | bytes 1966088 | tf_op jit(solution)/shard_map/ppermute | solution.py:288
  39.4 13.6 %all-to-all-done.1 = f32[8,160,256]{2,1,0:T(8,128)S(1)} async-done(((f32[8,160,256]{2,1,0:T(8,128)}), f32[8,160,256]{2,1,0:T(8,128)S(1)}, u32[]{:S(2)}, u32[]{:S(2)}) %all-to-all-start.1) | async-done | bytes 1310752 | tf_op jit(solution)/shard_map/all_to_all | solution.py:341
  53.0 0.8 reduce_sum.9
  53.7 12.3 %collective-permute-start.1 = (f32[160,256]{1,0:T(8,128)}, f32[160,256]{1,0:T(8,128)S(1)}, u32[]{:S(2)}, u32[]{:S(2)}) collective-permute-start(f32[160,256]{1,0:T(8,128)} %reduce_sum.9), channel_id=1, source_target_pairs={{0,16},{1,17},{2,18},{3,19},{4,20},{5,21},{6,22},{7,23},{8,24},{9,... | collective-permute-start | bytes 491528 | tf_op jit(solution)/shard_map/ppermute | solution.py:288
  66.0 7.0 %collective-permute-done.1 = f32[160,256]{1,0:T(8,128)S(1)} collective-permute-done((f32[160,256]{1,0:T(8,128)}, f32[160,256]{1,0:T(8,128)S(1)}, u32[]{:S(2)}, u32[]{:S(2)}) %collective-permute-start.1) | collective-permute-done | bytes 163872 | tf_op jit(solution)/shard_map/ppermute | solution.py:288
  73.0 0.9 bitcast_dynamic-update-slice_fusion.7
  73.9 1.3 collective-permute-start.2
  75.2 0.1 fusion
  75.3 1.3 collective-permute-start.5
  76.7 5.1 %collective-permute-start.11 = (f32[2,320,256]{2,1,0:T(8,128)S(1)}, f32[2,320,256]{2,1,0:T(8,128)S(1)}, u32[]{:S(2)}, u32[]{:S(2)}) collective-permute-start(f32[2,320,256]{2,1,0:T(8,128)S(1)} %behind.1), channel_id=1, source_target_pairs={{0,16},{1,17},{2,18},{3,19},{4,20},{5,21},{6,22},{7,23},{8,24},{9,... | collective-permute-start | bytes 1966088 | tf_op jit(solution)/shard_map/ppermute | solution.py:288
  81.8 0.3 collective-permute-start.4
  82.1 0.2 collective-permute-start.6
  82.4 1.5 collective-permute-start.7
  83.9 2.1 %collective-permute-done.4 = f32[160,256]{1,0:T(8,128)S(1)} collective-permute-done((f32[160,256]{1,0:T(8,128)S(1)}, f32[160,256]{1,0:T(8,128)S(1)}, u32[]{:S(2)}, u32[]{:S(2)}) %collective-permute-start.4) | collective-permute-done | bytes 163872 | tf_op jit(solution)/shard_map/ppermute | solution.py:296
  86.0 0.2 collective-permute-start.8
  86.3 12.4 %collective-permute-done.7 = f32[160,256]{1,0:T(8,128)S(1)} collective-permute-done((f32[160,256]{1,0:T(8,128)S(1)}, f32[160,256]{1,0:T(8,128)S(1)}, u32[]{:S(2)}, u32[]{:S(2)}) %collective-permute-start.7) | collective-permute-done | bytes 163872 | tf_op jit(solution)/shard_map/ppermute | solution.py:296
  98.8 10.2 %collective-permute-done.11 = f32[2,320,256]{2,1,0:T(8,128)S(1)} collective-permute-done((f32[2,320,256]{2,1,0:T(8,128)S(1)}, f32[2,320,256]{2,1,0:T(8,128)S(1)}, u32[]{:S(2)}, u32[]{:S(2)}) %collective-permute-start.11) | collective-permute-done | bytes 655392 | tf_op jit(solution)/shard_map/ppermute | solution.py:288
  109.0 0.1 broadcast_select_fusion.more_ref
  109.1 3.2 %all_products.1 = (f32[2,4,256,256]{3,2,1,0:T(8,128)S(1)}, f32[2,4,256,256]{3,2,1,0:T(8,128)S(1)}) custom-call(s32[4]{0:T(128)S(1)} %pad_add_fusion.place_ref, f32[2,320,256]{2,1,0:T(8,128)S(1)} %get-tuple-element.34.left_ref, f32[2,320,256]{2,1,0:T(8,128)S(1)} %broadcast_select_fusion.more_ref, f32[4,320,256]{2,1,0:T(8,128)S(1)} %all-to-all-done.rows_ref.right_ref, ...), custom_call_target="tpu_custom_call" | custom-call | tf_op jit(solution)/shard_map/all_products/pallas_call | solution.py:159
  112.3 1.8 collective-permute-start.12
  114.1 0.1 collective-permute-start.9
  114.2 5.6 %collective-permute-done.9.other_ref = f32[8,160,256]{2,1,0:T(8,128)S(1)} collective-permute-done((f32[8,160,256]{2,1,0:T(8,128)S(1)}, f32[8,160,256]{2,1,0:T(8,128)S(1)}, u32[]{:S(2)}, u32[]{:S(2)}) %collective-permute-start.9) | collective-permute-done | bytes 1310752 | tf_op jit(solution)/shard_map/ppermute | solution.py:300
  119.8 0.9 collect.1.gram_ref.after_ref
  120.6 0.2 add_pair.1
  120.9 1.3 copy-done
  122.2 4.5 %all-to-all-start.2 = ((f32[8,256,256]{2,1,0:T(8,128)}), f32[8,256,256]{2,1,0:T(8,128)}, u32[]{:S(2)}, u32[]{:S(2)}) async-start(f32[8,256,256]{2,1,0:T(8,128)} %bitcast.27), calls=%async_computation.2 | async-start | bytes 4194304 | tf_op jit(solution)/shard_map/all_to_all | solution.py:363
  126.7 11.2 %factor_step.4 = (f32[256,768]{1,0:T(8,128)S(1)}, f32[256,256]{1,0:T(8,128)S(1)}, f32[6,256,256]{2,1,0:T(8,128)S(1)}) custom-call(f32[10,256,256]{2,1,0:T(8,128)S(1)} %collect.1.gram_ref.after_ref), custom_call_target="tpu_custom_call" | custom-call | tf_op jit(solution)/shard_map/factor_step/pallas_call | solution.py:159
  137.9 0.7 copy-done.1
  138.6 10.5 %factor_step.5 = (f32[256,512]{1,0:T(8,128)S(1)}, f32[256,256]{1,0:T(8,128)S(1)}, f32[3,256,256]{2,1,0:T(8,128)S(1)}) custom-call(f32[6,256,256]{2,1,0:T(8,128)S(1)} %get-tuple-element.21.gram_ref), custom_call_target="tpu_custom_call" | custom-call | tf_op jit(solution)/shard_map/factor_step/pallas_call | solution.py:159
  149.1 5.1 %all-to-all-done.2.parts_ref = f32[8,256,256]{2,1,0:T(8,128)} async-done(((f32[8,256,256]{2,1,0:T(8,128)}), f32[8,256,256]{2,1,0:T(8,128)}, u32[]{:S(2)}, u32[]{:S(2)}) %all-to-all-start.2) | async-done | bytes 2097184 | tf_op jit(solution)/shard_map/all_to_all | solution.py:363
  154.2 1.7 sum_places.1.refs_7_
  155.9 0.6 collective-permute-start.13
  156.5 6.8 %collective-permute-done.14.refs_9_ = f32[256,256]{1,0:T(8,128)S(1)} collective-permute-done((f32[256,256]{1,0:T(8,128)S(1)}, f32[256,256]{1,0:T(8,128)S(1)}, u32[]{:S(2)}, u32[]{:S(2)}) %collective-permute-start.14) | collective-permute-done | bytes 262176 | tf_op jit(solution)/shard_map/ppermute | solution.py:296
  163.4 1.3 collective-permute-start.15
  164.7 9.8 %factor_step.6 = (f32[256,256]{1,0:T(8,128)S(1)}, f32[256,256]{1,0:T(8,128)S(1)}, f32[1,256,256]{2,1,0:T(8,128)S(1)}) custom-call(f32[3,256,256]{2,1,0:T(8,128)S(1)} %get-tuple-element.23.gram_ref), custom_call_target="tpu_custom_call" | custom-call | tf_op jit(solution)/shard_map/factor_step/pallas_call | solution.py:159
  174.4 9.1 %factor_step.7.refs_6_ = f32[256,256]{1,0:T(8,128)S(1)} custom-call(f32[1,256,256]{2,1,0:T(8,128)S(1)} %get-tuple-element.28.gram_ref), custom_call_target="tpu_custom_call" | custom-call | tf_op jit(solution)/shard_map/factor_step/pallas_call | solution.py:159
  183.6 5.8 %solve.1 = f32[256,256]{1,0:T(8,128)} custom-call(s32[4]{0:T(128)S(1)} %pad_add_fusion.place_ref, f32[256,768]{1,0:T(8,128)S(1)} %get-tuple-element.20.refs_0_, f32[256,512]{1,0:T(8,128)S(1)} %get-tuple-element.22.after_ref.refs_1_, f32[256,256]{1,0:T(8,128)S(1)} %get-tuple-element.24.refs_2_, f32[256,256]{1,0:T(8,128)S(1)} %copy-done.2, ...), custom_call_target="tpu_custom_call" | custom-call | tf_op jit(solution)/shard_map/solve/pallas_call | solution.py:159
  (27 shorter events, 0.4 us)
Async XLA Ops:
  0.0 2.2 %copy-start.3 = (f32[256,256]{1,0:T(8,128)S(1)}, f32[256,256]{1,0:T(8,128)}, u32[]{:S(2)}) copy-start(f32[256,256]{1,0:T(8,128)} %param.3) | copy-start | bytes 786436
  3.4 20.3 %all-to-all-start = ((f32[4,320,256]{2,1,0:T(8,128)}), f32[4,320,256]{2,1,0:T(8,128)S(1)}, u32[]{:S(2)}, u32[]{:S(2)}) async-start(f32[4,320,256]{2,1,0:T(8,128)} %bitcast.6), calls=%async_computation | async-start | bytes 2621440 | tf_op jit(solution)/shard_map/all_to_all | solution.py:325
  25.9 3.2 %collective-permute-start = (f32[5,256,256]{2,1,0:T(8,128)S(1)}, f32[5,256,256]{2,1,0:T(8,128)S(1)}, u32[]{:S(2)}, u32[]{:S(2)}) collective-permute-start(f32[5,256,256]{2,1,0:T(8,128)S(1)} %get-tuple-element.19), channel_id=1, source_target_pairs={{0,1},{1,0},{2,3},{3,2},{4,5},{5,4},{6,7},{7,6},{8,9},{9,8},{10,11... | collective-permute-start | bytes 3932168 | tf_op jit(solution)/shard_map/ppermute | solution.py:300
  30.4 22.5 %all-to-all-start.1 = ((f32[8,160,256]{2,1,0:T(8,128)}), f32[8,160,256]{2,1,0:T(8,128)S(1)}, u32[]{:S(2)}, u32[]{:S(2)}) async-start(f32[8,160,256]{2,1,0:T(8,128)} %bitcast.28), calls=%async_computation.1 | async-start | bytes 2621440 | tf_op jit(solution)/shard_map/all_to_all | solution.py:341
  34.3 40.9 %collective-permute-start.10 = (f32[2,320,256]{2,1,0:T(8,128)S(1)}, f32[2,320,256]{2,1,0:T(8,128)}, u32[]{:S(2)}, u32[]{:S(2)}) collective-permute-start(f32[2,320,256]{2,1,0:T(8,128)S(1)} %slice.8), channel_id=1, source_target_pairs={{0,16},{1,17},{2,18},{3,19},{4,20},{5,21},{6,22},{7,23},{8,24},{9,... | collective-permute-start | bytes 1966088 | tf_op jit(solution)/shard_map/ppermute | solution.py:288
  53.7 19.2 %collective-permute-start.1 = (f32[160,256]{1,0:T(8,128)}, f32[160,256]{1,0:T(8,128)S(1)}, u32[]{:S(2)}, u32[]{:S(2)}) collective-permute-start(f32[160,256]{1,0:T(8,128)} %reduce_sum.9), channel_id=1, source_target_pairs={{0,16},{1,17},{2,18},{3,19},{4,20},{5,21},{6,22},{7,23},{8,24},{9,... | collective-permute-start | bytes 491528 | tf_op jit(solution)/shard_map/ppermute | solution.py:288
  73.9 8.2 %collective-permute-start.2 = (f32[160,256]{1,0:T(8,128)S(1)}, f32[160,256]{1,0:T(8,128)S(1)}, u32[]{:S(2)}, u32[]{:S(2)}) collective-permute-start(f32[160,256]{1,0:T(8,128)S(1)} %get-tuple-element.32.after_ref), channel_id=1, source_target_pairs={{0,4},{2,6},{4,0},{6,2},{8,12},{10,14},{12,8},{14,10},{1,5},{3,7},... | collective-permute-start | bytes 491528 | tf_op jit(solution)/shard_map/ppermute | solution.py:296
  75.2 6.6 %collective-permute-start.3 = (f32[160,256]{1,0:T(8,128)S(1)}, f32[160,256]{1,0:T(8,128)S(1)}, u32[]{:S(2)}, u32[]{:S(2)}) collective-permute-start(f32[160,256]{1,0:T(8,128)S(1)} %get-tuple-element.32.after_ref), channel_id=1, source_target_pairs={{0,8},{2,10},{4,12},{6,14},{8,0},{10,2},{12,4},{14,6},{1,9},{3,11}... | collective-permute-start | bytes 491528 | tf_op jit(solution)/shard_map/ppermute | solution.py:296
  75.3 7.1 %collective-permute-start.5 = (f32[160,256]{1,0:T(8,128)S(1)}, f32[160,256]{1,0:T(8,128)S(1)}, u32[]{:S(2)}, u32[]{:S(2)}) collective-permute-start(f32[160,256]{1,0:T(8,128)S(1)} %get-tuple-element.32.after_ref), channel_id=1, source_target_pairs={{0,2},{2,0},{4,6},{6,4},{8,10},{10,8},{12,14},{14,12},{1,3},{3,1},... | collective-permute-start | bytes 491528 | tf_op jit(solution)/shard_map/ppermute | solution.py:296
  76.7 32.3 %collective-permute-start.11 = (f32[2,320,256]{2,1,0:T(8,128)S(1)}, f32[2,320,256]{2,1,0:T(8,128)S(1)}, u32[]{:S(2)}, u32[]{:S(2)}) collective-permute-start(f32[2,320,256]{2,1,0:T(8,128)S(1)} %behind.1), channel_id=1, source_target_pairs={{0,16},{1,17},{2,18},{3,19},{4,20},{5,21},{6,22},{7,23},{8,24},{9,... | collective-permute-start | bytes 1966088 | tf_op jit(solution)/shard_map/ppermute | solution.py:288
  81.8 4.2 %collective-permute-start.4 = (f32[160,256]{1,0:T(8,128)S(1)}, f32[160,256]{1,0:T(8,128)S(1)}, u32[]{:S(2)}, u32[]{:S(2)}) collective-permute-start(f32[160,256]{1,0:T(8,128)S(1)} %collective-permute-done.3), channel_id=1, source_target_pairs={{0,4},{2,6},{4,0},{6,2},{8,12},{10,14},{12,8},{14,10},{1,5},{3,7},... | collective-permute-start | bytes 491528 | tf_op jit(solution)/shard_map/ppermute | solution.py:296
  82.1 4.2 %collective-permute-start.6 = (f32[160,256]{1,0:T(8,128)S(1)}, f32[160,256]{1,0:T(8,128)S(1)}, u32[]{:S(2)}, u32[]{:S(2)}) collective-permute-start(f32[160,256]{1,0:T(8,128)S(1)} %collective-permute-done.2), channel_id=1, source_target_pairs={{0,2},{2,0},{4,6},{6,4},{8,10},{10,8},{12,14},{14,12},{1,3},{3,1},... | collective-permute-start | bytes 491528 | tf_op jit(solution)/shard_map/ppermute | solution.py:296
  82.4 16.4 %collective-permute-start.7 = (f32[160,256]{1,0:T(8,128)S(1)}, f32[160,256]{1,0:T(8,128)S(1)}, u32[]{:S(2)}, u32[]{:S(2)}) collective-permute-start(f32[160,256]{1,0:T(8,128)S(1)} %collective-permute-done.5), channel_id=1, source_target_pairs={{0,8},{2,10},{4,12},{6,14},{8,0},{10,2},{12,4},{14,6},{1,9},{3,11}... | collective-permute-start | bytes 491528 | tf_op jit(solution)/shard_map/ppermute | solution.py:296
  86.0 12.7 %collective-permute-start.8 = (f32[160,256]{1,0:T(8,128)S(1)}, f32[160,256]{1,0:T(8,128)S(1)}, u32[]{:S(2)}, u32[]{:S(2)}) collective-permute-start(f32[160,256]{1,0:T(8,128)S(1)} %collective-permute-done.4), channel_id=1, source_target_pairs={{0,2},{2,0},{4,6},{6,4},{8,10},{10,8},{12,14},{14,12},{1,3},{3,1},... | collective-permute-start | bytes 491528 | tf_op jit(solution)/shard_map/ppermute | solution.py:296
  112.3 8.3 %collective-permute-start.12 = (f32[2,4,256,256]{3,2,1,0:T(8,128)S(1)}, f32[2,4,256,256]{3,2,1,0:T(8,128)S(1)}, u32[]{:S(2)}, u32[]{:S(2)}) collective-permute-start(f32[2,4,256,256]{3,2,1,0:T(8,128)S(1)} %get-tuple-element.30), channel_id=1, source_target_pairs={{0,1},{1,0},{2,3},{3,2},{4,5},{5,4},{6,7},{7,6},{8,9},{9,8},{10,11... | collective-permute-start | bytes 6291464 | tf_op jit(solution)/shard_map/ppermute | solution.py:300
  114.1 5.7 %collective-permute-start.9 = (f32[8,160,256]{2,1,0:T(8,128)S(1)}, f32[8,160,256]{2,1,0:T(8,128)S(1)}, u32[]{:S(2)}, u32[]{:S(2)}) collective-permute-start(f32[8,160,256]{2,1,0:T(8,128)S(1)} %bitcast_dynamic-update-slice_fusion.mine_ref.after_ref), channel_id=1, source_target_pairs={{0,1},{1,0},{2,3},{3,2},{4,5},{5,4},{6,7},{7,6},{8,9},{9,8},{10,11... | collective-permute-start | bytes 3932168 | tf_op jit(solution)/shard_map/ppermute | solution.py:300
  120.9 1.3 copy-start
  122.2 32.0 %all-to-all-start.2 = ((f32[8,256,256]{2,1,0:T(8,128)}), f32[8,256,256]{2,1,0:T(8,128)}, u32[]{:S(2)}, u32[]{:S(2)}) async-start(f32[8,256,256]{2,1,0:T(8,128)} %bitcast.27), calls=%async_computation.2 | async-start | bytes 4194304 | tf_op jit(solution)/shard_map/all_to_all | solution.py:363
  137.9 0.7 copy-start.1
  155.9 27.7 %copy-start.2 = (f32[256,256]{1,0:T(8,128)S(1)}, f32[256,256]{1,0:T(8,128)}, u32[]{:S(2)}) copy-start(f32[256,256]{1,0:T(8,128)} %copy-done.1) | copy-start | bytes 786436
  155.9 7.5 %collective-permute-start.14 = (f32[256,256]{1,0:T(8,128)S(1)}, f32[256,256]{1,0:T(8,128)S(1)}, u32[]{:S(2)}, u32[]{:S(2)}) collective-permute-start(f32[256,256]{1,0:T(8,128)S(1)} %sum_places.1.refs_7_), channel_id=1, source_target_pairs={{0,2},{2,0},{4,6},{6,4},{8,10},{10,8},{12,14},{14,12},{1,3},{3,1},... | collective-permute-start | bytes 786440 | tf_op jit(solution)/shard_map/ppermute | solution.py:296
  155.9 27.6 %collective-permute-start.13 = (f32[256,256]{1,0:T(8,128)S(1)}, f32[256,256]{1,0:T(8,128)S(1)}, u32[]{:S(2)}, u32[]{:S(2)}) collective-permute-start(f32[256,256]{1,0:T(8,128)S(1)} %sum_places.1.refs_7_), channel_id=1, source_target_pairs={{0,1},{1,0},{2,3},{3,2},{4,5},{5,4},{6,7},{7,6},{8,9},{9,8},{10,11... | collective-permute-start | bytes 786440 | tf_op jit(solution)/shard_map/ppermute | solution.py:300
  163.4 20.2 %collective-permute-start.15 = (f32[256,256]{1,0:T(8,128)S(1)}, f32[256,256]{1,0:T(8,128)S(1)}, u32[]{:S(2)}, u32[]{:S(2)}) collective-permute-start(f32[256,256]{1,0:T(8,128)S(1)} %collective-permute-done.14.refs_9_), channel_id=1, source_target_pairs={{0,1},{1,0},{2,3},{3,2},{4,5},{5,4},{6,7},{7,6},{8,9},{9,8},{10,11... | collective-permute-start | bytes 786440 | tf_op jit(solution)/shard_map/ppermute | solution.py:300
where the time goes:
time: 192 us; the launch traced here: 189 us
  waiting for transfers between devices  81.9 us (43%)
  Pallas kernels  54.6 us (28%)
  starting transfers between devices  43.7 us (23%)
  other arithmetic  6.54 us (3%)
  local copies, waits for them, and re-layouts  2.2 us (1%)
    pallas_call x11, Pallas kernels, on_chip(): pl.pallas_call(kernel, out_shape=[jax.ShapeDtypeStruct(shape, jnp.float32...  54.6 us
    ppermute x3, starting transfers between devices, from_first(): got = lax.ppermute(value, 'hi', [(g, g + have) for g in range(more)])  22.5 us
    ppermute x8, waiting for transfers between devices, exchange(): lax.ppermute(value, ('lo', 'rh'), [(i, i ^ bits) for i in range(2 * P_SIZ...  21.4 us
    ppermute x3, waiting for transfers between devices, from_first(): got = lax.ppermute(value, 'hi', [(g, g + have) for g in range(more)])  17.1 us
    all_to_all x1, waiting for transfers between devices, on_device(): quarters = lax.all_to_all(quarters, 'lo', 0, 0)  16.5 us
    all_to_all x1, waiting for transfers between devices, on_device(): lax.all_to_all(gram.reshape(2 * P_SIZE, -1, B), ('rh', 'lo'), 0, 0)  13.6 us
    ppermute x5, waiting for transfers between devices, swap(): return lax.ppermute(value, 'rl', [(0, 1), (1, 0)])  8.25 us
    all_to_all x1, waiting for transfers between devices, on_device(): cross = lax.all_to_all(cross.reshape(2 * P_SIZE, B, B), ('rh', 'lo'), 0, 0)  5.06 us
  transfers between devices with their start and end apart: 19, of which 10 were waited for; matrix products, arithmetic and copies ran while one was open for 1% of the time, Pallas kernels for 22%

commit v1 on v0

--- a/solution.py
+++ b/solution.py
@@ -116,25 +116,18 @@
         send_ref[i] = work[(1 - side) * HALF + i]
 
 
-def all_products_kernel(
-    place_ref, left_ref, more_ref, right_ref, after_ref, keep_ref, send_ref, work
-):
+def all_products_kernel(place_ref, left_ref, right_ref, after_ref, keep_ref, send_ref, work):
     del after_ref
     side = place_ref[0]
-    right = jnp.concatenate([right_parts(right_ref[c]) for c in range(P_SIZE)], axis=1)
+    first = right_ref.shape[0] - P_SIZE
+    right = jnp.concatenate([right_parts(right_ref[first + c]) for c in range(P_SIZE)], axis=1)
     for r in range(P_SIZE):
-        left = left_ref[r] if r < P_SIZE // 2 else more_ref[r - P_SIZE // 2]
-        product = parts_dot(left_parts(left), right)
+        product = parts_dot(left_parts(left_ref[r]), right)
         for b in range(P_SIZE):
             work[r, b] = product[:, b * B : (b + 1) * B]
     for a in range(2):
         keep_ref[a] = work[2 * a + side]
         send_ref[a] = work[2 * a + 1 - side]
-
-
-def pass_kernel(value_ref, after_ref, out_ref):
-    del after_ref
-    out_ref[...] = value_ref[...]
 
 
 def add_kernel(left_ref, right_ref, after_ref, out_ref):
@@ -148,11 +141,6 @@
     for i in range(1, parts_ref.shape[0]):
         total = total + parts_ref[i]
     out_ref[...] = total
-
-
-def behind(value, after):
-    (value,) = on_chip(pass_kernel, [value.shape], "behind", value, after=(after,))
-    return value
 
 
 def on_chip(kernel, shapes, name, *operands, scratch=(), scalars=0, after=()):
@@ -164,7 +152,7 @@
         + [pl.BlockSpec(memory_space=pl.ANY)] * len(after),
         out_specs=[pl.BlockSpec(memory_space=pltpu.VMEM)] * len(shapes),
         scratch_shapes=list(scratch),
-        compiler_params=pltpu.CompilerParams(vmem_limit_bytes=32 * 1024 * 1024),
+        compiler_params=pltpu.CompilerParams(vmem_limit_bytes=16 * 1024 * 1024),
         name=name,
     )(*operands, *after)
 
@@ -260,10 +248,21 @@
 
 def solve_kernel(place_ref, *refs):
     rows, inverses = refs[: P_SIZE - 1], refs[P_SIZE - 1 : 2 * P_SIZE - 1]
-    own_refs, out_ref, own_ref = refs[2 * P_SIZE - 1 : -2], refs[-2], refs[-1]
+    gram_ref, own_refs, out_ref, own_ref = refs[-P_SIZE - 3], refs[-P_SIZE - 2 : -2], refs[-2], refs[-1]
     row_index, col_index = 2 * place_ref[1] + place_ref[0], place_ref[3]
-    for t in range(P_SIZE):
-        own_ref[row_index ^ t] = own_refs[t][...]
+
+    @pl.when(col_index >= P_SIZE)
+    def _():
+        for t in range(P_SIZE):
+            own_ref[row_index ^ t] = own_refs[t][...]
+
+    for c in range(P_SIZE):
+
+        @pl.when(col_index == c)
+        def _(c=c):
+            for r in range(P_SIZE):
+                own_ref[r] = gram_ref[PAIRS.index((min(r, c), c))]
+
     done = []
     for i in range(P_SIZE):
         block = own_ref[i]
@@ -296,8 +295,8 @@
     return lax.ppermute(value, ("lo", "rh"), [(i, i ^ bits) for i in range(2 * P_SIZE)])
 
 
-def swap(value):
-    return lax.ppermute(value, "rl", [(0, 1), (1, 0)])
+def swap(value, axis="rl"):
+    return lax.ppermute(value, axis, [(0, 1), (1, 0)])
 
 
 def spread(piece):
@@ -321,11 +320,13 @@
         arc_rows.shape
     )
     stacked = jnp.concatenate([r_slab, masked], axis=0)
-    quarters = stacked.reshape(P_SIZE, stacked.shape[0] // P_SIZE, columns)
-    quarters = lax.all_to_all(quarters, "lo", 0, 0)
     place = jnp.stack([side, high_row, low, col_index]).astype(jnp.int32)
-    half_panels = P_SIZE // 2
-    panels = from_first(quarters[:half_panels], n_hi)
+    in_two = n_hi == 2
+    owners = ("hi", "lo") if in_two else ("lo",)
+    shares = P_SIZE * n_hi if in_two else P_SIZE
+    blocks = stacked.reshape(shares, stacked.shape[0] // shares, columns)
+    blocks = lax.all_to_all(blocks, owners, 0, 0)
+    panels = blocks if in_two else from_first(blocks, n_hi)
 
     half = (HALF, B, B)
     keep, send = on_chip(
@@ -333,14 +334,13 @@
         [half, half],
         "upper_products",
         place,
-        quarters,
+        blocks,
         scalars=1,
         scratch=[pltpu.VMEM((len(PAIRS), B, B), jnp.float32)],
     )
     gram = keep + swap(send)
     gram = lax.all_to_all(gram.reshape(2 * P_SIZE, -1, B), ("rh", "lo"), 0, 0).sum(axis=0)
-    piece = from_first(gram, n_hi)
-    more_panels = from_first(behind(quarters[half_panels:], piece), n_hi)
+    piece = gram + swap(gram, "hi") if in_two else from_first(gram, n_hi)
     pieces = spread(piece)
     (gram,) = on_chip(
         collect_kernel, [(len(PAIRS), B, B)], "collect", place, pieces, swap(pieces), scalars=1
@@ -353,8 +353,7 @@
         "all_products",
         place,
         panels,
-        more_panels,
-        quarters,
+        blocks,
         scalars=1,
         scratch=[pltpu.VMEM((P_SIZE, P_SIZE, B, B), jnp.float32)],
         after=(pieces,),
@@ -362,7 +361,9 @@
     (cross,) = on_chip(add_kernel, [half], "add_pair", keep, swap(send), after=(gram,))
     cross = lax.all_to_all(cross.reshape(2 * P_SIZE, B, B), ("rh", "lo"), 0, 0)
     rows, inverses = factor(gram)
-    (mine,) = on_chip(sum_kernel, [(B, columns)], "sum_places", cross, after=(rows[1],))
+    (mine,) = on_chip(sum_kernel, [(B, columns)], "sum_places", cross, after=(rows[2],))
+    if in_two:
+        mine = mine + swap(mine, "hi")
     by_x = exchange(mine, 1, 0)
     own = [mine, swap(mine), by_x, swap(by_x)]
 
@@ -373,6 +374,7 @@
         place,
         *rows,
         *inverses,
+        gram,
         *own,
         scalars=1,
         scratch=[pltpu.VMEM((P_SIZE, B, columns), jnp.float32)],

time: 192 us -> 184 us (0.958)
  blocking collectives: 0 us -> 21.8 us
  starting transfers between devices: 43.7 us -> 26.3 us
  waiting for transfers between devices: 81.9 us -> 71.3 us
  local copies, waits for them, and re-layouts: 2.2 us -> 5.24 us
  other arithmetic: 6.54 us -> 3.68 us
    all_to_all x0 -> x1, blocking collectives: none -> 21.8 us  [on_device(): lax.all_to_all(gram.reshape(2 * P_SIZE, -1, B), ('rh', 'lo'), 0, 0)]
    ppermute x8 -> x7, starting transfers between devices: 26.8 us -> 7.7 us  [swap(): return lax.ppermute(value, axis, [(0, 1), (1, 0)])]
    all_to_all x1, waiting for transfers between devices: 5.06 us -> 0.01 us  [on_device(): cross = lax.all_to_all(cross.reshape(2 * P_SIZE, B, B), ('rh', 'lo'), 0, 0)]
    ppermute x8, waiting for transfers between devices: 21.4 us -> 16.5 us  [exchange(): lax.ppermute(value, ('lo', 'rh'), [(i, i ^ bits) for i in range(2 * P_SIZ...]
    unnamed x14 -> x30, local copies, waits for them, and re-layouts: 2.07 us -> 5.15 us
    ppermute x8, starting transfers between devices: 4.96 us -> 7.21 us  [exchange(): lax.ppermute(value, ('lo', 'rh'), [(i, i ^ bits) for i in range(2 * P_SIZ...]
    pallas_call x11 -> x10, Pallas kernels: 54.6 us -> 52.9 us  [on_chip(): pl.pallas_call(kernel, out_shape=[jax.ShapeDtypeStruct(shape, jnp.float32...]
    all_to_all x2 -> x1, starting transfers between devices: 7.5 us -> 5.72 us  [on_device(): blocks = lax.all_to_all(blocks, owners, 0, 0)]
  transfers between devices with their start and end apart: 19 -> 17, of which waited for: 10 -> 12; matrix products, arithmetic and copies ran while one was open for 1% -> 0% of each run, Pallas kernels for 22% -> 23%
where the time goes in v1:
time: 184 us; the launch traced here: 181 us
  waiting for transfers between devices  71.3 us (39%)
  Pallas kernels  52.9 us (29%)
  starting transfers between devices  26.3 us (14%)
  blocking collectives  21.8 us (12%)
  local copies, waits for them, and re-layouts  5.24 us (3%)
  other arithmetic  3.68 us (2%)
    pallas_call x10, Pallas kernels, on_chip(): pl.pallas_call(kernel, out_shape=[jax.ShapeDtypeStruct(shape, jnp.float32...  52.9 us
    all_to_all x1, waiting for transfers between devices, on_device(): blocks = lax.all_to_all(blocks, owners, 0, 0)  28.9 us
    ppermute x7, waiting for transfers between devices, swap(): return lax.ppermute(value, axis, [(0, 1), (1, 0)])  25.8 us
    all_to_all x1, blocking collectives, on_device(): lax.all_to_all(gram.reshape(2 * P_SIZE, -1, B), ('rh', 'lo'), 0, 0)  21.8 us
    ppermute x8, waiting for transfers between devices, exchange(): lax.ppermute(value, ('lo', 'rh'), [(i, i ^ bits) for i in range(2 * P_SIZ...  16.5 us
    ppermute x7, starting transfers between devices, swap(): return lax.ppermute(value, axis, [(0, 1), (1, 0)])  7.7 us
    ppermute x8, starting transfers between devices, exchange(): lax.ppermute(value, ('lo', 'rh'), [(i, i ^ bits) for i in range(2 * P_SIZ...  7.21 us
    all_to_all x1, starting transfers between devices, on_device(): blocks = lax.all_to_all(blocks, owners, 0, 0)  5.72 us
  transfers between devices with their start and end apart: 17, of which 12 were waited for; matrix products, arithmetic and copies ran while one was open for 0% of the time, Pallas kernels for 23%

profile of v1, /device:TPU:9, one launch (start us, length us, event | category | flops | bytes accessed | tf_op | source)
XLA Modules:
  0.0 181.4 jit_solution(15136426544438823586)
XLA Ops:
  0.0 0.7 convert_bitcast_fusion
  0.8 1.4 broadcast_multiply_fusion
  2.2 1.2 pad_maximum_fusion
  3.4 5.7 %all-to-all-start = ((f32[8,160,256]{2,1,0:T(8,128)}), f32[8,160,256]{2,1,0:T(8,128)S(1)}, u32[]{:S(2)}, u32[]{:S(2)}) async-start(f32[8,160,256]{2,1,0:T(8,128)} %bitcast.6), calls=%async_computation | async-start | bytes 2621440 | tf_op jit(solution)/shard_map/all_to_all | solution.py:328
  9.2 28.9 %all-to-all-done.rows_ref.left_ref.right_ref = f32[8,160,256]{2,1,0:T(8,128)S(1)} async-done(((f32[8,160,256]{2,1,0:T(8,128)}), f32[8,160,256]{2,1,0:T(8,128)S(1)}, u32[]{:S(2)}, u32[]{:S(2)}) %all-to-all-start) | async-done | bytes 1310752 | tf_op jit(solution)/shard_map/all_to_all | solution.py:328
  38.1 1.6 upper_products.1
  39.7 0.6 collective-permute-start
  40.3 2.7 %collective-permute-done = f32[5,256,256]{2,1,0:T(8,128)S(1)} collective-permute-done((f32[5,256,256]{2,1,0:T(8,128)S(1)}, f32[5,256,256]{2,1,0:T(8,128)S(1)}, u32[]{:S(2)}, u32[]{:S(2)}) %collective-permute-start) | collective-permute-done | bytes 1310752 | tf_op jit(solution)/shard_map/ppermute | solution.py:299
  43.0 0.2 add.13
  43.1 21.8 %all_to_all.15 = f32[8,160,256]{2,1,0:T(8,128)S(1)} all-to-all(f32[8,160,256]{2,1,0:T(8,128)S(1)} %bitcast.28), channel_id=1, replica_groups=mesh['hi'=2,'lo'=4,'rh'=2,'rl'=2] {'rh','lo'}, dimensions={0} | all-to-all | bytes 2621440 | tf_op jit(solution)/shard_map/all_to_all | solution.py:342
  65.0 0.1 reduce_sum.9
  65.1 1.3 collective-permute-start.1
  66.4 6.0 %collective-permute-done.1 = f32[160,256]{1,0:T(8,128)S(1)} collective-permute-done((f32[160,256]{1,0:T(8,128)S(1)}, f32[160,256]{1,0:T(8,128)S(1)}, u32[]{:S(2)}, u32[]{:S(2)}) %collective-permute-start.1) | collective-permute-done | bytes 163872 | tf_op jit(solution)/shard_map/ppermute | solution.py:299
  72.3 4.2 %collective-permute-start.3 = (f32[160,256]{1,0:T(8,128)S(1)}, f32[160,256]{1,0:T(8,128)S(1)}, u32[]{:S(2)}, u32[]{:S(2)}) collective-permute-start(f32[160,256]{1,0:T(8,128)S(1)} %get-tuple-element.32), channel_id=1, source_target_pairs={{0,8},{2,10},{4,12},{6,14},{8,0},{10,2},{12,4},{14,6},{1,9},{3,11}... | collective-permute-start | bytes 491528 | tf_op jit(solution)/shard_map/ppermute | solution.py:295
  76.5 0.5 collective-permute-start.5
  77.0 3.1 %collective-permute-done.3 = f32[160,256]{1,0:T(8,128)S(1)} collective-permute-done((f32[160,256]{1,0:T(8,128)S(1)}, f32[160,256]{1,0:T(8,128)S(1)}, u32[]{:S(2)}, u32[]{:S(2)}) %collective-permute-start.3) | collective-permute-done | bytes 163872 | tf_op jit(solution)/shard_map/ppermute | solution.py:295
  80.1 0.8 collective-permute-done.2
  81.0 0.5 collective-permute-start.6
  81.5 0.4 collective-permute-start.7
  81.9 2.4 %collective-permute-done.4 = f32[160,256]{1,0:T(8,128)S(1)} collective-permute-done((f32[160,256]{1,0:T(8,128)S(1)}, f32[160,256]{1,0:T(8,128)S(1)}, u32[]{:S(2)}, u32[]{:S(2)}) %collective-permute-start.4) | collective-permute-done | bytes 163872 | tf_op jit(solution)/shard_map/ppermute | solution.py:295
  84.3 0.4 collective-permute-start.8
  84.8 0.7 collective-permute-done.6
  85.5 0.5 collective-permute-done.7
  86.0 3.5 %collective-permute-done.8 = f32[160,256]{1,0:T(8,128)S(1)} collective-permute-done((f32[160,256]{1,0:T(8,128)S(1)}, f32[160,256]{1,0:T(8,128)S(1)}, u32[]{:S(2)}, u32[]{:S(2)}) %collective-permute-start.8) | collective-permute-done | bytes 163872 | tf_op jit(solution)/shard_map/ppermute | solution.py:295
  89.5 2.1 %all_products.1 = (f32[2,4,256,256]{3,2,1,0:T(8,128)S(1)}, f32[2,4,256,256]{3,2,1,0:T(8,128)S(1)}) custom-call(s32[4]{0:T(128)S(1)} %pad_add_fusion.place_ref, f32[8,160,256]{2,1,0:T(8,128)S(1)} %all-to-all-done.rows_ref.left_ref.right_ref, f32[8,160,256]{2,1,0:T(8,128)S(1)} %all-to-all-done.rows_ref.left_ref.right_ref, ...), custom_call_target="tpu_custom_call" | custom-call | tf_op jit(solution)/shard_map/all_products/pallas_call | solution.py:147
  91.6 2.9 %collective-permute-start.10 = (f32[2,4,256,256]{3,2,1,0:T(8,128)S(1)}, f32[2,4,256,256]{3,2,1,0:T(8,128)S(1)}, u32[]{:S(2)}, u32[]{:S(2)}) collective-permute-start(f32[2,4,256,256]{3,2,1,0:T(8,128)S(1)} %get-tuple-element.30), channel_id=1, source_target_pairs={{0,1},{1,0},{2,3},{3,2},{4,5},{5,4},{6,7},{7,6},{8,9},{9,8},{10,11... | collective-permute-start | bytes 6291464 | tf_op jit(solution)/shard_map/ppermute | solution.py:299
  94.5 5.6 %collective-permute-done.9.other_ref = f32[8,160,256]{2,1,0:T(8,128)S(1)} collective-permute-done((f32[8,160,256]{2,1,0:T(8,128)S(1)}, f32[8,160,256]{2,1,0:T(8,128)S(1)}, u32[]{:S(2)}, u32[]{:S(2)}) %collective-permute-start.9) | collective-permute-done | bytes 1310752 | tf_op jit(solution)/shard_map/ppermute | solution.py:299
  100.1 0.9 collect.1.gram_ref.after_ref.refs_7_
  101.0 0.2 add_pair.1
  101.2 1.3 copy-done
  102.6 5.7 %all-to-all-start.2 = ((f32[8,256,256]{2,1,0:T(8,128)}), f32[8,256,256]{2,1,0:T(8,128)}, u32[]{:S(2)}, u32[]{:S(2)}) async-start(f32[8,256,256]{2,1,0:T(8,128)} %bitcast.27), calls=%async_computation.2 | async-start | bytes 4194304 | tf_op jit(solution)/shard_map/all_to_all | solution.py:362
  108.3 11.2 %factor_step.4 = (f32[256,768]{1,0:T(8,128)S(1)}, f32[256,256]{1,0:T(8,128)S(1)}, f32[6,256,256]{2,1,0:T(8,128)S(1)}) custom-call(f32[10,256,256]{2,1,0:T(8,128)S(1)} %collect.1.gram_ref.after_ref.refs_7_), custom_call_target="tpu_custom_call" | custom-call | tf_op jit(solution)/shard_map/factor_step/pallas_call | solution.py:147
  119.5 0.9 copy-done.1
  120.4 0.7 copy-done.5
  121.1 10.3 %factor_step.5 = (f32[256,512]{1,0:T(8,128)S(1)}, f32[256,256]{1,0:T(8,128)S(1)}, f32[3,256,256]{2,1,0:T(8,128)S(1)}) custom-call(f32[6,256,256]{2,1,0:T(8,128)S(1)} %get-tuple-element.21.gram_ref), custom_call_target="tpu_custom_call" | custom-call | tf_op jit(solution)/shard_map/factor_step/pallas_call | solution.py:147
  131.4 0.7 copy-done.7
  132.1 10.0 %factor_step.6 = (f32[256,256]{1,0:T(8,128)S(1)}, f32[256,256]{1,0:T(8,128)S(1)}, f32[1,256,256]{2,1,0:T(8,128)S(1)}) custom-call(f32[3,256,256]{2,1,0:T(8,128)S(1)} %get-tuple-element.23.gram_ref), custom_call_target="tpu_custom_call" | custom-call | tf_op jit(solution)/shard_map/factor_step/pallas_call | solution.py:147
  142.1 0.7 copy-done.3
  142.8 0.7 copy-done.9
  143.5 1.7 sum_places.1
  145.3 0.7 collective-permute-start.11
  146.0 11.6 %collective-permute-done.11 = f32[256,256]{1,0:T(8,128)S(1)} collective-permute-done((f32[256,256]{1,0:T(8,128)S(1)}, f32[256,256]{1,0:T(8,128)S(1)}, u32[]{:S(2)}, u32[]{:S(2)}) %collective-permute-start.11) | collective-permute-done | bytes 262176 | tf_op jit(solution)/shard_map/ppermute | solution.py:299
  157.7 1.3 collective-permute-start.13
  159.0 0.8 collective-permute-start.12
  159.8 5.4 %collective-permute-done.13.refs_10_ = f32[256,256]{1,0:T(8,128)S(1)} collective-permute-done((f32[256,256]{1,0:T(8,128)S(1)}, f32[256,256]{1,0:T(8,128)S(1)}, u32[]{:S(2)}, u32[]{:S(2)}) %collective-permute-start.13) | collective-permute-done | bytes 262176 | tf_op jit(solution)/shard_map/ppermute | solution.py:295
  165.1 1.4 collective-permute-start.14
  166.5 9.1 %factor_step.7.refs_6_ = f32[256,256]{1,0:T(8,128)S(1)} custom-call(f32[1,256,256]{2,1,0:T(8,128)S(1)} %copy-done.4), custom_call_target="tpu_custom_call" | custom-call | tf_op jit(solution)/shard_map/factor_step/pallas_call | solution.py:147
  175.7 5.8 %solve.1 = f32[256,256]{1,0:T(8,128)} custom-call(s32[4]{0:T(128)S(1)} %pad_add_fusion.place_ref, f32[256,768]{1,0:T(8,128)S(1)} %copy-done.2, f32[256,512]{1,0:T(8,128)S(1)} %get-tuple-element.22.refs_1_, f32[256,256]{1,0:T(8,128)S(1)} %get-tuple-element.24.after_ref.refs_2_, f32[256,256]{1,0:T(8,128)S(1)} %copy-done.6, f32[256,256]{1,0:T(8,128)S(1)} %copy-done.8, ...), custom_call_target="tpu_custom_call" | custom-call | tf_op jit(solution)/shard_map/solve/pallas_call | solution.py:147
  (37 shorter events, 0.4 us)
Async XLA Ops:
  0.0 2.2 %copy-start.11 = (f32[256,256]{1,0:T(8,128)S(1)}, f32[256,256]{1,0:T(8,128)}, u32[]{:S(2)}) copy-start(f32[256,256]{1,0:T(8,128)} %param.3) | copy-start | bytes 786436
  3.4 34.7 %all-to-all-start = ((f32[8,160,256]{2,1,0:T(8,128)}), f32[8,160,256]{2,1,0:T(8,128)S(1)}, u32[]{:S(2)}, u32[]{:S(2)}) async-start(f32[8,160,256]{2,1,0:T(8,128)} %bitcast.6), calls=%async_computation | async-start | bytes 2621440 | tf_op jit(solution)/shard_map/all_to_all | solution.py:328
  39.7 3.3 %collective-permute-start = (f32[5,256,256]{2,1,0:T(8,128)S(1)}, f32[5,256,256]{2,1,0:T(8,128)S(1)}, u32[]{:S(2)}, u32[]{:S(2)}) collective-permute-start(f32[5,256,256]{2,1,0:T(8,128)S(1)} %get-tuple-element.19), channel_id=1, source_target_pairs={{0,1},{1,0},{2,3},{3,2},{4,5},{5,4},{6,7},{7,6},{8,9},{9,8},{10,11... | collective-permute-start | bytes 3932168 | tf_op jit(solution)/shard_map/ppermute | solution.py:299
  65.1 7.2 %collective-permute-start.1 = (f32[160,256]{1,0:T(8,128)S(1)}, f32[160,256]{1,0:T(8,128)S(1)}, u32[]{:S(2)}, u32[]{:S(2)}) collective-permute-start(f32[160,256]{1,0:T(8,128)S(1)} %reduce_sum.9), channel_id=1, source_target_pairs={{0,16},{16,0},{1,17},{17,1},{2,18},{18,2},{3,19},{19,3},{4,20},{20... | collective-permute-start | bytes 491528 | tf_op jit(solution)/shard_map/ppermute | solution.py:299
  72.3 7.8 %collective-permute-start.3 = (f32[160,256]{1,0:T(8,128)S(1)}, f32[160,256]{1,0:T(8,128)S(1)}, u32[]{:S(2)}, u32[]{:S(2)}) collective-permute-start(f32[160,256]{1,0:T(8,128)S(1)} %get-tuple-element.32), channel_id=1, source_target_pairs={{0,8},{2,10},{4,12},{6,14},{8,0},{10,2},{12,4},{14,6},{1,9},{3,11}... | collective-permute-start | bytes 491528 | tf_op jit(solution)/shard_map/ppermute | solution.py:295
  76.5 4.5 %collective-permute-start.2 = (f32[160,256]{1,0:T(8,128)S(1)}, f32[160,256]{1,0:T(8,128)S(1)}, u32[]{:S(2)}, u32[]{:S(2)}) collective-permute-start(f32[160,256]{1,0:T(8,128)S(1)} %get-tuple-element.32), channel_id=1, source_target_pairs={{0,4},{2,6},{4,0},{6,2},{8,12},{10,14},{12,8},{14,10},{1,5},{3,7},... | collective-permute-start | bytes 491528 | tf_op jit(solution)/shard_map/ppermute | solution.py:295
  76.5 5.0 %collective-permute-start.5 = (f32[160,256]{1,0:T(8,128)S(1)}, f32[160,256]{1,0:T(8,128)S(1)}, u32[]{:S(2)}, u32[]{:S(2)}) collective-permute-start(f32[160,256]{1,0:T(8,128)S(1)} %get-tuple-element.32), channel_id=1, source_target_pairs={{0,2},{2,0},{4,6},{6,4},{8,10},{10,8},{12,14},{14,12},{1,3},{3,1},... | collective-permute-start | bytes 491528 | tf_op jit(solution)/shard_map/ppermute | solution.py:295
  80.1 4.2 %collective-permute-start.4 = (f32[160,256]{1,0:T(8,128)S(1)}, f32[160,256]{1,0:T(8,128)S(1)}, u32[]{:S(2)}, u32[]{:S(2)}) collective-permute-start(f32[160,256]{1,0:T(8,128)S(1)} %collective-permute-done.3), channel_id=1, source_target_pairs={{0,4},{2,6},{4,0},{6,2},{8,12},{10,14},{12,8},{14,10},{1,5},{3,7},... | collective-permute-start | bytes 491528 | tf_op jit(solution)/shard_map/ppermute | solution.py:295
  81.0 4.5 %collective-permute-start.6 = (f32[160,256]{1,0:T(8,128)S(1)}, f32[160,256]{1,0:T(8,128)S(1)}, u32[]{:S(2)}, u32[]{:S(2)}) collective-permute-start(f32[160,256]{1,0:T(8,128)S(1)} %collective-permute-done.2), channel_id=1, source_target_pairs={{0,2},{2,0},{4,6},{6,4},{8,10},{10,8},{12,14},{14,12},{1,3},{3,1},... | collective-permute-start | bytes 491528 | tf_op jit(solution)/shard_map/ppermute | solution.py:295
  81.5 4.5 %collective-permute-start.7 = (f32[160,256]{1,0:T(8,128)S(1)}, f32[160,256]{1,0:T(8,128)S(1)}, u32[]{:S(2)}, u32[]{:S(2)}) collective-permute-start(f32[160,256]{1,0:T(8,128)S(1)} %collective-permute-done.5), channel_id=1, source_target_pairs={{0,8},{2,10},{4,12},{6,14},{8,0},{10,2},{12,4},{14,6},{1,9},{3,11}... | collective-permute-start | bytes 491528 | tf_op jit(solution)/shard_map/ppermute | solution.py:295
  84.3 5.2 %collective-permute-start.8 = (f32[160,256]{1,0:T(8,128)S(1)}, f32[160,256]{1,0:T(8,128)S(1)}, u32[]{:S(2)}, u32[]{:S(2)}) collective-permute-start(f32[160,256]{1,0:T(8,128)S(1)} %collective-permute-done.4), channel_id=1, source_target_pairs={{0,2},{2,0},{4,6},{6,4},{8,10},{10,8},{12,14},{14,12},{1,3},{3,1},... | collective-permute-start | bytes 491528 | tf_op jit(solution)/shard_map/ppermute | solution.py:295
  91.6 9.4 %collective-permute-start.10 = (f32[2,4,256,256]{3,2,1,0:T(8,128)S(1)}, f32[2,4,256,256]{3,2,1,0:T(8,128)S(1)}, u32[]{:S(2)}, u32[]{:S(2)}) collective-permute-start(f32[2,4,256,256]{3,2,1,0:T(8,128)S(1)} %get-tuple-element.30), channel_id=1, source_target_pairs={{0,1},{1,0},{2,3},{3,2},{4,5},{5,4},{6,7},{7,6},{8,9},{9,8},{10,11... | collective-permute-start | bytes 6291464 | tf_op jit(solution)/shard_map/ppermute | solution.py:299
  94.5 5.7 %collective-permute-start.9 = (f32[8,160,256]{2,1,0:T(8,128)S(1)}, f32[8,160,256]{2,1,0:T(8,128)S(1)}, u32[]{:S(2)}, u32[]{:S(2)}) collective-permute-start(f32[8,160,256]{2,1,0:T(8,128)S(1)} %bitcast_dynamic-update-slice_fusion.mine_ref.after_ref), channel_id=1, source_target_pairs={{0,1},{1,0},{2,3},{3,2},{4,5},{5,4},{6,7},{7,6},{8,9},{9,8},{10,11... | collective-permute-start | bytes 3932168 | tf_op jit(solution)/shard_map/ppermute | solution.py:299
  101.2 1.3 copy-start
  102.6 40.9 %all-to-all-start.2 = ((f32[8,256,256]{2,1,0:T(8,128)}), f32[8,256,256]{2,1,0:T(8,128)}, u32[]{:S(2)}, u32[]{:S(2)}) async-start(f32[8,256,256]{2,1,0:T(8,128)} %bitcast.27), calls=%async_computation.2 | async-start | bytes 4194304 | tf_op jit(solution)/shard_map/all_to_all | solution.py:362
  119.5 0.9 copy-start.1
  120.4 0.7 copy-start.5
  131.4 0.7 copy-start.7
  142.1 0.7 copy-start.3
  142.8 0.7 copy-start.9
  143.5 23.0 %copy-start.4 = (f32[1,256,256]{2,1,0:T(8,128)S(1)}, f32[1,256,256]{2,1,0:T(8,128)}, u32[]{:S(2)}) copy-start(f32[1,256,256]{2,1,0:T(8,128)} %copy-done.3) | copy-start | bytes 786436
  143.5 32.1 %copy-start.10 = (f32[256,256]{1,0:T(8,128)S(1)}, f32[256,256]{1,0:T(8,128)}, u32[]{:S(2)}) copy-start(f32[256,256]{1,0:T(8,128)} %copy-done.9) | copy-start | bytes 786436
  145.3 30.4 %copy-start.2 = (f32[256,768]{1,0:T(8,128)S(1)}, f32[256,768]{1,0:T(8,128)}, u32[]{:S(2)}) copy-start(f32[256,768]{1,0:T(8,128)} %copy-done.1) | copy-start | bytes 2359300
  145.3 30.4 %copy-start.6 = (f32[256,256]{1,0:T(8,128)S(1)}, f32[256,256]{1,0:T(8,128)}, u32[]{:S(2)}) copy-start(f32[256,256]{1,0:T(8,128)} %copy-done.5) | copy-start | bytes 786436
  145.3 30.4 %copy-start.8 = (f32[256,256]{1,0:T(8,128)S(1)}, f32[256,256]{1,0:T(8,128)}, u32[]{:S(2)}) copy-start(f32[256,256]{1,0:T(8,128)} %copy-done.7) | copy-start | bytes 786436
  145.3 12.4 %collective-permute-start.11 = (f32[256,256]{1,0:T(8,128)S(1)}, f32[256,256]{1,0:T(8,128)S(1)}, u32[]{:S(2)}, u32[]{:S(2)}) collective-permute-start(f32[256,256]{1,0:T(8,128)S(1)} %sum_places.1), channel_id=1, source_target_pairs={{0,16},{16,0},{1,17},{17,1},{2,18},{18,2},{3,19},{19,3},{4,20},{20... | collective-permute-start | bytes 786440 | tf_op jit(solution)/shard_map/ppermute | solution.py:299
  157.7 7.4 %collective-permute-start.13 = (f32[256,256]{1,0:T(8,128)S(1)}, f32[256,256]{1,0:T(8,128)S(1)}, u32[]{:S(2)}, u32[]{:S(2)}) collective-permute-start(f32[256,256]{1,0:T(8,128)S(1)} %add.15.refs_8_), channel_id=1, source_target_pairs={{0,2},{2,0},{4,6},{6,4},{8,10},{10,8},{12,14},{14,12},{1,3},{3,1},... | collective-permute-start | bytes 786440 | tf_op jit(solution)/shard_map/ppermute | solution.py:295
  159.0 16.6 %collective-permute-start.12 = (f32[256,256]{1,0:T(8,128)S(1)}, f32[256,256]{1,0:T(8,128)S(1)}, u32[]{:S(2)}, u32[]{:S(2)}) collective-permute-start(f32[256,256]{1,0:T(8,128)S(1)} %add.15.refs_8_), channel_id=1, source_target_pairs={{0,1},{1,0},{2,3},{3,2},{4,5},{5,4},{6,7},{7,6},{8,9},{9,8},{10,11... | collective-permute-start | bytes 786440 | tf_op jit(solution)/shard_map/ppermute | solution.py:299
  165.1 10.5 %collective-permute-start.14 = (f32[256,256]{1,0:T(8,128)S(1)}, f32[256,256]{1,0:T(8,128)S(1)}, u32[]{:S(2)}, u32[]{:S(2)}) collective-permute-start(f32[256,256]{1,0:T(8,128)S(1)} %collective-permute-done.13.refs_10_), channel_id=1, source_target_pairs={{0,1},{1,0},{2,3},{3,2},{4,5},{5,4},{6,7},{7,6},{8,9},{9,8},{10,11... | collective-permute-start | bytes 786440 | tf_op jit(solution)/shard_map/ppermute | solution.py:299

commit v2 on v1

--- a/solution.py
+++ b/solution.py
@@ -26,53 +26,67 @@
     )
 
 
+def lane(value, at):
+    return jnp.broadcast_to(value[:, at : at + 1], (SUB, NB))
+
+
+def row(value, at):
+    return jnp.broadcast_to(value[at : at + 1, :], (SUB, NB))
+
+
 def inverse_factor(rows):
     n = NB // SUB
-    tile = (SUB, NB)
-    row_id = lax.broadcasted_iota(jnp.int32, tile, 0)
-    col_id = lax.broadcasted_iota(jnp.int32, tile, 1)
-    right = [jnp.where(row_id + r * SUB == col_id, 1.0, 0.0).astype(jnp.float32) for r in range(n)]
+    row_id = lax.broadcasted_iota(jnp.int32, (SUB, NB), 0)
+    col_id = lax.broadcasted_iota(jnp.int32, (SUB, NB), 1)
+    order = range(SUB)
+    ahead = [lane(rows[0], m) for m in order]
     for b in range(n):
         j = b * SUB
-        head = rows[b]
-        pivot = {}
-        for k in range(SUB):
-            for m in range(k, SUB):
-                pivot[k, m] = jnp.broadcast_to(head[k : k + 1, j + m : j + m + 1], tile)
-        scale = []
-        for k in range(SUB):
+        pivot = {(k, m): row(ahead[m], k) for k in order for m in range(k, SUB)}
+        below = [[lane(rows[r], j + k) for k in order] for r in range(b + 1, n)]
+        if b + 1 < n:
+            ahead = [lane(rows[b + 1], j + SUB + m) for m in order]
+        scale, left = [], []
+        for k in order:
             scale.append(lax.rsqrt(pivot[k, k]))
             for m in range(k + 1, SUB):
                 pivot[k, m] = pivot[k, m] * scale[k]
             for m in range(k + 1, SUB):
                 for q in range(m, SUB):
                     pivot[m, q] = pivot[m, q] - pivot[k, m] * pivot[k, q]
-        top, top_right = [], []
-        for k in range(SUB):
-            here = jnp.broadcast_to(rows[b][k : k + 1, :], tile)
-            there = jnp.broadcast_to(right[b][k : k + 1, :], tile)
-            for m in range(k):
-                here = here - pivot[m, k] * top[m]
-                there = there - pivot[m, k] * top_right[m]
-            top.append(here * scale[k])
-            top_right.append(there * scale[k])
-        strip = top_right[0]
-        for k in range(1, SUB):
-            strip = jnp.where(row_id == k, top_right[k], strip)
-        for r in range(b + 1, n):
-            left = []
-            for k in range(SUB):
-                part = jnp.broadcast_to(rows[r][:, j + k : j + k + 1], tile)
+            if b + 1 < n:
+                part = below[0][k]
                 for m in range(k):
                     part = part - pivot[m, k] * left[m]
-                left.append(part * scale[k])
-            body, body_right = rows[r], right[r]
-            for k in range(SUB):
-                body = body - left[k] * top[k]
-                body_right = body_right - left[k] * top_right[k]
-            rows[r], right[r] = body, body_right
-        right[b] = strip
-    return right
+                part = part * scale[k]
+                left.append(part)
+                for m in order:
+                    ahead[m] = ahead[m] - part * row(part, m)
+        inside = (col_id >= j) & (col_id < j + SUB)
+        head = jnp.where(inside, jnp.where(col_id - j == row_id, 1.0, 0.0), rows[b])
+        top = []
+        for k in order:
+            part = row(head, k)
+            for m in range(k):
+                part = part - pivot[m, k] * top[m]
+            top.append(part * scale[k])
+        if b + 1 < n:
+            solved = [None] * SUB
+            for k in reversed(order):
+                part = top[k]
+                for m in range(k + 1, SUB):
+                    part = part - pivot[k, m] * solved[m]
+                solved[k] = part * scale[k]
+            for r in range(b + 1, n):
+                body = jnp.where(inside, 0.0, rows[r])
+                for k in order:
+                    body = body - below[r - b - 1][k] * solved[k]
+                rows[r] = body
+        strip = top[0]
+        for k in range(1, SUB):
+            strip = jnp.where(row_id == k, top[k], strip)
+        rows[b] = jnp.where(col_id < j + SUB, strip, 0.0)
+    return rows
 
 
 PAIRS = [(r, c) for r in range(P_SIZE) for c in range(r, P_SIZE)]
@@ -130,6 +144,21 @@
         send_ref[a] = work[2 * a + 1 - side]
 
 
+def tie_kernel(value_ref, after_ref, out_ref):
+    del value_ref, after_ref, out_ref
+
+
+def behind(value, after):
+    return pl.pallas_call(
+        tie_kernel,
+        out_shape=jax.ShapeDtypeStruct(value.shape, value.dtype),
+        in_specs=[pl.BlockSpec(memory_space=pl.ANY)] * 2,
+        out_specs=pl.BlockSpec(memory_space=pl.ANY),
+        input_output_aliases={0: 0},
+        name="behind",
+    )(value, after)
+
+
 def add_kernel(left_ref, right_ref, after_ref, out_ref):
     del after_ref
     out_ref[...] = left_ref[...] + right_ref[...]
@@ -157,10 +186,11 @@
     )(*operands, *after)
 
 
-def collect_kernel(place_ref, mine_ref, other_ref, gram_ref):
+def collect_kernel(place_ref, mine_ref, other_ref, gram_ref, token_ref):
     side, high, low = place_ref[0], place_ref[1], place_ref[2]
     at = high * P_SIZE + low
     rows = mine_ref.shape[1]
+    token_ref[...] = jnp.zeros_like(token_ref)
     for s in range(2):
         for p in range(PIECES // 2):
             start = ((s * PIECES) // 2 + p) * rows
@@ -299,6 +329,10 @@
     return lax.ppermute(value, axis, [(0, 1), (1, 0)])
 
 
+def across_rows(value, bits):
+    return lax.ppermute(value, ("rh", "rl"), [(i, i ^ bits) for i in range(P_SIZE)])
+
+
 def spread(piece):
     y, z, x = (0, 1), (0, 2), (1, 0)
     by_z, by_y, by_x = exchange(piece, *z), exchange(piece, *y), exchange(piece, *x)
@@ -340,14 +374,8 @@
     )
     gram = keep + swap(send)
     gram = lax.all_to_all(gram.reshape(2 * P_SIZE, -1, B), ("rh", "lo"), 0, 0).sum(axis=0)
-    piece = gram + swap(gram, "hi") if in_two else from_first(gram, n_hi)
-    pieces = spread(piece)
-    (gram,) = on_chip(
-        collect_kernel, [(len(PAIRS), B, B)], "collect", place, pieces, swap(pieces), scalars=1
-    )
-
     half = (2, P_SIZE, B, B)
-    keep, send = on_chip(
+    cross, send = on_chip(
         all_products_kernel,
         [half, half],
         "all_products",
@@ -356,16 +384,29 @@
         blocks,
         scalars=1,
         scratch=[pltpu.VMEM((P_SIZE, P_SIZE, B, B), jnp.float32)],
-        after=(pieces,),
-    )
-    (cross,) = on_chip(add_kernel, [half], "add_pair", keep, swap(send), after=(gram,))
-    cross = lax.all_to_all(cross.reshape(2 * P_SIZE, B, B), ("rh", "lo"), 0, 0)
+        after=(keep,),
+    )
+    cross = cross + swap(send)
+    piece = gram + swap(gram, "hi") if in_two else from_first(gram, n_hi)
+    pieces = spread(piece)
+    gram, token = on_chip(
+        collect_kernel,
+        [(len(PAIRS), B, B), (SUB, NB)],
+        "collect",
+        place,
+        pieces,
+        swap(pieces),
+        scalars=1,
+    )
+
+    cross = behind(cross.reshape(2 * P_SIZE, B, B), token)
+    cross = lax.all_to_all(cross, ("rh", "lo"), 0, 0)
     rows, inverses = factor(gram)
-    (mine,) = on_chip(sum_kernel, [(B, columns)], "sum_places", cross, after=(rows[2],))
+    (mine,) = on_chip(sum_kernel, [(B, columns)], "sum_places", cross, after=(rows[1],))
     if in_two:
-        mine = mine + swap(mine, "hi")
-    by_x = exchange(mine, 1, 0)
-    own = [mine, swap(mine), by_x, swap(by_x)]
+        other = swap(mine, "hi")
+        (mine,) = on_chip(add_kernel, [(B, columns)], "add_groups", mine, other, after=(rows[2],))
+    own = [mine] + [across_rows(mine, bits) for bits in range(1, P_SIZE)]
 
     (result,) = on_chip(
         solve_kernel,

time: 184 us -> 171 us (0.929)
  Pallas kernels: 52.9 us -> 42.5 us
  waiting for transfers between devices: 71.3 us -> 66.6 us
  other arithmetic: 3.68 us -> 6.66 us
  local copies, waits for them, and re-layouts: 5.24 us -> 3.28 us
    ppermute x7 -> x5, waiting for transfers between devices: 25.8 us -> 13.6 us  [swap(): return lax.ppermute(value, axis, [(0, 1), (1, 0)])]
    all_to_all x1, waiting for transfers between devices: 0.01 us -> 10.5 us  [on_device(): cross = lax.all_to_all(cross, ('rh', 'lo'), 0, 0)]
    pallas_call x10, Pallas kernels: 52.9 us -> 42.5 us  [on_chip(): pl.pallas_call(kernel, out_shape=[jax.ShapeDtypeStruct(shape, jnp.float32...]
    ppermute x8 -> x7, waiting for transfers between devices: 16.5 us -> 7.74 us  [exchange(): lax.ppermute(value, ('lo', 'rh'), [(i, i ^ bits) for i in range(2 * P_SIZ...]
    ppermute x0 -> x3, waiting for transfers between devices: none -> 5.83 us  [across_rows(): lax.ppermute(value, ('rh', 'rl'), [(i, i ^ bits) for i in range(P_SIZE)])]
    ppermute x0 -> x3, starting transfers between devices: none -> 2.21 us  [across_rows(): lax.ppermute(value, ('rh', 'rl'), [(i, i ^ bits) for i in range(P_SIZE)])]
    unnamed x30 -> x22, local copies, waits for them, and re-layouts: 5.15 us -> 3.19 us
    ppermute x7 -> x5, starting transfers between devices: 7.7 us -> 6.17 us  [swap(): return lax.ppermute(value, axis, [(0, 1), (1, 0)])]
  transfers between devices with their start and end apart: 17 -> 17, of which waited for: 12 -> 12; matrix products, arithmetic and copies ran while one was open for 0% -> 1% of each run, Pallas kernels for 23% -> 19%
where the time goes in v2:
time: 171 us; the launch traced here: 169 us
  waiting for transfers between devices  66.6 us (39%)
  Pallas kernels  42.5 us (25%)
  starting transfers between devices  27.5 us (16%)
  blocking collectives  21.9 us (13%)
  other arithmetic  6.66 us (4%)
  local copies, waits for them, and re-layouts  3.28 us (2%)
    pallas_call x10, Pallas kernels, on_chip(): pl.pallas_call(kernel, out_shape=[jax.ShapeDtypeStruct(shape, jnp.float32...  42.5 us
    all_to_all x1, waiting for transfers between devices, on_device(): blocks = lax.all_to_all(blocks, owners, 0, 0)  28.9 us
    all_to_all x1, blocking collectives, on_device(): lax.all_to_all(gram.reshape(2 * P_SIZE, -1, B), ('rh', 'lo'), 0, 0)  21.9 us
    ppermute x5, waiting for transfers between devices, swap(): return lax.ppermute(value, axis, [(0, 1), (1, 0)])  13.6 us
    all_to_all x1, waiting for transfers between devices, on_device(): cross = lax.all_to_all(cross, ('rh', 'lo'), 0, 0)  10.5 us
    ppermute x7, starting transfers between devices, exchange(): lax.ppermute(value, ('lo', 'rh'), [(i, i ^ bits) for i in range(2 * P_SIZ...  8.63 us
    ppermute x7, waiting for transfers between devices, exchange(): lax.ppermute(value, ('lo', 'rh'), [(i, i ^ bits) for i in range(2 * P_SIZ...  7.74 us
    ppermute x5, starting transfers between devices, swap(): return lax.ppermute(value, axis, [(0, 1), (1, 0)])  6.17 us
  transfers between devices with their start and end apart: 17, of which 12 were waited for; matrix products, arithmetic and copies ran while one was open for 1% of the time, Pallas kernels for 19%

profile of v2, /device:TPU:9, one launch (start us, length us, event | category | flops | bytes accessed | tf_op | source)
XLA Modules:
  0.0 168.8 jit_solution(8485226717078254215)
XLA Ops:
  0.0 0.7 convert_bitcast_fusion
  0.8 1.4 broadcast_multiply_fusion
  2.2 1.2 pad_maximum_fusion
  3.4 5.7 %all-to-all-start = ((f32[8,160,256]{2,1,0:T(8,128)}), f32[8,160,256]{2,1,0:T(8,128)S(1)}, u32[]{:S(2)}, u32[]{:S(2)}) async-start(f32[8,160,256]{2,1,0:T(8,128)} %bitcast.6), calls=%async_computation | async-start | bytes 2621440 | tf_op jit(solution)/shard_map/all_to_all | solution.py:362
  9.1 0.1 pad_add_fusion.place_ref
  9.2 28.9 %all-to-all-done.rows_ref.left_ref.right_ref = f32[8,160,256]{2,1,0:T(8,128)S(1)} async-done(((f32[8,160,256]{2,1,0:T(8,128)}), f32[8,160,256]{2,1,0:T(8,128)S(1)}, u32[]{:S(2)}, u32[]{:S(2)}) %all-to-all-start) | async-done | bytes 1310752 | tf_op jit(solution)/shard_map/all_to_all | solution.py:362
  38.1 1.6 upper_products.1
  39.7 0.6 collective-permute-start
  40.3 2.7 %collective-permute-done = f32[5,256,256]{2,1,0:T(8,128)S(1)} collective-permute-done((f32[5,256,256]{2,1,0:T(8,128)S(1)}, f32[5,256,256]{2,1,0:T(8,128)S(1)}, u32[]{:S(2)}, u32[]{:S(2)}) %collective-permute-start) | collective-permute-done | bytes 1310752 | tf_op jit(solution)/shard_map/ppermute | solution.py:329
  43.0 0.2 add.13
  43.2 21.9 %all_to_all.15 = f32[8,160,256]{2,1,0:T(8,128)} all-to-all(f32[8,160,256]{2,1,0:T(8,128)S(1)} %bitcast.28), channel_id=1, replica_groups=mesh['hi'=2,'lo'=4,'rh'=2,'rl'=2] {'rh','lo'}, dimensions={0} | all-to-all | bytes 2621440 | tf_op jit(solution)/shard_map/all_to_all | solution.py:376
  65.1 1.4 reduce_sum.9
  66.5 1.3 collective-permute-start.1
  67.8 6.0 %collective-permute-done.1 = f32[160,256]{1,0:T(8,128)S(1)} collective-permute-done((f32[160,256]{1,0:T(8,128)S(1)}, f32[160,256]{1,0:T(8,128)S(1)}, u32[]{:S(2)}, u32[]{:S(2)}) %collective-permute-start.1) | collective-permute-done | bytes 163872 | tf_op jit(solution)/shard_map/ppermute | solution.py:329
  73.8 4.2 %collective-permute-start.3 = (f32[160,256]{1,0:T(8,128)S(1)}, f32[160,256]{1,0:T(8,128)S(1)}, u32[]{:S(2)}, u32[]{:S(2)}) collective-permute-start(f32[160,256]{1,0:T(8,128)S(1)} %get-tuple-element.36), channel_id=1, source_target_pairs={{0,8},{2,10},{4,12},{6,14},{8,0},{10,2},{12,4},{14,6},{1,9},{3,11}... | collective-permute-start | bytes 491528 | tf_op jit(solution)/shard_map/ppermute | solution.py:325
  77.9 2.1 %all_products.1 = (f32[2,4,256,256]{3,2,1,0:T(8,128)S(1)}, f32[2,4,256,256]{3,2,1,0:T(8,128)S(1)}) custom-call(s32[4]{0:T(128)S(1)} %pad_add_fusion.place_ref, f32[8,160,256]{2,1,0:T(8,128)S(1)} %all-to-all-done.rows_ref.left_ref.right_ref, f32[8,160,256]{2,1,0:T(8,128)S(1)} %all-to-all-done.rows_ref.left_ref.right_ref, ...), custom_call_target="tpu_custom_call" | custom-call | tf_op jit(solution)/shard_map/all_products/pallas_call | solution.py:176
  80.1 1.3 collective-permute-start.10
  81.3 0.6 collective-permute-start.5
  81.9 1.7 %collective-permute-start.4 = (f32[160,256]{1,0:T(8,128)S(1)}, f32[160,256]{1,0:T(8,128)S(1)}, u32[]{:S(2)}, u32[]{:S(2)}) collective-permute-start(f32[160,256]{1,0:T(8,128)S(1)} %collective-permute-done.3), channel_id=1, source_target_pairs={{0,4},{2,6},{4,0},{6,2},{8,12},{10,14},{12,8},{14,10},{1,5},{3,7},... | collective-permute-start | bytes 491528 | tf_op jit(solution)/shard_map/ppermute | solution.py:325
  83.6 0.9 collective-permute-start.6
  84.6 2.5 %collective-permute-done.5 = f32[160,256]{1,0:T(8,128)S(1)} collective-permute-done((f32[160,256]{1,0:T(8,128)S(1)}, f32[160,256]{1,0:T(8,128)S(1)}, u32[]{:S(2)}, u32[]{:S(2)}) %collective-permute-start.5) | collective-permute-done | bytes 163872 | tf_op jit(solution)/shard_map/ppermute | solution.py:325
  87.1 1.2 collective-permute-start.8
  88.4 2.2 %collective-permute-done.6 = f32[160,256]{1,0:T(8,128)S(1)} collective-permute-done((f32[160,256]{1,0:T(8,128)S(1)}, f32[160,256]{1,0:T(8,128)S(1)}, u32[]{:S(2)}, u32[]{:S(2)}) %collective-permute-start.6) | collective-permute-done | bytes 163872 | tf_op jit(solution)/shard_map/ppermute | solution.py:325
  90.6 0.9 collective-permute-done.7
  91.5 2.1 %collective-permute-done.8 = f32[160,256]{1,0:T(8,128)S(1)} collective-permute-done((f32[160,256]{1,0:T(8,128)S(1)}, f32[160,256]{1,0:T(8,128)S(1)}, u32[]{:S(2)}, u32[]{:S(2)}) %collective-permute-start.8) | collective-permute-done | bytes 163872 | tf_op jit(solution)/shard_map/ppermute | solution.py:325
  93.7 1.4 collective-permute-start.9
  95.1 1.7 add.15
  96.7 1.0 collective-permute-done.9.other_ref
  97.7 0.9 collect.1
  98.6 0.6 copy-done.6
  99.2 4.8 %all-to-all-start.2 = ((f32[8,256,256]{2,1,0:T(8,128)}), f32[8,256,256]{2,1,0:T(8,128)}, u32[]{:S(2)}, u32[]{:S(2)}) async-start(f32[8,256,256]{2,1,0:T(8,128)} %behind.1), calls=%async_computation.2 | async-start | bytes 4194304 | tf_op jit(solution)/shard_map/all_to_all | solution.py:403
  104.0 8.7 %factor_step.4 = (f32[256,768]{1,0:T(8,128)S(1)}, f32[256,256]{1,0:T(8,128)S(1)}, f32[6,256,256]{2,1,0:T(8,128)S(1)}) custom-call(f32[10,256,256]{2,1,0:T(8,128)S(1)} %get-tuple-element.22.gram_ref.refs_7_), custom_call_target="tpu_custom_call" | custom-call | tf_op jit(solution)/shard_map/factor_step/pallas_call | solution.py:176
  112.7 0.9 copy-done.2
  113.6 7.8 %factor_step.5 = (f32[256,512]{1,0:T(8,128)S(1)}, f32[256,256]{1,0:T(8,128)S(1)}, f32[3,256,256]{2,1,0:T(8,128)S(1)}) custom-call(f32[6,256,256]{2,1,0:T(8,128)S(1)} %get-tuple-element.24.gram_ref), custom_call_target="tpu_custom_call" | custom-call | tf_op jit(solution)/shard_map/factor_step/pallas_call | solution.py:176
  121.4 0.9 copy-done
  122.3 0.7 copy-done.4
  123.0 10.5 %all-to-all-done.2.parts_ref = f32[8,256,256]{2,1,0:T(8,128)} async-done(((f32[8,256,256]{2,1,0:T(8,128)}), f32[8,256,256]{2,1,0:T(8,128)}, u32[]{:S(2)}, u32[]{:S(2)}) %all-to-all-start.2) | async-done | bytes 2097184 | tf_op jit(solution)/shard_map/all_to_all | solution.py:403
  133.5 1.8 %sum_places.1.left_ref = f32[256,256]{1,0:T(8,128)S(1)} custom-call(f32[8,256,256]{2,1,0:T(8,128)} %all-to-all-done.2.parts_ref, f32[256,512]{1,0:T(8,128)S(1)} %get-tuple-element.25.after_ref.refs_1_), custom_call_target="tpu_custom_call" | custom-call | tf_op jit(solution)/shard_map/sum_places/pallas_call | solution.py:176
  135.3 1.6 collective-permute-start.11
  136.9 7.4 %factor_step.6 = (f32[256,256]{1,0:T(8,128)S(1)}, f32[256,256]{1,0:T(8,128)S(1)}, f32[1,256,256]{2,1,0:T(8,128)S(1)}) custom-call(f32[3,256,256]{2,1,0:T(8,128)S(1)} %copy-done.1), custom_call_target="tpu_custom_call" | custom-call | tf_op jit(solution)/shard_map/factor_step/pallas_call | solution.py:176
  144.3 4.0 %collective-permute-done.11.right_ref = f32[256,256]{1,0:T(8,128)S(1)} collective-permute-done((f32[256,256]{1,0:T(8,128)S(1)}, f32[256,256]{1,0:T(8,128)S(1)}, u32[]{:S(2)}, u32[]{:S(2)}) %collective-permute-start.11) | collective-permute-done | bytes 262176 | tf_op jit(solution)/shard_map/ppermute | solution.py:329
  148.4 0.8 collective-permute-start.14
  149.2 1.3 collective-permute-start.13
  150.5 0.1 collective-permute-start.12
  150.6 6.5 %factor_step.7.refs_6_ = f32[256,256]{1,0:T(8,128)S(1)} custom-call(f32[1,256,256]{2,1,0:T(8,128)S(1)} %get-tuple-element.31.gram_ref), custom_call_target="tpu_custom_call" | custom-call | tf_op jit(solution)/shard_map/factor_step/pallas_call | solution.py:176
  157.1 0.2 collective-permute-done.14.refs_11_
  157.4 5.6 %collective-permute-done.13.refs_10_ = f32[256,256]{1,0:T(8,128)S(1)} collective-permute-done((f32[256,256]{1,0:T(8,128)S(1)}, f32[256,256]{1,0:T(8,128)S(1)}, u32[]{:S(2)}, u32[]{:S(2)}) %collective-permute-start.13) | collective-permute-done | bytes 262176 | tf_op jit(solution)/shard_map/ppermute | solution.py:333
  163.0 5.8 %solve.1 = f32[256,256]{1,0:T(8,128)} custom-call(s32[4]{0:T(128)S(1)} %pad_add_fusion.place_ref, f32[256,768]{1,0:T(8,128)S(1)} %copy-done.3, f32[256,512]{1,0:T(8,128)S(1)} %get-tuple-element.25.after_ref.refs_1_, f32[256,256]{1,0:T(8,128)S(1)} %get-tuple-element.27.after_ref.refs_2_, f32[256,256]{1,0:T(8,128)S(1)} %get-tuple-element.28.refs_3_, ...), custom_call_target="tpu_custom_call" | custom-call | tf_op jit(solution)/shard_map/solve/pallas_call | solution.py:176
  (30 shorter events, 0.3 us)
Async XLA Ops:
  0.0 2.2 %copy-start.7 = (f32[256,256]{1,0:T(8,128)S(1)}, f32[256,256]{1,0:T(8,128)}, u32[]{:S(2)}) copy-start(f32[256,256]{1,0:T(8,128)} %param.3) | copy-start | bytes 786436
  3.4 34.7 %all-to-all-start = ((f32[8,160,256]{2,1,0:T(8,128)}), f32[8,160,256]{2,1,0:T(8,128)S(1)}, u32[]{:S(2)}, u32[]{:S(2)}) async-start(f32[8,160,256]{2,1,0:T(8,128)} %bitcast.6), calls=%async_computation | async-start | bytes 2621440 | tf_op jit(solution)/shard_map/all_to_all | solution.py:362
  39.7 3.3 %collective-permute-start = (f32[5,256,256]{2,1,0:T(8,128)S(1)}, f32[5,256,256]{2,1,0:T(8,128)S(1)}, u32[]{:S(2)}, u32[]{:S(2)}) collective-permute-start(f32[5,256,256]{2,1,0:T(8,128)S(1)} %get-tuple-element.21), channel_id=1, source_target_pairs={{0,1},{1,0},{2,3},{3,2},{4,5},{5,4},{6,7},{7,6},{8,9},{9,8},{10,11... | collective-permute-start | bytes 3932168 | tf_op jit(solution)/shard_map/ppermute | solution.py:329
  66.5 7.2 %collective-permute-start.1 = (f32[160,256]{1,0:T(8,128)S(1)}, f32[160,256]{1,0:T(8,128)S(1)}, u32[]{:S(2)}, u32[]{:S(2)}) collective-permute-start(f32[160,256]{1,0:T(8,128)S(1)} %reduce_sum.9), channel_id=1, source_target_pairs={{0,16},{16,0},{1,17},{17,1},{2,18},{18,2},{3,19},{19,3},{4,20},{20... | collective-permute-start | bytes 491528 | tf_op jit(solution)/shard_map/ppermute | solution.py:329
  73.8 8.1 %collective-permute-start.3 = (f32[160,256]{1,0:T(8,128)S(1)}, f32[160,256]{1,0:T(8,128)S(1)}, u32[]{:S(2)}, u32[]{:S(2)}) collective-permute-start(f32[160,256]{1,0:T(8,128)S(1)} %get-tuple-element.36), channel_id=1, source_target_pairs={{0,8},{2,10},{4,12},{6,14},{8,0},{10,2},{12,4},{14,6},{1,9},{3,11}... | collective-permute-start | bytes 491528 | tf_op jit(solution)/shard_map/ppermute | solution.py:325
  77.9 5.7 %collective-permute-start.2 = (f32[160,256]{1,0:T(8,128)S(1)}, f32[160,256]{1,0:T(8,128)S(1)}, u32[]{:S(2)}, u32[]{:S(2)}) collective-permute-start(f32[160,256]{1,0:T(8,128)S(1)} %get-tuple-element.36), channel_id=1, source_target_pairs={{0,4},{2,6},{4,0},{6,2},{8,12},{10,14},{12,8},{14,10},{1,5},{3,7},... | collective-permute-start | bytes 491528 | tf_op jit(solution)/shard_map/ppermute | solution.py:325
  80.1 15.0 %collective-permute-start.10 = (f32[2,4,256,256]{3,2,1,0:T(8,128)S(1)}, f32[2,4,256,256]{3,2,1,0:T(8,128)S(1)}, u32[]{:S(2)}, u32[]{:S(2)}) collective-permute-start(f32[2,4,256,256]{3,2,1,0:T(8,128)S(1)} %get-tuple-element.33), channel_id=1, source_target_pairs={{0,1},{1,0},{2,3},{3,2},{4,5},{5,4},{6,7},{7,6},{8,9},{9,8},{10,11... | collective-permute-start | bytes 6291464 | tf_op jit(solution)/shard_map/ppermute | solution.py:329
  81.3 5.8 %collective-permute-start.5 = (f32[160,256]{1,0:T(8,128)S(1)}, f32[160,256]{1,0:T(8,128)S(1)}, u32[]{:S(2)}, u32[]{:S(2)}) collective-permute-start(f32[160,256]{1,0:T(8,128)S(1)} %get-tuple-element.36), channel_id=1, source_target_pairs={{0,2},{2,0},{4,6},{6,4},{8,10},{10,8},{12,14},{14,12},{1,3},{3,1},... | collective-permute-start | bytes 491528 | tf_op jit(solution)/shard_map/ppermute | solution.py:325
  81.9 5.2 %collective-permute-start.4 = (f32[160,256]{1,0:T(8,128)S(1)}, f32[160,256]{1,0:T(8,128)S(1)}, u32[]{:S(2)}, u32[]{:S(2)}) collective-permute-start(f32[160,256]{1,0:T(8,128)S(1)} %collective-permute-done.3), channel_id=1, source_target_pairs={{0,4},{2,6},{4,0},{6,2},{8,12},{10,14},{12,8},{14,10},{1,5},{3,7},... | collective-permute-start | bytes 491528 | tf_op jit(solution)/shard_map/ppermute | solution.py:325
  83.6 7.0 %collective-permute-start.6 = (f32[160,256]{1,0:T(8,128)S(1)}, f32[160,256]{1,0:T(8,128)S(1)}, u32[]{:S(2)}, u32[]{:S(2)}) collective-permute-start(f32[160,256]{1,0:T(8,128)S(1)} %collective-permute-done.2), channel_id=1, source_target_pairs={{0,2},{2,0},{4,6},{6,4},{8,10},{10,8},{12,14},{14,12},{1,3},{3,1},... | collective-permute-start | bytes 491528 | tf_op jit(solution)/shard_map/ppermute | solution.py:325
  87.1 4.4 %collective-permute-start.7 = (f32[160,256]{1,0:T(8,128)S(1)}, f32[160,256]{1,0:T(8,128)S(1)}, u32[]{:S(2)}, u32[]{:S(2)}) collective-permute-start(f32[160,256]{1,0:T(8,128)S(1)} %collective-permute-done.5), channel_id=1, source_target_pairs={{0,8},{2,10},{4,12},{6,14},{8,0},{10,2},{12,4},{14,6},{1,9},{3,11}... | collective-permute-start | bytes 491528 | tf_op jit(solution)/shard_map/ppermute | solution.py:325
  87.1 6.5 %collective-permute-start.8 = (f32[160,256]{1,0:T(8,128)S(1)}, f32[160,256]{1,0:T(8,128)S(1)}, u32[]{:S(2)}, u32[]{:S(2)}) collective-permute-start(f32[160,256]{1,0:T(8,128)S(1)} %collective-permute-done.4), channel_id=1, source_target_pairs={{0,2},{2,0},{4,6},{6,4},{8,10},{10,8},{12,14},{14,12},{1,3},{3,1},... | collective-permute-start | bytes 491528 | tf_op jit(solution)/shard_map/ppermute | solution.py:325
  93.7 4.1 %collective-permute-start.9 = (f32[8,160,256]{2,1,0:T(8,128)S(1)}, f32[8,160,256]{2,1,0:T(8,128)S(1)}, u32[]{:S(2)}, u32[]{:S(2)}) collective-permute-start(f32[8,160,256]{2,1,0:T(8,128)S(1)} %bitcast_dynamic-update-slice_fusion.mine_ref), channel_id=1, source_target_pairs={{0,1},{1,0},{2,3},{3,2},{4,5},{5,4},{6,7},{7,6},{8,9},{9,8},{10,11... | collective-permute-start | bytes 3932168 | tf_op jit(solution)/shard_map/ppermute | solution.py:329
  98.6 0.6 copy-start.6
  99.2 34.3 %all-to-all-start.2 = ((f32[8,256,256]{2,1,0:T(8,128)}), f32[8,256,256]{2,1,0:T(8,128)}, u32[]{:S(2)}, u32[]{:S(2)}) async-start(f32[8,256,256]{2,1,0:T(8,128)} %behind.1), calls=%async_computation.2 | async-start | bytes 4194304 | tf_op jit(solution)/shard_map/all_to_all | solution.py:403
  112.7 0.9 copy-start.2
  121.4 0.9 copy-start
  122.3 0.7 copy-start.4
  133.5 3.4 %copy-start.1 = (f32[3,256,256]{2,1,0:T(8,128)S(1)}, f32[3,256,256]{2,1,0:T(8,128)}, u32[]{:S(2)}) copy-start(f32[3,256,256]{2,1,0:T(8,128)} %copy-done) | copy-start | bytes 2359300
  135.3 27.7 %copy-start.3 = (f32[256,768]{1,0:T(8,128)S(1)}, f32[256,768]{1,0:T(8,128)}, u32[]{:S(2)}) copy-start(f32[256,768]{1,0:T(8,128)} %copy-done.2) | copy-start | bytes 2359300
  135.3 27.7 %copy-start.5 = (f32[256,256]{1,0:T(8,128)S(1)}, f32[256,256]{1,0:T(8,128)}, u32[]{:S(2)}) copy-start(f32[256,256]{1,0:T(8,128)} %copy-done.4) | copy-start | bytes 786436
  135.3 13.1 %collective-permute-start.11 = (f32[256,256]{1,0:T(8,128)S(1)}, f32[256,256]{1,0:T(8,128)S(1)}, u32[]{:S(2)}, u32[]{:S(2)}) collective-permute-start(f32[256,256]{1,0:T(8,128)S(1)} %sum_places.1.left_ref), channel_id=1, source_target_pairs={{0,16},{16,0},{1,17},{17,1},{2,18},{18,2},{3,19},{19,3},{4,20},{20... | collective-permute-start | bytes 786440 | tf_op jit(solution)/shard_map/ppermute | solution.py:329
  148.4 9.0 %collective-permute-start.14 = (f32[256,256]{1,0:T(8,128)S(1)}, f32[256,256]{1,0:T(8,128)S(1)}, u32[]{:S(2)}, u32[]{:S(2)}) collective-permute-start(f32[256,256]{1,0:T(8,128)S(1)} %add_groups.1.refs_8_), channel_id=1, source_target_pairs={{0,3},{1,2},{2,1},{3,0},{4,7},{5,6},{6,5},{7,4},{8,11},{9,10},{10,... | collective-permute-start | bytes 786440 | tf_op jit(solution)/shard_map/ppermute | solution.py:333
  149.2 13.8 %collective-permute-start.13 = (f32[256,256]{1,0:T(8,128)S(1)}, f32[256,256]{1,0:T(8,128)S(1)}, u32[]{:S(2)}, u32[]{:S(2)}) collective-permute-start(f32[256,256]{1,0:T(8,128)S(1)} %add_groups.1.refs_8_), channel_id=1, source_target_pairs={{0,2},{1,3},{2,0},{3,1},{4,6},{5,7},{6,4},{7,5},{8,10},{9,11},{10,... | collective-permute-start | bytes 786440 | tf_op jit(solution)/shard_map/ppermute | solution.py:333
  150.5 12.5 %collective-permute-start.12 = (f32[256,256]{1,0:T(8,128)S(1)}, f32[256,256]{1,0:T(8,128)S(1)}, u32[]{:S(2)}, u32[]{:S(2)}) collective-permute-start(f32[256,256]{1,0:T(8,128)S(1)} %add_groups.1.refs_8_), channel_id=1, source_target_pairs={{0,1},{1,0},{2,3},{3,2},{4,5},{5,4},{6,7},{7,6},{8,9},{9,8},{10,11... | collective-permute-start | bytes 786440 | tf_op jit(solution)/shard_map/ppermute | solution.py:333

commit v3 on v2

--- a/solution.py
+++ b/solution.py
@@ -115,33 +115,62 @@
     )
 
 
-def upper_products_kernel(place_ref, rows_ref, keep_ref, send_ref, work):
-    side = place_ref[0]
-    right = [right_parts(rows_ref[c]) for c in range(P_SIZE)]
+def mask_kernel(place_ref, arcs_ref, slab_ref, rows_ref, *refs):
+    pieces, work = refs[:-1], refs[-1]
+    top = slab_ref.shape[0]
+    work[:top, :] = slab_ref[...]
+    for a in range(arcs_ref.shape[0]):
+        live = arcs_ref[a, 0].astype(jnp.float32)
+        at = a * ARC_ROWS
+        work[top + at : top + at + ARC_ROWS, :] = rows_ref[at : at + ARC_ROWS, :] * live
+    count = pieces[0].shape[0]
+    for s, piece in enumerate(pieces):
+        start = pl.multiple_of((place_ref[4] ^ s) * count, 16)
+        piece[...] = work[pl.ds(start, count), :]
+
+
+def upper_products_kernel(place_ref, *refs):
+    blocks, (keep_ref, send_ref, columns, work) = refs[:-4], refs[-4:]
+    side, place, me = place_ref[0], place_ref[1] * P_SIZE + place_ref[2], place_ref[4]
+    for s, block in enumerate(blocks):
+        columns[me ^ s] = block[...]
+    right = [right_parts(columns[c]) for c in range(P_SIZE)]
     at = 0
     for r in range(P_SIZE):
         wide = jnp.concatenate(right[r:], axis=1)
-        product = parts_dot(left_parts(rows_ref[r]), wide)
+        product = parts_dot(left_parts(columns[r]), wide)
         for c in range(P_SIZE - r):
-            work[at] = product[:, c * B : (c + 1) * B]
+            work[at * B : (at + 1) * B, :] = product[:, c * B : (c + 1) * B]
             at += 1
-    for i in range(HALF):
-        keep_ref[i] = work[side * HALF + i]
-        send_ref[i] = work[(1 - side) * HALF + i]
-
-
-def all_products_kernel(place_ref, left_ref, right_ref, after_ref, keep_ref, send_ref, work):
-    del after_ref
-    side = place_ref[0]
-    first = right_ref.shape[0] - P_SIZE
-    right = jnp.concatenate([right_parts(right_ref[first + c]) for c in range(P_SIZE)], axis=1)
+    count = keep_ref.shape[1]
+    for t in range(PIECES // 2):
+        piece = place ^ t
+        here = pl.multiple_of((side * (PIECES // 2) + piece) * count, SUB)
+        there = pl.multiple_of(((1 - side) * (PIECES // 2) + piece) * count, SUB)
+        keep_ref[t] = work[pl.ds(here, count), :]
+        send_ref[t] = work[pl.ds(there, count), :]
+
+
+def all_products_kernel(n_left, place_ref, *refs):
+    blocks, (_, keep_ref, send_ref, columns, panels, work) = refs[:-6], refs[-6:]
+    left_blocks, right_blocks = blocks[:n_left], blocks[n_left:]
+    side, place, me = place_ref[0], place_ref[1] * P_SIZE + place_ref[2], place_ref[4]
+    for s, block in enumerate(right_blocks):
+        columns[me ^ s] = block[...]
+    for s, block in enumerate(left_blocks):
+        panels[me ^ s] = block[...]
+    left = panels if left_blocks else columns
+    first = columns.shape[0] - P_SIZE
+    right = jnp.concatenate([right_parts(columns[first + c]) for c in range(P_SIZE)], axis=1)
     for r in range(P_SIZE):
-        product = parts_dot(left_parts(left_ref[r]), right)
+        product = parts_dot(left_parts(left[r]), right)
         for b in range(P_SIZE):
-            work[r, b] = product[:, b * B : (b + 1) * B]
-    for a in range(2):
-        keep_ref[a] = work[2 * a + side]
-        send_ref[a] = work[2 * a + 1 - side]
+            work[r * P_SIZE + b] = product[:, b * B : (b + 1) * B]
+    for t in range(2 * P_SIZE):
+        spot = place ^ t
+        block = (2 * (spot // P_SIZE)) * P_SIZE + spot % P_SIZE
+        keep_ref[t] = work[block + side * P_SIZE]
+        send_ref[t] = work[block + (1 - side) * P_SIZE]
 
 
 def tie_kernel(value_ref, after_ref, out_ref):
@@ -164,16 +193,16 @@
     out_ref[...] = left_ref[...] + right_ref[...]
 
 
-def sum_kernel(parts_ref, after_ref, out_ref):
-    del after_ref
-    total = parts_ref[0]
-    for i in range(1, parts_ref.shape[0]):
-        total = total + parts_ref[i]
+def sum_kernel(*refs):
+    parts, out_ref = refs[:-2], refs[-1]
+    total = parts[0][...]
+    for part in parts[1:]:
+        total = total + part[...]
     out_ref[...] = total
 
 
 def on_chip(kernel, shapes, name, *operands, scratch=(), scalars=0, after=()):
-    return pl.pallas_call(
+    done = pl.pallas_call(
         kernel,
         out_shape=[jax.ShapeDtypeStruct(shape, jnp.float32) for shape in shapes],
         in_specs=[pl.BlockSpec(memory_space=pltpu.SMEM)] * scalars
@@ -184,6 +213,7 @@
         compiler_params=pltpu.CompilerParams(vmem_limit_bytes=16 * 1024 * 1024),
         name=name,
     )(*operands, *after)
+    return list(done)
 
 
 def collect_kernel(place_ref, mine_ref, other_ref, gram_ref, token_ref):
@@ -333,6 +363,13 @@
     return lax.ppermute(value, ("rh", "rl"), [(i, i ^ bits) for i in range(P_SIZE)])
 
 
+def collected(parts):
+    got = [parts[0]]
+    for t in range(1, 2 * P_SIZE):
+        got.append(exchange(parts[t], t // P_SIZE, t % P_SIZE))
+    return got
+
+
 def spread(piece):
     y, z, x = (0, 1), (0, 2), (1, 0)
     by_z, by_y, by_x = exchange(piece, *z), exchange(piece, *y), exchange(piece, *x)
@@ -347,43 +384,54 @@
     high_row, side = lax.axis_index("rh"), lax.axis_index("rl")
     col_index = lax.axis_index("hi") * P_SIZE + low
     row_index = high_row * 2 + side
-    n_arcs, blocks_here = arc_blocks.shape
     columns = arc_rows.shape[1]
-    live = arc_blocks.astype(jnp.float32)
-    masked = (arc_rows.reshape(n_arcs, ARC_ROWS, blocks_here, B) * live[:, None, :, None]).reshape(
-        arc_rows.shape
-    )
-    stacked = jnp.concatenate([r_slab, masked], axis=0)
-    place = jnp.stack([side, high_row, low, col_index]).astype(jnp.int32)
     in_two = n_hi == 2
     owners = ("hi", "lo") if in_two else ("lo",)
     shares = P_SIZE * n_hi if in_two else P_SIZE
-    blocks = stacked.reshape(shares, stacked.shape[0] // shares, columns)
-    blocks = lax.all_to_all(blocks, owners, 0, 0)
-    panels = blocks if in_two else from_first(blocks, n_hi)
-
-    half = (HALF, B, B)
+    me = col_index if in_two else low
+    place = jnp.stack([side, high_row, low, col_index, me]).astype(jnp.int32)
+    total = r_slab.shape[0] + arc_rows.shape[0]
+    share = (total // shares, columns)
+    blocks = on_chip(
+        mask_kernel,
+        [share] * shares,
+        "mask",
+        place,
+        arc_blocks,
+        r_slab,
+        arc_rows,
+        scalars=2,
+        scratch=[pltpu.VMEM((total, columns), jnp.float32)],
+    )
+    blocks = blocks[:1] + [
+        lax.ppermute(blocks[s], owners, [(i, i ^ s) for i in range(shares)])
+        for s in range(1, shares)
+    ]
+    panels = [] if in_two else [from_first(block, n_hi) for block in blocks]
+
+    half = (PIECES // 2, len(PAIRS) * B // PIECES, B)
+    gathered = pltpu.VMEM((shares, *share), jnp.float32)
     keep, send = on_chip(
         upper_products_kernel,
         [half, half],
         "upper_products",
         place,
-        blocks,
+        *blocks,
         scalars=1,
-        scratch=[pltpu.VMEM((len(PAIRS), B, B), jnp.float32)],
-    )
-    gram = keep + swap(send)
-    gram = lax.all_to_all(gram.reshape(2 * P_SIZE, -1, B), ("rh", "lo"), 0, 0).sum(axis=0)
-    half = (2, P_SIZE, B, B)
+        scratch=[gathered, pltpu.VMEM((len(PAIRS) * B, B), jnp.float32)],
+    )
+    gram = collected(keep + swap(send))
+    gram = functools.reduce(jnp.add, gram)
+    half = (2 * P_SIZE, B, B)
     cross, send = on_chip(
-        all_products_kernel,
+        functools.partial(all_products_kernel, len(panels)),
         [half, half],
         "all_products",
         place,
-        panels,
-        blocks,
+        *panels,
+        *blocks,
         scalars=1,
-        scratch=[pltpu.VMEM((P_SIZE, P_SIZE, B, B), jnp.float32)],
+        scratch=[gathered, gathered, pltpu.VMEM((P_SIZE * P_SIZE, B, B), jnp.float32)],
         after=(keep,),
     )
     cross = cross + swap(send)
@@ -398,11 +446,9 @@
         swap(pieces),
         scalars=1,
     )
-
-    cross = behind(cross.reshape(2 * P_SIZE, B, B), token)
-    cross = lax.all_to_all(cross, ("rh", "lo"), 0, 0)
+    cross = collected(behind(cross, token))
     rows, inverses = factor(gram)
-    (mine,) = on_chip(sum_kernel, [(B, columns)], "sum_places", cross, after=(rows[1],))
+    (mine,) = on_chip(sum_kernel, [(B, columns)], "sum_places", *cross, after=(rows[1],))
     if in_two:
         other = swap(mine, "hi")
         (mine,) = on_chip(add_kernel, [(B, columns)], "add_groups", mine, other, after=(rows[2],))

time: 171 us -> 163 us (0.953)
  blocking collectives: 21.9 us -> 0 us
  starting transfers between devices: 27.5 us -> 43.3 us
  other arithmetic: 6.66 us -> 1.99 us
  local copies, waits for them, and re-layouts: 3.28 us -> 5.37 us
    all_to_all x2 -> x0, waiting for transfers between devices: 39.5 us -> none  [the longest x1 28.9 us: on_device(): blocks = lax.all_to_all(blocks, owners, 0, 0)]
    ppermute x0 -> x7, waiting for transfers between devices: none -> 25.5 us  [on_device(): lax.ppermute(blocks[s], owners, [(i, i ^ s) for i in range(shares)])]
    all_to_all x1 -> x0, blocking collectives: 21.9 us -> none  [on_device(): lax.all_to_all(gram.reshape(2 * P_SIZE, -1, B), ('rh', 'lo'), 0, 0)]
    ppermute x7 -> x21, waiting for transfers between devices: 7.74 us -> 25.5 us  [exchange(): lax.ppermute(value, ('lo', 'rh'), [(i, i ^ bits) for i in range(2 * P_SIZ...]
    all_to_all x2 -> x0, starting transfers between devices: 10.5 us -> none  [the longest x1 5.72 us: on_device(): blocks = lax.all_to_all(blocks, owners, 0, 0)]
    ppermute x5, starting transfers between devices: 6.17 us -> 16.6 us  [swap(): return lax.ppermute(value, axis, [(0, 1), (1, 0)])]
    ppermute x7 -> x21, starting transfers between devices: 8.63 us -> 16.2 us  [exchange(): lax.ppermute(value, ('lo', 'rh'), [(i, i ^ bits) for i in range(2 * P_SIZ...]
    ppermute x0 -> x7, starting transfers between devices: none -> 7.55 us  [on_device(): lax.ppermute(blocks[s], owners, [(i, i ^ s) for i in range(shares)])]
  transfers between devices with their start and end apart: 17 -> 36, of which waited for: 12 -> 19; matrix products, arithmetic and copies ran while one was open for 1% -> 1% of each run, Pallas kernels for 19% -> 20%
where the time goes in v3:
time: 163 us; the launch traced here: 160 us
  waiting for transfers between devices  66.8 us (41%)
  starting transfers between devices  43.3 us (27%)
  Pallas kernels  42 us (26%)
  local copies, waits for them, and re-layouts  5.37 us (3%)
  other arithmetic  1.99 us (1%)
    pallas_call x11, Pallas kernels, on_chip(): pl.pallas_call(kernel, out_shape=[jax.ShapeDtypeStruct(shape, jnp.float32...  42 us
    ppermute x7, waiting for transfers between devices, on_device(): lax.ppermute(blocks[s], owners, [(i, i ^ s) for i in range(shares)])  25.5 us
    ppermute x21, waiting for transfers between devices, exchange(): lax.ppermute(value, ('lo', 'rh'), [(i, i ^ bits) for i in range(2 * P_SIZ...  25.5 us
    ppermute x5, starting transfers between devices, swap(): return lax.ppermute(value, axis, [(0, 1), (1, 0)])  16.6 us
    ppermute x21, starting transfers between devices, exchange(): lax.ppermute(value, ('lo', 'rh'), [(i, i ^ bits) for i in range(2 * P_SIZ...  16.2 us
    ppermute x5, waiting for transfers between devices, swap(): return lax.ppermute(value, axis, [(0, 1), (1, 0)])  10.4 us
    ppermute x7, starting transfers between devices, on_device(): lax.ppermute(blocks[s], owners, [(i, i ^ s) for i in range(shares)])  7.55 us
    ppermute x3, waiting for transfers between devices, across_rows(): lax.ppermute(value, ('rh', 'rl'), [(i, i ^ bits) for i in range(P_SIZE)])  5.39 us
  transfers between devices with their start and end apart: 36, of which 19 were waited for; matrix products, arithmetic and copies ran while one was open for 1% of the time, Pallas kernels for 20%

profile of v3, /device:TPU:9, one launch (start us, length us, event | category | flops | bytes accessed | tf_op | source)
XLA Modules:
  0.0 159.8 jit_solution(8393872149372150879)
XLA Ops:
  0.8 1.2 copy-done
  2.0 0.9 copy-done.1
  3.8 1.3 collective-permute-start
  5.2 1.2 collective-permute-start.2
  6.5 2.3 %collective-permute-start.3 = (f32[160,256]{1,0:T(8,128)S(1)}, f32[160,256]{1,0:T(8,128)S(1)}, u32[]{:S(2)}, u32[]{:S(2)}) collective-permute-start(f32[160,256]{1,0:T(8,128)S(1)} %get-tuple-element.32), channel_id=1, source_target_pairs={{0,16},{4,20},{8,24},{12,28},{16,0},{20,4},{24,8},{28,12},{1,17},{... | collective-permute-start | bytes 491528 | tf_op jit(solution)/shard_map/ppermute | solution.py:407
  8.8 1.0 collective-permute-start.4
  9.8 1.3 collective-permute-start.5
  11.3 5.9 %collective-permute-done.2.refs_3_ = f32[160,256]{1,0:T(8,128)S(1)} collective-permute-done((f32[160,256]{1,0:T(8,128)S(1)}, f32[160,256]{1,0:T(8,128)S(1)}, u32[]{:S(2)}, u32[]{:S(2)}) %collective-permute-start.2) | collective-permute-done | bytes 163872 | tf_op jit(solution)/shard_map/ppermute | solution.py:407
  17.9 10.4 %collective-permute-done.4.refs_5_ = f32[160,256]{1,0:T(8,128)S(1)} collective-permute-done((f32[160,256]{1,0:T(8,128)S(1)}, f32[160,256]{1,0:T(8,128)S(1)}, u32[]{:S(2)}, u32[]{:S(2)}) %collective-permute-start.4) | collective-permute-done | bytes 163872 | tf_op jit(solution)/shard_map/ppermute | solution.py:407
  28.3 3.7 %collective-permute-done.5.refs_6_ = f32[160,256]{1,0:T(8,128)S(1)} collective-permute-done((f32[160,256]{1,0:T(8,128)S(1)}, f32[160,256]{1,0:T(8,128)S(1)}, u32[]{:S(2)}, u32[]{:S(2)}) %collective-permute-start.5) | collective-permute-done | bytes 163872 | tf_op jit(solution)/shard_map/ppermute | solution.py:407
  31.9 4.9 %collective-permute-done.6.refs_7_ = f32[160,256]{1,0:T(8,128)S(1)} collective-permute-done((f32[160,256]{1,0:T(8,128)S(1)}, f32[160,256]{1,0:T(8,128)S(1)}, u32[]{:S(2)}, u32[]{:S(2)}) %collective-permute-start.6) | collective-permute-done | bytes 163872 | tf_op jit(solution)/shard_map/ppermute | solution.py:407
  36.9 1.7 %upper_products.1 = (f32[8,160,256]{2,1,0:T(8,128)S(1)}, f32[8,160,256]{2,1,0:T(8,128)S(1)}) custom-call(s32[5]{0:T(128)S(1)} %stack.47.place_ref, f32[160,256]{1,0:T(8,128)S(1)} %get-tuple-element.28.refs_0_, f32[160,256]{1,0:T(8,128)S(1)} %collective-permute-done.refs_1_, f32[160,256]{1,0:T(8,128)S(1)} %collective-permute-done.1.refs_2_, ...), custom_call_target="tpu_custom_call" | custom-call | tf_op jit(solution)/shard_map/upper_products/pallas_call | solution.py:205
  38.5 1.9 %collective-permute-start.7 = (f32[8,160,256]{2,1,0:T(8,128)S(1)}, f32[8,160,256]{2,1,0:T(8,128)S(1)}, u32[]{:S(2)}, u32[]{:S(2)}) collective-permute-start(f32[8,160,256]{2,1,0:T(8,128)S(1)} %get-tuple-element.37), channel_id=1, source_target_pairs={{0,1},{1,0},{2,3},{3,2},{4,5},{5,4},{6,7},{7,6},{8,9},{9,8},{10,11... | collective-permute-start | bytes 3932168 | tf_op jit(solution)/shard_map/ppermute | solution.py:359
  40.5 2.7 %collective-permute-done.7 = f32[8,160,256]{2,1,0:T(8,128)S(1)} collective-permute-done((f32[8,160,256]{2,1,0:T(8,128)S(1)}, f32[8,160,256]{2,1,0:T(8,128)S(1)}, u32[]{:S(2)}, u32[]{:S(2)}) %collective-permute-start.7) | collective-permute-done | bytes 1310752 | tf_op jit(solution)/shard_map/ppermute | solution.py:359
  43.5 1.3 collective-permute-start.11
  45.1 3.2 %collective-permute-start.13 = (f32[160,256]{1,0:T(8,128)S(1)}, f32[160,256]{1,0:T(8,128)S(1)}, u32[]{:S(2)}, u32[]{:S(2)}) collective-permute-start(f32[160,256]{1,0:T(8,128)S(1)} %get-tuple-element.63), channel_id=1, source_target_pairs={{0,10},{2,8},{4,14},{6,12},{8,2},{10,0},{12,6},{14,4},{1,11},{3,9}... | collective-permute-start | bytes 491528 | tf_op jit(solution)/shard_map/ppermute | solution.py:355
  48.3 1.6 collective-permute-done.10
  50.9 8.7 %collective-permute-done.12 = f32[160,256]{1,0:T(8,128)S(1)} collective-permute-done((f32[160,256]{1,0:T(8,128)S(1)}, f32[160,256]{1,0:T(8,128)S(1)}, u32[]{:S(2)}, u32[]{:S(2)}) %collective-permute-start.12) | collective-permute-done | bytes 163872 | tf_op jit(solution)/shard_map/ppermute | solution.py:355
  59.7 3.9 %collective-permute-start.15 = (f32[160,256]{1,0:T(8,128)S(1)}, f32[160,256]{1,0:T(8,128)S(1)}, u32[]{:S(2)}, u32[]{:S(2)}) collective-permute-start(f32[160,256]{1,0:T(8,128)S(1)} %fusion.6), channel_id=1, source_target_pairs={{0,16},{16,0},{1,17},{17,1},{2,18},{18,2},{3,19},{19,3},{4,20},{20... | collective-permute-start | bytes 491528 | tf_op jit(solution)/shard_map/ppermute | solution.py:359
  63.6 3.2 %collective-permute-done.15 = f32[160,256]{1,0:T(8,128)S(1)} collective-permute-done((f32[160,256]{1,0:T(8,128)S(1)}, f32[160,256]{1,0:T(8,128)S(1)}, u32[]{:S(2)}, u32[]{:S(2)}) %collective-permute-start.15) | collective-permute-done | bytes 163872 | tf_op jit(solution)/shard_map/ppermute | solution.py:359
  66.9 1.7 %collective-permute-start.17 = (f32[160,256]{1,0:T(8,128)S(1)}, f32[160,256]{1,0:T(8,128)S(1)}, u32[]{:S(2)}, u32[]{:S(2)}) collective-permute-start(f32[160,256]{1,0:T(8,128)S(1)} %get-tuple-element.52), channel_id=1, source_target_pairs={{0,8},{2,10},{4,12},{6,14},{8,0},{10,2},{12,4},{14,6},{1,9},{3,11}... | collective-permute-start | bytes 491528 | tf_op jit(solution)/shard_map/ppermute | solution.py:355
  68.9 2.2 %all_products.1 = (f32[8,256,256]{2,1,0:T(8,128)S(1)}, f32[8,256,256]{2,1,0:T(8,128)S(1)}) custom-call(s32[5]{0:T(128)S(1)} %stack.47.place_ref, f32[160,256]{1,0:T(8,128)S(1)} %get-tuple-element.28.refs_0_, f32[160,256]{1,0:T(8,128)S(1)} %collective-permute-done.refs_1_, f32[160,256]{1,0:T(8,128)S(1)} %collective-permute-done.1.refs_2_, ...), custom_call_target="tpu_custom_call" | custom-call | tf_op jit(solution)/shard_map/all_products/pallas_call | solution.py:205
  71.1 7.1 %collective-permute-start.24 = (f32[8,256,256]{2,1,0:T(8,128)S(1)}, f32[8,256,256]{2,1,0:T(8,128)S(1)}, u32[]{:S(2)}, u32[]{:S(2)}) collective-permute-start(f32[8,256,256]{2,1,0:T(8,128)S(1)} %get-tuple-element.49), channel_id=1, source_target_pairs={{0,1},{1,0},{2,3},{3,2},{4,5},{5,4},{6,7},{7,6},{8,9},{9,8},{10,11... | collective-permute-start | bytes 6291464 | tf_op jit(solution)/shard_map/ppermute | solution.py:359
  78.2 1.2 collective-permute-start.19
  79.8 4.2 %collective-permute-done.19 = f32[160,256]{1,0:T(8,128)S(1)} collective-permute-done((f32[160,256]{1,0:T(8,128)S(1)}, f32[160,256]{1,0:T(8,128)S(1)}, u32[]{:S(2)}, u32[]{:S(2)}) %collective-permute-start.19) | collective-permute-done | bytes 163872 | tf_op jit(solution)/shard_map/ppermute | solution.py:355
  84.0 0.9 collective-permute-done.18
  85.3 2.2 %collective-permute-done.20 = f32[160,256]{1,0:T(8,128)S(1)} collective-permute-done((f32[160,256]{1,0:T(8,128)S(1)}, f32[160,256]{1,0:T(8,128)S(1)}, u32[]{:S(2)}, u32[]{:S(2)}) %collective-permute-start.20) | collective-permute-done | bytes 163872 | tf_op jit(solution)/shard_map/ppermute | solution.py:355
  88.2 1.9 %collective-permute-done.22 = f32[160,256]{1,0:T(8,128)S(1)} collective-permute-done((f32[160,256]{1,0:T(8,128)S(1)}, f32[160,256]{1,0:T(8,128)S(1)}, u32[]{:S(2)}, u32[]{:S(2)}) %collective-permute-start.22) | collective-permute-done | bytes 163872 | tf_op jit(solution)/shard_map/ppermute | solution.py:355
  90.1 1.8 %collective-permute-start.23 = (f32[8,160,256]{2,1,0:T(8,128)S(1)}, f32[8,160,256]{2,1,0:T(8,128)S(1)}, u32[]{:S(2)}, u32[]{:S(2)}) collective-permute-start(f32[8,160,256]{2,1,0:T(8,128)S(1)} %bitcast_dynamic-update-slice_fusion.mine_ref), channel_id=1, source_target_pairs={{0,1},{1,0},{2,3},{3,2},{4,5},{5,4},{6,7},{7,6},{8,9},{9,8},{10,11... | collective-permute-start | bytes 3932168 | tf_op jit(solution)/shard_map/ppermute | solution.py:359
  91.9 1.7 %add.43.value_ref = f32[8,256,256]{2,1,0:T(8,128)} add(f32[8,256,256]{2,1,0:T(8,128)S(1)} %get-tuple-element.48, f32[8,256,256]{2,1,0:T(8,128)S(1)} %collective-permute-done.24) | non-fusion elementwise | flops 524288 | bytes 6291456 | tf_op jit(solution)/shard_map/add | solution.py:437
  93.6 1.0 collective-permute-done.23.other_ref
  94.6 1.0 collect.1
  96.2 1.6 %slice_bitcast_fusion = (f32[256,256]{1,0:T(8,128)S(1)}, f32[256,256]{1,0:T(8,128)S(1)}, f32[256,256]{1,0:T(8,128)S(1)}, f32[256,256]{1,0:T(8,128)S(1)}, f32[256...) fusion(f32[8,256,256]{2,1,0:T(8,128)} %behind.1), kind=kLoop, calls=%fused_computation | loop fusion | bytes 4194304 | tf_op jit(solution)/shard_map/squeeze | solution.py:369
  98.6 2.0 %collective-permute-start.27 = (f32[256,256]{1,0:T(8,128)S(1)}, f32[256,256]{1,0:T(8,128)S(1)}, u32[]{:S(2)}, u32[]{:S(2)}) collective-permute-start(f32[256,256]{1,0:T(8,128)S(1)} %get-tuple-element.57), channel_id=1, source_target_pairs={{0,12},{2,14},{4,8},{6,10},{8,4},{10,6},{12,0},{14,2},{1,13},{3,15... | collective-permute-start | bytes 786440 | tf_op jit(solution)/shard_map/ppermute | solution.py:355
  100.6 1.2 collective-permute-start.28
  101.8 3.6 %collective-permute-done.25.refs_1_ = f32[256,256]{1,0:T(8,128)S(1)} collective-permute-done((f32[256,256]{1,0:T(8,128)S(1)}, f32[256,256]{1,0:T(8,128)S(1)}, u32[]{:S(2)}, u32[]{:S(2)}) %collective-permute-start.25) | collective-permute-done | bytes 262176 | tf_op jit(solution)/shard_map/ppermute | solution.py:355
  105.4 1.5 collective-permute-start.30
  107.8 8.7 %factor_step.4 = (f32[256,768]{1,0:T(8,128)S(1)}, f32[256,256]{1,0:T(8,128)S(1)}, f32[6,256,256]{2,1,0:T(8,128)S(1)}) custom-call(f32[10,256,256]{2,1,0:T(8,128)S(1)} %get-tuple-element.38.gram_ref.refs_7_), custom_call_target="tpu_custom_call" | custom-call | tf_op jit(solution)/shard_map/factor_step/pallas_call | solution.py:205
  116.5 7.7 %factor_step.5 = (f32[256,512]{1,0:T(8,128)S(1)}, f32[256,256]{1,0:T(8,128)S(1)}, f32[3,256,256]{2,1,0:T(8,128)S(1)}) custom-call(f32[6,256,256]{2,1,0:T(8,128)S(1)} %get-tuple-element.40.gram_ref), custom_call_target="tpu_custom_call" | custom-call | tf_op jit(solution)/shard_map/factor_step/pallas_call | solution.py:205
  124.3 1.7 %collective-permute-done.31.refs_7_ = f32[256,256]{1,0:T(8,128)S(1)} collective-permute-done((f32[256,256]{1,0:T(8,128)S(1)}, f32[256,256]{1,0:T(8,128)S(1)}, u32[]{:S(2)}, u32[]{:S(2)}) %collective-permute-start.31) | collective-permute-done | bytes 262176 | tf_op jit(solution)/shard_map/ppermute | solution.py:355
  126.1 1.9 %collective-permute-start.32 = (f32[256,256]{1,0:T(8,128)S(1)}, f32[256,256]{1,0:T(8,128)S(1)}, u32[]{:S(2)}, u32[]{:S(2)}) collective-permute-start(f32[256,256]{1,0:T(8,128)S(1)} %sum_places.1.left_ref), channel_id=1, source_target_pairs={{0,16},{16,0},{1,17},{17,1},{2,18},{18,2},{3,19},{19,3},{4,20},{20... | collective-permute-start | bytes 786440 | tf_op jit(solution)/shard_map/ppermute | solution.py:359
  128.1 7.4 %factor_step.6 = (f32[256,256]{1,0:T(8,128)S(1)}, f32[256,256]{1,0:T(8,128)S(1)}, f32[1,256,256]{2,1,0:T(8,128)S(1)}) custom-call(f32[3,256,256]{2,1,0:T(8,128)S(1)} %get-tuple-element.42.gram_ref), custom_call_target="tpu_custom_call" | custom-call | tf_op jit(solution)/shard_map/factor_step/pallas_call | solution.py:205
  135.5 3.5 %collective-permute-done.32.right_ref = f32[256,256]{1,0:T(8,128)S(1)} collective-permute-done((f32[256,256]{1,0:T(8,128)S(1)}, f32[256,256]{1,0:T(8,128)S(1)}, u32[]{:S(2)}, u32[]{:S(2)}) %collective-permute-start.32) | collective-permute-done | bytes 262176 | tf_op jit(solution)/shard_map/ppermute | solution.py:359
  139.1 1.2 collective-permute-start.33
  140.6 1.4 collective-permute-start.35
  142.0 6.5 %factor_step.7.refs_6_ = f32[256,256]{1,0:T(8,128)S(1)} custom-call(f32[1,256,256]{2,1,0:T(8,128)S(1)} %get-tuple-element.47.gram_ref), custom_call_target="tpu_custom_call" | custom-call | tf_op jit(solution)/shard_map/factor_step/pallas_call | solution.py:205
  148.6 5.4 %collective-permute-done.35.refs_11_ = f32[256,256]{1,0:T(8,128)S(1)} collective-permute-done((f32[256,256]{1,0:T(8,128)S(1)}, f32[256,256]{1,0:T(8,128)S(1)}, u32[]{:S(2)}, u32[]{:S(2)}) %collective-permute-start.35) | collective-permute-done | bytes 262176 | tf_op jit(solution)/shard_map/ppermute | solution.py:363
  154.0 5.8 %solve.1 = f32[256,256]{1,0:T(8,128)} custom-call(s32[5]{0:T(128)S(1)} %stack.47.place_ref, f32[256,768]{1,0:T(8,128)S(1)} %get-tuple-element.39.refs_0_, f32[256,512]{1,0:T(8,128)S(1)} %get-tuple-element.41.refs_8_.refs_1_, f32[256,256]{1,0:T(8,128)S(1)} %get-tuple-element.43.after_ref.refs_2_, f32[256,256]{1,0:T(8,128)S(1)} %get-tuple-element.44.refs_3_, ...), custom_call_target="tpu_custom_call" | custom-call | tf_op jit(solution)/shard_map/solve/pallas_call | solution.py:205
  (57 shorter events, 8.9 us)
Async XLA Ops:
  0.8 1.2 copy-start
  2.0 0.9 copy-start.1
  3.8 6.0 %collective-permute-start = (f32[160,256]{1,0:T(8,128)S(1)}, f32[160,256]{1,0:T(8,128)S(1)}, u32[]{:S(2)}, u32[]{:S(2)}) collective-permute-start(f32[160,256]{1,0:T(8,128)S(1)} %get-tuple-element.29), channel_id=1, source_target_pairs={{0,4},{4,0},{8,12},{12,8},{16,20},{20,16},{24,28},{28,24},{1,5},{5... | collective-permute-start | bytes 491528 | tf_op jit(solution)/shard_map/ppermute | solution.py:407
  5.1 6.0 %collective-permute-start.1 = (f32[160,256]{1,0:T(8,128)S(1)}, f32[160,256]{1,0:T(8,128)S(1)}, u32[]{:S(2)}, u32[]{:S(2)}) collective-permute-start(f32[160,256]{1,0:T(8,128)S(1)} %get-tuple-element.30), channel_id=1, source_target_pairs={{0,8},{4,12},{8,0},{12,4},{16,24},{20,28},{24,16},{28,20},{1,9},{5... | collective-permute-start | bytes 491528 | tf_op jit(solution)/shard_map/ppermute | solution.py:407
  5.2 12.0 %collective-permute-start.2 = (f32[160,256]{1,0:T(8,128)S(1)}, f32[160,256]{1,0:T(8,128)S(1)}, u32[]{:S(2)}, u32[]{:S(2)}) collective-permute-start(f32[160,256]{1,0:T(8,128)S(1)} %get-tuple-element.31), channel_id=1, source_target_pairs={{0,12},{4,8},{8,4},{12,0},{16,28},{20,24},{24,20},{28,16},{1,13},{... | collective-permute-start | bytes 491528 | tf_op jit(solution)/shard_map/ppermute | solution.py:407
  6.5 11.4 %collective-permute-start.3 = (f32[160,256]{1,0:T(8,128)S(1)}, f32[160,256]{1,0:T(8,128)S(1)}, u32[]{:S(2)}, u32[]{:S(2)}) collective-permute-start(f32[160,256]{1,0:T(8,128)S(1)} %get-tuple-element.32), channel_id=1, source_target_pairs={{0,16},{4,20},{8,24},{12,28},{16,0},{20,4},{24,8},{28,12},{1,17},{... | collective-permute-start | bytes 491528 | tf_op jit(solution)/shard_map/ppermute | solution.py:407
  8.8 19.5 %collective-permute-start.4 = (f32[160,256]{1,0:T(8,128)S(1)}, f32[160,256]{1,0:T(8,128)S(1)}, u32[]{:S(2)}, u32[]{:S(2)}) collective-permute-start(f32[160,256]{1,0:T(8,128)S(1)} %get-tuple-element.33), channel_id=1, source_target_pairs={{0,20},{4,16},{8,28},{12,24},{16,4},{20,0},{24,12},{28,8},{1,21},{... | collective-permute-start | bytes 491528 | tf_op jit(solution)/shard_map/ppermute | solution.py:407
  9.8 22.1 %collective-permute-start.5 = (f32[160,256]{1,0:T(8,128)S(1)}, f32[160,256]{1,0:T(8,128)S(1)}, u32[]{:S(2)}, u32[]{:S(2)}) collective-permute-start(f32[160,256]{1,0:T(8,128)S(1)} %get-tuple-element.34), channel_id=1, source_target_pairs={{0,24},{4,28},{8,16},{12,20},{16,8},{20,12},{24,0},{28,4},{1,25},{... | collective-permute-start | bytes 491528 | tf_op jit(solution)/shard_map/ppermute | solution.py:407
  11.1 25.8 %collective-permute-start.6 = (f32[160,256]{1,0:T(8,128)S(1)}, f32[160,256]{1,0:T(8,128)S(1)}, u32[]{:S(2)}, u32[]{:S(2)}) collective-permute-start(f32[160,256]{1,0:T(8,128)S(1)} %get-tuple-element.35), channel_id=1, source_target_pairs={{0,28},{4,24},{8,20},{12,16},{16,12},{20,8},{24,4},{28,0},{1,29},{... | collective-permute-start | bytes 491528 | tf_op jit(solution)/shard_map/ppermute | solution.py:407
  38.5 4.6 %collective-permute-start.7 = (f32[8,160,256]{2,1,0:T(8,128)S(1)}, f32[8,160,256]{2,1,0:T(8,128)S(1)}, u32[]{:S(2)}, u32[]{:S(2)}) collective-permute-start(f32[8,160,256]{2,1,0:T(8,128)S(1)} %get-tuple-element.37), channel_id=1, source_target_pairs={{0,1},{1,0},{2,3},{3,2},{4,5},{5,4},{6,7},{7,6},{8,9},{9,8},{10,11... | collective-permute-start | bytes 3932168 | tf_op jit(solution)/shard_map/ppermute | solution.py:359
  43.4 6.5 %collective-permute-start.10 = (f32[160,256]{1,0:T(8,128)S(1)}, f32[160,256]{1,0:T(8,128)S(1)}, u32[]{:S(2)}, u32[]{:S(2)}) collective-permute-start(f32[160,256]{1,0:T(8,128)S(1)} %get-tuple-element.66), channel_id=1, source_target_pairs={{0,12},{2,14},{4,8},{6,10},{8,4},{10,6},{12,0},{14,2},{1,13},{3,15... | collective-permute-start | bytes 491528 | tf_op jit(solution)/shard_map/ppermute | solution.py:355
  43.5 6.6 %collective-permute-start.11 = (f32[160,256]{1,0:T(8,128)S(1)}, f32[160,256]{1,0:T(8,128)S(1)}, u32[]{:S(2)}, u32[]{:S(2)}) collective-permute-start(f32[160,256]{1,0:T(8,128)S(1)} %get-tuple-element.65), channel_id=1, source_target_pairs={{0,2},{2,0},{4,6},{6,4},{8,10},{10,8},{12,14},{14,12},{1,3},{3,1},... | collective-permute-start | bytes 491528 | tf_op jit(solution)/shard_map/ppermute | solution.py:355
  44.8 14.8 %collective-permute-start.12 = (f32[160,256]{1,0:T(8,128)S(1)}, f32[160,256]{1,0:T(8,128)S(1)}, u32[]{:S(2)}, u32[]{:S(2)}) collective-permute-start(f32[160,256]{1,0:T(8,128)S(1)} %get-tuple-element.64), channel_id=1, source_target_pairs={{0,6},{2,4},{4,2},{6,0},{8,14},{10,12},{12,10},{14,8},{1,7},{3,5},... | collective-permute-start | bytes 491528 | tf_op jit(solution)/shard_map/ppermute | solution.py:355
  45.1 14.5 %collective-permute-start.13 = (f32[160,256]{1,0:T(8,128)S(1)}, f32[160,256]{1,0:T(8,128)S(1)}, u32[]{:S(2)}, u32[]{:S(2)}) collective-permute-start(f32[160,256]{1,0:T(8,128)S(1)} %get-tuple-element.63), channel_id=1, source_target_pairs={{0,10},{2,8},{4,14},{6,12},{8,2},{10,0},{12,6},{14,4},{1,11},{3,9}... | collective-permute-start | bytes 491528 | tf_op jit(solution)/shard_map/ppermute | solution.py:355
  48.2 11.4 %collective-permute-start.14 = (f32[160,256]{1,0:T(8,128)S(1)}, f32[160,256]{1,0:T(8,128)S(1)}, u32[]{:S(2)}, u32[]{:S(2)}) collective-permute-start(f32[160,256]{1,0:T(8,128)S(1)} %get-tuple-element.62), channel_id=1, source_target_pairs={{0,14},{2,12},{4,10},{6,8},{8,6},{10,4},{12,2},{14,0},{1,15},{3,13... | collective-permute-start | bytes 491528 | tf_op jit(solution)/shard_map/ppermute | solution.py:355
  49.9 9.7 %collective-permute-start.8 = (f32[160,256]{1,0:T(8,128)S(1)}, f32[160,256]{1,0:T(8,128)S(1)}, u32[]{:S(2)}, u32[]{:S(2)}) collective-permute-start(f32[160,256]{1,0:T(8,128)S(1)} %get-tuple-element.61), channel_id=1, source_target_pairs={{0,4},{2,6},{4,0},{6,2},{8,12},{10,14},{12,8},{14,10},{1,5},{3,7},... | collective-permute-start | bytes 491528 | tf_op jit(solution)/shard_map/ppermute | solution.py:355
  50.1 9.5 %collective-permute-start.9 = (f32[160,256]{1,0:T(8,128)S(1)}, f32[160,256]{1,0:T(8,128)S(1)}, u32[]{:S(2)}, u32[]{:S(2)}) collective-permute-start(f32[160,256]{1,0:T(8,128)S(1)} %get-tuple-element.67), channel_id=1, source_target_pairs={{0,8},{2,10},{4,12},{6,14},{8,0},{10,2},{12,4},{14,6},{1,9},{3,11}... | collective-permute-start | bytes 491528 | tf_op jit(solution)/shard_map/ppermute | solution.py:355
  59.7 7.1 %collective-permute-start.15 = (f32[160,256]{1,0:T(8,128)S(1)}, f32[160,256]{1,0:T(8,128)S(1)}, u32[]{:S(2)}, u32[]{:S(2)}) collective-permute-start(f32[160,256]{1,0:T(8,128)S(1)} %fusion.6), channel_id=1, source_target_pairs={{0,16},{16,0},{1,17},{17,1},{2,18},{18,2},{3,19},{19,3},{4,20},{20... | collective-permute-start | bytes 491528 | tf_op jit(solution)/shard_map/ppermute | solution.py:359
  66.9 12.5 %collective-permute-start.17 = (f32[160,256]{1,0:T(8,128)S(1)}, f32[160,256]{1,0:T(8,128)S(1)}, u32[]{:S(2)}, u32[]{:S(2)}) collective-permute-start(f32[160,256]{1,0:T(8,128)S(1)} %get-tuple-element.52), channel_id=1, source_target_pairs={{0,8},{2,10},{4,12},{6,14},{8,0},{10,2},{12,4},{14,6},{1,9},{3,11}... | collective-permute-start | bytes 491528 | tf_op jit(solution)/shard_map/ppermute | solution.py:355
  68.6 10.9 %collective-permute-start.16 = (f32[160,256]{1,0:T(8,128)S(1)}, f32[160,256]{1,0:T(8,128)S(1)}, u32[]{:S(2)}, u32[]{:S(2)}) collective-permute-start(f32[160,256]{1,0:T(8,128)S(1)} %get-tuple-element.52), channel_id=1, source_target_pairs={{0,4},{2,6},{4,0},{6,2},{8,12},{10,14},{12,8},{14,10},{1,5},{3,7},... | collective-permute-start | bytes 491528 | tf_op jit(solution)/shard_map/ppermute | solution.py:355
  71.1 20.8 %collective-permute-start.24 = (f32[8,256,256]{2,1,0:T(8,128)S(1)}, f32[8,256,256]{2,1,0:T(8,128)S(1)}, u32[]{:S(2)}, u32[]{:S(2)}) collective-permute-start(f32[8,256,256]{2,1,0:T(8,128)S(1)} %get-tuple-element.49), channel_id=1, source_target_pairs={{0,1},{1,0},{2,3},{3,2},{4,5},{5,4},{6,7},{7,6},{8,9},{9,8},{10,11... | collective-permute-start | bytes 6291464 | tf_op jit(solution)/shard_map/ppermute | solution.py:359
  78.2 5.8 %collective-permute-start.19 = (f32[160,256]{1,0:T(8,128)S(1)}, f32[160,256]{1,0:T(8,128)S(1)}, u32[]{:S(2)}, u32[]{:S(2)}) collective-permute-start(f32[160,256]{1,0:T(8,128)S(1)} %get-tuple-element.52), channel_id=1, source_target_pairs={{0,2},{2,0},{4,6},{6,4},{8,10},{10,8},{12,14},{14,12},{1,3},{3,1},... | collective-permute-start | bytes 491528 | tf_op jit(solution)/shard_map/ppermute | solution.py:355
  79.4 5.4 %collective-permute-start.18 = (f32[160,256]{1,0:T(8,128)S(1)}, f32[160,256]{1,0:T(8,128)S(1)}, u32[]{:S(2)}, u32[]{:S(2)}) collective-permute-start(f32[160,256]{1,0:T(8,128)S(1)} %collective-permute-done.17), channel_id=1, source_target_pairs={{0,4},{2,6},{4,0},{6,2},{8,12},{10,14},{12,8},{14,10},{1,5},{3,7},... | collective-permute-start | bytes 491528 | tf_op jit(solution)/shard_map/ppermute | solution.py:355
  79.4 8.0 %collective-permute-start.20 = (f32[160,256]{1,0:T(8,128)S(1)}, f32[160,256]{1,0:T(8,128)S(1)}, u32[]{:S(2)}, u32[]{:S(2)}) collective-permute-start(f32[160,256]{1,0:T(8,128)S(1)} %collective-permute-done.16), channel_id=1, source_target_pairs={{0,2},{2,0},{4,6},{6,4},{8,10},{10,8},{12,14},{14,12},{1,3},{3,1},... | collective-permute-start | bytes 491528 | tf_op jit(solution)/shard_map/ppermute | solution.py:355
  84.0 4.3 %collective-permute-start.21 = (f32[160,256]{1,0:T(8,128)S(1)}, f32[160,256]{1,0:T(8,128)S(1)}, u32[]{:S(2)}, u32[]{:S(2)}) collective-permute-start(f32[160,256]{1,0:T(8,128)S(1)} %collective-permute-done.19), channel_id=1, source_target_pairs={{0,8},{2,10},{4,12},{6,14},{8,0},{10,2},{12,4},{14,6},{1,9},{3,11}... | collective-permute-start | bytes 491528 | tf_op jit(solution)/shard_map/ppermute | solution.py:355
  84.9 5.2 %collective-permute-start.22 = (f32[160,256]{1,0:T(8,128)S(1)}, f32[160,256]{1,0:T(8,128)S(1)}, u32[]{:S(2)}, u32[]{:S(2)}) collective-permute-start(f32[160,256]{1,0:T(8,128)S(1)} %collective-permute-done.18), channel_id=1, source_target_pairs={{0,2},{2,0},{4,6},{6,4},{8,10},{10,8},{12,14},{14,12},{1,3},{3,1},... | collective-permute-start | bytes 491528 | tf_op jit(solution)/shard_map/ppermute | solution.py:355
  90.1 4.5 %collective-permute-start.23 = (f32[8,160,256]{2,1,0:T(8,128)S(1)}, f32[8,160,256]{2,1,0:T(8,128)S(1)}, u32[]{:S(2)}, u32[]{:S(2)}) collective-permute-start(f32[8,160,256]{2,1,0:T(8,128)S(1)} %bitcast_dynamic-update-slice_fusion.mine_ref), channel_id=1, source_target_pairs={{0,1},{1,0},{2,3},{3,2},{4,5},{5,4},{6,7},{7,6},{8,9},{9,8},{10,11... | collective-permute-start | bytes 3932168 | tf_op jit(solution)/shard_map/ppermute | solution.py:359
  95.6 0.6 copy-start.2
  97.9 7.6 %collective-permute-start.25 = (f32[256,256]{1,0:T(8,128)S(1)}, f32[256,256]{1,0:T(8,128)S(1)}, u32[]{:S(2)}, u32[]{:S(2)}) collective-permute-start(f32[256,256]{1,0:T(8,128)S(1)} %get-tuple-element.59), channel_id=1, source_target_pairs={{0,4},{2,6},{4,0},{6,2},{8,12},{10,14},{12,8},{14,10},{1,5},{3,7},... | collective-permute-start | bytes 786440 | tf_op jit(solution)/shard_map/ppermute | solution.py:355
  97.9 9.0 %collective-permute-start.26 = (f32[256,256]{1,0:T(8,128)S(1)}, f32[256,256]{1,0:T(8,128)S(1)}, u32[]{:S(2)}, u32[]{:S(2)}) collective-permute-start(f32[256,256]{1,0:T(8,128)S(1)} %get-tuple-element.58), channel_id=1, source_target_pairs={{0,8},{2,10},{4,12},{6,14},{8,0},{10,2},{12,4},{14,6},{1,9},{3,11}... | collective-permute-start | bytes 786440 | tf_op jit(solution)/shard_map/ppermute | solution.py:355
  98.6 25.7 %collective-permute-start.27 = (f32[256,256]{1,0:T(8,128)S(1)}, f32[256,256]{1,0:T(8,128)S(1)}, u32[]{:S(2)}, u32[]{:S(2)}) collective-permute-start(f32[256,256]{1,0:T(8,128)S(1)} %get-tuple-element.57), channel_id=1, source_target_pairs={{0,12},{2,14},{4,8},{6,10},{8,4},{10,6},{12,0},{14,2},{1,13},{3,15... | collective-permute-start | bytes 786440 | tf_op jit(solution)/shard_map/ppermute | solution.py:355
  100.6 23.7 %collective-permute-start.28 = (f32[256,256]{1,0:T(8,128)S(1)}, f32[256,256]{1,0:T(8,128)S(1)}, u32[]{:S(2)}, u32[]{:S(2)}) collective-permute-start(f32[256,256]{1,0:T(8,128)S(1)} %get-tuple-element.56), channel_id=1, source_target_pairs={{0,2},{2,0},{4,6},{6,4},{8,10},{10,8},{12,14},{14,12},{1,3},{3,1},... | collective-permute-start | bytes 786440 | tf_op jit(solution)/shard_map/ppermute | solution.py:355
  101.8 22.5 %collective-permute-start.29 = (f32[256,256]{1,0:T(8,128)S(1)}, f32[256,256]{1,0:T(8,128)S(1)}, u32[]{:S(2)}, u32[]{:S(2)}) collective-permute-start(f32[256,256]{1,0:T(8,128)S(1)} %get-tuple-element.55), channel_id=1, source_target_pairs={{0,6},{2,4},{4,2},{6,0},{8,14},{10,12},{12,10},{14,8},{1,7},{3,5},... | collective-permute-start | bytes 786440 | tf_op jit(solution)/shard_map/ppermute | solution.py:355
  105.4 18.9 %collective-permute-start.30 = (f32[256,256]{1,0:T(8,128)S(1)}, f32[256,256]{1,0:T(8,128)S(1)}, u32[]{:S(2)}, u32[]{:S(2)}) collective-permute-start(f32[256,256]{1,0:T(8,128)S(1)} %get-tuple-element.54), channel_id=1, source_target_pairs={{0,10},{2,8},{4,14},{6,12},{8,2},{10,0},{12,6},{14,4},{1,11},{3,9}... | collective-permute-start | bytes 786440 | tf_op jit(solution)/shard_map/ppermute | solution.py:355
  107.0 19.0 %collective-permute-start.31 = (f32[256,256]{1,0:T(8,128)S(1)}, f32[256,256]{1,0:T(8,128)S(1)}, u32[]{:S(2)}, u32[]{:S(2)}) collective-permute-start(f32[256,256]{1,0:T(8,128)S(1)} %get-tuple-element.53), channel_id=1, source_target_pairs={{0,14},{2,12},{4,10},{6,8},{8,6},{10,4},{12,2},{14,0},{1,15},{3,13... | collective-permute-start | bytes 786440 | tf_op jit(solution)/shard_map/ppermute | solution.py:355
  126.1 12.9 %collective-permute-start.32 = (f32[256,256]{1,0:T(8,128)S(1)}, f32[256,256]{1,0:T(8,128)S(1)}, u32[]{:S(2)}, u32[]{:S(2)}) collective-permute-start(f32[256,256]{1,0:T(8,128)S(1)} %sum_places.1.left_ref), channel_id=1, source_target_pairs={{0,16},{16,0},{1,17},{17,1},{2,18},{18,2},{3,19},{19,3},{4,20},{20... | collective-permute-start | bytes 786440 | tf_op jit(solution)/shard_map/ppermute | solution.py:359
  139.1 9.5 %collective-permute-start.33 = (f32[256,256]{1,0:T(8,128)S(1)}, f32[256,256]{1,0:T(8,128)S(1)}, u32[]{:S(2)}, u32[]{:S(2)}) collective-permute-start(f32[256,256]{1,0:T(8,128)S(1)} %add_groups.1.refs_8_), channel_id=1, source_target_pairs={{0,1},{1,0},{2,3},{3,2},{4,5},{5,4},{6,7},{7,6},{8,9},{9,8},{10,11... | collective-permute-start | bytes 786440 | tf_op jit(solution)/shard_map/ppermute | solution.py:363
  140.3 8.3 %collective-permute-start.34 = (f32[256,256]{1,0:T(8,128)S(1)}, f32[256,256]{1,0:T(8,128)S(1)}, u32[]{:S(2)}, u32[]{:S(2)}) collective-permute-start(f32[256,256]{1,0:T(8,128)S(1)} %add_groups.1.refs_8_), channel_id=1, source_target_pairs={{0,2},{1,3},{2,0},{3,1},{4,6},{5,7},{6,4},{7,5},{8,10},{9,11},{10,... | collective-permute-start | bytes 786440 | tf_op jit(solution)/shard_map/ppermute | solution.py:363
  140.6 13.4 %collective-permute-start.35 = (f32[256,256]{1,0:T(8,128)S(1)}, f32[256,256]{1,0:T(8,128)S(1)}, u32[]{:S(2)}, u32[]{:S(2)}) collective-permute-start(f32[256,256]{1,0:T(8,128)S(1)} %add_groups.1.refs_8_), channel_id=1, source_target_pairs={{0,3},{1,2},{2,1},{3,0},{4,7},{5,6},{6,5},{7,4},{8,11},{9,10},{10,... | collective-permute-start | bytes 786440 | tf_op jit(solution)/shard_map/ppermute | solution.py:363

commit v4 on v2

--- a/solution.py
+++ b/solution.py
@@ -13,17 +13,35 @@
 ARC_ROWS = 128
 NB = 128
 SUB = 8
-HIGHEST = lax.Precision.HIGHEST
+
+
+def split(value):
+    high = value.astype(jnp.bfloat16)
+    return high, (value - high.astype(jnp.float32)).astype(jnp.bfloat16)
+
+
+def left_parts(value, axis=0):
+    high, low = split(value)
+    return jnp.concatenate([high, high, low], axis=axis)
+
+
+def right_parts(value):
+    high, low = split(value)
+    return jnp.concatenate([high, low, high], axis=0)
+
+
+def parts_dot(left, right):
+    return lax.dot_general(
+        left, right, (((0,), (0,)), ((), ())), preferred_element_type=jnp.float32
+    )
 
 
 def dot(left, right):
-    return jnp.dot(left, right, precision=HIGHEST, preferred_element_type=jnp.float32)
+    return jnp.dot(left_parts(left, 1), right_parts(right), preferred_element_type=jnp.float32)
 
 
 def dot_t(left, right):
-    return lax.dot_general(
-        left, right, (((0,), (0,)), ((), ())), precision=HIGHEST, preferred_element_type=jnp.float32
-    )
+    return parts_dot(left_parts(left), right_parts(right))
 
 
 def lane(value, at):
@@ -94,49 +112,49 @@
 PIECES = 4 * P_SIZE
 
 
-def split(value):
-    high = value.astype(jnp.bfloat16)
-    return high, (value - high.astype(jnp.float32)).astype(jnp.bfloat16)
-
-
-def left_parts(value):
-    high, low = split(value)
-    return jnp.concatenate([high, high, low], axis=0)
-
-
-def right_parts(value):
-    high, low = split(value)
-    return jnp.concatenate([high, low, high], axis=0)
-
-
-def parts_dot(left, right):
-    return lax.dot_general(
-        left, right, (((0,), (0,)), ((), ())), preferred_element_type=jnp.float32
-    )
-
-
-def upper_products_kernel(place_ref, rows_ref, keep_ref, send_ref, work):
-    side = place_ref[0]
-    right = [right_parts(rows_ref[c]) for c in range(P_SIZE)]
+def mask_kernel(arcs_ref, slab_ref, rows_ref, out_ref):
+    top = slab_ref.shape[0]
+    out_ref[:top, :] = slab_ref[...]
+    for a in range(arcs_ref.shape[0]):
+        live = arcs_ref[a, 0].astype(jnp.float32)
+        at = a * ARC_ROWS
+        out_ref[top + at : top + at + ARC_ROWS, :] = rows_ref[at : at + ARC_ROWS, :] * live
+
+
+def upper_products_kernel(place_ref, blocks_ref, keep_ref, send_ref, other_ref, work):
+    side, group = place_ref[0], place_ref[4]
+    right = [right_parts(blocks_ref[c]) for c in range(P_SIZE)]
     at = 0
     for r in range(P_SIZE):
         wide = jnp.concatenate(right[r:], axis=1)
-        product = parts_dot(left_parts(rows_ref[r]), wide)
+        product = parts_dot(left_parts(blocks_ref[r]), wide)
         for c in range(P_SIZE - r):
             work[at] = product[:, c * B : (c + 1) * B]
             at += 1
     for i in range(HALF):
         keep_ref[i] = work[side * HALF + i]
         send_ref[i] = work[(1 - side) * HALF + i]
-
-
-def all_products_kernel(place_ref, left_ref, right_ref, after_ref, keep_ref, send_ref, work):
-    del after_ref
-    side = place_ref[0]
-    first = right_ref.shape[0] - P_SIZE
-    right = jnp.concatenate([right_parts(right_ref[first + c]) for c in range(P_SIZE)], axis=1)
+    count = other_ref.shape[1]
+    start = pl.multiple_of(jnp.where(group == 0, count, 0), 16)
+    for c in range(P_SIZE):
+        other_ref[c] = blocks_ref[c, pl.ds(start, count), :]
+
+
+def all_products_kernel(place_ref, blocks_ref, got_ref, _, keep_ref, send_ref, pair, work):
+    side, group = place_ref[0], place_ref[4]
+    count = got_ref.shape[1]
+    if count < blocks_ref.shape[1]:
+        start = pl.multiple_of(jnp.where(group == 0, 0, count), 16)
+        mine = jnp.minimum(group, 1)
+        for c in range(P_SIZE):
+            pair[mine, c] = blocks_ref[c, pl.ds(start, count), :]
+            pair[1 - mine, c] = got_ref[c]
+        left, right = pair.at[0], pair.at[1]
+    else:
+        left, right = got_ref, blocks_ref
+    right = jnp.concatenate([right_parts(right[c]) for c in range(P_SIZE)], axis=1)
     for r in range(P_SIZE):
-        product = parts_dot(left_parts(left_ref[r]), right)
+        product = parts_dot(left_parts(left[r]), right)
         for b in range(P_SIZE):
             work[r, b] = product[:, b * B : (b + 1) * B]
     for a in range(2):
@@ -164,8 +182,7 @@
     out_ref[...] = left_ref[...] + right_ref[...]
 
 
-def sum_kernel(parts_ref, after_ref, out_ref):
-    del after_ref
+def sum_kernel(parts_ref, _, out_ref):
     total = parts_ref[0]
     for i in range(1, parts_ref.shape[0]):
         total = total + parts_ref[i]
@@ -173,7 +190,7 @@
 
 
 def on_chip(kernel, shapes, name, *operands, scratch=(), scalars=0, after=()):
-    return pl.pallas_call(
+    done = pl.pallas_call(
         kernel,
         out_shape=[jax.ShapeDtypeStruct(shape, jnp.float32) for shape in shapes],
         in_specs=[pl.BlockSpec(memory_space=pltpu.SMEM)] * scalars
@@ -184,13 +201,14 @@
         compiler_params=pltpu.CompilerParams(vmem_limit_bytes=16 * 1024 * 1024),
         name=name,
     )(*operands, *after)
-
-
-def collect_kernel(place_ref, mine_ref, other_ref, gram_ref, token_ref):
+    return list(done)
+
+
+def collect_kernel(place_ref, mine_ref, other_ref, _, gram_ref, token_ref):
     side, high, low = place_ref[0], place_ref[1], place_ref[2]
+    token_ref[...] = jnp.zeros_like(token_ref)
     at = high * P_SIZE + low
     rows = mine_ref.shape[1]
-    token_ref[...] = jnp.zeros_like(token_ref)
     for s in range(2):
         for p in range(PIECES // 2):
             start = ((s * PIECES) // 2 + p) * rows
@@ -347,31 +365,27 @@
     high_row, side = lax.axis_index("rh"), lax.axis_index("rl")
     col_index = lax.axis_index("hi") * P_SIZE + low
     row_index = high_row * 2 + side
-    n_arcs, blocks_here = arc_blocks.shape
     columns = arc_rows.shape[1]
-    live = arc_blocks.astype(jnp.float32)
-    masked = (arc_rows.reshape(n_arcs, ARC_ROWS, blocks_here, B) * live[:, None, :, None]).reshape(
-        arc_rows.shape
-    )
-    stacked = jnp.concatenate([r_slab, masked], axis=0)
-    place = jnp.stack([side, high_row, low, col_index]).astype(jnp.int32)
     in_two = n_hi == 2
-    owners = ("hi", "lo") if in_two else ("lo",)
-    shares = P_SIZE * n_hi if in_two else P_SIZE
-    blocks = stacked.reshape(shares, stacked.shape[0] // shares, columns)
-    blocks = lax.all_to_all(blocks, owners, 0, 0)
-    panels = blocks if in_two else from_first(blocks, n_hi)
+    place = jnp.stack([side, high_row, low, col_index, lax.axis_index("hi")]).astype(jnp.int32)
+    total = r_slab.shape[0] + arc_rows.shape[0]
+    share = total // P_SIZE
+    (stacked,) = on_chip(
+        mask_kernel, [(total, columns)], "mask", arc_blocks, r_slab, arc_rows, scalars=1
+    )
+    blocks = lax.all_to_all(stacked.reshape(P_SIZE, share, columns), "lo", 0, 0)
 
     half = (HALF, B, B)
-    keep, send = on_chip(
+    keep, send, other = on_chip(
         upper_products_kernel,
-        [half, half],
+        [half, half, (P_SIZE, share // 2, columns)],
         "upper_products",
         place,
         blocks,
         scalars=1,
         scratch=[pltpu.VMEM((len(PAIRS), B, B), jnp.float32)],
     )
+    got = swap(other, "hi") if in_two else from_first(blocks, n_hi)
     gram = keep + swap(send)
     gram = lax.all_to_all(gram.reshape(2 * P_SIZE, -1, B), ("rh", "lo"), 0, 0).sum(axis=0)
     half = (2, P_SIZE, B, B)
@@ -380,14 +394,17 @@
         [half, half],
         "all_products",
         place,
-        panels,
         blocks,
+        got,
         scalars=1,
-        scratch=[pltpu.VMEM((P_SIZE, P_SIZE, B, B), jnp.float32)],
-        after=(keep,),
+        scratch=[
+            pltpu.VMEM((2, P_SIZE, share // 2, columns), jnp.float32),
+            pltpu.VMEM((P_SIZE, P_SIZE, B, B), jnp.float32),
+        ],
+        after=(gram,),
     )
     cross = cross + swap(send)
-    piece = gram + swap(gram, "hi") if in_two else from_first(gram, n_hi)
+    piece = from_first(gram, n_hi)
     pieces = spread(piece)
     gram, token = on_chip(
         collect_kernel,
@@ -397,8 +414,8 @@
         pieces,
         swap(pieces),
         scalars=1,
-    )
-
+        after=(cross,),
+    )
     cross = behind(cross.reshape(2 * P_SIZE, B, B), token)
     cross = lax.all_to_all(cross, ("rh", "lo"), 0, 0)
     rows, inverses = factor(gram)

time: 171 us -> 174 us (1.018)
  blocking collectives: 21.9 us -> 0 us
  waiting for transfers between devices: 66.6 us -> 85.8 us
  starting transfers between devices: 27.5 us -> 34 us
  local copies, waits for them, and re-layouts: 3.28 us -> 7.66 us
  other arithmetic: 6.66 us -> 2.96 us
  Pallas kernels: 42.5 us -> 40.4 us
    all_to_all x1 -> x0, blocking collectives: 21.9 us -> none  [on_device(): lax.all_to_all(gram.reshape(2 * P_SIZE, -1, B), ('rh', 'lo'), 0, 0)]
    all_to_all x1 -> x2, waiting for transfers between devices: 28.9 us -> 42.3 us  [the longest x1 25.8 us: on_device(): lax.all_to_all(gram.reshape(2 * P_SIZE, -1, B), ('rh', 'lo'), 0, 0)]
    ppermute x0 -> x1, waiting for transfers between devices: none -> 6.67 us  [from_first(): got = lax.ppermute(value, 'hi', [(g, g + have) for g in range(more)])]
    ppermute x0 -> x1, starting transfers between devices: none -> 5.78 us  [from_first(): got = lax.ppermute(value, 'hi', [(g, g + have) for g in range(more)])]
    ppermute x7, starting transfers between devices: 8.63 us -> 3.09 us  [exchange(): lax.ppermute(value, ('lo', 'rh'), [(i, i ^ bits) for i in range(2 * P_SIZ...]
    unnamed x22 -> x31, local copies, waits for them, and re-layouts: 3.19 us -> 7.56 us
    ppermute x5, waiting for transfers between devices: 13.6 us -> 9.76 us  [swap(): return lax.ppermute(value, axis, [(0, 1), (1, 0)])]
    ppermute x5, starting transfers between devices: 6.17 us -> 9.09 us  [swap(): return lax.ppermute(value, axis, [(0, 1), (1, 0)])]
  transfers between devices with their start and end apart: 17 -> 19, of which waited for: 12 -> 14; matrix products, arithmetic and copies ran while one was open for 1% -> 1% of each run, Pallas kernels for 19% -> 17%
where the time goes in v4:
time: 174 us; the launch traced here: 171 us
  waiting for transfers between devices  85.8 us (49%)
  Pallas kernels  40.4 us (23%)
  starting transfers between devices  34 us (20%)
  local copies, waits for them, and re-layouts  7.66 us (4%)
  other arithmetic  2.96 us (2%)
    pallas_call x11, Pallas kernels, on_chip(): pl.pallas_call(kernel, out_shape=[jax.ShapeDtypeStruct(shape, jnp.float32...  40.4 us
    all_to_all x1, waiting for transfers between devices, on_device(): lax.all_to_all(gram.reshape(2 * P_SIZE, -1, B), ('rh', 'lo'), 0, 0)  25.8 us
    all_to_all x1, waiting for transfers between devices, on_device(): blocks = lax.all_to_all(stacked.reshape(P_SIZE, share, columns), 'lo', 0, 0)  16.5 us
    all_to_all x1, waiting for transfers between devices, on_device(): cross = lax.all_to_all(cross, ('rh', 'lo'), 0, 0)  12.7 us
    ppermute x5, waiting for transfers between devices, swap(): return lax.ppermute(value, axis, [(0, 1), (1, 0)])  9.76 us
    ppermute x5, starting transfers between devices, swap(): return lax.ppermute(value, axis, [(0, 1), (1, 0)])  9.09 us
    ppermute x7, waiting for transfers between devices, exchange(): lax.ppermute(value, ('lo', 'rh'), [(i, i ^ bits) for i in range(2 * P_SIZ...  8.92 us
    unnamed x31, local copies, waits for them, and re-layouts  7.56 us
  transfers between devices with their start and end apart: 19, of which 14 were waited for; matrix products, arithmetic and copies ran while one was open for 1% of the time, Pallas kernels for 17%

profile of v4, /device:TPU:9, one launch (start us, length us, event | category | flops | bytes accessed | tf_op | source)
XLA Modules:
  0.0 171.1 jit_solution(17419683089258753255)
XLA Ops:
  0.0 0.7 copy.5.arcs_ref
  0.7 1.2 copy-done.3
  2.0 0.9 copy-done.8
  2.9 1.8 %mask.1 = f32[1280,256]{1,0:T(8,128)} custom-call(s32[8,1]{1,0:T(8,128)S(1)} %copy.5.arcs_ref, f32[256,256]{1,0:T(8,128)S(1)} %copy-done.8, f32[1024,256]{1,0:T(8,128)S(1)} %copy-done.3), custom_call_target="tpu_custom_call" | custom-call | tf_op jit(solution)/shard_map/mask/pallas_call | solution.py:193
  4.7 3.7 %all-to-all-start = ((f32[4,320,256]{2,1,0:T(8,128)}), f32[4,320,256]{2,1,0:T(8,128)S(1)}, u32[]{:S(2)}, u32[]{:S(2)}) async-start(f32[4,320,256]{2,1,0:T(8,128)} %bitcast.5), calls=%async_computation | async-start | bytes 2621440 | tf_op jit(solution)/shard_map/all_to_all | solution.py:376
  8.4 16.5 %all-to-all-done.blocks_ref = f32[4,320,256]{2,1,0:T(8,128)S(1)} async-done(((f32[4,320,256]{2,1,0:T(8,128)}), f32[4,320,256]{2,1,0:T(8,128)S(1)}, u32[]{:S(2)}, u32[]{:S(2)}) %all-to-all-start) | async-done | bytes 1310752 | tf_op jit(solution)/shard_map/all_to_all | solution.py:376
  24.9 2.3 %upper_products.1 = (f32[5,256,256]{2,1,0:T(8,128)S(1)}, f32[5,256,256]{2,1,0:T(8,128)S(1)}, f32[4,160,256]{2,1,0:T(8,128)S(1)}) custom-call(s32[5]{0:T(128)S(1)} %stack.50.place_ref, f32[4,320,256]{2,1,0:T(8,128)S(1)} %all-to-all-done.blocks_ref), custom_call_target="tpu_custom_call" | custom-call | tf_op jit(solution)/shard_map/upper_products/pallas_call | solution.py:193
  27.3 0.6 collective-permute-start
  27.8 2.7 %collective-permute-done = f32[5,256,256]{2,1,0:T(8,128)S(1)} collective-permute-done((f32[5,256,256]{2,1,0:T(8,128)S(1)}, f32[5,256,256]{2,1,0:T(8,128)S(1)}, u32[]{:S(2)}, u32[]{:S(2)}) %collective-permute-start) | collective-permute-done | bytes 1310752 | tf_op jit(solution)/shard_map/ppermute | solution.py:347
  30.5 1.3 add.10
  31.7 4.5 %all-to-all-start.1 = ((f32[8,160,256]{2,1,0:T(8,128)}), f32[8,160,256]{2,1,0:T(8,128)}, u32[]{:S(2)}, u32[]{:S(2)}) async-start(f32[8,160,256]{2,1,0:T(8,128)} %bitcast.25), calls=%async_computation.1 | async-start | bytes 2621440 | tf_op jit(solution)/shard_map/all_to_all | solution.py:390
  36.2 2.3 %collective-permute-start.10 = (f32[4,160,256]{2,1,0:T(8,128)S(1)}, f32[4,160,256]{2,1,0:T(8,128)S(1)}, u32[]{:S(2)}, u32[]{:S(2)}) collective-permute-start(f32[4,160,256]{2,1,0:T(8,128)S(1)} %get-tuple-element.23), channel_id=1, source_target_pairs={{0,16},{16,0},{1,17},{17,1},{2,18},{18,2},{3,19},{19,3},{4,20},{20... | collective-permute-start | bytes 1966088 | tf_op jit(solution)/shard_map/ppermute | solution.py:347
  38.5 25.8 %all-to-all-done.1 = f32[8,160,256]{2,1,0:T(8,128)} async-done(((f32[8,160,256]{2,1,0:T(8,128)}), f32[8,160,256]{2,1,0:T(8,128)}, u32[]{:S(2)}, u32[]{:S(2)}) %all-to-all-start.1) | async-done | bytes 1310752 | tf_op jit(solution)/shard_map/all_to_all | solution.py:390
  64.3 1.4 reduce_sum.9._
  65.7 5.8 %collective-permute-start.1 = (f32[160,256]{1,0:T(8,128)S(1)}, f32[160,256]{1,0:T(8,128)S(1)}, u32[]{:S(2)}, u32[]{:S(2)}) collective-permute-start(f32[160,256]{1,0:T(8,128)S(1)} %reduce_sum.9._), channel_id=1, source_target_pairs={{0,16},{1,17},{2,18},{3,19},{4,20},{5,21},{6,22},{7,23},{8,24},{9,... | collective-permute-start | bytes 491528 | tf_op jit(solution)/shard_map/ppermute | solution.py:335
  71.5 6.7 %collective-permute-done.1 = f32[160,256]{1,0:T(8,128)S(1)} collective-permute-done((f32[160,256]{1,0:T(8,128)S(1)}, f32[160,256]{1,0:T(8,128)S(1)}, u32[]{:S(2)}, u32[]{:S(2)}) %collective-permute-start.1) | collective-permute-done | bytes 163872 | tf_op jit(solution)/shard_map/ppermute | solution.py:335
  78.4 2.2 %all_products.1 = (f32[2,4,256,256]{3,2,1,0:T(8,128)S(1)}, f32[2,4,256,256]{3,2,1,0:T(8,128)S(1)}) custom-call(s32[5]{0:T(128)S(1)} %stack.50.place_ref, f32[4,320,256]{2,1,0:T(8,128)S(1)} %all-to-all-done.blocks_ref, f32[4,160,256]{2,1,0:T(8,128)S(1)} %collective-permute-done.10.got_ref, f32[160,256]{1,0:T(8,128)S(1)} %reduce_sum.9._), custom_call_target="tpu_custom_call" | custom-call | tf_op jit(solution)/shard_map/all_products/pallas_call | solution.py:193
  80.6 0.6 collective-permute-start.11
  81.4 2.2 %collective-permute-done.3 = f32[160,256]{1,0:T(8,128)S(1)} collective-permute-done((f32[160,256]{1,0:T(8,128)S(1)}, f32[160,256]{1,0:T(8,128)S(1)}, u32[]{:S(2)}, u32[]{:S(2)}) %collective-permute-start.3) | collective-permute-done | bytes 163872 | tf_op jit(solution)/shard_map/ppermute | solution.py:343
  83.6 0.7 collective-permute-start.6
  84.4 2.6 %collective-permute-done.5 = f32[160,256]{1,0:T(8,128)S(1)} collective-permute-done((f32[160,256]{1,0:T(8,128)S(1)}, f32[160,256]{1,0:T(8,128)S(1)}, u32[]{:S(2)}, u32[]{:S(2)}) %collective-permute-start.5) | collective-permute-done | bytes 163872 | tf_op jit(solution)/shard_map/ppermute | solution.py:343
  86.9 1.6 collective-permute-start.7
  88.6 0.3 collective-permute-start.8
  88.9 1.1 collective-permute-done.6
  90.0 1.6 collective-permute-done.7
  91.7 1.4 collective-permute-done.8
  93.1 2.5 %collective-permute-start.9 = (f32[8,160,256]{2,1,0:T(8,128)S(1)}, f32[8,160,256]{2,1,0:T(8,128)S(1)}, u32[]{:S(2)}, u32[]{:S(2)}) collective-permute-start(f32[8,160,256]{2,1,0:T(8,128)S(1)} %bitcast_dynamic-update-slice_fusion.mine_ref), channel_id=1, source_target_pairs={{0,1},{1,0},{2,3},{3,2},{4,5},{5,4},{6,7},{7,6},{8,9},{9,8},{10,11... | collective-permute-start | bytes 3932168 | tf_op jit(solution)/shard_map/ppermute | solution.py:347
  95.6 0.3 add.11._
  95.9 2.4 %collective-permute-done.9.other_ref = f32[8,160,256]{2,1,0:T(8,128)S(1)} collective-permute-done((f32[8,160,256]{2,1,0:T(8,128)S(1)}, f32[8,160,256]{2,1,0:T(8,128)S(1)}, u32[]{:S(2)}, u32[]{:S(2)}) %collective-permute-start.9) | collective-permute-done | bytes 1310752 | tf_op jit(solution)/shard_map/ppermute | solution.py:347
  98.3 0.9 collect.1
  99.2 1.5 copy-done.1
  100.7 0.6 copy-done.11
  101.3 5.4 %all-to-all-start.2 = ((f32[8,256,256]{2,1,0:T(8,128)}), f32[8,256,256]{2,1,0:T(8,128)}, u32[]{:S(2)}, u32[]{:S(2)}) async-start(f32[8,256,256]{2,1,0:T(8,128)} %behind.1), calls=%async_computation.2 | async-start | bytes 4194304 | tf_op jit(solution)/shard_map/all_to_all | solution.py:420
  106.6 7.3 %factor_step.4 = (f32[256,768]{1,0:T(8,128)S(1)}, f32[256,256]{1,0:T(8,128)S(1)}, f32[6,256,256]{2,1,0:T(8,128)S(1)}) custom-call(f32[10,256,256]{2,1,0:T(8,128)S(1)} %copy-done.2), custom_call_target="tpu_custom_call" | custom-call | tf_op jit(solution)/shard_map/factor_step/pallas_call | solution.py:193
  114.0 0.9 copy-done.6
  114.9 7.0 %factor_step.5 = (f32[256,512]{1,0:T(8,128)S(1)}, f32[256,256]{1,0:T(8,128)S(1)}, f32[3,256,256]{2,1,0:T(8,128)S(1)}) custom-call(f32[6,256,256]{2,1,0:T(8,128)S(1)} %get-tuple-element.28.gram_ref), custom_call_target="tpu_custom_call" | custom-call | tf_op jit(solution)/shard_map/factor_step/pallas_call | solution.py:193
  121.9 0.9 copy-done.4
  122.8 0.7 copy-done.9
  123.5 12.7 %all-to-all-done.2.parts_ref = f32[8,256,256]{2,1,0:T(8,128)} async-done(((f32[8,256,256]{2,1,0:T(8,128)}), f32[8,256,256]{2,1,0:T(8,128)}, u32[]{:S(2)}, u32[]{:S(2)}) %all-to-all-start.2) | async-done | bytes 2097184 | tf_op jit(solution)/shard_map/all_to_all | solution.py:420
  136.2 1.8 %sum_places.1.left_ref = f32[256,256]{1,0:T(8,128)S(1)} custom-call(f32[8,256,256]{2,1,0:T(8,128)} %all-to-all-done.2.parts_ref, f32[256,512]{1,0:T(8,128)S(1)} %get-tuple-element.29._.refs_1_), custom_call_target="tpu_custom_call" | custom-call | tf_op jit(solution)/shard_map/sum_places/pallas_call | solution.py:193
  137.9 3.2 %collective-permute-start.12 = (f32[256,256]{1,0:T(8,128)S(1)}, f32[256,256]{1,0:T(8,128)S(1)}, u32[]{:S(2)}, u32[]{:S(2)}) collective-permute-start(f32[256,256]{1,0:T(8,128)S(1)} %sum_places.1.left_ref), channel_id=1, source_target_pairs={{0,16},{16,0},{1,17},{17,1},{2,18},{18,2},{3,19},{19,3},{4,20},{20... | collective-permute-start | bytes 786440 | tf_op jit(solution)/shard_map/ppermute | solution.py:347
  141.1 6.7 %factor_step.6 = (f32[256,256]{1,0:T(8,128)S(1)}, f32[256,256]{1,0:T(8,128)S(1)}, f32[1,256,256]{2,1,0:T(8,128)S(1)}) custom-call(f32[3,256,256]{2,1,0:T(8,128)S(1)} %copy-done.5), custom_call_target="tpu_custom_call" | custom-call | tf_op jit(solution)/shard_map/factor_step/pallas_call | solution.py:193
  147.8 4.7 %collective-permute-done.12.right_ref = f32[256,256]{1,0:T(8,128)S(1)} collective-permute-done((f32[256,256]{1,0:T(8,128)S(1)}, f32[256,256]{1,0:T(8,128)S(1)}, u32[]{:S(2)}, u32[]{:S(2)}) %collective-permute-start.12) | collective-permute-done | bytes 262176 | tf_op jit(solution)/shard_map/ppermute | solution.py:347
  152.6 0.8 collective-permute-start.13
  153.5 1.5 collective-permute-start.15
  155.1 6.4 %factor_step.7.refs_6_ = f32[256,256]{1,0:T(8,128)S(1)} custom-call(f32[1,256,256]{2,1,0:T(8,128)S(1)} %get-tuple-element.35.gram_ref), custom_call_target="tpu_custom_call" | custom-call | tf_op jit(solution)/shard_map/factor_step/pallas_call | solution.py:193
  161.5 5.5 %collective-permute-done.15.refs_11_ = f32[256,256]{1,0:T(8,128)S(1)} collective-permute-done((f32[256,256]{1,0:T(8,128)S(1)}, f32[256,256]{1,0:T(8,128)S(1)}, u32[]{:S(2)}, u32[]{:S(2)}) %collective-permute-start.15) | collective-permute-done | bytes 262176 | tf_op jit(solution)/shard_map/ppermute | solution.py:351
  167.0 4.1 %solve.1 = f32[256,256]{1,0:T(8,128)} custom-call(s32[5]{0:T(128)S(1)} %stack.50.place_ref, f32[256,768]{1,0:T(8,128)S(1)} %copy-done.7, f32[256,512]{1,0:T(8,128)S(1)} %get-tuple-element.29._.refs_1_, f32[256,256]{1,0:T(8,128)S(1)} %get-tuple-element.31.after_ref.refs_2_, f32[256,256]{1,0:T(8,128)S(1)} %get-tuple-element.32.refs_3_, ...), custom_call_target="tpu_custom_call" | custom-call | tf_op jit(solution)/shard_map/solve/pallas_call | solution.py:193
  (39 shorter events, 0.9 us)
Async XLA Ops:
  0.7 1.2 copy-start.3
  2.0 0.9 copy-start.8
  4.7 20.3 %all-to-all-start = ((f32[4,320,256]{2,1,0:T(8,128)}), f32[4,320,256]{2,1,0:T(8,128)S(1)}, u32[]{:S(2)}, u32[]{:S(2)}) async-start(f32[4,320,256]{2,1,0:T(8,128)} %bitcast.5), calls=%async_computation | async-start | bytes 2621440 | tf_op jit(solution)/shard_map/all_to_all | solution.py:376
  27.3 3.2 %collective-permute-start = (f32[5,256,256]{2,1,0:T(8,128)S(1)}, f32[5,256,256]{2,1,0:T(8,128)S(1)}, u32[]{:S(2)}, u32[]{:S(2)}) collective-permute-start(f32[5,256,256]{2,1,0:T(8,128)S(1)} %get-tuple-element.22), channel_id=1, source_target_pairs={{0,1},{1,0},{2,3},{3,2},{4,5},{5,4},{6,7},{7,6},{8,9},{9,8},{10,11... | collective-permute-start | bytes 3932168 | tf_op jit(solution)/shard_map/ppermute | solution.py:347
  31.7 32.6 %all-to-all-start.1 = ((f32[8,160,256]{2,1,0:T(8,128)}), f32[8,160,256]{2,1,0:T(8,128)}, u32[]{:S(2)}, u32[]{:S(2)}) async-start(f32[8,160,256]{2,1,0:T(8,128)} %bitcast.25), calls=%async_computation.1 | async-start | bytes 2621440 | tf_op jit(solution)/shard_map/all_to_all | solution.py:390
  36.2 42.2 %collective-permute-start.10 = (f32[4,160,256]{2,1,0:T(8,128)S(1)}, f32[4,160,256]{2,1,0:T(8,128)S(1)}, u32[]{:S(2)}, u32[]{:S(2)}) collective-permute-start(f32[4,160,256]{2,1,0:T(8,128)S(1)} %get-tuple-element.23), channel_id=1, source_target_pairs={{0,16},{16,0},{1,17},{17,1},{2,18},{18,2},{3,19},{19,3},{4,20},{20... | collective-permute-start | bytes 1966088 | tf_op jit(solution)/shard_map/ppermute | solution.py:347
  65.7 12.5 %collective-permute-start.1 = (f32[160,256]{1,0:T(8,128)S(1)}, f32[160,256]{1,0:T(8,128)S(1)}, u32[]{:S(2)}, u32[]{:S(2)}) collective-permute-start(f32[160,256]{1,0:T(8,128)S(1)} %reduce_sum.9._), channel_id=1, source_target_pairs={{0,16},{1,17},{2,18},{3,19},{4,20},{5,21},{6,22},{7,23},{8,24},{9,... | collective-permute-start | bytes 491528 | tf_op jit(solution)/shard_map/ppermute | solution.py:335
  78.2 5.3 %collective-permute-start.3 = (f32[160,256]{1,0:T(8,128)S(1)}, f32[160,256]{1,0:T(8,128)S(1)}, u32[]{:S(2)}, u32[]{:S(2)}) collective-permute-start(f32[160,256]{1,0:T(8,128)S(1)} %get-tuple-element.38), channel_id=1, source_target_pairs={{0,8},{2,10},{4,12},{6,14},{8,0},{10,2},{12,4},{14,6},{1,9},{3,11}... | collective-permute-start | bytes 491528 | tf_op jit(solution)/shard_map/ppermute | solution.py:343
  78.3 5.3 %collective-permute-start.2 = (f32[160,256]{1,0:T(8,128)S(1)}, f32[160,256]{1,0:T(8,128)S(1)}, u32[]{:S(2)}, u32[]{:S(2)}) collective-permute-start(f32[160,256]{1,0:T(8,128)S(1)} %get-tuple-element.38), channel_id=1, source_target_pairs={{0,4},{2,6},{4,0},{6,2},{8,12},{10,14},{12,8},{14,10},{1,5},{3,7},... | collective-permute-start | bytes 491528 | tf_op jit(solution)/shard_map/ppermute | solution.py:343
  80.6 15.1 %collective-permute-start.11 = (f32[2,4,256,256]{3,2,1,0:T(8,128)S(1)}, f32[2,4,256,256]{3,2,1,0:T(8,128)S(1)}, u32[]{:S(2)}, u32[]{:S(2)}) collective-permute-start(f32[2,4,256,256]{3,2,1,0:T(8,128)S(1)} %get-tuple-element.25), channel_id=1, source_target_pairs={{0,1},{1,0},{2,3},{3,2},{4,5},{5,4},{6,7},{7,6},{8,9},{9,8},{10,11... | collective-permute-start | bytes 6291464 | tf_op jit(solution)/shard_map/ppermute | solution.py:347
  81.1 5.8 %collective-permute-start.5 = (f32[160,256]{1,0:T(8,128)S(1)}, f32[160,256]{1,0:T(8,128)S(1)}, u32[]{:S(2)}, u32[]{:S(2)}) collective-permute-start(f32[160,256]{1,0:T(8,128)S(1)} %get-tuple-element.38), channel_id=1, source_target_pairs={{0,2},{2,0},{4,6},{6,4},{8,10},{10,8},{12,14},{14,12},{1,3},{3,1},... | collective-permute-start | bytes 491528 | tf_op jit(solution)/shard_map/ppermute | solution.py:343
  83.6 5.0 %collective-permute-start.4 = (f32[160,256]{1,0:T(8,128)S(1)}, f32[160,256]{1,0:T(8,128)S(1)}, u32[]{:S(2)}, u32[]{:S(2)}) collective-permute-start(f32[160,256]{1,0:T(8,128)S(1)} %collective-permute-done.3), channel_id=1, source_target_pairs={{0,4},{2,6},{4,0},{6,2},{8,12},{10,14},{12,8},{14,10},{1,5},{3,7},... | collective-permute-start | bytes 491528 | tf_op jit(solution)/shard_map/ppermute | solution.py:343
  83.6 6.4 %collective-permute-start.6 = (f32[160,256]{1,0:T(8,128)S(1)}, f32[160,256]{1,0:T(8,128)S(1)}, u32[]{:S(2)}, u32[]{:S(2)}) collective-permute-start(f32[160,256]{1,0:T(8,128)S(1)} %collective-permute-done.2), channel_id=1, source_target_pairs={{0,2},{2,0},{4,6},{6,4},{8,10},{10,8},{12,14},{14,12},{1,3},{3,1},... | collective-permute-start | bytes 491528 | tf_op jit(solution)/shard_map/ppermute | solution.py:343
  86.9 4.8 %collective-permute-start.7 = (f32[160,256]{1,0:T(8,128)S(1)}, f32[160,256]{1,0:T(8,128)S(1)}, u32[]{:S(2)}, u32[]{:S(2)}) collective-permute-start(f32[160,256]{1,0:T(8,128)S(1)} %collective-permute-done.5), channel_id=1, source_target_pairs={{0,8},{2,10},{4,12},{6,14},{8,0},{10,2},{12,4},{14,6},{1,9},{3,11}... | collective-permute-start | bytes 491528 | tf_op jit(solution)/shard_map/ppermute | solution.py:343
  88.6 4.5 %collective-permute-start.8 = (f32[160,256]{1,0:T(8,128)S(1)}, f32[160,256]{1,0:T(8,128)S(1)}, u32[]{:S(2)}, u32[]{:S(2)}) collective-permute-start(f32[160,256]{1,0:T(8,128)S(1)} %collective-permute-done.4), channel_id=1, source_target_pairs={{0,2},{2,0},{4,6},{6,4},{8,10},{10,8},{12,14},{14,12},{1,3},{3,1},... | collective-permute-start | bytes 491528 | tf_op jit(solution)/shard_map/ppermute | solution.py:343
  93.1 5.2 %collective-permute-start.9 = (f32[8,160,256]{2,1,0:T(8,128)S(1)}, f32[8,160,256]{2,1,0:T(8,128)S(1)}, u32[]{:S(2)}, u32[]{:S(2)}) collective-permute-start(f32[8,160,256]{2,1,0:T(8,128)S(1)} %bitcast_dynamic-update-slice_fusion.mine_ref), channel_id=1, source_target_pairs={{0,1},{1,0},{2,3},{3,2},{4,5},{5,4},{6,7},{7,6},{8,9},{9,8},{10,11... | collective-permute-start | bytes 3932168 | tf_op jit(solution)/shard_map/ppermute | solution.py:347
  95.9 3.3 %copy-start = (f32[2,4,256,256]{3,2,1,0:T(8,128)}, f32[2,4,256,256]{3,2,1,0:T(8,128)S(1)}, u32[]{:S(2)}) copy-start(f32[2,4,256,256]{3,2,1,0:T(8,128)S(1)} %add.11._) | copy-start | bytes 6291460
  99.2 1.5 copy-start.1
  100.7 0.6 copy-start.11
  101.3 5.4 %copy-start.2 = (f32[10,256,256]{2,1,0:T(8,128)S(1)}, f32[10,256,256]{2,1,0:T(8,128)}, u32[]{:S(2)}) copy-start(f32[10,256,256]{2,1,0:T(8,128)} %copy-done.1) | copy-start | bytes 7864324
  101.3 34.9 %all-to-all-start.2 = ((f32[8,256,256]{2,1,0:T(8,128)}), f32[8,256,256]{2,1,0:T(8,128)}, u32[]{:S(2)}, u32[]{:S(2)}) async-start(f32[8,256,256]{2,1,0:T(8,128)} %behind.1), calls=%async_computation.2 | async-start | bytes 4194304 | tf_op jit(solution)/shard_map/all_to_all | solution.py:420
  114.0 0.9 copy-start.6
  121.8 0.9 copy-start.4
  122.8 0.7 copy-start.9
  136.2 5.0 %copy-start.5 = (f32[3,256,256]{2,1,0:T(8,128)S(1)}, f32[3,256,256]{2,1,0:T(8,128)}, u32[]{:S(2)}) copy-start(f32[3,256,256]{2,1,0:T(8,128)} %copy-done.4) | copy-start | bytes 2359300
  137.9 29.1 %copy-start.7 = (f32[256,768]{1,0:T(8,128)S(1)}, f32[256,768]{1,0:T(8,128)}, u32[]{:S(2)}) copy-start(f32[256,768]{1,0:T(8,128)} %copy-done.6) | copy-start | bytes 2359300
  137.9 29.1 %copy-start.10 = (f32[256,256]{1,0:T(8,128)S(1)}, f32[256,256]{1,0:T(8,128)}, u32[]{:S(2)}) copy-start(f32[256,256]{1,0:T(8,128)} %copy-done.9) | copy-start | bytes 786436
  137.9 14.6 %collective-permute-start.12 = (f32[256,256]{1,0:T(8,128)S(1)}, f32[256,256]{1,0:T(8,128)S(1)}, u32[]{:S(2)}, u32[]{:S(2)}) collective-permute-start(f32[256,256]{1,0:T(8,128)S(1)} %sum_places.1.left_ref), channel_id=1, source_target_pairs={{0,16},{16,0},{1,17},{17,1},{2,18},{18,2},{3,19},{19,3},{4,20},{20... | collective-permute-start | bytes 786440 | tf_op jit(solution)/shard_map/ppermute | solution.py:347
  152.6 8.9 %collective-permute-start.13 = (f32[256,256]{1,0:T(8,128)S(1)}, f32[256,256]{1,0:T(8,128)S(1)}, u32[]{:S(2)}, u32[]{:S(2)}) collective-permute-start(f32[256,256]{1,0:T(8,128)S(1)} %add_groups.1.refs_8_), channel_id=1, source_target_pairs={{0,1},{1,0},{2,3},{3,2},{4,5},{5,4},{6,7},{7,6},{8,9},{9,8},{10,11... | collective-permute-start | bytes 786440 | tf_op jit(solution)/shard_map/ppermute | solution.py:351
  153.3 8.2 %collective-permute-start.14 = (f32[256,256]{1,0:T(8,128)S(1)}, f32[256,256]{1,0:T(8,128)S(1)}, u32[]{:S(2)}, u32[]{:S(2)}) collective-permute-start(f32[256,256]{1,0:T(8,128)S(1)} %add_groups.1.refs_8_), channel_id=1, source_target_pairs={{0,2},{1,3},{2,0},{3,1},{4,6},{5,7},{6,4},{7,5},{8,10},{9,11},{10,... | collective-permute-start | bytes 786440 | tf_op jit(solution)/shard_map/ppermute | solution.py:351
  153.5 13.5 %collective-permute-start.15 = (f32[256,256]{1,0:T(8,128)S(1)}, f32[256,256]{1,0:T(8,128)S(1)}, u32[]{:S(2)}, u32[]{:S(2)}) collective-permute-start(f32[256,256]{1,0:T(8,128)S(1)} %add_groups.1.refs_8_), channel_id=1, source_target_pairs={{0,3},{1,2},{2,1},{3,0},{4,7},{5,6},{6,5},{7,4},{8,11},{9,10},{10,... | collective-permute-start | bytes 786440 | tf_op jit(solution)/shard_map/ppermute | solution.py:351

commit v5 on v3

--- a/solution.py
+++ b/solution.py
@@ -13,17 +13,35 @@
 ARC_ROWS = 128
 NB = 128
 SUB = 8
-HIGHEST = lax.Precision.HIGHEST
+
+
+def split(value):
+    high = value.astype(jnp.bfloat16)
+    return high, (value - high.astype(jnp.float32)).astype(jnp.bfloat16)
+
+
+def left_parts(value, axis=0):
+    high, low = split(value)
+    return jnp.concatenate([high, high, low], axis=axis)
+
+
+def right_parts(value):
+    high, low = split(value)
+    return jnp.concatenate([high, low, high], axis=0)
+
+
+def parts_dot(left, right):
+    return lax.dot_general(
+        left, right, (((0,), (0,)), ((), ())), preferred_element_type=jnp.float32
+    )
 
 
 def dot(left, right):
-    return jnp.dot(left, right, precision=HIGHEST, preferred_element_type=jnp.float32)
+    return jnp.dot(left_parts(left, 1), right_parts(right), preferred_element_type=jnp.float32)
 
 
 def dot_t(left, right):
-    return lax.dot_general(
-        left, right, (((0,), (0,)), ((), ())), precision=HIGHEST, preferred_element_type=jnp.float32
-    )
+    return parts_dot(left_parts(left), right_parts(right))
 
 
 def lane(value, at):
@@ -94,35 +112,23 @@
 PIECES = 4 * P_SIZE
 
 
-def split(value):
-    high = value.astype(jnp.bfloat16)
-    return high, (value - high.astype(jnp.float32)).astype(jnp.bfloat16)
-
-
-def left_parts(value):
-    high, low = split(value)
-    return jnp.concatenate([high, high, low], axis=0)
-
-
-def right_parts(value):
-    high, low = split(value)
-    return jnp.concatenate([high, low, high], axis=0)
-
-
-def parts_dot(left, right):
-    return lax.dot_general(
-        left, right, (((0,), (0,)), ((), ())), preferred_element_type=jnp.float32
-    )
-
-
 def mask_kernel(place_ref, arcs_ref, slab_ref, rows_ref, *refs):
-    pieces, work = refs[:-1], refs[-1]
+    pieces, work, sems = refs[:-2], refs[-2], refs[-1]
     top = slab_ref.shape[0]
-    work[:top, :] = slab_ref[...]
-    for a in range(arcs_ref.shape[0]):
+    arcs = arcs_ref.shape[0]
+    copies = [pltpu.make_async_copy(slab_ref, work.at[pl.ds(0, top)], sems.at[arcs])]
+    for a in range(arcs):
+        part = pl.ds(a * ARC_ROWS, ARC_ROWS)
+        spot = pl.ds(top + a * ARC_ROWS, ARC_ROWS)
+        copies.append(pltpu.make_async_copy(rows_ref.at[part], work.at[spot], sems.at[a]))
+    for copy in copies:
+        copy.start()
+    for copy in copies:
+        copy.wait()
+    for a in range(arcs):
         live = arcs_ref[a, 0].astype(jnp.float32)
-        at = a * ARC_ROWS
-        work[top + at : top + at + ARC_ROWS, :] = rows_ref[at : at + ARC_ROWS, :] * live
+        spot = pl.ds(top + a * ARC_ROWS, ARC_ROWS)
+        work[spot, :] = work[spot, :] * live
     count = pieces[0].shape[0]
     for s, piece in enumerate(pieces):
         start = pl.multiple_of((place_ref[4] ^ s) * count, 16)
@@ -131,7 +137,7 @@
 
 def upper_products_kernel(place_ref, *refs):
     blocks, (keep_ref, send_ref, columns, work) = refs[:-4], refs[-4:]
-    side, place, me = place_ref[0], place_ref[1] * P_SIZE + place_ref[2], place_ref[4]
+    side, me = place_ref[0], place_ref[4]
     for s, block in enumerate(blocks):
         columns[me ^ s] = block[...]
     right = [right_parts(columns[c]) for c in range(P_SIZE)]
@@ -142,19 +148,15 @@
         for c in range(P_SIZE - r):
             work[at * B : (at + 1) * B, :] = product[:, c * B : (c + 1) * B]
             at += 1
-    count = keep_ref.shape[1]
-    for t in range(PIECES // 2):
-        piece = place ^ t
-        here = pl.multiple_of((side * (PIECES // 2) + piece) * count, SUB)
-        there = pl.multiple_of(((1 - side) * (PIECES // 2) + piece) * count, SUB)
-        keep_ref[t] = work[pl.ds(here, count), :]
-        send_ref[t] = work[pl.ds(there, count), :]
+    rows = HALF * B
+    keep_ref[...] = work[pl.ds(pl.multiple_of(side * rows, B), rows), :]
+    send_ref[...] = work[pl.ds(pl.multiple_of((1 - side) * rows, B), rows), :]
 
 
 def all_products_kernel(n_left, place_ref, *refs):
     blocks, (_, keep_ref, send_ref, columns, panels, work) = refs[:-6], refs[-6:]
     left_blocks, right_blocks = blocks[:n_left], blocks[n_left:]
-    side, place, me = place_ref[0], place_ref[1] * P_SIZE + place_ref[2], place_ref[4]
+    side, me = place_ref[0], place_ref[4]
     for s, block in enumerate(right_blocks):
         columns[me ^ s] = block[...]
     for s, block in enumerate(left_blocks):
@@ -166,11 +168,11 @@
         product = parts_dot(left_parts(left[r]), right)
         for b in range(P_SIZE):
             work[r * P_SIZE + b] = product[:, b * B : (b + 1) * B]
-    for t in range(2 * P_SIZE):
-        spot = place ^ t
-        block = (2 * (spot // P_SIZE)) * P_SIZE + spot % P_SIZE
-        keep_ref[t] = work[block + side * P_SIZE]
-        send_ref[t] = work[block + (1 - side) * P_SIZE]
+    for a in range(2):
+        for c in range(P_SIZE):
+            block = 2 * a * P_SIZE + c
+            keep_ref[a * P_SIZE + c] = work[block + side * P_SIZE]
+            send_ref[a * P_SIZE + c] = work[block + (1 - side) * P_SIZE]
 
 
 def tie_kernel(value_ref, after_ref, out_ref):
@@ -193,34 +195,33 @@
     out_ref[...] = left_ref[...] + right_ref[...]
 
 
-def sum_kernel(*refs):
-    parts, out_ref = refs[:-2], refs[-1]
-    total = parts[0][...]
-    for part in parts[1:]:
-        total = total + part[...]
+def sum_kernel(parts_ref, _, out_ref):
+    total = parts_ref[0]
+    for i in range(1, parts_ref.shape[0]):
+        total = total + parts_ref[i]
     out_ref[...] = total
 
 
-def on_chip(kernel, shapes, name, *operands, scratch=(), scalars=0, after=()):
+def on_chip(kernel, shapes, name, *operands, scratch=(), scalars=0, after=(), outside=()):
     done = pl.pallas_call(
         kernel,
         out_shape=[jax.ShapeDtypeStruct(shape, jnp.float32) for shape in shapes],
         in_specs=[pl.BlockSpec(memory_space=pltpu.SMEM)] * scalars
         + [pl.BlockSpec(memory_space=pltpu.VMEM)] * (len(operands) - scalars)
+        + [pl.BlockSpec(memory_space=pltpu.HBM)] * len(outside)
         + [pl.BlockSpec(memory_space=pl.ANY)] * len(after),
         out_specs=[pl.BlockSpec(memory_space=pltpu.VMEM)] * len(shapes),
         scratch_shapes=list(scratch),
         compiler_params=pltpu.CompilerParams(vmem_limit_bytes=16 * 1024 * 1024),
         name=name,
-    )(*operands, *after)
+    )(*operands, *outside, *after)
     return list(done)
 
 
-def collect_kernel(place_ref, mine_ref, other_ref, gram_ref, token_ref):
+def collect_kernel(place_ref, mine_ref, other_ref, gram_ref):
     side, high, low = place_ref[0], place_ref[1], place_ref[2]
     at = high * P_SIZE + low
     rows = mine_ref.shape[1]
-    token_ref[...] = jnp.zeros_like(token_ref)
     for s in range(2):
         for p in range(PIECES // 2):
             start = ((s * PIECES) // 2 + p) * rows
@@ -361,13 +362,6 @@
 
 def across_rows(value, bits):
     return lax.ppermute(value, ("rh", "rl"), [(i, i ^ bits) for i in range(P_SIZE)])
-
-
-def collected(parts):
-    got = [parts[0]]
-    for t in range(1, 2 * P_SIZE):
-        got.append(exchange(parts[t], t // P_SIZE, t % P_SIZE))
-    return got
 
 
 def spread(piece):
@@ -398,10 +392,12 @@
         "mask",
         place,
         arc_blocks,
-        r_slab,
-        arc_rows,
         scalars=2,
-        scratch=[pltpu.VMEM((total, columns), jnp.float32)],
+        scratch=[
+            pltpu.VMEM((total, columns), jnp.float32),
+            pltpu.SemaphoreType.DMA((arc_blocks.shape[0] + 1,)),
+        ],
+        outside=(r_slab, arc_rows),
     )
     blocks = blocks[:1] + [
         lax.ppermute(blocks[s], owners, [(i, i ^ s) for i in range(shares)])
@@ -409,7 +405,7 @@
     ]
     panels = [] if in_two else [from_first(block, n_hi) for block in blocks]
 
-    half = (PIECES // 2, len(PAIRS) * B // PIECES, B)
+    half = (HALF * B, B)
     gathered = pltpu.VMEM((shares, *share), jnp.float32)
     keep, send = on_chip(
         upper_products_kernel,
@@ -420,8 +416,8 @@
         scalars=1,
         scratch=[gathered, pltpu.VMEM((len(PAIRS) * B, B), jnp.float32)],
     )
-    gram = collected(keep + swap(send))
-    gram = functools.reduce(jnp.add, gram)
+    gram = (keep + swap(send)).reshape(PIECES // 2, -1, B)
+    gram = lax.all_to_all(gram, ("rh", "lo"), 0, 0)
     half = (2 * P_SIZE, B, B)
     cross, send = on_chip(
         functools.partial(all_products_kernel, len(panels)),
@@ -435,23 +431,24 @@
         after=(keep,),
     )
     cross = cross + swap(send)
+    (gram,) = on_chip(sum_kernel, [gram.shape[1:]], "sum_pieces", gram, after=(cross,))
+    cross = lax.all_to_all(behind(cross, gram), ("rh", "lo"), 0, 0)
     piece = gram + swap(gram, "hi") if in_two else from_first(gram, n_hi)
     pieces = spread(piece)
-    gram, token = on_chip(
+    (gram,) = on_chip(
         collect_kernel,
-        [(len(PAIRS), B, B), (SUB, NB)],
+        [(len(PAIRS), B, B)],
         "collect",
         place,
         pieces,
         swap(pieces),
         scalars=1,
     )
-    cross = collected(behind(cross, token))
     rows, inverses = factor(gram)
-    (mine,) = on_chip(sum_kernel, [(B, columns)], "sum_places", *cross, after=(rows[1],))
+    (mine,) = on_chip(sum_kernel, [(B, columns)], "sum_places", cross, after=(rows[0],))
     if in_two:
         other = swap(mine, "hi")
-        (mine,) = on_chip(add_kernel, [(B, columns)], "add_groups", mine, other, after=(rows[2],))
+        (mine,) = on_chip(add_kernel, [(B, columns)], "add_groups", mine, other, after=(rows[1],))
     own = [mine] + [across_rows(mine, bits) for bits in range(1, P_SIZE)]
 
     (result,) = on_chip(

time: 163 us -> 176 us (1.080)
  the two profiles are of different devices: /device:TPU:9 before, /device:TPU:0 now
where the time goes in v5:
time: 176 us
  waiting for transfers between devices  79.4 us (45%)
  starting transfers between devices  45 us (26%)
  Pallas kernels  40.5 us (23%)
  local copies, waits for them, and re-layouts  9.31 us (5%)
    ppermute x5, waiting for transfers between devices, swap(): return lax.ppermute(value, axis, [(0, 1), (1, 0)])  41.5 us
    pallas_call x12, Pallas kernels, on_chip(): pl.pallas_call(kernel, out_shape=[jax.ShapeDtypeStruct(shape, jnp.float32...  40.5 us
    ppermute x7, waiting for transfers between devices, on_device(): lax.ppermute(blocks[s], owners, [(i, i ^ s) for i in range(shares)])  17.6 us
    ppermute x7, starting transfers between devices, on_device(): lax.ppermute(blocks[s], owners, [(i, i ^ s) for i in range(shares)])  13.6 us
    ppermute x7, starting transfers between devices, exchange(): lax.ppermute(value, ('lo', 'rh'), [(i, i ^ bits) for i in range(2 * P_SIZ...  12.2 us
    ppermute x7, waiting for transfers between devices, exchange(): lax.ppermute(value, ('lo', 'rh'), [(i, i ^ bits) for i in range(2 * P_SIZ...  10.9 us
    all_to_all x1, waiting for transfers between devices, on_device(): gram = lax.all_to_all(gram, ('rh', 'lo'), 0, 0)  9.4 us
    unnamed x41, local copies, waits for them, and re-layouts  9.21 us
  transfers between devices with their start and end apart: 24, of which 15 were waited for; matrix products, arithmetic and copies ran while one was open for 0% of the time, Pallas kernels for 17%

profile of v5, /device:TPU:0, one launch (start us, length us, event | category | flops | bytes accessed | tf_op | source)
XLA Modules:
  0.0 176.1 jit_solution(17007024563223849776)
XLA Ops:
  0.0 0.7 copy.5.arcs_ref
  0.8 1.2 copy-done.5
  2.0 0.9 copy-done.14
  3.0 2.2 %mask.1 = (f32[160,256]{1,0:T(8,128)S(1)}, f32[160,256]{1,0:T(8,128)S(1)}, f32[160,256]{1,0:T(8,128)S(1)}, f32[160,256]{1,0:T(8,128)S(1)}, f32[160,256]{1,0:T(8,...) custom-call(s32[5]{0:T(128)S(1)} %stack.47.place_ref, s32[8,1]{1,0:T(8,128)S(1)} %copy.5.arcs_ref, ...), custom_call_target="tpu_custom_call" | custom-call | tf_op jit(solution)/shard_map/mask/pallas_call | solution.py:206
  5.2 3.0 %collective-permute-start = (f32[160,256]{1,0:T(8,128)S(1)}, f32[160,256]{1,0:T(8,128)S(1)}, u32[]{:S(2)}, u32[]{:S(2)}) collective-permute-start(f32[160,256]{1,0:T(8,128)S(1)} %get-tuple-element.27), channel_id=1, source_target_pairs={{0,4},{4,0},{8,12},{12,8},{16,20},{20,16},{24,28},{28,24},{1,5},{5... | collective-permute-start | bytes 491528 | tf_op jit(solution)/shard_map/ppermute | solution.py:403
  8.3 1.6 collective-permute-start.1
  9.8 3.0 %collective-permute-start.3 = (f32[160,256]{1,0:T(8,128)S(1)}, f32[160,256]{1,0:T(8,128)S(1)}, u32[]{:S(2)}, u32[]{:S(2)}) collective-permute-start(f32[160,256]{1,0:T(8,128)S(1)} %get-tuple-element.30), channel_id=1, source_target_pairs={{0,16},{4,20},{8,24},{12,28},{16,0},{20,4},{24,8},{28,12},{1,17},{... | collective-permute-start | bytes 491528 | tf_op jit(solution)/shard_map/ppermute | solution.py:403
  12.8 1.3 collective-permute-start.4
  14.1 3.6 %collective-permute-start.5 = (f32[160,256]{1,0:T(8,128)S(1)}, f32[160,256]{1,0:T(8,128)S(1)}, u32[]{:S(2)}, u32[]{:S(2)}) collective-permute-start(f32[160,256]{1,0:T(8,128)S(1)} %get-tuple-element.32), channel_id=1, source_target_pairs={{0,24},{4,28},{8,16},{12,20},{16,8},{20,12},{24,0},{28,4},{1,25},{... | collective-permute-start | bytes 491528 | tf_op jit(solution)/shard_map/ppermute | solution.py:403
  17.7 3.6 %collective-permute-done.1.refs_2_ = f32[160,256]{1,0:T(8,128)S(1)} collective-permute-done((f32[160,256]{1,0:T(8,128)S(1)}, f32[160,256]{1,0:T(8,128)S(1)}, u32[]{:S(2)}, u32[]{:S(2)}) %collective-permute-start.1) | collective-permute-done | bytes 163872 | tf_op jit(solution)/shard_map/ppermute | solution.py:403
  21.3 1.1 collective-permute-start.6
  22.8 13.6 %collective-permute-done.4.refs_5_ = f32[160,256]{1,0:T(8,128)S(1)} collective-permute-done((f32[160,256]{1,0:T(8,128)S(1)}, f32[160,256]{1,0:T(8,128)S(1)}, u32[]{:S(2)}, u32[]{:S(2)}) %collective-permute-start.4) | collective-permute-done | bytes 163872 | tf_op jit(solution)/shard_map/ppermute | solution.py:403
  36.5 1.7 upper_products.1
  38.2 3.0 %collective-permute-done.7 = f32[1280,256]{1,0:T(8,128)S(1)} collective-permute-done((f32[1280,256]{1,0:T(8,128)S(1)}, f32[1280,256]{1,0:T(8,128)S(1)}, u32[]{:S(2)}, u32[]{:S(2)}) %collective-permute-start.7) | collective-permute-done | bytes 1310752 | tf_op jit(solution)/shard_map/ppermute | solution.py:360
  41.2 1.3 add.13
  42.5 8.3 %all-to-all-start = ((f32[8,160,256]{2,1,0:T(8,128)}), f32[8,160,256]{2,1,0:T(8,128)S(1)}, u32[]{:S(2)}, u32[]{:S(2)}) async-start(f32[8,160,256]{2,1,0:T(8,128)} %bitcast.21), calls=%async_computation | async-start | bytes 2621440 | tf_op jit(solution)/shard_map/all_to_all | solution.py:420
  50.9 0.9 copy-done.7
  51.8 0.9 copy-done.9
  52.7 0.9 copy-done.11
  53.6 0.9 copy-done.13
  54.5 2.2 %all_products.1 = (f32[8,256,256]{2,1,0:T(8,128)S(1)}, f32[8,256,256]{2,1,0:T(8,128)S(1)}) custom-call(s32[5]{0:T(128)S(1)} %stack.47.place_ref, f32[160,256]{1,0:T(8,128)S(1)} %get-tuple-element.26.refs_0_, f32[160,256]{1,0:T(8,128)S(1)} %collective-permute-done.refs_1_, f32[160,256]{1,0:T(8,128)S(1)} %collective-permute-done.1.refs_2_, ...), custom_call_target="tpu_custom_call" | custom-call | tf_op jit(solution)/shard_map/all_products/pallas_call | solution.py:206
  56.8 4.1 %collective-permute-done.8 = f32[8,256,256]{2,1,0:T(8,128)S(1)} collective-permute-done((f32[8,256,256]{2,1,0:T(8,128)S(1)}, f32[8,256,256]{2,1,0:T(8,128)S(1)}, u32[]{:S(2)}, u32[]{:S(2)}) %collective-permute-start.8) | collective-permute-done | bytes 2097184 | tf_op jit(solution)/shard_map/ppermute | solution.py:360
  61.2 9.4 %all-to-all-done.parts_ref = f32[8,160,256]{2,1,0:T(8,128)S(1)} async-done(((f32[8,160,256]{2,1,0:T(8,128)}), f32[8,160,256]{2,1,0:T(8,128)S(1)}, u32[]{:S(2)}, u32[]{:S(2)}) %all-to-all-start) | async-done | bytes 1310752 | tf_op jit(solution)/shard_map/all_to_all | solution.py:420
  71.4 4.5 %all-to-all-start.1 = ((f32[8,256,256]{2,1,0:T(8,128)}), f32[8,256,256]{2,1,0:T(8,128)}, u32[]{:S(2)}, u32[]{:S(2)}) async-start(f32[8,256,256]{2,1,0:T(8,128)} %behind.1), calls=%async_computation.1 | async-start | bytes 4194304 | tf_op jit(solution)/shard_map/all_to_all | solution.py:435
  75.9 3.7 %collective-permute-start.9 = (f32[160,256]{1,0:T(8,128)S(1)}, f32[160,256]{1,0:T(8,128)S(1)}, u32[]{:S(2)}, u32[]{:S(2)}) collective-permute-start(f32[160,256]{1,0:T(8,128)S(1)} %copy-done.4), channel_id=1, source_target_pairs={{0,16},{16,0},{1,17},{17,1},{2,18},{18,2},{3,19},{19,3},{4,20},{20... | collective-permute-start | bytes 491528 | tf_op jit(solution)/shard_map/ppermute | solution.py:360
  79.6 24.0 %collective-permute-done.9 = f32[160,256]{1,0:T(8,128)S(1)} collective-permute-done((f32[160,256]{1,0:T(8,128)S(1)}, f32[160,256]{1,0:T(8,128)S(1)}, u32[]{:S(2)}, u32[]{:S(2)}) %collective-permute-start.9) | collective-permute-done | bytes 163872 | tf_op jit(solution)/shard_map/ppermute | solution.py:360
  103.5 9.0 %collective-permute-start.11 = (f32[160,256]{1,0:T(8,128)S(1)}, f32[160,256]{1,0:T(8,128)S(1)}, u32[]{:S(2)}, u32[]{:S(2)}) collective-permute-start(f32[160,256]{1,0:T(8,128)S(1)} %get-tuple-element.48), channel_id=1, source_target_pairs={{0,8},{2,10},{4,12},{6,14},{8,0},{10,2},{12,4},{14,6},{1,9},{3,11}... | collective-permute-start | bytes 491528 | tf_op jit(solution)/shard_map/ppermute | solution.py:356
  112.5 1.1 collective-permute-start.13
  113.6 2.2 %collective-permute-done.11 = f32[160,256]{1,0:T(8,128)S(1)} collective-permute-done((f32[160,256]{1,0:T(8,128)S(1)}, f32[160,256]{1,0:T(8,128)S(1)}, u32[]{:S(2)}, u32[]{:S(2)}) %collective-permute-start.11) | collective-permute-done | bytes 163872 | tf_op jit(solution)/shard_map/ppermute | solution.py:356
  115.8 3.3 %collective-permute-done.10 = f32[160,256]{1,0:T(8,128)S(1)} collective-permute-done((f32[160,256]{1,0:T(8,128)S(1)}, f32[160,256]{1,0:T(8,128)S(1)}, u32[]{:S(2)}, u32[]{:S(2)}) %collective-permute-start.10) | collective-permute-done | bytes 163872 | tf_op jit(solution)/shard_map/ppermute | solution.py:356
  119.1 1.1 collective-permute-start.14
  120.2 0.9 collective-permute-done.12
  121.2 1.1 collective-permute-start.16
  122.2 2.7 %collective-permute-done.14 = f32[160,256]{1,0:T(8,128)S(1)} collective-permute-done((f32[160,256]{1,0:T(8,128)S(1)}, f32[160,256]{1,0:T(8,128)S(1)}, u32[]{:S(2)}, u32[]{:S(2)}) %collective-permute-start.14) | collective-permute-done | bytes 163872 | tf_op jit(solution)/shard_map/ppermute | solution.py:356
  125.5 1.2 collective-permute-done.16
  126.8 3.0 %collective-permute-done.17.other_ref = f32[8,160,256]{2,1,0:T(8,128)S(1)} collective-permute-done((f32[8,160,256]{2,1,0:T(8,128)S(1)}, f32[8,160,256]{2,1,0:T(8,128)S(1)}, u32[]{:S(2)}, u32[]{:S(2)}) %collective-permute-start.17) | collective-permute-done | bytes 1310752 | tf_op jit(solution)/shard_map/ppermute | solution.py:360
  129.8 1.0 collect.1.gram_ref.refs_7_
  130.9 7.3 %factor_step.4 = (f32[256,768]{1,0:T(8,128)S(1)}, f32[256,256]{1,0:T(8,128)S(1)}, f32[6,256,256]{2,1,0:T(8,128)S(1)}) custom-call(f32[10,256,256]{2,1,0:T(8,128)S(1)} %collect.1.gram_ref.refs_7_), custom_call_target="tpu_custom_call" | custom-call | tf_op jit(solution)/shard_map/factor_step/pallas_call | solution.py:206
  138.2 1.2 copy-done.1
  139.4 0.7 copy-done.15
  140.1 1.8 %sum_places.1.left_ref = f32[256,256]{1,0:T(8,128)S(1)} custom-call(f32[8,256,256]{2,1,0:T(8,128)} %all-to-all-done.1.parts_ref, f32[256,768]{1,0:T(8,128)S(1)} %get-tuple-element.38._.refs_0_), custom_call_target="tpu_custom_call" | custom-call | tf_op jit(solution)/shard_map/sum_places/pallas_call | solution.py:206
  142.6 7.0 %factor_step.5 = (f32[256,512]{1,0:T(8,128)S(1)}, f32[256,256]{1,0:T(8,128)S(1)}, f32[3,256,256]{2,1,0:T(8,128)S(1)}) custom-call(f32[6,256,256]{2,1,0:T(8,128)S(1)} %copy-done.2), custom_call_target="tpu_custom_call" | custom-call | tf_op jit(solution)/shard_map/factor_step/pallas_call | solution.py:206
  149.5 7.3 %collective-permute-done.18.right_ref = f32[256,256]{1,0:T(8,128)S(1)} collective-permute-done((f32[256,256]{1,0:T(8,128)S(1)}, f32[256,256]{1,0:T(8,128)S(1)}, u32[]{:S(2)}, u32[]{:S(2)}) %collective-permute-start.18) | collective-permute-done | bytes 262176 | tf_op jit(solution)/shard_map/ppermute | solution.py:360
  157.0 1.1 collective-permute-start.20
  158.1 0.7 collective-permute-start.19
  158.8 6.7 %factor_step.6 = (f32[256,256]{1,0:T(8,128)S(1)}, f32[256,256]{1,0:T(8,128)S(1)}, f32[1,256,256]{2,1,0:T(8,128)S(1)}) custom-call(f32[3,256,256]{2,1,0:T(8,128)S(1)} %get-tuple-element.41.gram_ref), custom_call_target="tpu_custom_call" | custom-call | tf_op jit(solution)/shard_map/factor_step/pallas_call | solution.py:206
  165.5 6.5 %factor_step.7.refs_6_ = f32[256,256]{1,0:T(8,128)S(1)} custom-call(f32[1,256,256]{2,1,0:T(8,128)S(1)} %get-tuple-element.46.gram_ref), custom_call_target="tpu_custom_call" | custom-call | tf_op jit(solution)/shard_map/factor_step/pallas_call | solution.py:206
  172.0 4.0 %solve.1 = f32[256,256]{1,0:T(8,128)} custom-call(s32[5]{0:T(128)S(1)} %stack.47.place_ref, f32[256,768]{1,0:T(8,128)S(1)} %get-tuple-element.38._.refs_0_, f32[256,512]{1,0:T(8,128)S(1)} %get-tuple-element.40.after_ref.refs_1_, f32[256,256]{1,0:T(8,128)S(1)} %get-tuple-element.42.refs_2_, f32[256,256]{1,0:T(8,128)S(1)} %copy-done.16, ...), custom_call_target="tpu_custom_call" | custom-call | tf_op jit(solution)/shard_map/solve/pallas_call | solution.py:206
  (59 shorter events, 3.1 us)
Async XLA Ops:
  0.8 1.2 copy-start.5
  2.0 0.9 copy-start.14
  5.2 8.9 %collective-permute-start = (f32[160,256]{1,0:T(8,128)S(1)}, f32[160,256]{1,0:T(8,128)S(1)}, u32[]{:S(2)}, u32[]{:S(2)}) collective-permute-start(f32[160,256]{1,0:T(8,128)S(1)} %get-tuple-element.27), channel_id=1, source_target_pairs={{0,4},{4,0},{8,12},{12,8},{16,20},{20,16},{24,28},{28,24},{1,5},{5... | collective-permute-start | bytes 491528 | tf_op jit(solution)/shard_map/ppermute | solution.py:403
  8.3 13.1 %collective-permute-start.1 = (f32[160,256]{1,0:T(8,128)S(1)}, f32[160,256]{1,0:T(8,128)S(1)}, u32[]{:S(2)}, u32[]{:S(2)}) collective-permute-start(f32[160,256]{1,0:T(8,128)S(1)} %get-tuple-element.28), channel_id=1, source_target_pairs={{0,8},{4,12},{8,0},{12,4},{16,24},{20,28},{24,16},{28,20},{1,9},{5... | collective-permute-start | bytes 491528 | tf_op jit(solution)/shard_map/ppermute | solution.py:403
  9.8 13.0 %collective-permute-start.2 = (f32[160,256]{1,0:T(8,128)S(1)}, f32[160,256]{1,0:T(8,128)S(1)}, u32[]{:S(2)}, u32[]{:S(2)}) collective-permute-start(f32[160,256]{1,0:T(8,128)S(1)} %get-tuple-element.29), channel_id=1, source_target_pairs={{0,12},{4,8},{8,4},{12,0},{16,28},{20,24},{24,20},{28,16},{1,13},{... | collective-permute-start | bytes 491528 | tf_op jit(solution)/shard_map/ppermute | solution.py:403
  9.8 13.0 %collective-permute-start.3 = (f32[160,256]{1,0:T(8,128)S(1)}, f32[160,256]{1,0:T(8,128)S(1)}, u32[]{:S(2)}, u32[]{:S(2)}) collective-permute-start(f32[160,256]{1,0:T(8,128)S(1)} %get-tuple-element.30), channel_id=1, source_target_pairs={{0,16},{4,20},{8,24},{12,28},{16,0},{20,4},{24,8},{28,12},{1,17},{... | collective-permute-start | bytes 491528 | tf_op jit(solution)/shard_map/ppermute | solution.py:403
  12.8 23.6 %collective-permute-start.4 = (f32[160,256]{1,0:T(8,128)S(1)}, f32[160,256]{1,0:T(8,128)S(1)}, u32[]{:S(2)}, u32[]{:S(2)}) collective-permute-start(f32[160,256]{1,0:T(8,128)S(1)} %get-tuple-element.31), channel_id=1, source_target_pairs={{0,20},{4,16},{8,28},{12,24},{16,4},{20,0},{24,12},{28,8},{1,21},{... | collective-permute-start | bytes 491528 | tf_op jit(solution)/shard_map/ppermute | solution.py:403
  14.1 22.3 %collective-permute-start.5 = (f32[160,256]{1,0:T(8,128)S(1)}, f32[160,256]{1,0:T(8,128)S(1)}, u32[]{:S(2)}, u32[]{:S(2)}) collective-permute-start(f32[160,256]{1,0:T(8,128)S(1)} %get-tuple-element.32), channel_id=1, source_target_pairs={{0,24},{4,28},{8,16},{12,20},{16,8},{20,12},{24,0},{28,4},{1,25},{... | collective-permute-start | bytes 491528 | tf_op jit(solution)/shard_map/ppermute | solution.py:403
  21.3 15.1 %collective-permute-start.6 = (f32[160,256]{1,0:T(8,128)S(1)}, f32[160,256]{1,0:T(8,128)S(1)}, u32[]{:S(2)}, u32[]{:S(2)}) collective-permute-start(f32[160,256]{1,0:T(8,128)S(1)} %get-tuple-element.33), channel_id=1, source_target_pairs={{0,28},{4,24},{8,20},{12,16},{16,12},{20,8},{24,4},{28,0},{1,29},{... | collective-permute-start | bytes 491528 | tf_op jit(solution)/shard_map/ppermute | solution.py:403
  22.8 19.7 %copy-start.6 = (f32[160,256]{1,0:T(8,128)}, f32[160,256]{1,0:T(8,128)S(1)}, u32[]{:S(2)}) copy-start(f32[160,256]{1,0:T(8,128)S(1)} %collective-permute-done.3.refs_4_) | copy-start | bytes 491524
  36.4 6.1 %copy-start.8 = (f32[160,256]{1,0:T(8,128)}, f32[160,256]{1,0:T(8,128)S(1)}, u32[]{:S(2)}) copy-start(f32[160,256]{1,0:T(8,128)S(1)} %collective-permute-done.4.refs_5_) | copy-start | bytes 491524
  36.4 6.1 %copy-start.10 = (f32[160,256]{1,0:T(8,128)}, f32[160,256]{1,0:T(8,128)S(1)}, u32[]{:S(2)}) copy-start(f32[160,256]{1,0:T(8,128)S(1)} %collective-permute-done.5.refs_6_) | copy-start | bytes 491524
  36.4 6.1 %copy-start.12 = (f32[160,256]{1,0:T(8,128)}, f32[160,256]{1,0:T(8,128)S(1)}, u32[]{:S(2)}) copy-start(f32[160,256]{1,0:T(8,128)S(1)} %collective-permute-done.6.refs_7_) | copy-start | bytes 491524
  38.1 3.1 %collective-permute-start.7 = (f32[1280,256]{1,0:T(8,128)S(1)}, f32[1280,256]{1,0:T(8,128)S(1)}, u32[]{:S(2)}, u32[]{:S(2)}) collective-permute-start(f32[1280,256]{1,0:T(8,128)S(1)} %get-tuple-element.35), channel_id=1, source_target_pairs={{0,1},{1,0},{2,3},{3,2},{4,5},{5,4},{6,7},{7,6},{8,9},{9,8},{10,11... | collective-permute-start | bytes 3932168 | tf_op jit(solution)/shard_map/ppermute | solution.py:360
  42.5 28.1 %all-to-all-start = ((f32[8,160,256]{2,1,0:T(8,128)}), f32[8,160,256]{2,1,0:T(8,128)S(1)}, u32[]{:S(2)}, u32[]{:S(2)}) async-start(f32[8,160,256]{2,1,0:T(8,128)} %bitcast.21), calls=%async_computation | async-start | bytes 2621440 | tf_op jit(solution)/shard_map/all_to_all | solution.py:420
  50.9 0.9 copy-start.7
  51.8 0.9 copy-start.9
  52.7 0.9 copy-start.11
  53.6 0.9 copy-start.13
  56.7 4.2 %collective-permute-start.8 = (f32[8,256,256]{2,1,0:T(8,128)S(1)}, f32[8,256,256]{2,1,0:T(8,128)S(1)}, u32[]{:S(2)}, u32[]{:S(2)}) collective-permute-start(f32[8,256,256]{2,1,0:T(8,128)S(1)} %get-tuple-element.37), channel_id=1, source_target_pairs={{0,1},{1,0},{2,3},{3,2},{4,5},{5,4},{6,7},{7,6},{8,9},{9,8},{10,11... | collective-permute-start | bytes 6291464 | tf_op jit(solution)/shard_map/ppermute | solution.py:360
  61.2 9.5 %copy-start = (f32[8,256,256]{2,1,0:T(8,128)}, f32[8,256,256]{2,1,0:T(8,128)S(1)}, u32[]{:S(2)}) copy-start(f32[8,256,256]{2,1,0:T(8,128)S(1)} %add.14._.value_ref) | copy-start | bytes 6291460
  70.7 0.7 copy-start.3
  71.4 4.5 %copy-start.4 = (f32[160,256]{1,0:T(8,128)S(1)}, f32[160,256]{1,0:T(8,128)}, u32[]{:S(2)}) copy-start(f32[160,256]{1,0:T(8,128)} %copy-done.3) | copy-start | bytes 491524
  71.4 68.7 %all-to-all-start.1 = ((f32[8,256,256]{2,1,0:T(8,128)}), f32[8,256,256]{2,1,0:T(8,128)}, u32[]{:S(2)}, u32[]{:S(2)}) async-start(f32[8,256,256]{2,1,0:T(8,128)} %behind.1), calls=%async_computation.1 | async-start | bytes 4194304 | tf_op jit(solution)/shard_map/all_to_all | solution.py:435
  75.9 27.6 %collective-permute-start.9 = (f32[160,256]{1,0:T(8,128)S(1)}, f32[160,256]{1,0:T(8,128)S(1)}, u32[]{:S(2)}, u32[]{:S(2)}) collective-permute-start(f32[160,256]{1,0:T(8,128)S(1)} %copy-done.4), channel_id=1, source_target_pairs={{0,16},{16,0},{1,17},{17,1},{2,18},{18,2},{3,19},{19,3},{4,20},{20... | collective-permute-start | bytes 491528 | tf_op jit(solution)/shard_map/ppermute | solution.py:360
  103.5 12.3 %collective-permute-start.11 = (f32[160,256]{1,0:T(8,128)S(1)}, f32[160,256]{1,0:T(8,128)S(1)}, u32[]{:S(2)}, u32[]{:S(2)}) collective-permute-start(f32[160,256]{1,0:T(8,128)S(1)} %get-tuple-element.48), channel_id=1, source_target_pairs={{0,8},{2,10},{4,12},{6,14},{8,0},{10,2},{12,4},{14,6},{1,9},{3,11}... | collective-permute-start | bytes 491528 | tf_op jit(solution)/shard_map/ppermute | solution.py:356
  112.5 6.6 %collective-permute-start.10 = (f32[160,256]{1,0:T(8,128)S(1)}, f32[160,256]{1,0:T(8,128)S(1)}, u32[]{:S(2)}, u32[]{:S(2)}) collective-permute-start(f32[160,256]{1,0:T(8,128)S(1)} %get-tuple-element.48), channel_id=1, source_target_pairs={{0,4},{2,6},{4,0},{6,2},{8,12},{10,14},{12,8},{14,10},{1,5},{3,7},... | collective-permute-start | bytes 491528 | tf_op jit(solution)/shard_map/ppermute | solution.py:356
  112.5 7.7 %collective-permute-start.13 = (f32[160,256]{1,0:T(8,128)S(1)}, f32[160,256]{1,0:T(8,128)S(1)}, u32[]{:S(2)}, u32[]{:S(2)}) collective-permute-start(f32[160,256]{1,0:T(8,128)S(1)} %get-tuple-element.48), channel_id=1, source_target_pairs={{0,2},{2,0},{4,6},{6,4},{8,10},{10,8},{12,14},{14,12},{1,3},{3,1},... | collective-permute-start | bytes 491528 | tf_op jit(solution)/shard_map/ppermute | solution.py:356
  115.8 5.3 %collective-permute-start.12 = (f32[160,256]{1,0:T(8,128)S(1)}, f32[160,256]{1,0:T(8,128)S(1)}, u32[]{:S(2)}, u32[]{:S(2)}) collective-permute-start(f32[160,256]{1,0:T(8,128)S(1)} %collective-permute-done.11), channel_id=1, source_target_pairs={{0,4},{2,6},{4,0},{6,2},{8,12},{10,14},{12,8},{14,10},{1,5},{3,7},... | collective-permute-start | bytes 491528 | tf_op jit(solution)/shard_map/ppermute | solution.py:356
  119.1 5.8 %collective-permute-start.14 = (f32[160,256]{1,0:T(8,128)S(1)}, f32[160,256]{1,0:T(8,128)S(1)}, u32[]{:S(2)}, u32[]{:S(2)}) collective-permute-start(f32[160,256]{1,0:T(8,128)S(1)} %collective-permute-done.10), channel_id=1, source_target_pairs={{0,2},{2,0},{4,6},{6,4},{8,10},{10,8},{12,14},{14,12},{1,3},{3,1},... | collective-permute-start | bytes 491528 | tf_op jit(solution)/shard_map/ppermute | solution.py:356
  120.2 5.3 %collective-permute-start.15 = (f32[160,256]{1,0:T(8,128)S(1)}, f32[160,256]{1,0:T(8,128)S(1)}, u32[]{:S(2)}, u32[]{:S(2)}) collective-permute-start(f32[160,256]{1,0:T(8,128)S(1)} %collective-permute-done.13), channel_id=1, source_target_pairs={{0,8},{2,10},{4,12},{6,14},{8,0},{10,2},{12,4},{14,6},{1,9},{3,11}... | collective-permute-start | bytes 491528 | tf_op jit(solution)/shard_map/ppermute | solution.py:356
  121.2 5.6 %collective-permute-start.16 = (f32[160,256]{1,0:T(8,128)S(1)}, f32[160,256]{1,0:T(8,128)S(1)}, u32[]{:S(2)}, u32[]{:S(2)}) collective-permute-start(f32[160,256]{1,0:T(8,128)S(1)} %collective-permute-done.12), channel_id=1, source_target_pairs={{0,2},{2,0},{4,6},{6,4},{8,10},{10,8},{12,14},{14,12},{1,3},{3,1},... | collective-permute-start | bytes 491528 | tf_op jit(solution)/shard_map/ppermute | solution.py:356
  126.7 3.1 %collective-permute-start.17 = (f32[8,160,256]{2,1,0:T(8,128)S(1)}, f32[8,160,256]{2,1,0:T(8,128)S(1)}, u32[]{:S(2)}, u32[]{:S(2)}) collective-permute-start(f32[8,160,256]{2,1,0:T(8,128)S(1)} %bitcast_dynamic-update-slice_fusion.mine_ref), channel_id=1, source_target_pairs={{0,1},{1,0},{2,3},{3,2},{4,5},{5,4},{6,7},{7,6},{8,9},{9,8},{10,11... | collective-permute-start | bytes 3932168 | tf_op jit(solution)/shard_map/ppermute | solution.py:360
  138.2 1.2 copy-start.1
  139.4 0.7 copy-start.15
  140.1 2.4 %copy-start.2 = (f32[6,256,256]{2,1,0:T(8,128)S(1)}, f32[6,256,256]{2,1,0:T(8,128)}, u32[]{:S(2)}) copy-start(f32[6,256,256]{2,1,0:T(8,128)} %copy-done.1) | copy-start | bytes 4718596
  141.9 14.9 %collective-permute-start.18 = (f32[256,256]{1,0:T(8,128)S(1)}, f32[256,256]{1,0:T(8,128)S(1)}, u32[]{:S(2)}, u32[]{:S(2)}) collective-permute-start(f32[256,256]{1,0:T(8,128)S(1)} %sum_places.1.left_ref), channel_id=1, source_target_pairs={{0,16},{16,0},{1,17},{17,1},{2,18},{18,2},{3,19},{19,3},{4,20},{20... | collective-permute-start | bytes 786440 | tf_op jit(solution)/shard_map/ppermute | solution.py:360
  156.9 15.2 %copy-start.16 = (f32[256,256]{1,0:T(8,128)S(1)}, f32[256,256]{1,0:T(8,128)}, u32[]{:S(2)}) copy-start(f32[256,256]{1,0:T(8,128)} %copy-done.15) | copy-start | bytes 786436
  156.9 15.1 %collective-permute-start.21 = (f32[256,256]{1,0:T(8,128)S(1)}, f32[256,256]{1,0:T(8,128)S(1)}, u32[]{:S(2)}, u32[]{:S(2)}) collective-permute-start(f32[256,256]{1,0:T(8,128)S(1)} %add_groups.1.refs_8_), channel_id=1, source_target_pairs={{0,3},{1,2},{2,1},{3,0},{4,7},{5,6},{6,5},{7,4},{8,11},{9,10},{10,... | collective-permute-start | bytes 786440 | tf_op jit(solution)/shard_map/ppermute | solution.py:364
  157.0 15.0 %collective-permute-start.20 = (f32[256,256]{1,0:T(8,128)S(1)}, f32[256,256]{1,0:T(8,128)S(1)}, u32[]{:S(2)}, u32[]{:S(2)}) collective-permute-start(f32[256,256]{1,0:T(8,128)S(1)} %add_groups.1.refs_8_), channel_id=1, source_target_pairs={{0,2},{1,3},{2,0},{3,1},{4,6},{5,7},{6,4},{7,5},{8,10},{9,11},{10,... | collective-permute-start | bytes 786440 | tf_op jit(solution)/shard_map/ppermute | solution.py:364
  158.1 13.9 %collective-permute-start.19 = (f32[256,256]{1,0:T(8,128)S(1)}, f32[256,256]{1,0:T(8,128)S(1)}, u32[]{:S(2)}, u32[]{:S(2)}) collective-permute-start(f32[256,256]{1,0:T(8,128)S(1)} %add_groups.1.refs_8_), channel_id=1, source_target_pairs={{0,1},{1,0},{2,3},{3,2},{4,5},{5,4},{6,7},{7,6},{8,9},{9,8},{10,11... | collective-permute-start | bytes 786440 | tf_op jit(solution)/shard_map/ppermute | solution.py:364

commit v6 on v5

--- a/solution.py
+++ b/solution.py
@@ -108,12 +108,11 @@
 
 
 PAIRS = [(r, c) for r in range(P_SIZE) for c in range(r, P_SIZE)]
-HALF = len(PAIRS) // 2
-PIECES = 4 * P_SIZE
+CHUNKS = 2
 
 
 def mask_kernel(place_ref, arcs_ref, slab_ref, rows_ref, *refs):
-    pieces, work, sems = refs[:-2], refs[-2], refs[-1]
+    chunks, work, sems = refs[:-2], refs[-2], refs[-1]
     top = slab_ref.shape[0]
     arcs = arcs_ref.shape[0]
     copies = [pltpu.make_async_copy(slab_ref, work.at[pl.ds(0, top)], sems.at[arcs])]
@@ -129,77 +128,53 @@
         live = arcs_ref[a, 0].astype(jnp.float32)
         spot = pl.ds(top + a * ARC_ROWS, ARC_ROWS)
         work[spot, :] = work[spot, :] * live
-    count = pieces[0].shape[0]
-    for s, piece in enumerate(pieces):
-        start = pl.multiple_of((place_ref[4] ^ s) * count, 16)
-        piece[...] = work[pl.ds(start, count), :]
-
-
-def upper_products_kernel(place_ref, *refs):
-    blocks, (keep_ref, send_ref, columns, work) = refs[:-4], refs[-4:]
-    side, me = place_ref[0], place_ref[4]
-    for s, block in enumerate(blocks):
-        columns[me ^ s] = block[...]
-    right = [right_parts(columns[c]) for c in range(P_SIZE)]
-    at = 0
-    for r in range(P_SIZE):
-        wide = jnp.concatenate(right[r:], axis=1)
-        product = parts_dot(left_parts(columns[r]), wide)
-        for c in range(P_SIZE - r):
-            work[at * B : (at + 1) * B, :] = product[:, c * B : (c + 1) * B]
-            at += 1
-    rows = HALF * B
-    keep_ref[...] = work[pl.ds(pl.multiple_of(side * rows, B), rows), :]
-    send_ref[...] = work[pl.ds(pl.multiple_of((1 - side) * rows, B), rows), :]
-
-
-def all_products_kernel(n_left, place_ref, *refs):
-    blocks, (_, keep_ref, send_ref, columns, panels, work) = refs[:-6], refs[-6:]
-    left_blocks, right_blocks = blocks[:n_left], blocks[n_left:]
-    side, me = place_ref[0], place_ref[4]
-    for s, block in enumerate(right_blocks):
-        columns[me ^ s] = block[...]
-    for s, block in enumerate(left_blocks):
-        panels[me ^ s] = block[...]
-    left = panels if left_blocks else columns
-    first = columns.shape[0] - P_SIZE
-    right = jnp.concatenate([right_parts(columns[first + c]) for c in range(P_SIZE)], axis=1)
-    for r in range(P_SIZE):
-        product = parts_dot(left_parts(left[r]), right)
-        for b in range(P_SIZE):
-            work[r * P_SIZE + b] = product[:, b * B : (b + 1) * B]
-    for a in range(2):
-        for c in range(P_SIZE):
-            block = 2 * a * P_SIZE + c
-            keep_ref[a * P_SIZE + c] = work[block + side * P_SIZE]
-            send_ref[a * P_SIZE + c] = work[block + (1 - side) * P_SIZE]
-
-
-def tie_kernel(value_ref, after_ref, out_ref):
-    del value_ref, after_ref, out_ref
-
-
-def behind(value, after):
-    return pl.pallas_call(
-        tie_kernel,
-        out_shape=jax.ShapeDtypeStruct(value.shape, value.dtype),
-        in_specs=[pl.BlockSpec(memory_space=pl.ANY)] * 2,
-        out_specs=pl.BlockSpec(memory_space=pl.ANY),
-        input_output_aliases={0: 0},
-        name="behind",
-    )(value, after)
+    count = chunks[0].shape[0]
+    if len(chunks) > CHUNKS:
+        first = jnp.where(place_ref[4] == 0, 0, CHUNKS * count)
+    else:
+        first = 0
+    for s, chunk in enumerate(chunks):
+        start = first + s * count if s < CHUNKS else CHUNKS * count - first + (s - CHUNKS) * count
+        chunk[...] = work[pl.ds(pl.multiple_of(start, 16), count), :]
+
+
+def products_kernel(place_ref, *refs):
+    panels, right = refs[: P_SIZE * CHUNKS], refs[P_SIZE * CHUNKS : (P_SIZE + 1) * CHUNKS]
+    keep_ref, keep_cross_ref, send_ref, work = refs[(P_SIZE + 1) * CHUNKS :]
+    side, own = place_ref[0], place_ref[2]
+
+    def whole(chunks):
+        return jnp.concatenate([chunk[...] for chunk in chunks], axis=0)
+
+    both = jnp.concatenate(
+        [right_parts(whole(panels[:CHUNKS])), right_parts(whole(right))], axis=1
+    )
+    for t in range(P_SIZE):
+        left = left_parts(whole(panels[t * CHUNKS : (t + 1) * CHUNKS]))
+        product = parts_dot(left, both)
+        work[0, own ^ t] = product[:, :B]
+        work[1, own ^ t] = product[:, B:]
+    for h in range(2):
+        keep_ref[h] = work[0, 2 * h + side]
+        keep_cross_ref[h] = work[1, 2 * h + side]
+        for k in range(2):
+            send_ref[k, h] = work[k, 2 * h + 1 - side]
+
+
+def pick_kernel(k, place_ref, keep_ref, got_ref, _, own_ref, other_ref):
+    high = place_ref[1]
+    own_ref[...] = keep_ref[high] + got_ref[k, high]
+    other_ref[...] = keep_ref[1 - high] + got_ref[k, 1 - high]
+
+
+def stack_kernel(first_ref, second_ref, _, out_ref):
+    out_ref[0] = first_ref[...]
+    out_ref[1] = second_ref[...]
 
 
 def add_kernel(left_ref, right_ref, after_ref, out_ref):
     del after_ref
     out_ref[...] = left_ref[...] + right_ref[...]
-
-
-def sum_kernel(parts_ref, _, out_ref):
-    total = parts_ref[0]
-    for i in range(1, parts_ref.shape[0]):
-        total = total + parts_ref[i]
-    out_ref[...] = total
 
 
 def on_chip(kernel, shapes, name, *operands, scratch=(), scalars=0, after=(), outside=()):
@@ -219,27 +194,17 @@
 
 
 def collect_kernel(place_ref, mine_ref, other_ref, gram_ref):
-    side, high, low = place_ref[0], place_ref[1], place_ref[2]
-    at = high * P_SIZE + low
-    rows = mine_ref.shape[1]
-    for s in range(2):
-        for p in range(PIECES // 2):
-            start = ((s * PIECES) // 2 + p) * rows
-            end = start + rows
-            while start < end:
-                block, first = start // B, start % B
-                count = min(end - start, B - first)
-                skip = rows - (end - start)
-
-                @pl.when(side == s)
-                def _(block=block, first=first, count=count, skip=skip, p=p):
-                    gram_ref[block, first : first + count] = mine_ref[p ^ at, skip : skip + count]
-
-                @pl.when(side != s)
-                def _(block=block, first=first, count=count, skip=skip, p=p):
-                    gram_ref[block, first : first + count] = other_ref[p ^ at, skip : skip + count]
-
-                start += count
+    side, at = place_ref[0], place_ref[1] * P_SIZE + place_ref[2]
+    for i, (r, c) in enumerate(PAIRS):
+        spot = ((r // 2) * P_SIZE + c) ^ at
+
+        @pl.when(side == r % 2)
+        def _(i=i, spot=spot):
+            gram_ref[i] = mine_ref[spot]
+
+        @pl.when(side != r % 2)
+        def _(i=i, spot=spot):
+            gram_ref[i] = other_ref[spot]
 
 
 def factor_step_kernel(n, gram_ref, *rest):
@@ -309,13 +274,14 @@
 
 def solve_kernel(place_ref, *refs):
     rows, inverses = refs[: P_SIZE - 1], refs[P_SIZE - 1 : 2 * P_SIZE - 1]
-    gram_ref, own_refs, out_ref, own_ref = refs[-P_SIZE - 3], refs[-P_SIZE - 2 : -2], refs[-2], refs[-1]
+    gram_ref, pair_ref, other_ref, out_ref, own_ref = refs[-5:]
     row_index, col_index = 2 * place_ref[1] + place_ref[0], place_ref[3]
 
     @pl.when(col_index >= P_SIZE)
     def _():
-        for t in range(P_SIZE):
-            own_ref[row_index ^ t] = own_refs[t][...]
+        for h in range(2):
+            own_ref[row_index ^ (2 * h)] = pair_ref[h]
+            own_ref[row_index ^ (2 * h + 1)] = other_ref[h]
 
     for c in range(P_SIZE):
 
@@ -360,8 +326,8 @@
     return lax.ppermute(value, axis, [(0, 1), (1, 0)])
 
 
-def across_rows(value, bits):
-    return lax.ppermute(value, ("rh", "rl"), [(i, i ^ bits) for i in range(P_SIZE)])
+def other_group(value):
+    return lax.ppermute(value, ("hi", "lo"), [(i, i ^ 6) for i in range(2 * P_SIZE)])
 
 
 def spread(piece):
@@ -374,21 +340,18 @@
 
 def on_device(r_slab, arc_rows, arc_blocks):
     n_hi = lax.axis_size("hi")
-    low = lax.axis_index("lo")
+    group, low = lax.axis_index("hi"), lax.axis_index("lo")
     high_row, side = lax.axis_index("rh"), lax.axis_index("rl")
-    col_index = lax.axis_index("hi") * P_SIZE + low
-    row_index = high_row * 2 + side
+    col_index = group * P_SIZE + low
     columns = arc_rows.shape[1]
     in_two = n_hi == 2
-    owners = ("hi", "lo") if in_two else ("lo",)
-    shares = P_SIZE * n_hi if in_two else P_SIZE
-    me = col_index if in_two else low
-    place = jnp.stack([side, high_row, low, col_index, me]).astype(jnp.int32)
+    panel = low ^ (2 * group) if in_two else low
+    place = jnp.stack([side, high_row, panel, col_index, group]).astype(jnp.int32)
     total = r_slab.shape[0] + arc_rows.shape[0]
-    share = (total // shares, columns)
-    blocks = on_chip(
+    parts = 2 * CHUNKS if in_two else CHUNKS
+    chunks = on_chip(
         mask_kernel,
-        [share] * shares,
+        [(total // parts, columns)] * parts,
         "mask",
         place,
         arc_blocks,
@@ -399,41 +362,54 @@
         ],
         outside=(r_slab, arc_rows),
     )
-    blocks = blocks[:1] + [
-        lax.ppermute(blocks[s], owners, [(i, i ^ s) for i in range(shares)])
-        for s in range(1, shares)
+    if in_two:
+        kept, got = chunks[:CHUNKS], [other_group(chunk) for chunk in chunks[CHUNKS:]]
+        first = [jnp.where(group == 0, k, g) for k, g in zip(kept, got)]
+        right = [jnp.where(group == 0, g, k) for k, g in zip(kept, got)]
+    else:
+        first, right = [from_first(chunk, n_hi) for chunk in chunks], chunks
+    y, z = (0, 1), (0, 2)
+    by_y, by_z = exchange(first[0], *y), exchange(first[1], *z)
+    panels = [
+        first[0],
+        first[1],
+        by_y,
+        exchange(first[1], *y),
+        exchange(first[0], *z),
+        by_z,
+        exchange(by_y, *z),
+        exchange(by_z, *y),
     ]
-    panels = [] if in_two else [from_first(block, n_hi) for block in blocks]
-
-    half = (HALF * B, B)
-    gathered = pltpu.VMEM((shares, *share), jnp.float32)
-    keep, send = on_chip(
-        upper_products_kernel,
-        [half, half],
-        "upper_products",
-        place,
-        *blocks,
-        scalars=1,
-        scratch=[gathered, pltpu.VMEM((len(PAIRS) * B, B), jnp.float32)],
-    )
-    gram = (keep + swap(send)).reshape(PIECES // 2, -1, B)
-    gram = lax.all_to_all(gram, ("rh", "lo"), 0, 0)
-    half = (2 * P_SIZE, B, B)
-    cross, send = on_chip(
-        functools.partial(all_products_kernel, len(panels)),
-        [half, half],
-        "all_products",
+
+    pair, block = (2, B, B), (B, B)
+    keep, keep_cross, send = on_chip(
+        products_kernel,
+        [pair, pair, (2, *pair)],
+        "products",
         place,
         *panels,
-        *blocks,
+        *right,
         scalars=1,
-        scratch=[gathered, gathered, pltpu.VMEM((P_SIZE * P_SIZE, B, B), jnp.float32)],
-        after=(keep,),
-    )
-    cross = cross + swap(send)
-    (gram,) = on_chip(sum_kernel, [gram.shape[1:]], "sum_pieces", gram, after=(cross,))
-    cross = lax.all_to_all(behind(cross, gram), ("rh", "lo"), 0, 0)
-    piece = gram + swap(gram, "hi") if in_two else from_first(gram, n_hi)
+        scratch=[pltpu.VMEM((2, P_SIZE, B, B), jnp.float32)],
+    )
+    got = swap(send)
+
+    def picked(k, kept, after):
+        return on_chip(
+            functools.partial(pick_kernel, k),
+            [block, block],
+            "pick",
+            place,
+            kept,
+            got,
+            scalars=1,
+            after=(after,),
+        )
+
+    mine, other = picked(0, keep, send)
+    piece = mine + exchange(other, 1, 0)
+    if in_two:
+        piece = piece + other_group(piece)
     pieces = spread(piece)
     (gram,) = on_chip(
         collect_kernel,
@@ -444,13 +420,17 @@
         swap(pieces),
         scalars=1,
     )
+
+    def added(left, right, after):
+        (total,) = on_chip(add_kernel, [block], "add", left, right, after=(after,))
+        return total
+
     rows, inverses = factor(gram)
-    (mine,) = on_chip(sum_kernel, [(B, columns)], "sum_places", cross, after=(rows[0],))
+    mine, other = picked(1, keep_cross, gram)
+    mine = added(mine, exchange(other, 1, 0), rows[0])
     if in_two:
-        other = swap(mine, "hi")
-        (mine,) = on_chip(add_kernel, [(B, columns)], "add_groups", mine, other, after=(rows[1],))
-    own = [mine] + [across_rows(mine, bits) for bits in range(1, P_SIZE)]
-
+        mine = added(mine, other_group(mine), rows[1])
+    (own,) = on_chip(stack_kernel, [pair], "stack", mine, exchange(mine, 1, 0), after=(rows[2],))
     (result,) = on_chip(
         solve_kernel,
         [(B, columns)],
@@ -459,7 +439,8 @@
         *rows,
         *inverses,
         gram,
-        *own,
+        own,
+        swap(own),
         scalars=1,
         scratch=[pltpu.VMEM((P_SIZE, B, columns), jnp.float32)],
     )

time: 176 us -> 155 us (0.88)
  the two profiles are of different devices: /device:TPU:0 before, /device:TPU:9 now
where the time goes in v6:
time: 155 us
  waiting for transfers between devices  86.9 us (56%)
  Pallas kernels  39.1 us (25%)
  starting transfers between devices  25.7 us (17%)
  local copies, waits for them, and re-layouts  3.12 us (2%)
    ppermute x4, waiting for transfers between devices, other_group(): lax.ppermute(value, ('hi', 'lo'), [(i, i ^ 6) for i in range(2 * P_SIZE)])  43.8 us
    pallas_call x13, Pallas kernels, on_chip(): pl.pallas_call(kernel, out_shape=[jax.ShapeDtypeStruct(shape, jnp.float32...  39.1 us
    ppermute x16, waiting for transfers between devices, exchange(): lax.ppermute(value, ('lo', 'rh'), [(i, i ^ bits) for i in range(2 * P_SIZ...  37 us
    ppermute x16, starting transfers between devices, exchange(): lax.ppermute(value, ('lo', 'rh'), [(i, i ^ bits) for i in range(2 * P_SIZ...  14.7 us
    ppermute x3, starting transfers between devices, swap(): return lax.ppermute(value, axis, [(0, 1), (1, 0)])  7.12 us
    ppermute x3, waiting for transfers between devices, swap(): return lax.ppermute(value, axis, [(0, 1), (1, 0)])  6.08 us
    ppermute x4, starting transfers between devices, other_group(): lax.ppermute(value, ('hi', 'lo'), [(i, i ^ 6) for i in range(2 * P_SIZE)])  3.89 us
  transfers between devices with their start and end apart: 23, of which 14 were waited for; matrix products, arithmetic and copies ran while one was open for 0% of the time, Pallas kernels for 18%

profile of v6, /device:TPU:9, one launch (start us, length us, event | category | flops | bytes accessed | tf_op | source)
XLA Modules:
  0.0 155.1 jit_solution(6691633875591804865)
XLA Ops:
  0.0 0.7 copy.4.arcs_ref
  0.7 0.1 stack.51.place_ref
  0.8 1.2 copy-done
  2.0 0.9 copy-done.1
  3.0 2.2 %mask.1 = (f32[320,256]{1,0:T(8,128)S(1)}, f32[320,256]{1,0:T(8,128)S(1)}, f32[320,256]{1,0:T(8,128)S(1)}, f32[320,256]{1,0:T(8,128)S(1)}) custom-call(s32[5]{0:T(128)S(1)} %stack.51.place_ref, s32[8,1]{1,0:T(8,128)S(1)} %copy.4.arcs_ref, f32[256,256]{1,0:T(8,128)S(1)} %copy-done.1, f32[1024,256]{1,0:T(8,128)S(1)} %copy-done), custom_call_target="tpu_custom_call" | custom-call | tf_op jit(solution)/shard_map/mask/pallas_call | solution.py:181
  5.2 1.4 collective-permute-start
  6.6 0.2 collective-permute-start.1
  6.8 21.3 %collective-permute-done = f32[320,256]{1,0:T(8,128)S(1)} collective-permute-done((f32[320,256]{1,0:T(8,128)S(1)}, f32[320,256]{1,0:T(8,128)S(1)}, u32[]{:S(2)}, u32[]{:S(2)}) %collective-permute-start) | collective-permute-done | bytes 327712 | tf_op jit(solution)/shard_map/ppermute | solution.py:330
  28.1 1.3 collective-permute-start.2
  29.5 5.7 %collective-permute-done.1 = f32[320,256]{1,0:T(8,128)S(1)} collective-permute-done((f32[320,256]{1,0:T(8,128)S(1)}, f32[320,256]{1,0:T(8,128)S(1)}, u32[]{:S(2)}, u32[]{:S(2)}) %collective-permute-start.1) | collective-permute-done | bytes 327712 | tf_op jit(solution)/shard_map/ppermute | solution.py:330
  35.2 1.5 collective-permute-start.4
  36.7 1.2 collective-permute-start.3
  38.0 5.1 %collective-permute-done.5.refs_5_ = f32[320,256]{1,0:T(8,128)S(1)} collective-permute-done((f32[320,256]{1,0:T(8,128)S(1)}, f32[320,256]{1,0:T(8,128)S(1)}, u32[]{:S(2)}, u32[]{:S(2)}) %collective-permute-start.5) | collective-permute-done | bytes 327712 | tf_op jit(solution)/shard_map/ppermute | solution.py:322
  43.1 1.2 collective-permute-start.7
  44.3 5.8 %collective-permute-done.4.refs_4_ = f32[320,256]{1,0:T(8,128)S(1)} collective-permute-done((f32[320,256]{1,0:T(8,128)S(1)}, f32[320,256]{1,0:T(8,128)S(1)}, u32[]{:S(2)}, u32[]{:S(2)}) %collective-permute-start.4) | collective-permute-done | bytes 327712 | tf_op jit(solution)/shard_map/ppermute | solution.py:322
  50.1 7.0 %collective-permute-done.6.refs_6_ = f32[320,256]{1,0:T(8,128)S(1)} collective-permute-done((f32[320,256]{1,0:T(8,128)S(1)}, f32[320,256]{1,0:T(8,128)S(1)}, u32[]{:S(2)}, u32[]{:S(2)}) %collective-permute-start.6) | collective-permute-done | bytes 327712 | tf_op jit(solution)/shard_map/ppermute | solution.py:322
  57.1 3.1 %products.1 = (f32[2,256,256]{2,1,0:T(8,128)S(1)}, f32[2,256,256]{2,1,0:T(8,128)S(1)}, f32[2,2,256,256]{3,2,1,0:T(8,128)S(1)}) custom-call(s32[5]{0:T(128)S(1)} %stack.51.place_ref, f32[320,256]{1,0:T(8,128)S(1)} %get-tuple-element.50.refs_0_, f32[320,256]{1,0:T(8,128)S(1)} %get-tuple-element.48.refs_1_, f32[320,256]{1,0:T(8,128)S(1)} %collective-permute-done.2.refs_2_, ...), custom_call_target="tpu_custom_call" | custom-call | tf_op jit(solution)/shard_map/products/pallas_call | solution.py:181
  60.2 2.3 %collective-permute-start.8 = (f32[2,2,256,256]{3,2,1,0:T(8,128)S(1)}, f32[2,2,256,256]{3,2,1,0:T(8,128)S(1)}, u32[]{:S(2)}, u32[]{:S(2)}) collective-permute-start(f32[2,2,256,256]{3,2,1,0:T(8,128)S(1)} %get-tuple-element.30._), channel_id=1, source_target_pairs={{0,1},{1,0},{2,3},{3,2},{4,5},{5,4},{6,7},{7,6},{8,9},{9,8},{10,11... | collective-permute-start | bytes 3145736 | tf_op jit(solution)/shard_map/ppermute | solution.py:326
  62.6 2.3 %collective-permute-done.8.got_ref = f32[2,2,256,256]{3,2,1,0:T(8,128)S(1)} collective-permute-done((f32[2,2,256,256]{3,2,1,0:T(8,128)S(1)}, f32[2,2,256,256]{3,2,1,0:T(8,128)S(1)}, u32[]{:S(2)}, u32[]{:S(2)}) %collective-permute-start.8) | collective-permute-done | bytes 1048608 | tf_op jit(solution)/shard_map/ppermute | solution.py:326
  64.9 0.6 pick.2
  65.5 1.3 collective-permute-start.9
  66.7 6.3 %collective-permute-done.9 = f32[256,256]{1,0:T(8,128)S(1)} collective-permute-done((f32[256,256]{1,0:T(8,128)S(1)}, f32[256,256]{1,0:T(8,128)S(1)}, u32[]{:S(2)}, u32[]{:S(2)}) %collective-permute-start.9) | collective-permute-done | bytes 262176 | tf_op jit(solution)/shard_map/ppermute | solution.py:322
  73.1 1.2 collective-permute-start.10
  74.3 12.1 %collective-permute-done.10 = f32[256,256]{1,0:T(8,128)S(1)} collective-permute-done((f32[256,256]{1,0:T(8,128)S(1)}, f32[256,256]{1,0:T(8,128)S(1)}, u32[]{:S(2)}, u32[]{:S(2)}) %collective-permute-start.10) | collective-permute-done | bytes 262176 | tf_op jit(solution)/shard_map/ppermute | solution.py:330
  86.4 1.3 collective-permute-start.11
  87.7 1.2 collective-permute-start.14
  88.9 4.1 %collective-permute-done.12 = f32[256,256]{1,0:T(8,128)S(1)} collective-permute-done((f32[256,256]{1,0:T(8,128)S(1)}, f32[256,256]{1,0:T(8,128)S(1)}, u32[]{:S(2)}, u32[]{:S(2)}) %collective-permute-start.12) | collective-permute-done | bytes 262176 | tf_op jit(solution)/shard_map/ppermute | solution.py:322
  93.0 1.2 collective-permute-start.13
  94.3 1.2 collective-permute-start.15
  95.5 0.4 collective-permute-start.16
  95.9 2.9 %collective-permute-done.13 = f32[256,256]{1,0:T(8,128)S(1)} collective-permute-done((f32[256,256]{1,0:T(8,128)S(1)}, f32[256,256]{1,0:T(8,128)S(1)}, u32[]{:S(2)}, u32[]{:S(2)}) %collective-permute-start.13) | collective-permute-done | bytes 262176 | tf_op jit(solution)/shard_map/ppermute | solution.py:322
  98.7 1.2 collective-permute-start.17
  100.0 1.1 collective-permute-done.16
  101.1 4.8 %collective-permute-done.17 = f32[256,256]{1,0:T(8,128)S(1)} collective-permute-done((f32[256,256]{1,0:T(8,128)S(1)}, f32[256,256]{1,0:T(8,128)S(1)}, u32[]{:S(2)}, u32[]{:S(2)}) %collective-permute-start.17) | collective-permute-done | bytes 262176 | tf_op jit(solution)/shard_map/ppermute | solution.py:322
  105.9 2.8 %collective-permute-start.18 = (f32[8,256,256]{2,1,0:T(8,128)S(1)}, f32[8,256,256]{2,1,0:T(8,128)S(1)}, u32[]{:S(2)}, u32[]{:S(2)}) collective-permute-start(f32[8,256,256]{2,1,0:T(8,128)S(1)} %bitcast_dynamic-update-slice_fusion.mine_ref), channel_id=1, source_target_pairs={{0,1},{1,0},{2,3},{3,2},{4,5},{5,4},{6,7},{7,6},{8,9},{9,8},{10,11... | collective-permute-start | bytes 6291464 | tf_op jit(solution)/shard_map/ppermute | solution.py:326
  108.7 3.8 %collective-permute-done.18.other_ref = f32[8,256,256]{2,1,0:T(8,128)S(1)} collective-permute-done((f32[8,256,256]{2,1,0:T(8,128)S(1)}, f32[8,256,256]{2,1,0:T(8,128)S(1)}, u32[]{:S(2)}, u32[]{:S(2)}) %collective-permute-start.18) | collective-permute-done | bytes 2097184 | tf_op jit(solution)/shard_map/ppermute | solution.py:326
  112.5 0.9 collect.1.gram_ref._.refs_7_
  113.5 0.6 pick.3
  114.1 1.3 collective-permute-start.19
  115.4 7.3 %factor_step.4 = (f32[256,768]{1,0:T(8,128)S(1)}, f32[256,256]{1,0:T(8,128)S(1)}, f32[6,256,256]{2,1,0:T(8,128)S(1)}) custom-call(f32[10,256,256]{2,1,0:T(8,128)S(1)} %collect.1.gram_ref._.refs_7_), custom_call_target="tpu_custom_call" | custom-call | tf_op jit(solution)/shard_map/factor_step/pallas_call | solution.py:181
  122.7 1.2 collective-permute-start.20
  123.9 7.0 %factor_step.5 = (f32[256,512]{1,0:T(8,128)S(1)}, f32[256,256]{1,0:T(8,128)S(1)}, f32[3,256,256]{2,1,0:T(8,128)S(1)}) custom-call(f32[6,256,256]{2,1,0:T(8,128)S(1)} %get-tuple-element.34.gram_ref), custom_call_target="tpu_custom_call" | custom-call | tf_op jit(solution)/shard_map/factor_step/pallas_call | solution.py:181
  130.9 4.7 %collective-permute-done.20.right_ref = f32[256,256]{1,0:T(8,128)S(1)} collective-permute-done((f32[256,256]{1,0:T(8,128)S(1)}, f32[256,256]{1,0:T(8,128)S(1)}, u32[]{:S(2)}, u32[]{:S(2)}) %collective-permute-start.20) | collective-permute-done | bytes 262176 | tf_op jit(solution)/shard_map/ppermute | solution.py:330
  135.7 0.2 collective-permute-start.21
  135.9 6.7 %factor_step.6 = (f32[256,256]{1,0:T(8,128)S(1)}, f32[256,256]{1,0:T(8,128)S(1)}, f32[1,256,256]{2,1,0:T(8,128)S(1)}) custom-call(f32[3,256,256]{2,1,0:T(8,128)S(1)} %get-tuple-element.36.gram_ref), custom_call_target="tpu_custom_call" | custom-call | tf_op jit(solution)/shard_map/factor_step/pallas_call | solution.py:181
  142.7 2.0 %collective-permute-start.22 = (f32[2,256,256]{2,1,0:T(8,128)S(1)}, f32[2,256,256]{2,1,0:T(8,128)S(1)}, u32[]{:S(2)}, u32[]{:S(2)}) collective-permute-start(f32[2,256,256]{2,1,0:T(8,128)S(1)} %stack.61.refs_8_), channel_id=1, source_target_pairs={{0,1},{1,0},{2,3},{3,2},{4,5},{5,4},{6,7},{7,6},{8,9},{9,8},{10,11... | collective-permute-start | bytes 1572872 | tf_op jit(solution)/shard_map/ppermute | solution.py:326
  144.6 6.4 %factor_step.7.refs_6_ = f32[256,256]{1,0:T(8,128)S(1)} custom-call(f32[1,256,256]{2,1,0:T(8,128)S(1)} %get-tuple-element.41.gram_ref), custom_call_target="tpu_custom_call" | custom-call | tf_op jit(solution)/shard_map/factor_step/pallas_call | solution.py:181
  151.1 4.1 %solve.1 = f32[256,256]{1,0:T(8,128)} custom-call(s32[5]{0:T(128)S(1)} %stack.51.place_ref, f32[256,768]{1,0:T(8,128)S(1)} %get-tuple-element.33.after_ref.refs_0_, f32[256,512]{1,0:T(8,128)S(1)} %get-tuple-element.35.after_ref.refs_1_, f32[256,256]{1,0:T(8,128)S(1)} %get-tuple-element.37._.refs_2_, f32[256,256]{1,0:T(8,128)S(1)} %get-tuple-element.38.refs_3_, ...), custom_call_target="tpu_custom_call" | custom-call | tf_op jit(solution)/shard_map/solve/pallas_call | solution.py:181
  (28 shorter events, 0.6 us)
Async XLA Ops:
  0.8 1.2 copy-start
  2.0 0.9 copy-start.1
  5.2 22.9 %collective-permute-start = (f32[320,256]{1,0:T(8,128)S(1)}, f32[320,256]{1,0:T(8,128)S(1)}, u32[]{:S(2)}, u32[]{:S(2)}) collective-permute-start(f32[320,256]{1,0:T(8,128)S(1)} %get-tuple-element.26), channel_id=1, source_target_pairs={{0,24},{4,28},{8,16},{12,20},{16,8},{20,12},{24,0},{28,4},{1,25},{... | collective-permute-start | bytes 983048 | tf_op jit(solution)/shard_map/ppermute | solution.py:330
  6.6 28.5 %collective-permute-start.1 = (f32[320,256]{1,0:T(8,128)S(1)}, f32[320,256]{1,0:T(8,128)S(1)}, u32[]{:S(2)}, u32[]{:S(2)}) collective-permute-start(f32[320,256]{1,0:T(8,128)S(1)} %get-tuple-element.28), channel_id=1, source_target_pairs={{0,24},{4,28},{8,16},{12,20},{16,8},{20,12},{24,0},{28,4},{1,25},{... | collective-permute-start | bytes 983048 | tf_op jit(solution)/shard_map/ppermute | solution.py:330
  28.1 9.8 %collective-permute-start.2 = (f32[320,256]{1,0:T(8,128)S(1)}, f32[320,256]{1,0:T(8,128)S(1)}, u32[]{:S(2)}, u32[]{:S(2)}) collective-permute-start(f32[320,256]{1,0:T(8,128)S(1)} %get-tuple-element.50.refs_0_), channel_id=1, source_target_pairs={{0,4},{2,6},{4,0},{6,2},{8,12},{10,14},{12,8},{14,10},{1,5},{3,7},... | collective-permute-start | bytes 983048 | tf_op jit(solution)/shard_map/ppermute | solution.py:322
  35.2 7.9 %collective-permute-start.5 = (f32[320,256]{1,0:T(8,128)S(1)}, f32[320,256]{1,0:T(8,128)S(1)}, u32[]{:S(2)}, u32[]{:S(2)}) collective-permute-start(f32[320,256]{1,0:T(8,128)S(1)} %get-tuple-element.48.refs_1_), channel_id=1, source_target_pairs={{0,8},{2,10},{4,12},{6,14},{8,0},{10,2},{12,4},{14,6},{1,9},{3,11}... | collective-permute-start | bytes 983048 | tf_op jit(solution)/shard_map/ppermute | solution.py:322
  35.2 14.9 %collective-permute-start.4 = (f32[320,256]{1,0:T(8,128)S(1)}, f32[320,256]{1,0:T(8,128)S(1)}, u32[]{:S(2)}, u32[]{:S(2)}) collective-permute-start(f32[320,256]{1,0:T(8,128)S(1)} %get-tuple-element.50.refs_0_), channel_id=1, source_target_pairs={{0,8},{2,10},{4,12},{6,14},{8,0},{10,2},{12,4},{14,6},{1,9},{3,11}... | collective-permute-start | bytes 983048 | tf_op jit(solution)/shard_map/ppermute | solution.py:322
  36.7 13.4 %collective-permute-start.3 = (f32[320,256]{1,0:T(8,128)S(1)}, f32[320,256]{1,0:T(8,128)S(1)}, u32[]{:S(2)}, u32[]{:S(2)}) collective-permute-start(f32[320,256]{1,0:T(8,128)S(1)} %get-tuple-element.48.refs_1_), channel_id=1, source_target_pairs={{0,4},{2,6},{4,0},{6,2},{8,12},{10,14},{12,8},{14,10},{1,5},{3,7},... | collective-permute-start | bytes 983048 | tf_op jit(solution)/shard_map/ppermute | solution.py:322
  37.9 19.2 %collective-permute-start.6 = (f32[320,256]{1,0:T(8,128)S(1)}, f32[320,256]{1,0:T(8,128)S(1)}, u32[]{:S(2)}, u32[]{:S(2)}) collective-permute-start(f32[320,256]{1,0:T(8,128)S(1)} %collective-permute-done.2.refs_2_), channel_id=1, source_target_pairs={{0,8},{2,10},{4,12},{6,14},{8,0},{10,2},{12,4},{14,6},{1,9},{3,11}... | collective-permute-start | bytes 983048 | tf_op jit(solution)/shard_map/ppermute | solution.py:322
  43.1 14.0 %collective-permute-start.7 = (f32[320,256]{1,0:T(8,128)S(1)}, f32[320,256]{1,0:T(8,128)S(1)}, u32[]{:S(2)}, u32[]{:S(2)}) collective-permute-start(f32[320,256]{1,0:T(8,128)S(1)} %collective-permute-done.5.refs_5_), channel_id=1, source_target_pairs={{0,4},{2,6},{4,0},{6,2},{8,12},{10,14},{12,8},{14,10},{1,5},{3,7},... | collective-permute-start | bytes 983048 | tf_op jit(solution)/shard_map/ppermute | solution.py:322
  60.2 4.6 %collective-permute-start.8 = (f32[2,2,256,256]{3,2,1,0:T(8,128)S(1)}, f32[2,2,256,256]{3,2,1,0:T(8,128)S(1)}, u32[]{:S(2)}, u32[]{:S(2)}) collective-permute-start(f32[2,2,256,256]{3,2,1,0:T(8,128)S(1)} %get-tuple-element.30._), channel_id=1, source_target_pairs={{0,1},{1,0},{2,3},{3,2},{4,5},{5,4},{6,7},{7,6},{8,9},{9,8},{10,11... | collective-permute-start | bytes 3145736 | tf_op jit(solution)/shard_map/ppermute | solution.py:326
  65.5 7.6 %collective-permute-start.9 = (f32[256,256]{1,0:T(8,128)S(1)}, f32[256,256]{1,0:T(8,128)S(1)}, u32[]{:S(2)}, u32[]{:S(2)}) collective-permute-start(f32[256,256]{1,0:T(8,128)S(1)} %get-tuple-element.32), channel_id=1, source_target_pairs={{0,2},{2,0},{4,6},{6,4},{8,10},{10,8},{12,14},{14,12},{1,3},{3,1},... | collective-permute-start | bytes 786440 | tf_op jit(solution)/shard_map/ppermute | solution.py:322
  73.1 13.2 %collective-permute-start.10 = (f32[256,256]{1,0:T(8,128)S(1)}, f32[256,256]{1,0:T(8,128)S(1)}, u32[]{:S(2)}, u32[]{:S(2)}) collective-permute-start(f32[256,256]{1,0:T(8,128)S(1)} %add.12), channel_id=1, source_target_pairs={{0,24},{4,28},{8,16},{12,20},{16,8},{20,12},{24,0},{28,4},{1,25},{... | collective-permute-start | bytes 786440 | tf_op jit(solution)/shard_map/ppermute | solution.py:330
  86.4 6.7 %collective-permute-start.12 = (f32[256,256]{1,0:T(8,128)S(1)}, f32[256,256]{1,0:T(8,128)S(1)}, u32[]{:S(2)}, u32[]{:S(2)}) collective-permute-start(f32[256,256]{1,0:T(8,128)S(1)} %get-tuple-element.46), channel_id=1, source_target_pairs={{0,8},{2,10},{4,12},{6,14},{8,0},{10,2},{12,4},{14,6},{1,9},{3,11}... | collective-permute-start | bytes 786440 | tf_op jit(solution)/shard_map/ppermute | solution.py:322
  86.4 7.8 %collective-permute-start.11 = (f32[256,256]{1,0:T(8,128)S(1)}, f32[256,256]{1,0:T(8,128)S(1)}, u32[]{:S(2)}, u32[]{:S(2)}) collective-permute-start(f32[256,256]{1,0:T(8,128)S(1)} %get-tuple-element.46), channel_id=1, source_target_pairs={{0,4},{2,6},{4,0},{6,2},{8,12},{10,14},{12,8},{14,10},{1,5},{3,7},... | collective-permute-start | bytes 786440 | tf_op jit(solution)/shard_map/ppermute | solution.py:322
  87.7 7.8 %collective-permute-start.14 = (f32[256,256]{1,0:T(8,128)S(1)}, f32[256,256]{1,0:T(8,128)S(1)}, u32[]{:S(2)}, u32[]{:S(2)}) collective-permute-start(f32[256,256]{1,0:T(8,128)S(1)} %get-tuple-element.46), channel_id=1, source_target_pairs={{0,2},{2,0},{4,6},{6,4},{8,10},{10,8},{12,14},{14,12},{1,3},{3,1},... | collective-permute-start | bytes 786440 | tf_op jit(solution)/shard_map/ppermute | solution.py:322
  93.0 5.7 %collective-permute-start.13 = (f32[256,256]{1,0:T(8,128)S(1)}, f32[256,256]{1,0:T(8,128)S(1)}, u32[]{:S(2)}, u32[]{:S(2)}) collective-permute-start(f32[256,256]{1,0:T(8,128)S(1)} %collective-permute-done.12), channel_id=1, source_target_pairs={{0,4},{2,6},{4,0},{6,2},{8,12},{10,14},{12,8},{14,10},{1,5},{3,7},... | collective-permute-start | bytes 786440 | tf_op jit(solution)/shard_map/ppermute | solution.py:322
  94.3 5.7 %collective-permute-start.15 = (f32[256,256]{1,0:T(8,128)S(1)}, f32[256,256]{1,0:T(8,128)S(1)}, u32[]{:S(2)}, u32[]{:S(2)}) collective-permute-start(f32[256,256]{1,0:T(8,128)S(1)} %collective-permute-done.11), channel_id=1, source_target_pairs={{0,2},{2,0},{4,6},{6,4},{8,10},{10,8},{12,14},{14,12},{1,3},{3,1},... | collective-permute-start | bytes 786440 | tf_op jit(solution)/shard_map/ppermute | solution.py:322
  95.5 5.6 %collective-permute-start.16 = (f32[256,256]{1,0:T(8,128)S(1)}, f32[256,256]{1,0:T(8,128)S(1)}, u32[]{:S(2)}, u32[]{:S(2)}) collective-permute-start(f32[256,256]{1,0:T(8,128)S(1)} %collective-permute-done.14), channel_id=1, source_target_pairs={{0,8},{2,10},{4,12},{6,14},{8,0},{10,2},{12,4},{14,6},{1,9},{3,11}... | collective-permute-start | bytes 786440 | tf_op jit(solution)/shard_map/ppermute | solution.py:322
  98.7 7.2 %collective-permute-start.17 = (f32[256,256]{1,0:T(8,128)S(1)}, f32[256,256]{1,0:T(8,128)S(1)}, u32[]{:S(2)}, u32[]{:S(2)}) collective-permute-start(f32[256,256]{1,0:T(8,128)S(1)} %collective-permute-done.13), channel_id=1, source_target_pairs={{0,2},{2,0},{4,6},{6,4},{8,10},{10,8},{12,14},{14,12},{1,3},{3,1},... | collective-permute-start | bytes 786440 | tf_op jit(solution)/shard_map/ppermute | solution.py:322
  105.9 6.6 %collective-permute-start.18 = (f32[8,256,256]{2,1,0:T(8,128)S(1)}, f32[8,256,256]{2,1,0:T(8,128)S(1)}, u32[]{:S(2)}, u32[]{:S(2)}) collective-permute-start(f32[8,256,256]{2,1,0:T(8,128)S(1)} %bitcast_dynamic-update-slice_fusion.mine_ref), channel_id=1, source_target_pairs={{0,1},{1,0},{2,3},{3,2},{4,5},{5,4},{6,7},{7,6},{8,9},{9,8},{10,11... | collective-permute-start | bytes 6291464 | tf_op jit(solution)/shard_map/ppermute | solution.py:326
  114.1 8.6 %collective-permute-start.19 = (f32[256,256]{1,0:T(8,128)S(1)}, f32[256,256]{1,0:T(8,128)S(1)}, u32[]{:S(2)}, u32[]{:S(2)}) collective-permute-start(f32[256,256]{1,0:T(8,128)S(1)} %get-tuple-element.44), channel_id=1, source_target_pairs={{0,2},{2,0},{4,6},{6,4},{8,10},{10,8},{12,14},{14,12},{1,3},{3,1},... | collective-permute-start | bytes 786440 | tf_op jit(solution)/shard_map/ppermute | solution.py:322
  122.7 12.9 %collective-permute-start.20 = (f32[256,256]{1,0:T(8,128)S(1)}, f32[256,256]{1,0:T(8,128)S(1)}, u32[]{:S(2)}, u32[]{:S(2)}) collective-permute-start(f32[256,256]{1,0:T(8,128)S(1)} %add.15.left_ref), channel_id=1, source_target_pairs={{0,24},{4,28},{8,16},{12,20},{16,8},{20,12},{24,0},{28,4},{1,25},{... | collective-permute-start | bytes 786440 | tf_op jit(solution)/shard_map/ppermute | solution.py:330
  135.7 7.0 %collective-permute-start.21 = (f32[256,256]{1,0:T(8,128)S(1)}, f32[256,256]{1,0:T(8,128)S(1)}, u32[]{:S(2)}, u32[]{:S(2)}) collective-permute-start(f32[256,256]{1,0:T(8,128)S(1)} %add.16.first_ref), channel_id=1, source_target_pairs={{0,2},{2,0},{4,6},{6,4},{8,10},{10,8},{12,14},{14,12},{1,3},{3,1},... | collective-permute-start | bytes 786440 | tf_op jit(solution)/shard_map/ppermute | solution.py:322
  142.7 8.4 %collective-permute-start.22 = (f32[2,256,256]{2,1,0:T(8,128)S(1)}, f32[2,256,256]{2,1,0:T(8,128)S(1)}, u32[]{:S(2)}, u32[]{:S(2)}) collective-permute-start(f32[2,256,256]{2,1,0:T(8,128)S(1)} %stack.61.refs_8_), channel_id=1, source_target_pairs={{0,1},{1,0},{2,3},{3,2},{4,5},{5,4},{6,7},{7,6},{8,9},{9,8},{10,11... | collective-permute-start | bytes 1572872 | tf_op jit(solution)/shard_map/ppermute | solution.py:326

commit v7 on v6

--- a/solution.py
+++ b/solution.py
@@ -108,63 +108,75 @@
 
 
 PAIRS = [(r, c) for r in range(P_SIZE) for c in range(r, P_SIZE)]
+PIECES = 4 * P_SIZE
 CHUNKS = 2
 
 
 def mask_kernel(place_ref, arcs_ref, slab_ref, rows_ref, *refs):
-    chunks, work, sems = refs[:-2], refs[-2], refs[-1]
+    chunks, quarters, work = refs[:CHUNKS], refs[CHUNKS:-1], refs[-1]
     top = slab_ref.shape[0]
-    arcs = arcs_ref.shape[0]
-    copies = [pltpu.make_async_copy(slab_ref, work.at[pl.ds(0, top)], sems.at[arcs])]
-    for a in range(arcs):
-        part = pl.ds(a * ARC_ROWS, ARC_ROWS)
-        spot = pl.ds(top + a * ARC_ROWS, ARC_ROWS)
-        copies.append(pltpu.make_async_copy(rows_ref.at[part], work.at[spot], sems.at[a]))
-    for copy in copies:
-        copy.start()
-    for copy in copies:
-        copy.wait()
-    for a in range(arcs):
+    work[:top, :] = slab_ref[...]
+    for a in range(arcs_ref.shape[0]):
         live = arcs_ref[a, 0].astype(jnp.float32)
-        spot = pl.ds(top + a * ARC_ROWS, ARC_ROWS)
-        work[spot, :] = work[spot, :] * live
+        at = a * ARC_ROWS
+        work[top + at : top + at + ARC_ROWS, :] = rows_ref[at : at + ARC_ROWS, :] * live
     count = chunks[0].shape[0]
-    if len(chunks) > CHUNKS:
-        first = jnp.where(place_ref[4] == 0, 0, CHUNKS * count)
-    else:
-        first = 0
     for s, chunk in enumerate(chunks):
-        start = first + s * count if s < CHUNKS else CHUNKS * count - first + (s - CHUNKS) * count
-        chunk[...] = work[pl.ds(pl.multiple_of(start, 16), count), :]
-
-
-def products_kernel(place_ref, *refs):
-    panels, right = refs[: P_SIZE * CHUNKS], refs[P_SIZE * CHUNKS : (P_SIZE + 1) * CHUNKS]
-    keep_ref, keep_cross_ref, send_ref, work = refs[(P_SIZE + 1) * CHUNKS :]
-    side, own = place_ref[0], place_ref[2]
+        chunk[...] = work[s * count : (s + 1) * count, :]
+    count = quarters[0].shape[0]
+    for t, quarter in enumerate(quarters):
+        start = pl.multiple_of((place_ref[4] ^ t) * count, 16)
+        quarter[...] = work[pl.ds(start, count), :]
+
+
+def upper_products_kernel(n_blocks, place_ref, *refs):
+    blocks, (keep_ref, send_ref, columns, work) = refs[:n_blocks], refs[-4:]
+    side, place, low = place_ref[0], place_ref[1] * P_SIZE + place_ref[4], place_ref[4]
+    for t, block in enumerate(blocks):
+        columns[low ^ t] = block[...]
+    right = [right_parts(columns[c]) for c in range(P_SIZE)]
+    at = 0
+    for r in range(P_SIZE):
+        wide = jnp.concatenate(right[r:], axis=1)
+        product = parts_dot(left_parts(columns[r]), wide)
+        for c in range(P_SIZE - r):
+            work[at * B : (at + 1) * B, :] = product[:, c * B : (c + 1) * B]
+            at += 1
+    count = keep_ref.shape[1]
+    for t in range(PIECES // 2):
+        piece = place ^ t
+        here = pl.multiple_of((side * (PIECES // 2) + piece) * count, SUB)
+        there = pl.multiple_of(((1 - side) * (PIECES // 2) + piece) * count, SUB)
+        keep_ref[t] = work[pl.ds(here, count), :]
+        send_ref[t] = work[pl.ds(there, count), :]
+
+
+def cross_products_kernel(place_ref, *refs):
+    panel, columns = refs[:CHUNKS], refs[CHUNKS : (P_SIZE + 1) * CHUNKS]
+    _, keep_ref, send_ref, work = refs[(P_SIZE + 1) * CHUNKS :]
+    side, low = place_ref[0], place_ref[4]
 
     def whole(chunks):
         return jnp.concatenate([chunk[...] for chunk in chunks], axis=0)
 
-    both = jnp.concatenate(
-        [right_parts(whole(panels[:CHUNKS])), right_parts(whole(right))], axis=1
-    )
+    left = left_parts(whole(panel))
     for t in range(P_SIZE):
-        left = left_parts(whole(panels[t * CHUNKS : (t + 1) * CHUNKS]))
-        product = parts_dot(left, both)
-        work[0, own ^ t] = product[:, :B]
-        work[1, own ^ t] = product[:, B:]
+        right = right_parts(whole(columns[t * CHUNKS : (t + 1) * CHUNKS]))
+        work[low ^ t] = parts_dot(left, right)
     for h in range(2):
-        keep_ref[h] = work[0, 2 * h + side]
-        keep_cross_ref[h] = work[1, 2 * h + side]
-        for k in range(2):
-            send_ref[k, h] = work[k, 2 * h + 1 - side]
-
-
-def pick_kernel(k, place_ref, keep_ref, got_ref, _, own_ref, other_ref):
+        keep_ref[h] = work[2 * h + side]
+        send_ref[h] = work[2 * h + 1 - side]
+
+
+def pick_kernel(place_ref, keep_ref, got_ref, _, own_ref, other_ref):
     high = place_ref[1]
-    own_ref[...] = keep_ref[high] + got_ref[k, high]
-    other_ref[...] = keep_ref[1 - high] + got_ref[k, 1 - high]
+    own_ref[...] = keep_ref[high] + got_ref[high]
+    other_ref[...] = keep_ref[1 - high] + got_ref[1 - high]
+
+
+def pass_kernel(*refs):
+    for value_ref, out_ref in zip(refs, refs[-CHUNKS:]):
+        out_ref[...] = value_ref[...]
 
 
 def stack_kernel(first_ref, second_ref, _, out_ref):
@@ -172,8 +184,8 @@
     out_ref[1] = second_ref[...]
 
 
-def add_kernel(left_ref, right_ref, after_ref, out_ref):
-    del after_ref
+def add_kernel(left_ref, right_ref, *refs):
+    out_ref = refs[-1]
     out_ref[...] = left_ref[...] + right_ref[...]
 
 
@@ -194,17 +206,27 @@
 
 
 def collect_kernel(place_ref, mine_ref, other_ref, gram_ref):
-    side, at = place_ref[0], place_ref[1] * P_SIZE + place_ref[2]
-    for i, (r, c) in enumerate(PAIRS):
-        spot = ((r // 2) * P_SIZE + c) ^ at
-
-        @pl.when(side == r % 2)
-        def _(i=i, spot=spot):
-            gram_ref[i] = mine_ref[spot]
-
-        @pl.when(side != r % 2)
-        def _(i=i, spot=spot):
-            gram_ref[i] = other_ref[spot]
+    side, high, low = place_ref[0], place_ref[1], place_ref[2]
+    at = high * P_SIZE + low
+    rows = mine_ref.shape[1]
+    for s in range(2):
+        for p in range(PIECES // 2):
+            start = ((s * PIECES) // 2 + p) * rows
+            end = start + rows
+            while start < end:
+                block, first = start // B, start % B
+                count = min(end - start, B - first)
+                skip = rows - (end - start)
+
+                @pl.when(side == s)
+                def _(block=block, first=first, count=count, skip=skip, p=p):
+                    gram_ref[block, first : first + count] = mine_ref[p ^ at, skip : skip + count]
+
+                @pl.when(side != s)
+                def _(block=block, first=first, count=count, skip=skip, p=p):
+                    gram_ref[block, first : first + count] = other_ref[p ^ at, skip : skip + count]
+
+                start += count
 
 
 def factor_step_kernel(n, gram_ref, *rest):
@@ -308,6 +330,9 @@
 
 def from_first(value, n_hi):
     at = lax.axis_index("hi")
+    if n_hi == 2:
+        got = lax.ppermute(value, ("hi", "lo"), [(i, i ^ 6) for i in range(P_SIZE)])
+        return jnp.where(at == 0, value, got)
     have = 1
     while have < n_hi:
         more = min(have, n_hi - have)
@@ -317,24 +342,42 @@
     return value
 
 
-def exchange(value, high_bits, low_bits):
-    bits = low_bits * 2 + high_bits
-    return lax.ppermute(value, ("lo", "rh"), [(i, i ^ bits) for i in range(2 * P_SIZE)])
-
-
-def swap(value, axis="rl"):
-    return lax.ppermute(value, axis, [(0, 1), (1, 0)])
-
-
-def other_group(value):
-    return lax.ppermute(value, ("hi", "lo"), [(i, i ^ 6) for i in range(2 * P_SIZE)])
-
-
-def spread(piece):
+def exchange(value, high_bits, low_bits, groups):
+    count, bits = 2 * P_SIZE, low_bits * 2 + high_bits
+    pairs = [(g * count + i, g * count + (i ^ bits)) for g in groups for i in range(count)]
+    return lax.ppermute(value, ("hi", "lo", "rh"), pairs)
+
+
+def swap(value):
+    return lax.ppermute(value, "rl", [(0, 1), (1, 0)])
+
+
+def transposed(value, flip, groups):
+    rows = P_SIZE
+    pairs = []
+    for g in groups:
+        for low in range(P_SIZE):
+            for r in range(rows):
+                source = (g * P_SIZE + low) * rows + r
+                pairs.append((source, (g * P_SIZE + r) * rows + (low ^ flip)))
+    return lax.ppermute(value, ("hi", "lo", "rh", "rl"), pairs)
+
+
+def collected(parts, groups):
+    got = [parts[0]]
+    for t in range(1, PIECES // 2):
+        got.append(exchange(parts[t], t // P_SIZE, t % P_SIZE, groups))
+    return functools.reduce(jnp.add, got)
+
+
+def spread(piece, groups):
+    def go(value, bits):
+        return exchange(value, *bits, groups)
+
     y, z, x = (0, 1), (0, 2), (1, 0)
-    by_z, by_y, by_x = exchange(piece, *z), exchange(piece, *y), exchange(piece, *x)
-    by_zy, by_yx, by_xz = exchange(by_z, *y), exchange(by_y, *x), exchange(by_x, *z)
-    by_zyx = exchange(by_zy, *x)
+    by_z, by_y, by_x = go(piece, z), go(piece, y), go(piece, x)
+    by_zy, by_yx, by_xz = go(by_z, y), go(by_y, x), go(by_x, z)
+    by_zyx = go(by_zy, x)
     return jnp.stack([piece, by_y, by_z, by_zy, by_x, by_yx, by_xz, by_zyx])
 
 
@@ -344,73 +387,73 @@
     high_row, side = lax.axis_index("rh"), lax.axis_index("rl")
     col_index = group * P_SIZE + low
     columns = arc_rows.shape[1]
-    in_two = n_hi == 2
-    panel = low ^ (2 * group) if in_two else low
-    place = jnp.stack([side, high_row, panel, col_index, group]).astype(jnp.int32)
+    flip = 2 if n_hi == 2 else 0
+    panel = jnp.where(group == 0, low, low ^ flip)
+    place = jnp.stack([side, high_row, panel, col_index, low]).astype(jnp.int32)
+    first, others, every = range(1), range(1, n_hi), range(n_hi)
     total = r_slab.shape[0] + arc_rows.shape[0]
-    parts = 2 * CHUNKS if in_two else CHUNKS
-    chunks = on_chip(
+    share = (total // P_SIZE, columns)
+    pieces = on_chip(
         mask_kernel,
-        [(total // parts, columns)] * parts,
+        [(total // CHUNKS, columns)] * CHUNKS + [share] * P_SIZE,
         "mask",
         place,
         arc_blocks,
+        r_slab,
+        arc_rows,
         scalars=2,
+        scratch=[pltpu.VMEM((total, columns), jnp.float32)],
+    )
+    chunks, quarters = pieces[:CHUNKS], pieces[CHUNKS:]
+    blocks = [quarters[0]] + [exchange(quarters[t], 0, t, first) for t in range(1, P_SIZE)]
+
+    panels = [from_first(chunk, n_hi) for chunk in chunks]
+    chunks = on_chip(
+        pass_kernel, [chunk.shape for chunk in chunks], "chunks", *chunks, after=blocks[1:]
+    )
+    y, z = (0, 1), (0, 2)
+    by_y, by_z = exchange(chunks[0], *y, others), exchange(chunks[1], *z, others)
+    group_columns = [
+        chunks[0],
+        chunks[1],
+        by_y,
+        exchange(chunks[1], *y, others),
+        exchange(chunks[0], *z, others),
+        by_z,
+        exchange(by_y, *z, others),
+        exchange(by_z, *y, others),
+    ]
+
+    half = (PIECES // 2, len(PAIRS) * B // PIECES, B)
+    keep, send = on_chip(
+        functools.partial(upper_products_kernel, P_SIZE),
+        [half, half],
+        "upper_products",
+        place,
+        *blocks,
+        scalars=1,
+        after=group_columns[2:] + panels,
         scratch=[
-            pltpu.VMEM((total, columns), jnp.float32),
-            pltpu.SemaphoreType.DMA((arc_blocks.shape[0] + 1,)),
+            pltpu.VMEM((P_SIZE, *share), jnp.float32),
+            pltpu.VMEM((len(PAIRS) * B, B), jnp.float32),
         ],
-        outside=(r_slab, arc_rows),
-    )
-    if in_two:
-        kept, got = chunks[:CHUNKS], [other_group(chunk) for chunk in chunks[CHUNKS:]]
-        first = [jnp.where(group == 0, k, g) for k, g in zip(kept, got)]
-        right = [jnp.where(group == 0, g, k) for k, g in zip(kept, got)]
-    else:
-        first, right = [from_first(chunk, n_hi) for chunk in chunks], chunks
-    y, z = (0, 1), (0, 2)
-    by_y, by_z = exchange(first[0], *y), exchange(first[1], *z)
-    panels = [
-        first[0],
-        first[1],
-        by_y,
-        exchange(first[1], *y),
-        exchange(first[0], *z),
-        by_z,
-        exchange(by_y, *z),
-        exchange(by_z, *y),
-    ]
-
+    )
+    (summed,) = on_chip(add_kernel, [half], "add_pair", keep, swap(send))
+    piece = from_first(collected(summed, first), n_hi)
     pair, block = (2, B, B), (B, B)
-    keep, keep_cross, send = on_chip(
-        products_kernel,
-        [pair, pair, (2, *pair)],
-        "products",
+    keep_cross, send = on_chip(
+        cross_products_kernel,
+        [pair, pair],
+        "cross_products",
         place,
         *panels,
-        *right,
+        *group_columns,
         scalars=1,
-        scratch=[pltpu.VMEM((2, P_SIZE, B, B), jnp.float32)],
-    )
-    got = swap(send)
-
-    def picked(k, kept, after):
-        return on_chip(
-            functools.partial(pick_kernel, k),
-            [block, block],
-            "pick",
-            place,
-            kept,
-            got,
-            scalars=1,
-            after=(after,),
-        )
-
-    mine, other = picked(0, keep, send)
-    piece = mine + exchange(other, 1, 0)
-    if in_two:
-        piece = piece + other_group(piece)
-    pieces = spread(piece)
+        scratch=[pltpu.VMEM((P_SIZE, B, B), jnp.float32)],
+        after=(piece,),
+    )
+    got_cross = swap(send)
+    pieces = spread(piece, every)
     (gram,) = on_chip(
         collect_kernel,
         [(len(PAIRS), B, B)],
@@ -426,11 +469,21 @@
         return total
 
     rows, inverses = factor(gram)
-    mine, other = picked(1, keep_cross, gram)
-    mine = added(mine, exchange(other, 1, 0), rows[0])
-    if in_two:
-        mine = added(mine, other_group(mine), rows[1])
-    (own,) = on_chip(stack_kernel, [pair], "stack", mine, exchange(mine, 1, 0), after=(rows[2],))
+    mine, other = on_chip(
+        pick_kernel,
+        [block, block],
+        "pick",
+        place,
+        keep_cross,
+        got_cross,
+        scalars=1,
+        after=(gram,),
+    )
+    mine = added(mine, exchange(other, 1, 0, others), rows[0])
+    mine = transposed(mine, flip, others)
+    mine, _ = on_chip(pass_kernel, [block, block], "row_block", mine, mine, after=(rows[1],))
+    by_x = exchange(mine, 1, 0, others)
+    (own,) = on_chip(stack_kernel, [pair], "stack", mine, by_x, after=(rows[2],))
     (result,) = on_chip(
         solve_kernel,
         [(B, columns)],

time: 155 us -> 179 us (1.15)
  the two profiles are of different devices: /device:TPU:9 before, /device:TPU:17 now
where the time goes in v7:
time: 179 us; the launch traced here: 178 us
  waiting for transfers between devices  85.2 us (48%)
  starting transfers between devices  48.9 us (27%)
  Pallas kernels  40.1 us (22%)
  local copies, waits for them, and re-layouts  3.15 us (2%)
    ppermute x3, waiting for transfers between devices, from_first(): got = lax.ppermute(value, ('hi', 'lo'), [(i, i ^ 6) for i in range(P_SIZE)])  54.8 us
    pallas_call x15, Pallas kernels, on_chip(): pl.pallas_call(kernel, out_shape=[jax.ShapeDtypeStruct(shape, jnp.float32...  40.1 us
    ppermute x25, starting transfers between devices, exchange(): return lax.ppermute(value, ('hi', 'lo', 'rh'), pairs)  30.5 us
    ppermute x25, waiting for transfers between devices, exchange(): return lax.ppermute(value, ('hi', 'lo', 'rh'), pairs)  26.8 us
    ppermute x4, starting transfers between devices, swap(): return lax.ppermute(value, 'rl', [(0, 1), (1, 0)])  10.8 us
    ppermute x3, starting transfers between devices, from_first(): got = lax.ppermute(value, ('hi', 'lo'), [(i, i ^ 6) for i in range(P_SIZE)])  3.88 us
    ppermute x1, starting transfers between devices, transposed(): return lax.ppermute(value, ('hi', 'lo', 'rh', 'rl'), pairs)  3.67 us
    ppermute x4, waiting for transfers between devices, swap(): return lax.ppermute(value, 'rl', [(0, 1), (1, 0)])  3.67 us
  transfers between devices with their start and end apart: 33, of which 13 were waited for; matrix products, arithmetic and copies ran while one was open for 0% of the time, Pallas kernels for 18%

profile of v7, /device:TPU:17, one launch (start us, length us, event | category | flops | bytes accessed | tf_op | source)
XLA Modules:
  0.0 178.1 jit_solution(12776117949147234439)
XLA Ops:
  0.0 0.7 copy.4.arcs_ref
  0.8 1.2 copy-done
  2.0 0.9 copy-done.1
  3.0 0.9 mask.1
  3.9 0.7 collective-permute-start
  4.5 0.7 collective-permute-start.1
  5.2 0.7 collective-permute-start.2
  5.9 1.3 collective-permute-start.9
  7.3 3.1 %collective-permute-start.3 = (f32[640,256]{1,0:T(8,128)S(1)}, f32[640,256]{1,0:T(8,128)S(1)}, u32[]{:S(2)}, u32[]{:S(2)}) collective-permute-start(f32[640,256]{1,0:T(8,128)S(1)} %get-tuple-element.35.refs_2_), channel_id=1, source_target_pairs={{16,20},{18,22},{20,16},{22,18},{24,28},{26,30},{28,24},{30,26},{1... | collective-permute-start | bytes 1966088 | tf_op jit(solution)/shard_map/ppermute | solution.py:348
  10.5 3.2 %collective-permute-start.6 = (f32[640,256]{1,0:T(8,128)S(1)}, f32[640,256]{1,0:T(8,128)S(1)}, u32[]{:S(2)}, u32[]{:S(2)}) collective-permute-start(f32[640,256]{1,0:T(8,128)S(1)} %get-tuple-element.36.refs_3_), channel_id=1, source_target_pairs={{16,24},{18,26},{20,28},{22,30},{24,16},{26,18},{28,20},{30,22},{1... | collective-permute-start | bytes 1966088 | tf_op jit(solution)/shard_map/ppermute | solution.py:348
  13.7 1.3 collective-permute-start.10
  15.0 2.1 %collective-permute-start.5 = (f32[640,256]{1,0:T(8,128)S(1)}, f32[640,256]{1,0:T(8,128)S(1)}, u32[]{:S(2)}, u32[]{:S(2)}) collective-permute-start(f32[640,256]{1,0:T(8,128)S(1)} %get-tuple-element.35.refs_2_), channel_id=1, source_target_pairs={{16,24},{18,26},{20,28},{22,30},{24,16},{26,18},{28,20},{30,22},{1... | collective-permute-start | bytes 1966088 | tf_op jit(solution)/shard_map/ppermute | solution.py:348
  17.1 38.2 %collective-permute-done.9 = f32[640,256]{1,0:T(8,128)S(1)} collective-permute-done((f32[640,256]{1,0:T(8,128)S(1)}, f32[640,256]{1,0:T(8,128)S(1)}, u32[]{:S(2)}, u32[]{:S(2)}) %collective-permute-start.9) | collective-permute-done | bytes 655392 | tf_op jit(solution)/shard_map/ppermute | solution.py:334
  55.3 3.1 %collective-permute-start.4 = (f32[640,256]{1,0:T(8,128)S(1)}, f32[640,256]{1,0:T(8,128)S(1)}, u32[]{:S(2)}, u32[]{:S(2)}) collective-permute-start(f32[640,256]{1,0:T(8,128)S(1)} %get-tuple-element.36.refs_3_), channel_id=1, source_target_pairs={{16,20},{18,22},{20,16},{22,18},{24,28},{26,30},{28,24},{30,26},{1... | collective-permute-start | bytes 1966088 | tf_op jit(solution)/shard_map/ppermute | solution.py:348
  58.5 1.9 %collective-permute-start.7 = (f32[640,256]{1,0:T(8,128)S(1)}, f32[640,256]{1,0:T(8,128)S(1)}, u32[]{:S(2)}, u32[]{:S(2)}) collective-permute-start(f32[640,256]{1,0:T(8,128)S(1)} %collective-permute-done.3.refs_4_), channel_id=1, source_target_pairs={{16,24},{18,26},{20,28},{22,30},{24,16},{26,18},{28,20},{30,22},{1... | collective-permute-start | bytes 1966088 | tf_op jit(solution)/shard_map/ppermute | solution.py:348
  60.4 2.1 %collective-permute-start.8 = (f32[640,256]{1,0:T(8,128)S(1)}, f32[640,256]{1,0:T(8,128)S(1)}, u32[]{:S(2)}, u32[]{:S(2)}) collective-permute-start(f32[640,256]{1,0:T(8,128)S(1)} %collective-permute-done.6.refs_7_), channel_id=1, source_target_pairs={{16,20},{18,22},{20,16},{22,18},{24,28},{26,30},{28,24},{30,26},{1... | collective-permute-start | bytes 1966088 | tf_op jit(solution)/shard_map/ppermute | solution.py:348
  62.6 6.7 %collective-permute-done.10 = f32[640,256]{1,0:T(8,128)S(1)} collective-permute-done((f32[640,256]{1,0:T(8,128)S(1)}, f32[640,256]{1,0:T(8,128)S(1)}, u32[]{:S(2)}, u32[]{:S(2)}) %collective-permute-start.10) | collective-permute-done | bytes 655392 | tf_op jit(solution)/shard_map/ppermute | solution.py:334
  69.5 13.5 %collective-permute-done.7.refs_8_ = f32[640,256]{1,0:T(8,128)S(1)} collective-permute-done((f32[640,256]{1,0:T(8,128)S(1)}, f32[640,256]{1,0:T(8,128)S(1)}, u32[]{:S(2)}, u32[]{:S(2)}) %collective-permute-start.7) | collective-permute-done | bytes 655392 | tf_op jit(solution)/shard_map/ppermute | solution.py:348
  83.5 2.3 %upper_products.1 = (f32[8,160,256]{2,1,0:T(8,128)S(1)}, f32[8,160,256]{2,1,0:T(8,128)S(1)}) custom-call(s32[5]{0:T(128)S(1)} %stack.51.place_ref, f32[320,256]{1,0:T(8,128)S(1)} %get-tuple-element.29.refs_0_, f32[320,256]{1,0:T(8,128)S(1)} %collective-permute-done.refs_2_.refs_1_, f32[320,256]{1,0:T(8,128)S(1)} %collective-permute-done.1.refs_3_.refs_2_, ...), custom_call_target="tpu_custom_call" | custom-call | tf_op jit(solution)/shard_map/upper_products/pallas_call | solution.py:193
  85.9 4.9 %collective-permute-start.11 = (f32[8,160,256]{2,1,0:T(8,128)S(1)}, f32[8,160,256]{2,1,0:T(8,128)S(1)}, u32[]{:S(2)}, u32[]{:S(2)}) collective-permute-start(f32[8,160,256]{2,1,0:T(8,128)S(1)} %get-tuple-element.38), channel_id=1, source_target_pairs={{0,1},{1,0},{2,3},{3,2},{4,5},{5,4},{6,7},{7,6},{8,9},{9,8},{10,11... | collective-permute-start | bytes 3932168 | tf_op jit(solution)/shard_map/ppermute | solution.py:352
  90.8 2.7 %collective-permute-done.11.right_ref = f32[8,160,256]{2,1,0:T(8,128)S(1)} collective-permute-done((f32[8,160,256]{2,1,0:T(8,128)S(1)}, f32[8,160,256]{2,1,0:T(8,128)S(1)}, u32[]{:S(2)}, u32[]{:S(2)}) %collective-permute-start.11) | collective-permute-done | bytes 1310752 | tf_op jit(solution)/shard_map/ppermute | solution.py:352
  93.7 0.7 collective-permute-start.12
  94.4 0.7 collective-permute-start.18
  95.7 0.7 collective-permute-start.16
  97.1 0.7 collective-permute-start.14
  97.8 0.7 collective-permute-start.13
  98.6 1.3 collective-permute-start.19
  99.9 9.8 %collective-permute-done.19 = f32[160,256]{1,0:T(8,128)S(1)} collective-permute-done((f32[160,256]{1,0:T(8,128)S(1)}, f32[160,256]{1,0:T(8,128)S(1)}, u32[]{:S(2)}, u32[]{:S(2)}) %collective-permute-start.19) | collective-permute-done | bytes 163872 | tf_op jit(solution)/shard_map/ppermute | solution.py:334
  109.8 1.2 collective-permute-start.23
  111.6 2.5 %collective-permute-done.23 = f32[160,256]{1,0:T(8,128)S(1)} collective-permute-done((f32[160,256]{1,0:T(8,128)S(1)}, f32[160,256]{1,0:T(8,128)S(1)}, u32[]{:S(2)}, u32[]{:S(2)}) %collective-permute-start.23) | collective-permute-done | bytes 163872 | tf_op jit(solution)/shard_map/ppermute | solution.py:348
  114.0 1.5 collective-permute-done.21
  116.0 0.9 collective-permute-start.24
  117.0 3.0 %collective-permute-done.22 = f32[160,256]{1,0:T(8,128)S(1)} collective-permute-done((f32[160,256]{1,0:T(8,128)S(1)}, f32[160,256]{1,0:T(8,128)S(1)}, u32[]{:S(2)}, u32[]{:S(2)}) %collective-permute-start.22) | collective-permute-done | bytes 163872 | tf_op jit(solution)/shard_map/ppermute | solution.py:348
  120.5 5.1 %collective-permute-done.26 = f32[160,256]{1,0:T(8,128)S(1)} collective-permute-done((f32[160,256]{1,0:T(8,128)S(1)}, f32[160,256]{1,0:T(8,128)S(1)}, u32[]{:S(2)}, u32[]{:S(2)}) %collective-permute-start.26) | collective-permute-done | bytes 163872 | tf_op jit(solution)/shard_map/ppermute | solution.py:348
  125.6 4.5 %collective-permute-start.27 = (f32[8,160,256]{2,1,0:T(8,128)S(1)}, f32[8,160,256]{2,1,0:T(8,128)S(1)}, u32[]{:S(2)}, u32[]{:S(2)}) collective-permute-start(f32[8,160,256]{2,1,0:T(8,128)S(1)} %bitcast_dynamic-update-slice_fusion.mine_ref), channel_id=1, source_target_pairs={{0,1},{1,0},{2,3},{3,2},{4,5},{5,4},{6,7},{7,6},{8,9},{9,8},{10,11... | collective-permute-start | bytes 3932168 | tf_op jit(solution)/shard_map/ppermute | solution.py:352
  130.1 3.1 %cross_products.1 = (f32[2,256,256]{2,1,0:T(8,128)S(1)}, f32[2,256,256]{2,1,0:T(8,128)S(1)}) custom-call(s32[5]{0:T(128)S(1)} %stack.51.place_ref, f32[640,256]{1,0:T(8,128)S(1)} %broadcast_select_fusion.1.refs_10_.refs_0_, f32[640,256]{1,0:T(8,128)S(1)} %broadcast_select_fusion.refs_11_.refs_1_, f32[640,256]{1,0:T(8,128)S(1)} %get-tuple-element.35.refs_2_, ...), custom_call_target="tpu_custom_call" | custom-call | tf_op jit(solution)/shard_map/cross_products/pallas_call | solution.py:193
  133.3 0.9 collect.1.gram_ref._.refs_7_
  134.1 1.0 collective-permute-done.28.got_ref
  135.7 2.1 %collective-permute-start.29 = (f32[256,256]{1,0:T(8,128)S(1)}, f32[256,256]{1,0:T(8,128)S(1)}, u32[]{:S(2)}, u32[]{:S(2)}) collective-permute-start(f32[256,256]{1,0:T(8,128)S(1)} %get-tuple-element.51), channel_id=1, source_target_pairs={{16,18},{18,16},{20,22},{22,20},{24,26},{26,24},{28,30},{30,28},{1... | collective-permute-start | bytes 786440 | tf_op jit(solution)/shard_map/ppermute | solution.py:348
  137.9 7.3 %factor_step.4 = (f32[256,768]{1,0:T(8,128)S(1)}, f32[256,256]{1,0:T(8,128)S(1)}, f32[6,256,256]{2,1,0:T(8,128)S(1)}) custom-call(f32[10,256,256]{2,1,0:T(8,128)S(1)} %collect.1.gram_ref._.refs_7_), custom_call_target="tpu_custom_call" | custom-call | tf_op jit(solution)/shard_map/factor_step/pallas_call | solution.py:193
  145.4 3.7 %collective-permute-start.30 = (f32[256,256]{1,0:T(8,128)S(1)}, f32[256,256]{1,0:T(8,128)S(1)}, u32[]{:S(2)}, u32[]{:S(2)}) collective-permute-start(f32[256,256]{1,0:T(8,128)S(1)} %add.82), channel_id=1, source_target_pairs={{16,18},{17,22},{18,26},{19,30},{20,19},{21,23},{22,27},{23,31},{2... | collective-permute-start | bytes 786440 | tf_op jit(solution)/shard_map/ppermute | solution.py:363
  149.1 7.0 %factor_step.5 = (f32[256,512]{1,0:T(8,128)S(1)}, f32[256,256]{1,0:T(8,128)S(1)}, f32[3,256,256]{2,1,0:T(8,128)S(1)}) custom-call(f32[6,256,256]{2,1,0:T(8,128)S(1)} %get-tuple-element.40.gram_ref), custom_call_target="tpu_custom_call" | custom-call | tf_op jit(solution)/shard_map/factor_step/pallas_call | solution.py:193
  156.1 0.7 row_block.1
  156.9 2.8 %collective-permute-start.31 = (f32[256,256]{1,0:T(8,128)S(1)}, f32[256,256]{1,0:T(8,128)S(1)}, u32[]{:S(2)}, u32[]{:S(2)}) collective-permute-start(f32[256,256]{1,0:T(8,128)S(1)} %get-tuple-element.52.first_ref), channel_id=1, source_target_pairs={{16,18},{18,16},{20,22},{22,20},{24,26},{26,24},{28,30},{30,28},{1... | collective-permute-start | bytes 786440 | tf_op jit(solution)/shard_map/ppermute | solution.py:348
  159.7 6.7 %factor_step.6 = (f32[256,256]{1,0:T(8,128)S(1)}, f32[256,256]{1,0:T(8,128)S(1)}, f32[1,256,256]{2,1,0:T(8,128)S(1)}) custom-call(f32[3,256,256]{2,1,0:T(8,128)S(1)} %get-tuple-element.42.gram_ref), custom_call_target="tpu_custom_call" | custom-call | tf_op jit(solution)/shard_map/factor_step/pallas_call | solution.py:193
  166.5 1.3 collective-permute-start.32
  167.8 6.2 %factor_step.7.refs_6_ = f32[256,256]{1,0:T(8,128)S(1)} custom-call(f32[1,256,256]{2,1,0:T(8,128)S(1)} %get-tuple-element.47.gram_ref), custom_call_target="tpu_custom_call" | custom-call | tf_op jit(solution)/shard_map/factor_step/pallas_call | solution.py:193
  174.0 4.1 %solve.1 = f32[256,256]{1,0:T(8,128)} custom-call(s32[5]{0:T(128)S(1)} %stack.51.place_ref, f32[256,768]{1,0:T(8,128)S(1)} %get-tuple-element.39.refs_0_, f32[256,512]{1,0:T(8,128)S(1)} %get-tuple-element.41.refs_2_.refs_1_, f32[256,256]{1,0:T(8,128)S(1)} %get-tuple-element.43._.refs_2_, f32[256,256]{1,0:T(8,128)S(1)} %get-tuple-element.44.refs_3_, ...), custom_call_target="tpu_custom_call" | custom-call | tf_op jit(solution)/shard_map/solve/pallas_call | solution.py:193
  (51 shorter events, 5.3 us)
Async XLA Ops:
  0.8 1.2 copy-start
  2.0 0.9 copy-start.1
  3.9 3.4 %collective-permute-start = (f32[320,256]{1,0:T(8,128)S(1)}, f32[320,256]{1,0:T(8,128)S(1)}, u32[]{:S(2)}, u32[]{:S(2)}) collective-permute-start(f32[320,256]{1,0:T(8,128)S(1)} %get-tuple-element.30), channel_id=1, source_target_pairs={{0,4},{2,6},{4,0},{6,2},{8,12},{10,14},{12,8},{14,10},{1,5},{3,7},... | collective-permute-start | bytes 983048 | tf_op jit(solution)/shard_map/ppermute | solution.py:348
  4.5 2.7 %collective-permute-start.1 = (f32[320,256]{1,0:T(8,128)S(1)}, f32[320,256]{1,0:T(8,128)S(1)}, u32[]{:S(2)}, u32[]{:S(2)}) collective-permute-start(f32[320,256]{1,0:T(8,128)S(1)} %get-tuple-element.31), channel_id=1, source_target_pairs={{0,8},{2,10},{4,12},{6,14},{8,0},{10,2},{12,4},{14,6},{1,9},{3,11}... | collective-permute-start | bytes 983048 | tf_op jit(solution)/shard_map/ppermute | solution.py:348
  5.2 2.0 %collective-permute-start.2 = (f32[320,256]{1,0:T(8,128)S(1)}, f32[320,256]{1,0:T(8,128)S(1)}, u32[]{:S(2)}, u32[]{:S(2)}) collective-permute-start(f32[320,256]{1,0:T(8,128)S(1)} %get-tuple-element.32), channel_id=1, source_target_pairs={{0,12},{2,14},{4,8},{6,10},{8,4},{10,6},{12,0},{14,2},{1,13},{3,15... | collective-permute-start | bytes 983048 | tf_op jit(solution)/shard_map/ppermute | solution.py:348
  5.9 49.4 %collective-permute-start.9 = (f32[640,256]{1,0:T(8,128)S(1)}, f32[640,256]{1,0:T(8,128)S(1)}, u32[]{:S(2)}, u32[]{:S(2)}) collective-permute-start(f32[640,256]{1,0:T(8,128)S(1)} %get-tuple-element.33.refs_0_), channel_id=1, source_target_pairs={{0,24},{4,28},{8,16},{12,20},{1,25},{5,29},{9,17},{13,21},{2,26},{... | collective-permute-start | bytes 1966088 | tf_op jit(solution)/shard_map/ppermute | solution.py:334
  7.3 51.1 %collective-permute-start.3 = (f32[640,256]{1,0:T(8,128)S(1)}, f32[640,256]{1,0:T(8,128)S(1)}, u32[]{:S(2)}, u32[]{:S(2)}) collective-permute-start(f32[640,256]{1,0:T(8,128)S(1)} %get-tuple-element.35.refs_2_), channel_id=1, source_target_pairs={{16,20},{18,22},{20,16},{22,18},{24,28},{26,30},{28,24},{30,26},{1... | collective-permute-start | bytes 1966088 | tf_op jit(solution)/shard_map/ppermute | solution.py:348
  10.5 49.9 %collective-permute-start.6 = (f32[640,256]{1,0:T(8,128)S(1)}, f32[640,256]{1,0:T(8,128)S(1)}, u32[]{:S(2)}, u32[]{:S(2)}) collective-permute-start(f32[640,256]{1,0:T(8,128)S(1)} %get-tuple-element.36.refs_3_), channel_id=1, source_target_pairs={{16,24},{18,26},{20,28},{22,30},{24,16},{26,18},{28,20},{30,22},{1... | collective-permute-start | bytes 1966088 | tf_op jit(solution)/shard_map/ppermute | solution.py:348
  13.7 55.6 %collective-permute-start.10 = (f32[640,256]{1,0:T(8,128)S(1)}, f32[640,256]{1,0:T(8,128)S(1)}, u32[]{:S(2)}, u32[]{:S(2)}) collective-permute-start(f32[640,256]{1,0:T(8,128)S(1)} %get-tuple-element.34.refs_1_), channel_id=1, source_target_pairs={{0,24},{4,28},{8,16},{12,20},{1,25},{5,29},{9,17},{13,21},{2,26},{... | collective-permute-start | bytes 1966088 | tf_op jit(solution)/shard_map/ppermute | solution.py:334
  15.0 54.4 %collective-permute-start.5 = (f32[640,256]{1,0:T(8,128)S(1)}, f32[640,256]{1,0:T(8,128)S(1)}, u32[]{:S(2)}, u32[]{:S(2)}) collective-permute-start(f32[640,256]{1,0:T(8,128)S(1)} %get-tuple-element.35.refs_2_), channel_id=1, source_target_pairs={{16,24},{18,26},{20,28},{22,30},{24,16},{26,18},{28,20},{30,22},{1... | collective-permute-start | bytes 1966088 | tf_op jit(solution)/shard_map/ppermute | solution.py:348
  55.3 14.2 %collective-permute-start.4 = (f32[640,256]{1,0:T(8,128)S(1)}, f32[640,256]{1,0:T(8,128)S(1)}, u32[]{:S(2)}, u32[]{:S(2)}) collective-permute-start(f32[640,256]{1,0:T(8,128)S(1)} %get-tuple-element.36.refs_3_), channel_id=1, source_target_pairs={{16,20},{18,22},{20,16},{22,18},{24,28},{26,30},{28,24},{30,26},{1... | collective-permute-start | bytes 1966088 | tf_op jit(solution)/shard_map/ppermute | solution.py:348
  58.5 24.5 %collective-permute-start.7 = (f32[640,256]{1,0:T(8,128)S(1)}, f32[640,256]{1,0:T(8,128)S(1)}, u32[]{:S(2)}, u32[]{:S(2)}) collective-permute-start(f32[640,256]{1,0:T(8,128)S(1)} %collective-permute-done.3.refs_4_), channel_id=1, source_target_pairs={{16,24},{18,26},{20,28},{22,30},{24,16},{26,18},{28,20},{30,22},{1... | collective-permute-start | bytes 1966088 | tf_op jit(solution)/shard_map/ppermute | solution.py:348
  60.4 23.1 %collective-permute-start.8 = (f32[640,256]{1,0:T(8,128)S(1)}, f32[640,256]{1,0:T(8,128)S(1)}, u32[]{:S(2)}, u32[]{:S(2)}) collective-permute-start(f32[640,256]{1,0:T(8,128)S(1)} %collective-permute-done.6.refs_7_), channel_id=1, source_target_pairs={{16,20},{18,22},{20,16},{22,18},{24,28},{26,30},{28,24},{30,26},{1... | collective-permute-start | bytes 1966088 | tf_op jit(solution)/shard_map/ppermute | solution.py:348
  85.9 7.6 %collective-permute-start.11 = (f32[8,160,256]{2,1,0:T(8,128)S(1)}, f32[8,160,256]{2,1,0:T(8,128)S(1)}, u32[]{:S(2)}, u32[]{:S(2)}) collective-permute-start(f32[8,160,256]{2,1,0:T(8,128)S(1)} %get-tuple-element.38), channel_id=1, source_target_pairs={{0,1},{1,0},{2,3},{3,2},{4,5},{5,4},{6,7},{7,6},{8,9},{9,8},{10,11... | collective-permute-start | bytes 3932168 | tf_op jit(solution)/shard_map/ppermute | solution.py:352
  93.7 3.4 %collective-permute-start.12 = (f32[160,256]{1,0:T(8,128)S(1)}, f32[160,256]{1,0:T(8,128)S(1)}, u32[]{:S(2)}, u32[]{:S(2)}) collective-permute-start(f32[160,256]{1,0:T(8,128)S(1)} %get-tuple-element.55), channel_id=1, source_target_pairs={{0,4},{2,6},{4,0},{6,2},{8,12},{10,14},{12,8},{14,10},{1,5},{3,7},... | collective-permute-start | bytes 491528 | tf_op jit(solution)/shard_map/ppermute | solution.py:348
  94.4 3.4 %collective-permute-start.18 = (f32[160,256]{1,0:T(8,128)S(1)}, f32[160,256]{1,0:T(8,128)S(1)}, u32[]{:S(2)}, u32[]{:S(2)}) collective-permute-start(f32[160,256]{1,0:T(8,128)S(1)} %get-tuple-element.56), channel_id=1, source_target_pairs={{0,14},{2,12},{4,10},{6,8},{8,6},{10,4},{12,2},{14,0},{1,15},{3,13... | collective-permute-start | bytes 491528 | tf_op jit(solution)/shard_map/ppermute | solution.py:348
  95.1 3.4 %collective-permute-start.17 = (f32[160,256]{1,0:T(8,128)S(1)}, f32[160,256]{1,0:T(8,128)S(1)}, u32[]{:S(2)}, u32[]{:S(2)}) collective-permute-start(f32[160,256]{1,0:T(8,128)S(1)} %get-tuple-element.57), channel_id=1, source_target_pairs={{0,10},{2,8},{4,14},{6,12},{8,2},{10,0},{12,6},{14,4},{1,11},{3,9}... | collective-permute-start | bytes 491528 | tf_op jit(solution)/shard_map/ppermute | solution.py:348
  95.7 2.8 %collective-permute-start.16 = (f32[160,256]{1,0:T(8,128)S(1)}, f32[160,256]{1,0:T(8,128)S(1)}, u32[]{:S(2)}, u32[]{:S(2)}) collective-permute-start(f32[160,256]{1,0:T(8,128)S(1)} %get-tuple-element.58), channel_id=1, source_target_pairs={{0,6},{2,4},{4,2},{6,0},{8,14},{10,12},{12,10},{14,8},{1,7},{3,5},... | collective-permute-start | bytes 491528 | tf_op jit(solution)/shard_map/ppermute | solution.py:348
  96.4 2.1 %collective-permute-start.15 = (f32[160,256]{1,0:T(8,128)S(1)}, f32[160,256]{1,0:T(8,128)S(1)}, u32[]{:S(2)}, u32[]{:S(2)}) collective-permute-start(f32[160,256]{1,0:T(8,128)S(1)} %get-tuple-element.59), channel_id=1, source_target_pairs={{0,2},{2,0},{4,6},{6,4},{8,10},{10,8},{12,14},{14,12},{1,3},{3,1},... | collective-permute-start | bytes 491528 | tf_op jit(solution)/shard_map/ppermute | solution.py:348
  97.1 1.4 collective-permute-start.14
  97.8 0.7 collective-permute-start.13
  98.6 11.1 %collective-permute-start.19 = (f32[160,256]{1,0:T(8,128)S(1)}, f32[160,256]{1,0:T(8,128)S(1)}, u32[]{:S(2)}, u32[]{:S(2)}) collective-permute-start(f32[160,256]{1,0:T(8,128)S(1)} %fusion.6), channel_id=1, source_target_pairs={{0,24},{4,28},{8,16},{12,20},{1,25},{5,29},{9,17},{13,21},{2,26},{... | collective-permute-start | bytes 491528 | tf_op jit(solution)/shard_map/ppermute | solution.py:334
  109.8 4.2 %collective-permute-start.23 = (f32[160,256]{1,0:T(8,128)S(1)}, f32[160,256]{1,0:T(8,128)S(1)}, u32[]{:S(2)}, u32[]{:S(2)}) collective-permute-start(f32[160,256]{1,0:T(8,128)S(1)} %get-tuple-element.54.refs_10_), channel_id=1, source_target_pairs={{0,2},{2,0},{4,6},{6,4},{8,10},{10,8},{12,14},{14,12},{16,18},{18,... | collective-permute-start | bytes 491528 | tf_op jit(solution)/shard_map/ppermute | solution.py:348
  111.0 4.5 %collective-permute-start.21 = (f32[160,256]{1,0:T(8,128)S(1)}, f32[160,256]{1,0:T(8,128)S(1)}, u32[]{:S(2)}, u32[]{:S(2)}) collective-permute-start(f32[160,256]{1,0:T(8,128)S(1)} %get-tuple-element.54.refs_10_), channel_id=1, source_target_pairs={{0,8},{2,10},{4,12},{6,14},{8,0},{10,2},{12,4},{14,6},{16,24},{18,... | collective-permute-start | bytes 491528 | tf_op jit(solution)/shard_map/ppermute | solution.py:348
  111.0 5.0 %collective-permute-start.20 = (f32[160,256]{1,0:T(8,128)S(1)}, f32[160,256]{1,0:T(8,128)S(1)}, u32[]{:S(2)}, u32[]{:S(2)}) collective-permute-start(f32[160,256]{1,0:T(8,128)S(1)} %get-tuple-element.54.refs_10_), channel_id=1, source_target_pairs={{0,4},{2,6},{4,0},{6,2},{8,12},{10,14},{12,8},{14,10},{16,20},{18,... | collective-permute-start | bytes 491528 | tf_op jit(solution)/shard_map/ppermute | solution.py:348
  114.0 6.5 %collective-permute-start.25 = (f32[160,256]{1,0:T(8,128)S(1)}, f32[160,256]{1,0:T(8,128)S(1)}, u32[]{:S(2)}, u32[]{:S(2)}) collective-permute-start(f32[160,256]{1,0:T(8,128)S(1)} %collective-permute-done.23), channel_id=1, source_target_pairs={{0,8},{2,10},{4,12},{6,14},{8,0},{10,2},{12,4},{14,6},{16,24},{18,... | collective-permute-start | bytes 491528 | tf_op jit(solution)/shard_map/ppermute | solution.py:348
  115.5 4.5 %collective-permute-start.22 = (f32[160,256]{1,0:T(8,128)S(1)}, f32[160,256]{1,0:T(8,128)S(1)}, u32[]{:S(2)}, u32[]{:S(2)}) collective-permute-start(f32[160,256]{1,0:T(8,128)S(1)} %collective-permute-done.21), channel_id=1, source_target_pairs={{0,4},{2,6},{4,0},{6,2},{8,12},{10,14},{12,8},{14,10},{16,20},{18,... | collective-permute-start | bytes 491528 | tf_op jit(solution)/shard_map/ppermute | solution.py:348
  116.0 4.5 %collective-permute-start.24 = (f32[160,256]{1,0:T(8,128)S(1)}, f32[160,256]{1,0:T(8,128)S(1)}, u32[]{:S(2)}, u32[]{:S(2)}) collective-permute-start(f32[160,256]{1,0:T(8,128)S(1)} %collective-permute-done.20), channel_id=1, source_target_pairs={{0,2},{2,0},{4,6},{6,4},{8,10},{10,8},{12,14},{14,12},{16,18},{18,... | collective-permute-start | bytes 491528 | tf_op jit(solution)/shard_map/ppermute | solution.py:348
  120.0 5.6 %collective-permute-start.26 = (f32[160,256]{1,0:T(8,128)S(1)}, f32[160,256]{1,0:T(8,128)S(1)}, u32[]{:S(2)}, u32[]{:S(2)}) collective-permute-start(f32[160,256]{1,0:T(8,128)S(1)} %collective-permute-done.22), channel_id=1, source_target_pairs={{0,2},{2,0},{4,6},{6,4},{8,10},{10,8},{12,14},{14,12},{16,18},{18,... | collective-permute-start | bytes 491528 | tf_op jit(solution)/shard_map/ppermute | solution.py:348
  125.6 7.6 %collective-permute-start.27 = (f32[8,160,256]{2,1,0:T(8,128)S(1)}, f32[8,160,256]{2,1,0:T(8,128)S(1)}, u32[]{:S(2)}, u32[]{:S(2)}) collective-permute-start(f32[8,160,256]{2,1,0:T(8,128)S(1)} %bitcast_dynamic-update-slice_fusion.mine_ref), channel_id=1, source_target_pairs={{0,1},{1,0},{2,3},{3,2},{4,5},{5,4},{6,7},{7,6},{8,9},{9,8},{10,11... | collective-permute-start | bytes 3932168 | tf_op jit(solution)/shard_map/ppermute | solution.py:352
  133.2 2.0 %collective-permute-start.28 = (f32[2,256,256]{2,1,0:T(8,128)S(1)}, f32[2,256,256]{2,1,0:T(8,128)S(1)}, u32[]{:S(2)}, u32[]{:S(2)}) collective-permute-start(f32[2,256,256]{2,1,0:T(8,128)S(1)} %get-tuple-element.49), channel_id=1, source_target_pairs={{0,1},{1,0},{2,3},{3,2},{4,5},{5,4},{6,7},{7,6},{8,9},{9,8},{10,11... | collective-permute-start | bytes 1572872 | tf_op jit(solution)/shard_map/ppermute | solution.py:352
  135.7 9.7 %collective-permute-start.29 = (f32[256,256]{1,0:T(8,128)S(1)}, f32[256,256]{1,0:T(8,128)S(1)}, u32[]{:S(2)}, u32[]{:S(2)}) collective-permute-start(f32[256,256]{1,0:T(8,128)S(1)} %get-tuple-element.51), channel_id=1, source_target_pairs={{16,18},{18,16},{20,22},{22,20},{24,26},{26,24},{28,30},{30,28},{1... | collective-permute-start | bytes 786440 | tf_op jit(solution)/shard_map/ppermute | solution.py:348
  145.4 10.7 %collective-permute-start.30 = (f32[256,256]{1,0:T(8,128)S(1)}, f32[256,256]{1,0:T(8,128)S(1)}, u32[]{:S(2)}, u32[]{:S(2)}) collective-permute-start(f32[256,256]{1,0:T(8,128)S(1)} %add.82), channel_id=1, source_target_pairs={{16,18},{17,22},{18,26},{19,30},{20,19},{21,23},{22,27},{23,31},{2... | collective-permute-start | bytes 786440 | tf_op jit(solution)/shard_map/ppermute | solution.py:363
  156.9 9.5 %collective-permute-start.31 = (f32[256,256]{1,0:T(8,128)S(1)}, f32[256,256]{1,0:T(8,128)S(1)}, u32[]{:S(2)}, u32[]{:S(2)}) collective-permute-start(f32[256,256]{1,0:T(8,128)S(1)} %get-tuple-element.52.first_ref), channel_id=1, source_target_pairs={{16,18},{18,16},{20,22},{22,20},{24,26},{26,24},{28,30},{30,28},{1... | collective-permute-start | bytes 786440 | tf_op jit(solution)/shard_map/ppermute | solution.py:348
  166.5 7.6 %collective-permute-start.32 = (f32[2,256,256]{2,1,0:T(8,128)S(1)}, f32[2,256,256]{2,1,0:T(8,128)S(1)}, u32[]{:S(2)}, u32[]{:S(2)}) collective-permute-start(f32[2,256,256]{2,1,0:T(8,128)S(1)} %stack.61.refs_8_), channel_id=1, source_target_pairs={{0,1},{1,0},{2,3},{3,2},{4,5},{5,4},{6,7},{7,6},{8,9},{9,8},{10,11... | collective-permute-start | bytes 1572872 | tf_op jit(solution)/shard_map/ppermute | solution.py:352

commit v8 on v6

--- a/solution.py
+++ b/solution.py
@@ -112,22 +112,13 @@
 
 
 def mask_kernel(place_ref, arcs_ref, slab_ref, rows_ref, *refs):
-    chunks, work, sems = refs[:-2], refs[-2], refs[-1]
+    chunks, work = refs[:-1], refs[-1]
     top = slab_ref.shape[0]
-    arcs = arcs_ref.shape[0]
-    copies = [pltpu.make_async_copy(slab_ref, work.at[pl.ds(0, top)], sems.at[arcs])]
-    for a in range(arcs):
-        part = pl.ds(a * ARC_ROWS, ARC_ROWS)
-        spot = pl.ds(top + a * ARC_ROWS, ARC_ROWS)
-        copies.append(pltpu.make_async_copy(rows_ref.at[part], work.at[spot], sems.at[a]))
-    for copy in copies:
-        copy.start()
-    for copy in copies:
-        copy.wait()
-    for a in range(arcs):
+    work[:top, :] = slab_ref[...]
+    for a in range(arcs_ref.shape[0]):
         live = arcs_ref[a, 0].astype(jnp.float32)
-        spot = pl.ds(top + a * ARC_ROWS, ARC_ROWS)
-        work[spot, :] = work[spot, :] * live
+        at = a * ARC_ROWS
+        work[top + at : top + at + ARC_ROWS, :] = rows_ref[at : at + ARC_ROWS, :] * live
     count = chunks[0].shape[0]
     if len(chunks) > CHUNKS:
         first = jnp.where(place_ref[4] == 0, 0, CHUNKS * count)
@@ -138,9 +129,23 @@
         chunk[...] = work[pl.ds(pl.multiple_of(start, 16), count), :]
 
 
+def select_kernel(place_ref, kept_ref, got_ref, *refs):
+    panel_ref, right_ref = refs[-2:]
+
+    @pl.when(place_ref[4] == 0)
+    def _():
+        panel_ref[...] = kept_ref[...]
+        right_ref[...] = got_ref[...]
+
+    @pl.when(place_ref[4] != 0)
+    def _():
+        panel_ref[...] = got_ref[...]
+        right_ref[...] = kept_ref[...]
+
+
 def products_kernel(place_ref, *refs):
     panels, right = refs[: P_SIZE * CHUNKS], refs[P_SIZE * CHUNKS : (P_SIZE + 1) * CHUNKS]
-    keep_ref, keep_cross_ref, send_ref, work = refs[(P_SIZE + 1) * CHUNKS :]
+    keep_ref, keep_cross_ref, send_ref, upper, cross = refs[(P_SIZE + 1) * CHUNKS :]
     side, own = place_ref[0], place_ref[2]
 
     def whole(chunks):
@@ -152,19 +157,34 @@
     for t in range(P_SIZE):
         left = left_parts(whole(panels[t * CHUNKS : (t + 1) * CHUNKS]))
         product = parts_dot(left, both)
-        work[0, own ^ t] = product[:, :B]
-        work[1, own ^ t] = product[:, B:]
+        cross[own ^ t] = product[:, B:]
+        if t == 0:
+            upper[:B, :] = product[:, :B]
+            continue
+        at = B + (t - 1) * B // 2
+
+        @pl.when(own < (own ^ t))
+        def _(at=at, product=product):
+            upper[at : at + B // 2, :] = product[:, : B // 2].T
+
+        @pl.when(own > (own ^ t))
+        def _(at=at, product=product):
+            upper[at : at + B // 2, :] = product[B // 2 :, :B]
+
+    count = keep_ref.shape[1]
     for h in range(2):
-        keep_ref[h] = work[0, 2 * h + side]
-        keep_cross_ref[h] = work[1, 2 * h + side]
-        for k in range(2):
-            send_ref[k, h] = work[k, 2 * h + 1 - side]
-
-
-def pick_kernel(k, place_ref, keep_ref, got_ref, _, own_ref, other_ref):
+        here, there = 2 * h + side, 2 * h + 1 - side
+        keep_ref[h] = upper[pl.ds(pl.multiple_of(here * count, SUB), count), :]
+        keep_cross_ref[h] = cross[here]
+        send_ref[h, :count] = upper[pl.ds(pl.multiple_of(there * count, SUB), count), :]
+        send_ref[h, count:] = cross[there]
+
+
+def pick_kernel(first, place_ref, keep_ref, got_ref, _, own_ref, other_ref):
     high = place_ref[1]
-    own_ref[...] = keep_ref[high] + got_ref[k, high]
-    other_ref[...] = keep_ref[1 - high] + got_ref[k, 1 - high]
+    rows = pl.ds(first, own_ref.shape[0])
+    own_ref[...] = keep_ref[high] + got_ref[high, rows]
+    other_ref[...] = keep_ref[1 - high] + got_ref[1 - high, rows]
 
 
 def stack_kernel(first_ref, second_ref, _, out_ref):
@@ -195,16 +215,31 @@
 
 def collect_kernel(place_ref, mine_ref, other_ref, gram_ref):
     side, at = place_ref[0], place_ref[1] * P_SIZE + place_ref[2]
-    for i, (r, c) in enumerate(PAIRS):
-        spot = ((r // 2) * P_SIZE + c) ^ at
-
-        @pl.when(side == r % 2)
-        def _(i=i, spot=spot):
-            gram_ref[i] = mine_ref[spot]
-
-        @pl.when(side != r % 2)
-        def _(i=i, spot=spot):
-            gram_ref[i] = other_ref[spot]
+    count = mine_ref.shape[1]
+    for q in range(P_SIZE):
+        runs = [(q, q, 0, B)]
+        for t in range(1, P_SIZE):
+            j = q ^ t
+            runs.append((min(q, j), max(q, j), 0 if q < j else B // 2, B // 2))
+        done = 0
+        for r, c, first, size in runs:
+            block, start, end = PAIRS.index((r, c)), done, done + size
+            while start < end:
+                piece, skip = start // count, start % count
+                rows = min(end - start, count - skip)
+                spot = ((piece // 2) * P_SIZE + q) ^ at
+                into = slice(first + start - done, first + start - done + rows)
+
+                @pl.when(side == piece % 2)
+                def _(block=block, into=into, spot=spot, skip=skip, rows=rows):
+                    gram_ref[block, into] = mine_ref[spot, skip : skip + rows]
+
+                @pl.when(side != piece % 2)
+                def _(block=block, into=into, spot=spot, skip=skip, rows=rows):
+                    gram_ref[block, into] = other_ref[spot, skip : skip + rows]
+
+                start += rows
+            done = end
 
 
 def factor_step_kernel(n, gram_ref, *rest):
@@ -355,49 +390,58 @@
         "mask",
         place,
         arc_blocks,
+        r_slab,
+        arc_rows,
         scalars=2,
-        scratch=[
-            pltpu.VMEM((total, columns), jnp.float32),
-            pltpu.SemaphoreType.DMA((arc_blocks.shape[0] + 1,)),
-        ],
-        outside=(r_slab, arc_rows),
-    )
-    if in_two:
-        kept, got = chunks[:CHUNKS], [other_group(chunk) for chunk in chunks[CHUNKS:]]
-        first = [jnp.where(group == 0, k, g) for k, g in zip(kept, got)]
-        right = [jnp.where(group == 0, g, k) for k, g in zip(kept, got)]
-    else:
-        first, right = [from_first(chunk, n_hi) for chunk in chunks], chunks
+        scratch=[pltpu.VMEM((total, columns), jnp.float32)],
+    )
     y, z = (0, 1), (0, 2)
-    by_y, by_z = exchange(first[0], *y), exchange(first[1], *z)
-    panels = [
-        first[0],
-        first[1],
-        by_y,
-        exchange(first[1], *y),
-        exchange(first[0], *z),
-        by_z,
-        exchange(by_y, *z),
-        exchange(by_z, *y),
-    ]
+
+    def halves(k, after):
+        if not in_two:
+            return from_first(chunks[k], n_hi), chunks[k]
+        shape = chunks[k].shape
+        return on_chip(
+            select_kernel,
+            [shape, shape],
+            "select",
+            place,
+            chunks[k],
+            other_group(chunks[CHUNKS + k]),
+            scalars=1,
+            after=after,
+        )
+
+    first, first_right = halves(0, ())
+    first_y, first_z = exchange(first, *y), exchange(first, *z)
+    first_zy = exchange(first_y, *z)
+    second, second_right = halves(1, (first_z, first_zy))
+    second_y, second_z = exchange(second, *y), exchange(second, *z)
+    second_zy = exchange(second_z, *y)
+    panels = [first, second, first_y, second_y, first_z, second_z, first_zy, second_zy]
+    right = [first_right, second_right]
 
     pair, block = (2, B, B), (B, B)
+    count = len(PAIRS) * B // P_SIZE // P_SIZE
     keep, keep_cross, send = on_chip(
         products_kernel,
-        [pair, pair, (2, *pair)],
+        [(2, count, B), pair, (2, count + B, B)],
         "products",
         place,
         *panels,
         *right,
         scalars=1,
-        scratch=[pltpu.VMEM((2, P_SIZE, B, B), jnp.float32)],
+        scratch=[
+            pltpu.VMEM((P_SIZE * count, B), jnp.float32),
+            pltpu.VMEM((P_SIZE, B, B), jnp.float32),
+        ],
     )
     got = swap(send)
 
-    def picked(k, kept, after):
+    def picked(first, kept, after):
         return on_chip(
-            functools.partial(pick_kernel, k),
-            [block, block],
+            functools.partial(pick_kernel, first),
+            [kept.shape[1:]] * 2,
             "pick",
             place,
             kept,
@@ -426,7 +470,7 @@
         return total
 
     rows, inverses = factor(gram)
-    mine, other = picked(1, keep_cross, gram)
+    mine, other = picked(count, keep_cross, gram)
     mine = added(mine, exchange(other, 1, 0), rows[0])
     if in_two:
         mine = added(mine, other_group(mine), rows[1])

time: 155 us -> 145 us (0.935)
  waiting for transfers between devices: 86.9 us -> 68.9 us
  starting transfers between devices: 25.7 us -> 33.2 us
    ppermute x4, waiting for transfers between devices: 43.8 us -> 24.2 us  [other_group(): lax.ppermute(value, ('hi', 'lo'), [(i, i ^ 6) for i in range(2 * P_SIZE)])]
    ppermute x16, starting transfers between devices: 14.7 us -> 19.2 us  [exchange(): lax.ppermute(value, ('lo', 'rh'), [(i, i ^ bits) for i in range(2 * P_SIZ...]
    ppermute x3, starting transfers between devices: 7.12 us -> 10.4 us  [swap(): return lax.ppermute(value, axis, [(0, 1), (1, 0)])]
    ppermute x16, waiting for transfers between devices: 37 us -> 40 us  [exchange(): lax.ppermute(value, ('lo', 'rh'), [(i, i ^ bits) for i in range(2 * P_SIZ...]
    pallas_call x13 -> x15, Pallas kernels: 39.1 us -> 39.4 us  [on_chip(): pl.pallas_call(kernel, out_shape=[jax.ShapeDtypeStruct(shape, jnp.float32...]
  transfers between devices with their start and end apart: 23 -> 23, of which waited for: 14 -> 15; matrix products, arithmetic and copies ran while one was open for 0% -> 0% of each run, Pallas kernels for 18% -> 19%
where the time goes in v8:
time: 145 us
  waiting for transfers between devices  68.9 us (48%)
  Pallas kernels  39.4 us (27%)
  starting transfers between devices  33.2 us (23%)
  local copies, waits for them, and re-layouts  3.07 us (2%)
    ppermute x16, waiting for transfers between devices, exchange(): lax.ppermute(value, ('lo', 'rh'), [(i, i ^ bits) for i in range(2 * P_SIZ...  40 us
    pallas_call x15, Pallas kernels, on_chip(): pl.pallas_call(kernel, out_shape=[jax.ShapeDtypeStruct(shape, jnp.float32...  39.4 us
    ppermute x4, waiting for transfers between devices, other_group(): lax.ppermute(value, ('hi', 'lo'), [(i, i ^ 6) for i in range(2 * P_SIZE)])  24.2 us
    ppermute x16, starting transfers between devices, exchange(): lax.ppermute(value, ('lo', 'rh'), [(i, i ^ bits) for i in range(2 * P_SIZ...  19.2 us
    ppermute x3, starting transfers between devices, swap(): return lax.ppermute(value, axis, [(0, 1), (1, 0)])  10.4 us
    ppermute x3, waiting for transfers between devices, swap(): return lax.ppermute(value, axis, [(0, 1), (1, 0)])  4.67 us
    ppermute x4, starting transfers between devices, other_group(): lax.ppermute(value, ('hi', 'lo'), [(i, i ^ 6) for i in range(2 * P_SIZE)])  3.63 us
    unnamed x11, local copies, waits for them, and re-layouts  2.98 us
  transfers between devices with their start and end apart: 23, of which 15 were waited for; matrix products, arithmetic and copies ran while one was open for 0% of the time, Pallas kernels for 19%

profile of v8, /device:TPU:9, one launch (start us, length us, event | category | flops | bytes accessed | tf_op | source)
XLA Modules:
  0.0 144.9 jit_solution(17125761336619124561)
XLA Ops:
  0.0 0.7 copy.4.arcs_ref
  0.8 1.2 copy-done
  2.0 0.9 copy-done.1
  3.0 0.8 mask.1
  3.8 1.4 collective-permute-start
  5.1 14.5 %collective-permute-done.got_ref = f32[320,256]{1,0:T(8,128)S(1)} collective-permute-done((f32[320,256]{1,0:T(8,128)S(1)}, f32[320,256]{1,0:T(8,128)S(1)}, u32[]{:S(2)}, u32[]{:S(2)}) %collective-permute-start) | collective-permute-done | bytes 327712 | tf_op jit(solution)/shard_map/ppermute | solution.py:365
  19.6 0.6 select.2
  20.2 8.3 %collective-permute-start.3 = (f32[320,256]{1,0:T(8,128)S(1)}, f32[320,256]{1,0:T(8,128)S(1)}, u32[]{:S(2)}, u32[]{:S(2)}) collective-permute-start(f32[320,256]{1,0:T(8,128)S(1)} %get-tuple-element.31.refs_0_), channel_id=1, source_target_pairs={{0,4},{2,6},{4,0},{6,2},{8,12},{10,14},{12,8},{14,10},{1,5},{3,7},... | collective-permute-start | bytes 983048 | tf_op jit(solution)/shard_map/ppermute | solution.py:357
  28.6 6.2 %collective-permute-done.3.refs_2_ = f32[320,256]{1,0:T(8,128)S(1)} collective-permute-done((f32[320,256]{1,0:T(8,128)S(1)}, f32[320,256]{1,0:T(8,128)S(1)}, u32[]{:S(2)}, u32[]{:S(2)}) %collective-permute-start.3) | collective-permute-done | bytes 327712 | tf_op jit(solution)/shard_map/ppermute | solution.py:357
  34.7 1.4 collective-permute-done.1.got_ref
  36.1 7.3 %collective-permute-done.4.refs_1_.refs_6_ = f32[320,256]{1,0:T(8,128)S(1)} collective-permute-done((f32[320,256]{1,0:T(8,128)S(1)}, f32[320,256]{1,0:T(8,128)S(1)}, u32[]{:S(2)}, u32[]{:S(2)}) %collective-permute-start.4) | collective-permute-done | bytes 327712 | tf_op jit(solution)/shard_map/ppermute | solution.py:357
  43.5 0.6 select.3
  44.1 0.1 collective-permute-start.5
  44.3 6.7 %collective-permute-done.6.refs_5_ = f32[320,256]{1,0:T(8,128)S(1)} collective-permute-done((f32[320,256]{1,0:T(8,128)S(1)}, f32[320,256]{1,0:T(8,128)S(1)}, u32[]{:S(2)}, u32[]{:S(2)}) %collective-permute-start.6) | collective-permute-done | bytes 327712 | tf_op jit(solution)/shard_map/ppermute | solution.py:357
  51.0 6.2 %collective-permute-done.7.refs_7_ = f32[320,256]{1,0:T(8,128)S(1)} collective-permute-done((f32[320,256]{1,0:T(8,128)S(1)}, f32[320,256]{1,0:T(8,128)S(1)}, u32[]{:S(2)}, u32[]{:S(2)}) %collective-permute-start.7) | collective-permute-done | bytes 327712 | tf_op jit(solution)/shard_map/ppermute | solution.py:357
  57.2 3.6 %products.1 = (f32[2,160,256]{2,1,0:T(8,128)S(1)}, f32[2,256,256]{2,1,0:T(8,128)S(1)}, f32[2,416,256]{2,1,0:T(8,128)S(1)}) custom-call(s32[5]{0:T(128)S(1)} %stack.51.place_ref, f32[320,256]{1,0:T(8,128)S(1)} %get-tuple-element.31.refs_0_, f32[320,256]{1,0:T(8,128)S(1)} %get-tuple-element.34.refs_1_, f32[320,256]{1,0:T(8,128)S(1)} %collective-permute-done.3.refs_2_, ...), custom_call_target="tpu_custom_call" | custom-call | tf_op jit(solution)/shard_map/products/pallas_call | solution.py:201
  60.7 4.3 %collective-permute-start.8 = (f32[2,416,256]{2,1,0:T(8,128)S(1)}, f32[2,416,256]{2,1,0:T(8,128)S(1)}, u32[]{:S(2)}, u32[]{:S(2)}) collective-permute-start(f32[2,416,256]{2,1,0:T(8,128)S(1)} %get-tuple-element.38._), channel_id=1, source_target_pairs={{0,1},{1,0},{2,3},{3,2},{4,5},{5,4},{6,7},{7,6},{8,9},{9,8},{10,11... | collective-permute-start | bytes 2555912 | tf_op jit(solution)/shard_map/ppermute | solution.py:361
  65.0 2.0 %collective-permute-done.8.got_ref = f32[2,416,256]{2,1,0:T(8,128)S(1)} collective-permute-done((f32[2,416,256]{2,1,0:T(8,128)S(1)}, f32[2,416,256]{2,1,0:T(8,128)S(1)}, u32[]{:S(2)}, u32[]{:S(2)}) %collective-permute-start.8) | collective-permute-done | bytes 852000 | tf_op jit(solution)/shard_map/ppermute | solution.py:361
  67.0 0.6 pick.2
  67.6 1.3 collective-permute-start.9
  68.9 4.2 %collective-permute-done.9 = f32[160,256]{1,0:T(8,128)S(1)} collective-permute-done((f32[160,256]{1,0:T(8,128)S(1)}, f32[160,256]{1,0:T(8,128)S(1)}, u32[]{:S(2)}, u32[]{:S(2)}) %collective-permute-start.9) | collective-permute-done | bytes 163872 | tf_op jit(solution)/shard_map/ppermute | solution.py:357
  73.1 1.1 collective-permute-start.10
  74.2 3.4 %collective-permute-done.10 = f32[160,256]{1,0:T(8,128)S(1)} collective-permute-done((f32[160,256]{1,0:T(8,128)S(1)}, f32[160,256]{1,0:T(8,128)S(1)}, u32[]{:S(2)}, u32[]{:S(2)}) %collective-permute-start.10) | collective-permute-done | bytes 163872 | tf_op jit(solution)/shard_map/ppermute | solution.py:365
  77.7 3.5 %collective-permute-start.12 = (f32[160,256]{1,0:T(8,128)S(1)}, f32[160,256]{1,0:T(8,128)S(1)}, u32[]{:S(2)}, u32[]{:S(2)}) collective-permute-start(f32[160,256]{1,0:T(8,128)S(1)} %get-tuple-element.54), channel_id=1, source_target_pairs={{0,8},{2,10},{4,12},{6,14},{8,0},{10,2},{12,4},{14,6},{1,9},{3,11}... | collective-permute-start | bytes 491528 | tf_op jit(solution)/shard_map/ppermute | solution.py:357
  81.1 0.2 collective-permute-start.11
  81.4 1.2 collective-permute-start.14
  82.6 1.3 collective-permute-done.12
  83.9 0.2 collective-permute-start.13
  84.1 1.2 collective-permute-done.11
  85.3 1.2 collective-permute-start.15
  86.5 0.3 collective-permute-start.16
  86.9 3.0 %collective-permute-done.13 = f32[160,256]{1,0:T(8,128)S(1)} collective-permute-done((f32[160,256]{1,0:T(8,128)S(1)}, f32[160,256]{1,0:T(8,128)S(1)}, u32[]{:S(2)}, u32[]{:S(2)}) %collective-permute-start.13) | collective-permute-done | bytes 163872 | tf_op jit(solution)/shard_map/ppermute | solution.py:357
  89.9 1.2 collective-permute-start.17
  91.2 3.9 %collective-permute-done.17 = f32[160,256]{1,0:T(8,128)S(1)} collective-permute-done((f32[160,256]{1,0:T(8,128)S(1)}, f32[160,256]{1,0:T(8,128)S(1)}, u32[]{:S(2)}, u32[]{:S(2)}) %collective-permute-start.17) | collective-permute-done | bytes 163872 | tf_op jit(solution)/shard_map/ppermute | solution.py:357
  95.1 4.3 %collective-permute-start.18 = (f32[8,160,256]{2,1,0:T(8,128)S(1)}, f32[8,160,256]{2,1,0:T(8,128)S(1)}, u32[]{:S(2)}, u32[]{:S(2)}) collective-permute-start(f32[8,160,256]{2,1,0:T(8,128)S(1)} %bitcast_dynamic-update-slice_fusion.mine_ref), channel_id=1, source_target_pairs={{0,1},{1,0},{2,3},{3,2},{4,5},{5,4},{6,7},{7,6},{8,9},{9,8},{10,11... | collective-permute-start | bytes 3932168 | tf_op jit(solution)/shard_map/ppermute | solution.py:361
  99.4 2.7 %collective-permute-done.18.other_ref = f32[8,160,256]{2,1,0:T(8,128)S(1)} collective-permute-done((f32[8,160,256]{2,1,0:T(8,128)S(1)}, f32[8,160,256]{2,1,0:T(8,128)S(1)}, u32[]{:S(2)}, u32[]{:S(2)}) %collective-permute-start.18) | collective-permute-done | bytes 1310752 | tf_op jit(solution)/shard_map/ppermute | solution.py:361
  102.1 1.1 collect.1.gram_ref._.refs_7_
  103.2 0.6 pick.3
  103.8 1.3 collective-permute-start.19
  105.0 7.3 %factor_step.4 = (f32[256,768]{1,0:T(8,128)S(1)}, f32[256,256]{1,0:T(8,128)S(1)}, f32[6,256,256]{2,1,0:T(8,128)S(1)}) custom-call(f32[10,256,256]{2,1,0:T(8,128)S(1)} %collect.1.gram_ref._.refs_7_), custom_call_target="tpu_custom_call" | custom-call | tf_op jit(solution)/shard_map/factor_step/pallas_call | solution.py:201
  112.4 1.1 collective-permute-start.20
  113.6 7.0 %factor_step.5 = (f32[256,512]{1,0:T(8,128)S(1)}, f32[256,256]{1,0:T(8,128)S(1)}, f32[3,256,256]{2,1,0:T(8,128)S(1)}) custom-call(f32[6,256,256]{2,1,0:T(8,128)S(1)} %get-tuple-element.42.gram_ref), custom_call_target="tpu_custom_call" | custom-call | tf_op jit(solution)/shard_map/factor_step/pallas_call | solution.py:201
  120.6 4.9 %collective-permute-done.20.right_ref = f32[256,256]{1,0:T(8,128)S(1)} collective-permute-done((f32[256,256]{1,0:T(8,128)S(1)}, f32[256,256]{1,0:T(8,128)S(1)}, u32[]{:S(2)}, u32[]{:S(2)}) %collective-permute-start.20) | collective-permute-done | bytes 262176 | tf_op jit(solution)/shard_map/ppermute | solution.py:365
  125.5 0.2 collective-permute-start.21
  125.7 6.7 %factor_step.6 = (f32[256,256]{1,0:T(8,128)S(1)}, f32[256,256]{1,0:T(8,128)S(1)}, f32[1,256,256]{2,1,0:T(8,128)S(1)}) custom-call(f32[3,256,256]{2,1,0:T(8,128)S(1)} %get-tuple-element.44.gram_ref), custom_call_target="tpu_custom_call" | custom-call | tf_op jit(solution)/shard_map/factor_step/pallas_call | solution.py:201
  132.5 1.9 %collective-permute-start.22 = (f32[2,256,256]{2,1,0:T(8,128)S(1)}, f32[2,256,256]{2,1,0:T(8,128)S(1)}, u32[]{:S(2)}, u32[]{:S(2)}) collective-permute-start(f32[2,256,256]{2,1,0:T(8,128)S(1)} %stack.61.refs_8_), channel_id=1, source_target_pairs={{0,1},{1,0},{2,3},{3,2},{4,5},{5,4},{6,7},{7,6},{8,9},{9,8},{10,11... | collective-permute-start | bytes 1572872 | tf_op jit(solution)/shard_map/ppermute | solution.py:361
  134.4 6.4 %factor_step.7.refs_6_ = f32[256,256]{1,0:T(8,128)S(1)} custom-call(f32[1,256,256]{2,1,0:T(8,128)S(1)} %get-tuple-element.49.gram_ref), custom_call_target="tpu_custom_call" | custom-call | tf_op jit(solution)/shard_map/factor_step/pallas_call | solution.py:201
  140.8 4.1 %solve.1 = f32[256,256]{1,0:T(8,128)} custom-call(s32[5]{0:T(128)S(1)} %stack.51.place_ref, f32[256,768]{1,0:T(8,128)S(1)} %get-tuple-element.41.after_ref.refs_0_, f32[256,512]{1,0:T(8,128)S(1)} %get-tuple-element.43.after_ref.refs_1_, f32[256,256]{1,0:T(8,128)S(1)} %get-tuple-element.45._.refs_2_, f32[256,256]{1,0:T(8,128)S(1)} %get-tuple-element.46.refs_3_, ...), custom_call_target="tpu_custom_call" | custom-call | tf_op jit(solution)/shard_map/solve/pallas_call | solution.py:201
  (28 shorter events, 0.4 us)
Async XLA Ops:
  0.8 1.2 copy-start
  2.0 0.9 copy-start.1
  3.8 15.9 %collective-permute-start = (f32[320,256]{1,0:T(8,128)S(1)}, f32[320,256]{1,0:T(8,128)S(1)}, u32[]{:S(2)}, u32[]{:S(2)}) collective-permute-start(f32[320,256]{1,0:T(8,128)S(1)} %get-tuple-element.30), channel_id=1, source_target_pairs={{0,24},{4,28},{8,16},{12,20},{16,8},{20,12},{24,0},{28,4},{1,25},{... | collective-permute-start | bytes 983048 | tf_op jit(solution)/shard_map/ppermute | solution.py:365
  20.2 14.5 %collective-permute-start.3 = (f32[320,256]{1,0:T(8,128)S(1)}, f32[320,256]{1,0:T(8,128)S(1)}, u32[]{:S(2)}, u32[]{:S(2)}) collective-permute-start(f32[320,256]{1,0:T(8,128)S(1)} %get-tuple-element.31.refs_0_), channel_id=1, source_target_pairs={{0,4},{2,6},{4,0},{6,2},{8,12},{10,14},{12,8},{14,10},{1,5},{3,7},... | collective-permute-start | bytes 983048 | tf_op jit(solution)/shard_map/ppermute | solution.py:357
  28.6 7.6 %collective-permute-start.1 = (f32[320,256]{1,0:T(8,128)S(1)}, f32[320,256]{1,0:T(8,128)S(1)}, u32[]{:S(2)}, u32[]{:S(2)}) collective-permute-start(f32[320,256]{1,0:T(8,128)S(1)} %get-tuple-element.33), channel_id=1, source_target_pairs={{0,24},{4,28},{8,16},{12,20},{16,8},{20,12},{24,0},{28,4},{1,25},{... | collective-permute-start | bytes 983048 | tf_op jit(solution)/shard_map/ppermute | solution.py:365
  28.6 7.6 %collective-permute-start.2 = (f32[320,256]{1,0:T(8,128)S(1)}, f32[320,256]{1,0:T(8,128)S(1)}, u32[]{:S(2)}, u32[]{:S(2)}) collective-permute-start(f32[320,256]{1,0:T(8,128)S(1)} %get-tuple-element.31.refs_0_), channel_id=1, source_target_pairs={{0,8},{2,10},{4,12},{6,14},{8,0},{10,2},{12,4},{14,6},{1,9},{3,11}... | collective-permute-start | bytes 983048 | tf_op jit(solution)/shard_map/ppermute | solution.py:357
  34.7 8.8 %collective-permute-start.4 = (f32[320,256]{1,0:T(8,128)S(1)}, f32[320,256]{1,0:T(8,128)S(1)}, u32[]{:S(2)}, u32[]{:S(2)}) collective-permute-start(f32[320,256]{1,0:T(8,128)S(1)} %collective-permute-done.3.refs_2_), channel_id=1, source_target_pairs={{0,8},{2,10},{4,12},{6,14},{8,0},{10,2},{12,4},{14,6},{1,9},{3,11}... | collective-permute-start | bytes 983048 | tf_op jit(solution)/shard_map/ppermute | solution.py:357
  44.1 6.9 %collective-permute-start.6 = (f32[320,256]{1,0:T(8,128)S(1)}, f32[320,256]{1,0:T(8,128)S(1)}, u32[]{:S(2)}, u32[]{:S(2)}) collective-permute-start(f32[320,256]{1,0:T(8,128)S(1)} %get-tuple-element.34.refs_1_), channel_id=1, source_target_pairs={{0,8},{2,10},{4,12},{6,14},{8,0},{10,2},{12,4},{14,6},{1,9},{3,11}... | collective-permute-start | bytes 983048 | tf_op jit(solution)/shard_map/ppermute | solution.py:357
  44.1 6.8 %collective-permute-start.5 = (f32[320,256]{1,0:T(8,128)S(1)}, f32[320,256]{1,0:T(8,128)S(1)}, u32[]{:S(2)}, u32[]{:S(2)}) collective-permute-start(f32[320,256]{1,0:T(8,128)S(1)} %get-tuple-element.34.refs_1_), channel_id=1, source_target_pairs={{0,4},{2,6},{4,0},{6,2},{8,12},{10,14},{12,8},{14,10},{1,5},{3,7},... | collective-permute-start | bytes 983048 | tf_op jit(solution)/shard_map/ppermute | solution.py:357
  50.9 6.2 %collective-permute-start.7 = (f32[320,256]{1,0:T(8,128)S(1)}, f32[320,256]{1,0:T(8,128)S(1)}, u32[]{:S(2)}, u32[]{:S(2)}) collective-permute-start(f32[320,256]{1,0:T(8,128)S(1)} %collective-permute-done.6.refs_5_), channel_id=1, source_target_pairs={{0,4},{2,6},{4,0},{6,2},{8,12},{10,14},{12,8},{14,10},{1,5},{3,7},... | collective-permute-start | bytes 983048 | tf_op jit(solution)/shard_map/ppermute | solution.py:357
  60.7 6.3 %collective-permute-start.8 = (f32[2,416,256]{2,1,0:T(8,128)S(1)}, f32[2,416,256]{2,1,0:T(8,128)S(1)}, u32[]{:S(2)}, u32[]{:S(2)}) collective-permute-start(f32[2,416,256]{2,1,0:T(8,128)S(1)} %get-tuple-element.38._), channel_id=1, source_target_pairs={{0,1},{1,0},{2,3},{3,2},{4,5},{5,4},{6,7},{7,6},{8,9},{9,8},{10,11... | collective-permute-start | bytes 2555912 | tf_op jit(solution)/shard_map/ppermute | solution.py:361
  67.6 5.5 %collective-permute-start.9 = (f32[160,256]{1,0:T(8,128)S(1)}, f32[160,256]{1,0:T(8,128)S(1)}, u32[]{:S(2)}, u32[]{:S(2)}) collective-permute-start(f32[160,256]{1,0:T(8,128)S(1)} %get-tuple-element.40), channel_id=1, source_target_pairs={{0,2},{2,0},{4,6},{6,4},{8,10},{10,8},{12,14},{14,12},{1,3},{3,1},... | collective-permute-start | bytes 491528 | tf_op jit(solution)/shard_map/ppermute | solution.py:357
  73.1 4.6 %collective-permute-start.10 = (f32[160,256]{1,0:T(8,128)S(1)}, f32[160,256]{1,0:T(8,128)S(1)}, u32[]{:S(2)}, u32[]{:S(2)}) collective-permute-start(f32[160,256]{1,0:T(8,128)S(1)} %add.12), channel_id=1, source_target_pairs={{0,24},{4,28},{8,16},{12,20},{16,8},{20,12},{24,0},{28,4},{1,25},{... | collective-permute-start | bytes 491528 | tf_op jit(solution)/shard_map/ppermute | solution.py:365
  77.7 6.2 %collective-permute-start.12 = (f32[160,256]{1,0:T(8,128)S(1)}, f32[160,256]{1,0:T(8,128)S(1)}, u32[]{:S(2)}, u32[]{:S(2)}) collective-permute-start(f32[160,256]{1,0:T(8,128)S(1)} %get-tuple-element.54), channel_id=1, source_target_pairs={{0,8},{2,10},{4,12},{6,14},{8,0},{10,2},{12,4},{14,6},{1,9},{3,11}... | collective-permute-start | bytes 491528 | tf_op jit(solution)/shard_map/ppermute | solution.py:357
  81.1 4.2 %collective-permute-start.11 = (f32[160,256]{1,0:T(8,128)S(1)}, f32[160,256]{1,0:T(8,128)S(1)}, u32[]{:S(2)}, u32[]{:S(2)}) collective-permute-start(f32[160,256]{1,0:T(8,128)S(1)} %get-tuple-element.54), channel_id=1, source_target_pairs={{0,4},{2,6},{4,0},{6,2},{8,12},{10,14},{12,8},{14,10},{1,5},{3,7},... | collective-permute-start | bytes 491528 | tf_op jit(solution)/shard_map/ppermute | solution.py:357
  81.4 5.2 %collective-permute-start.14 = (f32[160,256]{1,0:T(8,128)S(1)}, f32[160,256]{1,0:T(8,128)S(1)}, u32[]{:S(2)}, u32[]{:S(2)}) collective-permute-start(f32[160,256]{1,0:T(8,128)S(1)} %get-tuple-element.54), channel_id=1, source_target_pairs={{0,2},{2,0},{4,6},{6,4},{8,10},{10,8},{12,14},{14,12},{1,3},{3,1},... | collective-permute-start | bytes 491528 | tf_op jit(solution)/shard_map/ppermute | solution.py:357
  83.9 6.0 %collective-permute-start.13 = (f32[160,256]{1,0:T(8,128)S(1)}, f32[160,256]{1,0:T(8,128)S(1)}, u32[]{:S(2)}, u32[]{:S(2)}) collective-permute-start(f32[160,256]{1,0:T(8,128)S(1)} %collective-permute-done.12), channel_id=1, source_target_pairs={{0,4},{2,6},{4,0},{6,2},{8,12},{10,14},{12,8},{14,10},{1,5},{3,7},... | collective-permute-start | bytes 491528 | tf_op jit(solution)/shard_map/ppermute | solution.py:357
  85.3 5.8 %collective-permute-start.15 = (f32[160,256]{1,0:T(8,128)S(1)}, f32[160,256]{1,0:T(8,128)S(1)}, u32[]{:S(2)}, u32[]{:S(2)}) collective-permute-start(f32[160,256]{1,0:T(8,128)S(1)} %collective-permute-done.11), channel_id=1, source_target_pairs={{0,2},{2,0},{4,6},{6,4},{8,10},{10,8},{12,14},{14,12},{1,3},{3,1},... | collective-permute-start | bytes 491528 | tf_op jit(solution)/shard_map/ppermute | solution.py:357
  86.5 4.6 %collective-permute-start.16 = (f32[160,256]{1,0:T(8,128)S(1)}, f32[160,256]{1,0:T(8,128)S(1)}, u32[]{:S(2)}, u32[]{:S(2)}) collective-permute-start(f32[160,256]{1,0:T(8,128)S(1)} %collective-permute-done.14), channel_id=1, source_target_pairs={{0,8},{2,10},{4,12},{6,14},{8,0},{10,2},{12,4},{14,6},{1,9},{3,11}... | collective-permute-start | bytes 491528 | tf_op jit(solution)/shard_map/ppermute | solution.py:357
  89.9 5.2 %collective-permute-start.17 = (f32[160,256]{1,0:T(8,128)S(1)}, f32[160,256]{1,0:T(8,128)S(1)}, u32[]{:S(2)}, u32[]{:S(2)}) collective-permute-start(f32[160,256]{1,0:T(8,128)S(1)} %collective-permute-done.13), channel_id=1, source_target_pairs={{0,2},{2,0},{4,6},{6,4},{8,10},{10,8},{12,14},{14,12},{1,3},{3,1},... | collective-permute-start | bytes 491528 | tf_op jit(solution)/shard_map/ppermute | solution.py:357
  95.1 7.0 %collective-permute-start.18 = (f32[8,160,256]{2,1,0:T(8,128)S(1)}, f32[8,160,256]{2,1,0:T(8,128)S(1)}, u32[]{:S(2)}, u32[]{:S(2)}) collective-permute-start(f32[8,160,256]{2,1,0:T(8,128)S(1)} %bitcast_dynamic-update-slice_fusion.mine_ref), channel_id=1, source_target_pairs={{0,1},{1,0},{2,3},{3,2},{4,5},{5,4},{6,7},{7,6},{8,9},{9,8},{10,11... | collective-permute-start | bytes 3932168 | tf_op jit(solution)/shard_map/ppermute | solution.py:361
  103.8 8.6 %collective-permute-start.19 = (f32[256,256]{1,0:T(8,128)S(1)}, f32[256,256]{1,0:T(8,128)S(1)}, u32[]{:S(2)}, u32[]{:S(2)}) collective-permute-start(f32[256,256]{1,0:T(8,128)S(1)} %get-tuple-element.52), channel_id=1, source_target_pairs={{0,2},{2,0},{4,6},{6,4},{8,10},{10,8},{12,14},{14,12},{1,3},{3,1},... | collective-permute-start | bytes 786440 | tf_op jit(solution)/shard_map/ppermute | solution.py:357
  112.4 13.0 %collective-permute-start.20 = (f32[256,256]{1,0:T(8,128)S(1)}, f32[256,256]{1,0:T(8,128)S(1)}, u32[]{:S(2)}, u32[]{:S(2)}) collective-permute-start(f32[256,256]{1,0:T(8,128)S(1)} %add.15.left_ref), channel_id=1, source_target_pairs={{0,24},{4,28},{8,16},{12,20},{16,8},{20,12},{24,0},{28,4},{1,25},{... | collective-permute-start | bytes 786440 | tf_op jit(solution)/shard_map/ppermute | solution.py:365
  125.5 7.0 %collective-permute-start.21 = (f32[256,256]{1,0:T(8,128)S(1)}, f32[256,256]{1,0:T(8,128)S(1)}, u32[]{:S(2)}, u32[]{:S(2)}) collective-permute-start(f32[256,256]{1,0:T(8,128)S(1)} %add.16.first_ref), channel_id=1, source_target_pairs={{0,2},{2,0},{4,6},{6,4},{8,10},{10,8},{12,14},{14,12},{1,3},{3,1},... | collective-permute-start | bytes 786440 | tf_op jit(solution)/shard_map/ppermute | solution.py:357
  132.5 8.3 %collective-permute-start.22 = (f32[2,256,256]{2,1,0:T(8,128)S(1)}, f32[2,256,256]{2,1,0:T(8,128)S(1)}, u32[]{:S(2)}, u32[]{:S(2)}) collective-permute-start(f32[2,256,256]{2,1,0:T(8,128)S(1)} %stack.61.refs_8_), channel_id=1, source_target_pairs={{0,1},{1,0},{2,3},{3,2},{4,5},{5,4},{6,7},{7,6},{8,9},{9,8},{10,11... | collective-permute-start | bytes 1572872 | tf_op jit(solution)/shard_map/ppermute | solution.py:361

commit v9 on v8

--- a/solution.py
+++ b/solution.py
@@ -187,6 +187,10 @@
     other_ref[...] = keep_ref[1 - high] + got_ref[1 - high, rows]
 
 
+def pass_kernel(value_ref, _, out_ref):
+    out_ref[...] = value_ref[...]
+
+
 def stack_kernel(first_ref, second_ref, _, out_ref):
     out_ref[0] = first_ref[...]
     out_ref[1] = second_ref[...]
@@ -397,25 +401,27 @@
     )
     y, z = (0, 1), (0, 2)
 
-    def halves(k, after):
+    def halves(k, sent_after, after):
         if not in_two:
             return from_first(chunks[k], n_hi), chunks[k]
-        shape = chunks[k].shape
+        shape, sent = chunks[k].shape, chunks[CHUNKS + k]
+        if sent_after:
+            (sent,) = on_chip(pass_kernel, [shape], "sent", sent, after=sent_after)
         return on_chip(
             select_kernel,
             [shape, shape],
             "select",
             place,
             chunks[k],
-            other_group(chunks[CHUNKS + k]),
+            other_group(sent),
             scalars=1,
             after=after,
         )
 
-    first, first_right = halves(0, ())
+    first, first_right = halves(0, (), ())
     first_y, first_z = exchange(first, *y), exchange(first, *z)
     first_zy = exchange(first_y, *z)
-    second, second_right = halves(1, (first_z, first_zy))
+    second, second_right = halves(1, (first_y,), (first_z, first_zy))
     second_y, second_z = exchange(second, *y), exchange(second, *z)
     second_zy = exchange(second_z, *y)
     panels = [first, second, first_y, second_y, first_z, second_z, first_zy, second_zy]

time: 145 us -> 146 us (level)
  waiting for transfers between devices: 68.9 us -> 75.4 us
  starting transfers between devices: 33.2 us -> 27.2 us
    ppermute x4, waiting for transfers between devices: 24.2 us -> 39.3 us  [other_group(): lax.ppermute(value, ('hi', 'lo'), [(i, i ^ 6) for i in range(2 * P_SIZE)])]
    ppermute x16, waiting for transfers between devices: 40 us -> 31.4 us  [exchange(): lax.ppermute(value, ('lo', 'rh'), [(i, i ^ bits) for i in range(2 * P_SIZ...]
    ppermute x16, starting transfers between devices: 19.2 us -> 12.5 us  [exchange(): lax.ppermute(value, ('lo', 'rh'), [(i, i ^ bits) for i in range(2 * P_SIZ...]
    ppermute x4, starting transfers between devices: 3.63 us -> 5.45 us  [other_group(): lax.ppermute(value, ('hi', 'lo'), [(i, i ^ 6) for i in range(2 * P_SIZE)])]
    pallas_call x15 -> x16, Pallas kernels: 39.4 us -> 39.4 us  [on_chip(): pl.pallas_call(kernel, out_shape=[jax.ShapeDtypeStruct(shape, jnp.float32...]
  transfers between devices with their start and end apart: 23 -> 23, of which waited for: 15 -> 16; matrix products, arithmetic and copies ran while one was open for 0% -> 0% of each run, Pallas kernels for 19% -> 19%
where the time goes in v9:
time: 146 us; the launch traced here: 145 us
  waiting for transfers between devices  75.4 us (52%)
  Pallas kernels  39.4 us (27%)
  starting transfers between devices  27.2 us (19%)
  local copies, waits for them, and re-layouts  3.07 us (2%)
    pallas_call x16, Pallas kernels, on_chip(): pl.pallas_call(kernel, out_shape=[jax.ShapeDtypeStruct(shape, jnp.float32...  39.4 us
    ppermute x4, waiting for transfers between devices, other_group(): lax.ppermute(value, ('hi', 'lo'), [(i, i ^ 6) for i in range(2 * P_SIZE)])  39.3 us
    ppermute x16, waiting for transfers between devices, exchange(): lax.ppermute(value, ('lo', 'rh'), [(i, i ^ bits) for i in range(2 * P_SIZ...  31.4 us
    ppermute x16, starting transfers between devices, exchange(): lax.ppermute(value, ('lo', 'rh'), [(i, i ^ bits) for i in range(2 * P_SIZ...  12.5 us
    ppermute x3, starting transfers between devices, swap(): return lax.ppermute(value, axis, [(0, 1), (1, 0)])  9.23 us
    ppermute x4, starting transfers between devices, other_group(): lax.ppermute(value, ('hi', 'lo'), [(i, i ^ 6) for i in range(2 * P_SIZE)])  5.45 us
    ppermute x3, waiting for transfers between devices, swap(): return lax.ppermute(value, axis, [(0, 1), (1, 0)])  4.67 us
    unnamed x11, local copies, waits for them, and re-layouts  2.98 us
  transfers between devices with their start and end apart: 23, of which 16 were waited for; matrix products, arithmetic and copies ran while one was open for 0% of the time, Pallas kernels for 19%

profile of v9, /device:TPU:9, one launch (start us, length us, event | category | flops | bytes accessed | tf_op | source)
XLA Modules:
  0.0 145.4 jit_solution(3703081810213828957)
XLA Ops:
  0.0 0.7 copy.4.arcs_ref
  0.8 1.2 copy-done
  2.0 0.9 copy-done.1
  3.0 0.8 mask.1
  3.8 1.4 collective-permute-start
  5.1 14.5 %collective-permute-done.got_ref = f32[320,256]{1,0:T(8,128)S(1)} collective-permute-done((f32[320,256]{1,0:T(8,128)S(1)}, f32[320,256]{1,0:T(8,128)S(1)}, u32[]{:S(2)}, u32[]{:S(2)}) %collective-permute-start) | collective-permute-done | bytes 327712 | tf_op jit(solution)/shard_map/ppermute | solution.py:369
  19.6 0.6 select.2
  20.2 1.3 collective-permute-start.1
  21.5 6.6 %collective-permute-done.1._.refs_2_ = f32[320,256]{1,0:T(8,128)S(1)} collective-permute-done((f32[320,256]{1,0:T(8,128)S(1)}, f32[320,256]{1,0:T(8,128)S(1)}, u32[]{:S(2)}, u32[]{:S(2)}) %collective-permute-start.1) | collective-permute-done | bytes 327712 | tf_op jit(solution)/shard_map/ppermute | solution.py:361
  28.2 1.0 collective-permute-start.2
  29.2 13.8 %collective-permute-done.2.got_ref = f32[320,256]{1,0:T(8,128)S(1)} collective-permute-done((f32[320,256]{1,0:T(8,128)S(1)}, f32[320,256]{1,0:T(8,128)S(1)}, u32[]{:S(2)}, u32[]{:S(2)}) %collective-permute-start.2) | collective-permute-done | bytes 327712 | tf_op jit(solution)/shard_map/ppermute | solution.py:369
  43.2 0.6 select.3
  43.8 0.8 collective-permute-start.6
  44.6 0.7 collective-permute-start.5
  45.3 5.2 %collective-permute-done.6.refs_5_ = f32[320,256]{1,0:T(8,128)S(1)} collective-permute-done((f32[320,256]{1,0:T(8,128)S(1)}, f32[320,256]{1,0:T(8,128)S(1)}, u32[]{:S(2)}, u32[]{:S(2)}) %collective-permute-start.6) | collective-permute-done | bytes 327712 | tf_op jit(solution)/shard_map/ppermute | solution.py:361
  50.5 0.8 collective-permute-start.7
  51.6 6.8 %collective-permute-done.7.refs_7_ = f32[320,256]{1,0:T(8,128)S(1)} collective-permute-done((f32[320,256]{1,0:T(8,128)S(1)}, f32[320,256]{1,0:T(8,128)S(1)}, u32[]{:S(2)}, u32[]{:S(2)}) %collective-permute-start.7) | collective-permute-done | bytes 327712 | tf_op jit(solution)/shard_map/ppermute | solution.py:361
  58.4 3.6 %products.1 = (f32[2,160,256]{2,1,0:T(8,128)S(1)}, f32[2,256,256]{2,1,0:T(8,128)S(1)}, f32[2,416,256]{2,1,0:T(8,128)S(1)}) custom-call(s32[5]{0:T(128)S(1)} %stack.51.place_ref, f32[320,256]{1,0:T(8,128)S(1)} %get-tuple-element.31.refs_0_, f32[320,256]{1,0:T(8,128)S(1)} %get-tuple-element.34.refs_1_, f32[320,256]{1,0:T(8,128)S(1)} %collective-permute-done.1._.refs_2_, ...), custom_call_target="tpu_custom_call" | custom-call | tf_op jit(solution)/shard_map/products/pallas_call | solution.py:205
  62.0 3.4 %collective-permute-start.8 = (f32[2,416,256]{2,1,0:T(8,128)S(1)}, f32[2,416,256]{2,1,0:T(8,128)S(1)}, u32[]{:S(2)}, u32[]{:S(2)}) collective-permute-start(f32[2,416,256]{2,1,0:T(8,128)S(1)} %get-tuple-element.38._), channel_id=1, source_target_pairs={{0,1},{1,0},{2,3},{3,2},{4,5},{5,4},{6,7},{7,6},{8,9},{9,8},{10,11... | collective-permute-start | bytes 2555912 | tf_op jit(solution)/shard_map/ppermute | solution.py:365
  65.4 2.0 %collective-permute-done.8.got_ref = f32[2,416,256]{2,1,0:T(8,128)S(1)} collective-permute-done((f32[2,416,256]{2,1,0:T(8,128)S(1)}, f32[2,416,256]{2,1,0:T(8,128)S(1)}, u32[]{:S(2)}, u32[]{:S(2)}) %collective-permute-start.8) | collective-permute-done | bytes 852000 | tf_op jit(solution)/shard_map/ppermute | solution.py:365
  67.4 0.6 pick.2
  67.9 1.3 collective-permute-start.9
  69.2 4.2 %collective-permute-done.9 = f32[160,256]{1,0:T(8,128)S(1)} collective-permute-done((f32[160,256]{1,0:T(8,128)S(1)}, f32[160,256]{1,0:T(8,128)S(1)}, u32[]{:S(2)}, u32[]{:S(2)}) %collective-permute-start.9) | collective-permute-done | bytes 163872 | tf_op jit(solution)/shard_map/ppermute | solution.py:361
  73.5 1.6 %collective-permute-start.10 = (f32[160,256]{1,0:T(8,128)S(1)}, f32[160,256]{1,0:T(8,128)S(1)}, u32[]{:S(2)}, u32[]{:S(2)}) collective-permute-start(f32[160,256]{1,0:T(8,128)S(1)} %add.12), channel_id=1, source_target_pairs={{0,24},{4,28},{8,16},{12,20},{16,8},{20,12},{24,0},{28,4},{1,25},{... | collective-permute-start | bytes 491528 | tf_op jit(solution)/shard_map/ppermute | solution.py:369
  75.0 6.7 %collective-permute-done.10 = f32[160,256]{1,0:T(8,128)S(1)} collective-permute-done((f32[160,256]{1,0:T(8,128)S(1)}, f32[160,256]{1,0:T(8,128)S(1)}, u32[]{:S(2)}, u32[]{:S(2)}) %collective-permute-start.10) | collective-permute-done | bytes 163872 | tf_op jit(solution)/shard_map/ppermute | solution.py:369
  81.8 0.8 collective-permute-start.11
  82.6 1.2 collective-permute-start.14
  83.8 2.1 %collective-permute-done.12 = f32[160,256]{1,0:T(8,128)S(1)} collective-permute-done((f32[160,256]{1,0:T(8,128)S(1)}, f32[160,256]{1,0:T(8,128)S(1)}, u32[]{:S(2)}, u32[]{:S(2)}) %collective-permute-start.12) | collective-permute-done | bytes 163872 | tf_op jit(solution)/shard_map/ppermute | solution.py:361
  86.0 0.7 collective-permute-start.13
  86.7 1.2 collective-permute-start.15
  88.0 1.1 collective-permute-start.16
  89.1 1.2 collective-permute-done.13
  90.3 1.2 collective-permute-start.17
  91.5 0.9 collective-permute-done.16
  92.5 3.8 %collective-permute-done.17 = f32[160,256]{1,0:T(8,128)S(1)} collective-permute-done((f32[160,256]{1,0:T(8,128)S(1)}, f32[160,256]{1,0:T(8,128)S(1)}, u32[]{:S(2)}, u32[]{:S(2)}) %collective-permute-start.17) | collective-permute-done | bytes 163872 | tf_op jit(solution)/shard_map/ppermute | solution.py:361
  96.3 3.7 %collective-permute-start.18 = (f32[8,160,256]{2,1,0:T(8,128)S(1)}, f32[8,160,256]{2,1,0:T(8,128)S(1)}, u32[]{:S(2)}, u32[]{:S(2)}) collective-permute-start(f32[8,160,256]{2,1,0:T(8,128)S(1)} %bitcast_dynamic-update-slice_fusion.mine_ref), channel_id=1, source_target_pairs={{0,1},{1,0},{2,3},{3,2},{4,5},{5,4},{6,7},{7,6},{8,9},{9,8},{10,11... | collective-permute-start | bytes 3932168 | tf_op jit(solution)/shard_map/ppermute | solution.py:365
  100.0 2.7 %collective-permute-done.18.other_ref = f32[8,160,256]{2,1,0:T(8,128)S(1)} collective-permute-done((f32[8,160,256]{2,1,0:T(8,128)S(1)}, f32[8,160,256]{2,1,0:T(8,128)S(1)}, u32[]{:S(2)}, u32[]{:S(2)}) %collective-permute-start.18) | collective-permute-done | bytes 1310752 | tf_op jit(solution)/shard_map/ppermute | solution.py:365
  102.6 1.1 collect.1.gram_ref._.refs_7_
  103.7 0.6 pick.3
  104.3 1.2 collective-permute-start.19
  105.5 7.3 %factor_step.4 = (f32[256,768]{1,0:T(8,128)S(1)}, f32[256,256]{1,0:T(8,128)S(1)}, f32[6,256,256]{2,1,0:T(8,128)S(1)}) custom-call(f32[10,256,256]{2,1,0:T(8,128)S(1)} %collect.1.gram_ref._.refs_7_), custom_call_target="tpu_custom_call" | custom-call | tf_op jit(solution)/shard_map/factor_step/pallas_call | solution.py:205
  112.9 1.5 %collective-permute-start.20 = (f32[256,256]{1,0:T(8,128)S(1)}, f32[256,256]{1,0:T(8,128)S(1)}, u32[]{:S(2)}, u32[]{:S(2)}) collective-permute-start(f32[256,256]{1,0:T(8,128)S(1)} %add.15.left_ref), channel_id=1, source_target_pairs={{0,24},{4,28},{8,16},{12,20},{16,8},{20,12},{24,0},{28,4},{1,25},{... | collective-permute-start | bytes 786440 | tf_op jit(solution)/shard_map/ppermute | solution.py:369
  114.4 7.0 %factor_step.5 = (f32[256,512]{1,0:T(8,128)S(1)}, f32[256,256]{1,0:T(8,128)S(1)}, f32[3,256,256]{2,1,0:T(8,128)S(1)}) custom-call(f32[6,256,256]{2,1,0:T(8,128)S(1)} %get-tuple-element.42.gram_ref), custom_call_target="tpu_custom_call" | custom-call | tf_op jit(solution)/shard_map/factor_step/pallas_call | solution.py:205
  121.4 4.4 %collective-permute-done.20.right_ref = f32[256,256]{1,0:T(8,128)S(1)} collective-permute-done((f32[256,256]{1,0:T(8,128)S(1)}, f32[256,256]{1,0:T(8,128)S(1)}, u32[]{:S(2)}, u32[]{:S(2)}) %collective-permute-start.20) | collective-permute-done | bytes 262176 | tf_op jit(solution)/shard_map/ppermute | solution.py:369
  125.9 6.7 %factor_step.6 = (f32[256,256]{1,0:T(8,128)S(1)}, f32[256,256]{1,0:T(8,128)S(1)}, f32[1,256,256]{2,1,0:T(8,128)S(1)}) custom-call(f32[3,256,256]{2,1,0:T(8,128)S(1)} %get-tuple-element.44.gram_ref), custom_call_target="tpu_custom_call" | custom-call | tf_op jit(solution)/shard_map/factor_step/pallas_call | solution.py:205
  132.7 2.2 %collective-permute-start.22 = (f32[2,256,256]{2,1,0:T(8,128)S(1)}, f32[2,256,256]{2,1,0:T(8,128)S(1)}, u32[]{:S(2)}, u32[]{:S(2)}) collective-permute-start(f32[2,256,256]{2,1,0:T(8,128)S(1)} %stack.61.refs_8_), channel_id=1, source_target_pairs={{0,1},{1,0},{2,3},{3,2},{4,5},{5,4},{6,7},{7,6},{8,9},{9,8},{10,11... | collective-permute-start | bytes 1572872 | tf_op jit(solution)/shard_map/ppermute | solution.py:365
  134.9 6.4 %factor_step.7.refs_6_ = f32[256,256]{1,0:T(8,128)S(1)} custom-call(f32[1,256,256]{2,1,0:T(8,128)S(1)} %get-tuple-element.49.gram_ref), custom_call_target="tpu_custom_call" | custom-call | tf_op jit(solution)/shard_map/factor_step/pallas_call | solution.py:205
  141.3 4.1 %solve.1 = f32[256,256]{1,0:T(8,128)} custom-call(s32[5]{0:T(128)S(1)} %stack.51.place_ref, f32[256,768]{1,0:T(8,128)S(1)} %get-tuple-element.41.after_ref.refs_0_, f32[256,512]{1,0:T(8,128)S(1)} %get-tuple-element.43.after_ref.refs_1_, f32[256,256]{1,0:T(8,128)S(1)} %get-tuple-element.45._.refs_2_, f32[256,256]{1,0:T(8,128)S(1)} %get-tuple-element.46.refs_3_, ...), custom_call_target="tpu_custom_call" | custom-call | tf_op jit(solution)/shard_map/solve/pallas_call | solution.py:205
  (29 shorter events, 1.0 us)
Async XLA Ops:
  0.8 1.2 copy-start
  2.0 0.9 copy-start.1
  3.8 15.9 %collective-permute-start = (f32[320,256]{1,0:T(8,128)S(1)}, f32[320,256]{1,0:T(8,128)S(1)}, u32[]{:S(2)}, u32[]{:S(2)}) collective-permute-start(f32[320,256]{1,0:T(8,128)S(1)} %get-tuple-element.30), channel_id=1, source_target_pairs={{0,24},{4,28},{8,16},{12,20},{16,8},{20,12},{24,0},{28,4},{1,25},{... | collective-permute-start | bytes 983048 | tf_op jit(solution)/shard_map/ppermute | solution.py:369
  20.2 7.9 %collective-permute-start.1 = (f32[320,256]{1,0:T(8,128)S(1)}, f32[320,256]{1,0:T(8,128)S(1)}, u32[]{:S(2)}, u32[]{:S(2)}) collective-permute-start(f32[320,256]{1,0:T(8,128)S(1)} %get-tuple-element.31.refs_0_), channel_id=1, source_target_pairs={{0,4},{2,6},{4,0},{6,2},{8,12},{10,14},{12,8},{14,10},{1,5},{3,7},... | collective-permute-start | bytes 983048 | tf_op jit(solution)/shard_map/ppermute | solution.py:361
  21.5 7.6 %collective-permute-start.3 = (f32[320,256]{1,0:T(8,128)S(1)}, f32[320,256]{1,0:T(8,128)S(1)}, u32[]{:S(2)}, u32[]{:S(2)}) collective-permute-start(f32[320,256]{1,0:T(8,128)S(1)} %get-tuple-element.31.refs_0_), channel_id=1, source_target_pairs={{0,8},{2,10},{4,12},{6,14},{8,0},{10,2},{12,4},{14,6},{1,9},{3,11}... | collective-permute-start | bytes 983048 | tf_op jit(solution)/shard_map/ppermute | solution.py:361
  28.2 14.8 %collective-permute-start.2 = (f32[320,256]{1,0:T(8,128)S(1)}, f32[320,256]{1,0:T(8,128)S(1)}, u32[]{:S(2)}, u32[]{:S(2)}) collective-permute-start(f32[320,256]{1,0:T(8,128)S(1)} %sent.1), channel_id=1, source_target_pairs={{0,24},{4,28},{8,16},{12,20},{16,8},{20,12},{24,0},{28,4},{1,25},{... | collective-permute-start | bytes 983048 | tf_op jit(solution)/shard_map/ppermute | solution.py:369
  29.2 14.0 %collective-permute-start.4 = (f32[320,256]{1,0:T(8,128)S(1)}, f32[320,256]{1,0:T(8,128)S(1)}, u32[]{:S(2)}, u32[]{:S(2)}) collective-permute-start(f32[320,256]{1,0:T(8,128)S(1)} %collective-permute-done.1._.refs_2_), channel_id=1, source_target_pairs={{0,8},{2,10},{4,12},{6,14},{8,0},{10,2},{12,4},{14,6},{1,9},{3,11}... | collective-permute-start | bytes 983048 | tf_op jit(solution)/shard_map/ppermute | solution.py:361
  43.8 6.7 %collective-permute-start.6 = (f32[320,256]{1,0:T(8,128)S(1)}, f32[320,256]{1,0:T(8,128)S(1)}, u32[]{:S(2)}, u32[]{:S(2)}) collective-permute-start(f32[320,256]{1,0:T(8,128)S(1)} %get-tuple-element.34.refs_1_), channel_id=1, source_target_pairs={{0,8},{2,10},{4,12},{6,14},{8,0},{10,2},{12,4},{14,6},{1,9},{3,11}... | collective-permute-start | bytes 983048 | tf_op jit(solution)/shard_map/ppermute | solution.py:361
  44.6 7.0 %collective-permute-start.5 = (f32[320,256]{1,0:T(8,128)S(1)}, f32[320,256]{1,0:T(8,128)S(1)}, u32[]{:S(2)}, u32[]{:S(2)}) collective-permute-start(f32[320,256]{1,0:T(8,128)S(1)} %get-tuple-element.34.refs_1_), channel_id=1, source_target_pairs={{0,4},{2,6},{4,0},{6,2},{8,12},{10,14},{12,8},{14,10},{1,5},{3,7},... | collective-permute-start | bytes 983048 | tf_op jit(solution)/shard_map/ppermute | solution.py:361
  50.5 7.9 %collective-permute-start.7 = (f32[320,256]{1,0:T(8,128)S(1)}, f32[320,256]{1,0:T(8,128)S(1)}, u32[]{:S(2)}, u32[]{:S(2)}) collective-permute-start(f32[320,256]{1,0:T(8,128)S(1)} %collective-permute-done.6.refs_5_), channel_id=1, source_target_pairs={{0,4},{2,6},{4,0},{6,2},{8,12},{10,14},{12,8},{14,10},{1,5},{3,7},... | collective-permute-start | bytes 983048 | tf_op jit(solution)/shard_map/ppermute | solution.py:361
  62.0 5.4 %collective-permute-start.8 = (f32[2,416,256]{2,1,0:T(8,128)S(1)}, f32[2,416,256]{2,1,0:T(8,128)S(1)}, u32[]{:S(2)}, u32[]{:S(2)}) collective-permute-start(f32[2,416,256]{2,1,0:T(8,128)S(1)} %get-tuple-element.38._), channel_id=1, source_target_pairs={{0,1},{1,0},{2,3},{3,2},{4,5},{5,4},{6,7},{7,6},{8,9},{9,8},{10,11... | collective-permute-start | bytes 2555912 | tf_op jit(solution)/shard_map/ppermute | solution.py:365
  67.9 5.5 %collective-permute-start.9 = (f32[160,256]{1,0:T(8,128)S(1)}, f32[160,256]{1,0:T(8,128)S(1)}, u32[]{:S(2)}, u32[]{:S(2)}) collective-permute-start(f32[160,256]{1,0:T(8,128)S(1)} %get-tuple-element.40), channel_id=1, source_target_pairs={{0,2},{2,0},{4,6},{6,4},{8,10},{10,8},{12,14},{14,12},{1,3},{3,1},... | collective-permute-start | bytes 491528 | tf_op jit(solution)/shard_map/ppermute | solution.py:361
  73.5 8.3 %collective-permute-start.10 = (f32[160,256]{1,0:T(8,128)S(1)}, f32[160,256]{1,0:T(8,128)S(1)}, u32[]{:S(2)}, u32[]{:S(2)}) collective-permute-start(f32[160,256]{1,0:T(8,128)S(1)} %add.12), channel_id=1, source_target_pairs={{0,24},{4,28},{8,16},{12,20},{16,8},{20,12},{24,0},{28,4},{1,25},{... | collective-permute-start | bytes 491528 | tf_op jit(solution)/shard_map/ppermute | solution.py:369
  81.7 4.2 %collective-permute-start.12 = (f32[160,256]{1,0:T(8,128)S(1)}, f32[160,256]{1,0:T(8,128)S(1)}, u32[]{:S(2)}, u32[]{:S(2)}) collective-permute-start(f32[160,256]{1,0:T(8,128)S(1)} %get-tuple-element.54), channel_id=1, source_target_pairs={{0,8},{2,10},{4,12},{6,14},{8,0},{10,2},{12,4},{14,6},{1,9},{3,11}... | collective-permute-start | bytes 491528 | tf_op jit(solution)/shard_map/ppermute | solution.py:361
  81.8 4.9 %collective-permute-start.11 = (f32[160,256]{1,0:T(8,128)S(1)}, f32[160,256]{1,0:T(8,128)S(1)}, u32[]{:S(2)}, u32[]{:S(2)}) collective-permute-start(f32[160,256]{1,0:T(8,128)S(1)} %get-tuple-element.54), channel_id=1, source_target_pairs={{0,4},{2,6},{4,0},{6,2},{8,12},{10,14},{12,8},{14,10},{1,5},{3,7},... | collective-permute-start | bytes 491528 | tf_op jit(solution)/shard_map/ppermute | solution.py:361
  82.6 5.3 %collective-permute-start.14 = (f32[160,256]{1,0:T(8,128)S(1)}, f32[160,256]{1,0:T(8,128)S(1)}, u32[]{:S(2)}, u32[]{:S(2)}) collective-permute-start(f32[160,256]{1,0:T(8,128)S(1)} %get-tuple-element.54), channel_id=1, source_target_pairs={{0,2},{2,0},{4,6},{6,4},{8,10},{10,8},{12,14},{14,12},{1,3},{3,1},... | collective-permute-start | bytes 491528 | tf_op jit(solution)/shard_map/ppermute | solution.py:361
  86.0 4.3 %collective-permute-start.13 = (f32[160,256]{1,0:T(8,128)S(1)}, f32[160,256]{1,0:T(8,128)S(1)}, u32[]{:S(2)}, u32[]{:S(2)}) collective-permute-start(f32[160,256]{1,0:T(8,128)S(1)} %collective-permute-done.12), channel_id=1, source_target_pairs={{0,4},{2,6},{4,0},{6,2},{8,12},{10,14},{12,8},{14,10},{1,5},{3,7},... | collective-permute-start | bytes 491528 | tf_op jit(solution)/shard_map/ppermute | solution.py:361
  86.7 4.8 %collective-permute-start.15 = (f32[160,256]{1,0:T(8,128)S(1)}, f32[160,256]{1,0:T(8,128)S(1)}, u32[]{:S(2)}, u32[]{:S(2)}) collective-permute-start(f32[160,256]{1,0:T(8,128)S(1)} %collective-permute-done.11), channel_id=1, source_target_pairs={{0,2},{2,0},{4,6},{6,4},{8,10},{10,8},{12,14},{14,12},{1,3},{3,1},... | collective-permute-start | bytes 491528 | tf_op jit(solution)/shard_map/ppermute | solution.py:361
  88.0 4.5 %collective-permute-start.16 = (f32[160,256]{1,0:T(8,128)S(1)}, f32[160,256]{1,0:T(8,128)S(1)}, u32[]{:S(2)}, u32[]{:S(2)}) collective-permute-start(f32[160,256]{1,0:T(8,128)S(1)} %collective-permute-done.14), channel_id=1, source_target_pairs={{0,8},{2,10},{4,12},{6,14},{8,0},{10,2},{12,4},{14,6},{1,9},{3,11}... | collective-permute-start | bytes 491528 | tf_op jit(solution)/shard_map/ppermute | solution.py:361
  90.3 6.0 %collective-permute-start.17 = (f32[160,256]{1,0:T(8,128)S(1)}, f32[160,256]{1,0:T(8,128)S(1)}, u32[]{:S(2)}, u32[]{:S(2)}) collective-permute-start(f32[160,256]{1,0:T(8,128)S(1)} %collective-permute-done.13), channel_id=1, source_target_pairs={{0,2},{2,0},{4,6},{6,4},{8,10},{10,8},{12,14},{14,12},{1,3},{3,1},... | collective-permute-start | bytes 491528 | tf_op jit(solution)/shard_map/ppermute | solution.py:361
  96.3 6.3 %collective-permute-start.18 = (f32[8,160,256]{2,1,0:T(8,128)S(1)}, f32[8,160,256]{2,1,0:T(8,128)S(1)}, u32[]{:S(2)}, u32[]{:S(2)}) collective-permute-start(f32[8,160,256]{2,1,0:T(8,128)S(1)} %bitcast_dynamic-update-slice_fusion.mine_ref), channel_id=1, source_target_pairs={{0,1},{1,0},{2,3},{3,2},{4,5},{5,4},{6,7},{7,6},{8,9},{9,8},{10,11... | collective-permute-start | bytes 3932168 | tf_op jit(solution)/shard_map/ppermute | solution.py:365
  104.3 8.5 %collective-permute-start.19 = (f32[256,256]{1,0:T(8,128)S(1)}, f32[256,256]{1,0:T(8,128)S(1)}, u32[]{:S(2)}, u32[]{:S(2)}) collective-permute-start(f32[256,256]{1,0:T(8,128)S(1)} %get-tuple-element.52), channel_id=1, source_target_pairs={{0,2},{2,0},{4,6},{6,4},{8,10},{10,8},{12,14},{14,12},{1,3},{3,1},... | collective-permute-start | bytes 786440 | tf_op jit(solution)/shard_map/ppermute | solution.py:361
  112.9 12.9 %collective-permute-start.20 = (f32[256,256]{1,0:T(8,128)S(1)}, f32[256,256]{1,0:T(8,128)S(1)}, u32[]{:S(2)}, u32[]{:S(2)}) collective-permute-start(f32[256,256]{1,0:T(8,128)S(1)} %add.15.left_ref), channel_id=1, source_target_pairs={{0,24},{4,28},{8,16},{12,20},{16,8},{20,12},{24,0},{28,4},{1,25},{... | collective-permute-start | bytes 786440 | tf_op jit(solution)/shard_map/ppermute | solution.py:369
  125.8 6.8 %collective-permute-start.21 = (f32[256,256]{1,0:T(8,128)S(1)}, f32[256,256]{1,0:T(8,128)S(1)}, u32[]{:S(2)}, u32[]{:S(2)}) collective-permute-start(f32[256,256]{1,0:T(8,128)S(1)} %add.16.first_ref), channel_id=1, source_target_pairs={{0,2},{2,0},{4,6},{6,4},{8,10},{10,8},{12,14},{14,12},{1,3},{3,1},... | collective-permute-start | bytes 786440 | tf_op jit(solution)/shard_map/ppermute | solution.py:361
  132.7 8.6 %collective-permute-start.22 = (f32[2,256,256]{2,1,0:T(8,128)S(1)}, f32[2,256,256]{2,1,0:T(8,128)S(1)}, u32[]{:S(2)}, u32[]{:S(2)}) collective-permute-start(f32[2,256,256]{2,1,0:T(8,128)S(1)} %stack.61.refs_8_), channel_id=1, source_target_pairs={{0,1},{1,0},{2,3},{3,2},{4,5},{5,4},{6,7},{7,6},{8,9},{9,8},{10,11... | collective-permute-start | bytes 1572872 | tf_op jit(solution)/shard_map/ppermute | solution.py:365

commit v10 on v8

--- a/solution.py
+++ b/solution.py
@@ -108,7 +108,7 @@
 
 
 PAIRS = [(r, c) for r in range(P_SIZE) for c in range(r, P_SIZE)]
-CHUNKS = 2
+CHUNKS = 4
 
 
 def mask_kernel(place_ref, arcs_ref, slab_ref, rows_ref, *refs):
@@ -412,14 +412,19 @@
             after=after,
         )
 
-    first, first_right = halves(0, ())
-    first_y, first_z = exchange(first, *y), exchange(first, *z)
-    first_zy = exchange(first_y, *z)
-    second, second_right = halves(1, (first_z, first_zy))
-    second_y, second_z = exchange(second, *y), exchange(second, *z)
-    second_zy = exchange(second_z, *y)
-    panels = [first, second, first_y, second_y, first_z, second_z, first_zy, second_zy]
-    right = [first_right, second_right]
+    panels, right, before, relayed = [[] for _ in range(P_SIZE)], [], (), ()
+    for k in range(CHUNKS):
+        own, own_right = halves(k, before)
+        early, late = (y, z) if k % 2 == 0 else (z, y)
+        by_early, by_late = exchange(own, *early), exchange(own, *late)
+        before = (by_early, by_late, *relayed)
+        by_both = exchange(by_early, *late)
+        relayed = (by_both,)
+        by_y, by_z = (by_early, by_late) if k % 2 == 0 else (by_late, by_early)
+        for chunks_of, chunk in zip(panels, (own, by_y, by_z, by_both)):
+            chunks_of.append(chunk)
+        right.append(own_right)
+    panels = [chunk for chunks_of in panels for chunk in chunks_of]
 
     pair, block = (2, B, B), (B, B)
     count = len(PAIRS) * B // P_SIZE // P_SIZE

time: 145 us -> 143 us (0.986)
  waiting for transfers between devices: 68.9 us -> 57.7 us
  starting transfers between devices: 33.2 us -> 40.8 us
    ppermute x16 -> x22, waiting for transfers between devices: 40 us -> 25.1 us  [exchange(): lax.ppermute(value, ('lo', 'rh'), [(i, i ^ bits) for i in range(2 * P_SIZ...]
    ppermute x3, starting transfers between devices: 10.4 us -> 15.4 us  [swap(): return lax.ppermute(value, axis, [(0, 1), (1, 0)])]
    ppermute x4 -> x6, waiting for transfers between devices: 24.2 us -> 28 us  [other_group(): lax.ppermute(value, ('hi', 'lo'), [(i, i ^ 6) for i in range(2 * P_SIZE)])]
    ppermute x16 -> x22, starting transfers between devices: 19.2 us -> 21.3 us  [exchange(): lax.ppermute(value, ('lo', 'rh'), [(i, i ^ bits) for i in range(2 * P_SIZ...]
    pallas_call x15 -> x17, Pallas kernels: 39.4 us -> 40.5 us  [on_chip(): pl.pallas_call(kernel, out_shape=[jax.ShapeDtypeStruct(shape, jnp.float32...]
    ppermute x4 -> x6, starting transfers between devices: 3.63 us -> 4.11 us  [other_group(): lax.ppermute(value, ('hi', 'lo'), [(i, i ^ 6) for i in range(2 * P_SIZE)])]
  transfers between devices with their start and end apart: 23 -> 31, of which waited for: 15 -> 19; matrix products, arithmetic and copies ran while one was open for 0% -> 0% of each run, Pallas kernels for 19% -> 20%
where the time goes in v10:
time: 143 us; the launch traced here: 142 us
  waiting for transfers between devices  57.7 us (40%)
  starting transfers between devices  40.8 us (29%)
  Pallas kernels  40.5 us (28%)
  local copies, waits for them, and re-layouts  3.07 us (2%)
    pallas_call x17, Pallas kernels, on_chip(): pl.pallas_call(kernel, out_shape=[jax.ShapeDtypeStruct(shape, jnp.float32...  40.5 us
    ppermute x6, waiting for transfers between devices, other_group(): lax.ppermute(value, ('hi', 'lo'), [(i, i ^ 6) for i in range(2 * P_SIZE)])  28 us
    ppermute x22, waiting for transfers between devices, exchange(): lax.ppermute(value, ('lo', 'rh'), [(i, i ^ bits) for i in range(2 * P_SIZ...  25.1 us
    ppermute x22, starting transfers between devices, exchange(): lax.ppermute(value, ('lo', 'rh'), [(i, i ^ bits) for i in range(2 * P_SIZ...  21.3 us
    ppermute x3, starting transfers between devices, swap(): return lax.ppermute(value, axis, [(0, 1), (1, 0)])  15.4 us
    ppermute x3, waiting for transfers between devices, swap(): return lax.ppermute(value, axis, [(0, 1), (1, 0)])  4.67 us
    ppermute x6, starting transfers between devices, other_group(): lax.ppermute(value, ('hi', 'lo'), [(i, i ^ 6) for i in range(2 * P_SIZE)])  4.11 us
    unnamed x11, local copies, waits for them, and re-layouts  2.98 us
  transfers between devices with their start and end apart: 31, of which 19 were waited for; matrix products, arithmetic and copies ran while one was open for 0% of the time, Pallas kernels for 20%

profile of v10, /device:TPU:9, one launch (start us, length us, event | category | flops | bytes accessed | tf_op | source)
XLA Modules:
  0.0 142.5 jit_solution(3158447022545579761)
XLA Ops:
  0.8 1.2 copy-done
  2.0 0.9 copy-done.1
  3.8 1.4 collective-permute-start
  5.3 10.8 %collective-permute-done.got_ref = f32[160,256]{1,0:T(8,128)S(1)} collective-permute-done((f32[160,256]{1,0:T(8,128)S(1)}, f32[160,256]{1,0:T(8,128)S(1)}, u32[]{:S(2)}, u32[]{:S(2)}) %collective-permute-start) | collective-permute-done | bytes 163872 | tf_op jit(solution)/shard_map/ppermute | solution.py:365
  16.8 1.3 collective-permute-start.2
  18.1 1.5 %collective-permute-done.1.got_ref = f32[160,256]{1,0:T(8,128)S(1)} collective-permute-done((f32[160,256]{1,0:T(8,128)S(1)}, f32[160,256]{1,0:T(8,128)S(1)}, u32[]{:S(2)}, u32[]{:S(2)}) %collective-permute-start.1) | collective-permute-done | bytes 163872 | tf_op jit(solution)/shard_map/ppermute | solution.py:365
  19.6 1.3 collective-permute-done.3.refs_1_.refs_8_
  21.6 1.7 %collective-permute-start.5 = (f32[160,256]{1,0:T(8,128)S(1)}, f32[160,256]{1,0:T(8,128)S(1)}, u32[]{:S(2)}, u32[]{:S(2)}) collective-permute-start(f32[160,256]{1,0:T(8,128)S(1)} %get-tuple-element.42.refs_1_), channel_id=1, source_target_pairs={{0,8},{2,10},{4,12},{6,14},{8,0},{10,2},{12,4},{14,6},{1,9},{3,11}... | collective-permute-start | bytes 491528 | tf_op jit(solution)/shard_map/ppermute | solution.py:357
  23.3 1.1 collective-permute-start.4
  24.4 1.0 collective-permute-start.7
  25.4 1.2 collective-permute-start.6
  27.3 2.3 %collective-permute-done.4.got_ref = f32[160,256]{1,0:T(8,128)S(1)} collective-permute-done((f32[160,256]{1,0:T(8,128)S(1)}, f32[160,256]{1,0:T(8,128)S(1)}, u32[]{:S(2)}, u32[]{:S(2)}) %collective-permute-start.4) | collective-permute-done | bytes 163872 | tf_op jit(solution)/shard_map/ppermute | solution.py:365
  29.6 2.5 %collective-permute-done.7.refs_2_.refs_12_ = f32[160,256]{1,0:T(8,128)S(1)} collective-permute-done((f32[160,256]{1,0:T(8,128)S(1)}, f32[160,256]{1,0:T(8,128)S(1)}, u32[]{:S(2)}, u32[]{:S(2)}) %collective-permute-start.7) | collective-permute-done | bytes 163872 | tf_op jit(solution)/shard_map/ppermute | solution.py:357
  32.7 0.9 collective-permute-start.10
  33.6 1.2 collective-permute-start.9
  34.9 4.1 %collective-permute-done.10.refs_1_.refs_10_ = f32[160,256]{1,0:T(8,128)S(1)} collective-permute-done((f32[160,256]{1,0:T(8,128)S(1)}, f32[160,256]{1,0:T(8,128)S(1)}, u32[]{:S(2)}, u32[]{:S(2)}) %collective-permute-start.10) | collective-permute-done | bytes 163872 | tf_op jit(solution)/shard_map/ppermute | solution.py:357
  39.5 1.6 %collective-permute-start.13 = (f32[160,256]{1,0:T(8,128)S(1)}, f32[160,256]{1,0:T(8,128)S(1)}, u32[]{:S(2)}, u32[]{:S(2)}) collective-permute-start(f32[160,256]{1,0:T(8,128)S(1)} %get-tuple-element.48.refs_3_), channel_id=1, source_target_pairs={{0,8},{2,10},{4,12},{6,14},{8,0},{10,2},{12,4},{14,6},{1,9},{3,11}... | collective-permute-start | bytes 491528 | tf_op jit(solution)/shard_map/ppermute | solution.py:357
  41.1 1.2 collective-permute-start.12
  42.4 2.6 %collective-permute-done.13.refs_11_ = f32[160,256]{1,0:T(8,128)S(1)} collective-permute-done((f32[160,256]{1,0:T(8,128)S(1)}, f32[160,256]{1,0:T(8,128)S(1)}, u32[]{:S(2)}, u32[]{:S(2)}) %collective-permute-start.13) | collective-permute-done | bytes 163872 | tf_op jit(solution)/shard_map/ppermute | solution.py:357
  45.0 1.2 collective-permute-start.15
  46.3 1.0 collective-permute-done.14.refs_14_
  47.3 1.9 %collective-permute-done.15.refs_15_ = f32[160,256]{1,0:T(8,128)S(1)} collective-permute-done((f32[160,256]{1,0:T(8,128)S(1)}, f32[160,256]{1,0:T(8,128)S(1)}, u32[]{:S(2)}, u32[]{:S(2)}) %collective-permute-start.15) | collective-permute-done | bytes 163872 | tf_op jit(solution)/shard_map/ppermute | solution.py:357
  49.2 3.6 %products.1 = (f32[2,160,256]{2,1,0:T(8,128)S(1)}, f32[2,256,256]{2,1,0:T(8,128)S(1)}, f32[2,416,256]{2,1,0:T(8,128)S(1)}) custom-call(s32[5]{0:T(128)S(1)} %stack.51.place_ref, f32[160,256]{1,0:T(8,128)S(1)} %get-tuple-element.39.refs_0_, f32[160,256]{1,0:T(8,128)S(1)} %get-tuple-element.42.refs_1_, f32[160,256]{1,0:T(8,128)S(1)} %get-tuple-element.45.refs_2_, ...), custom_call_target="tpu_custom_call" | custom-call | tf_op jit(solution)/shard_map/products/pallas_call | solution.py:201
  52.8 9.8 %collective-permute-start.16 = (f32[2,416,256]{2,1,0:T(8,128)S(1)}, f32[2,416,256]{2,1,0:T(8,128)S(1)}, u32[]{:S(2)}, u32[]{:S(2)}) collective-permute-start(f32[2,416,256]{2,1,0:T(8,128)S(1)} %get-tuple-element.54._), channel_id=1, source_target_pairs={{0,1},{1,0},{2,3},{3,2},{4,5},{5,4},{6,7},{7,6},{8,9},{9,8},{10,11... | collective-permute-start | bytes 2555912 | tf_op jit(solution)/shard_map/ppermute | solution.py:361
  62.6 2.0 %collective-permute-done.16.got_ref = f32[2,416,256]{2,1,0:T(8,128)S(1)} collective-permute-done((f32[2,416,256]{2,1,0:T(8,128)S(1)}, f32[2,416,256]{2,1,0:T(8,128)S(1)}, u32[]{:S(2)}, u32[]{:S(2)}) %collective-permute-start.16) | collective-permute-done | bytes 852000 | tf_op jit(solution)/shard_map/ppermute | solution.py:361
  65.2 1.3 collective-permute-start.17
  66.5 4.2 %collective-permute-done.17 = f32[160,256]{1,0:T(8,128)S(1)} collective-permute-done((f32[160,256]{1,0:T(8,128)S(1)}, f32[160,256]{1,0:T(8,128)S(1)}, u32[]{:S(2)}, u32[]{:S(2)}) %collective-permute-start.17) | collective-permute-done | bytes 163872 | tf_op jit(solution)/shard_map/ppermute | solution.py:357
  71.3 8.1 %collective-permute-done.18 = f32[160,256]{1,0:T(8,128)S(1)} collective-permute-done((f32[160,256]{1,0:T(8,128)S(1)}, f32[160,256]{1,0:T(8,128)S(1)}, u32[]{:S(2)}, u32[]{:S(2)}) %collective-permute-start.18) | collective-permute-done | bytes 163872 | tf_op jit(solution)/shard_map/ppermute | solution.py:365
  79.4 1.2 collective-permute-start.19
  80.7 1.2 collective-permute-start.22
  81.9 1.7 %collective-permute-done.20 = f32[160,256]{1,0:T(8,128)S(1)} collective-permute-done((f32[160,256]{1,0:T(8,128)S(1)}, f32[160,256]{1,0:T(8,128)S(1)}, u32[]{:S(2)}, u32[]{:S(2)}) %collective-permute-start.20) | collective-permute-done | bytes 163872 | tf_op jit(solution)/shard_map/ppermute | solution.py:357
  83.6 1.2 collective-permute-start.21
  84.8 1.2 collective-permute-start.23
  86.7 1.1 collective-permute-done.21
  87.8 1.2 collective-permute-start.25
  89.0 1.5 %collective-permute-done.24 = f32[160,256]{1,0:T(8,128)S(1)} collective-permute-done((f32[160,256]{1,0:T(8,128)S(1)}, f32[160,256]{1,0:T(8,128)S(1)}, u32[]{:S(2)}, u32[]{:S(2)}) %collective-permute-start.24) | collective-permute-done | bytes 163872 | tf_op jit(solution)/shard_map/ppermute | solution.py:357
  90.5 3.0 %collective-permute-done.25 = f32[160,256]{1,0:T(8,128)S(1)} collective-permute-done((f32[160,256]{1,0:T(8,128)S(1)}, f32[160,256]{1,0:T(8,128)S(1)}, u32[]{:S(2)}, u32[]{:S(2)}) %collective-permute-start.25) | collective-permute-done | bytes 163872 | tf_op jit(solution)/shard_map/ppermute | solution.py:357
  93.6 3.5 %collective-permute-start.26 = (f32[8,160,256]{2,1,0:T(8,128)S(1)}, f32[8,160,256]{2,1,0:T(8,128)S(1)}, u32[]{:S(2)}, u32[]{:S(2)}) collective-permute-start(f32[8,160,256]{2,1,0:T(8,128)S(1)} %bitcast_dynamic-update-slice_fusion.mine_ref), channel_id=1, source_target_pairs={{0,1},{1,0},{2,3},{3,2},{4,5},{5,4},{6,7},{7,6},{8,9},{9,8},{10,11... | collective-permute-start | bytes 3932168 | tf_op jit(solution)/shard_map/ppermute | solution.py:361
  97.0 2.7 %collective-permute-done.26.other_ref = f32[8,160,256]{2,1,0:T(8,128)S(1)} collective-permute-done((f32[8,160,256]{2,1,0:T(8,128)S(1)}, f32[8,160,256]{2,1,0:T(8,128)S(1)}, u32[]{:S(2)}, u32[]{:S(2)}) %collective-permute-start.26) | collective-permute-done | bytes 1310752 | tf_op jit(solution)/shard_map/ppermute | solution.py:361
  99.7 1.1 collect.1.gram_ref._.refs_7_
  101.4 1.3 collective-permute-start.27
  102.7 7.3 %factor_step.4 = (f32[256,768]{1,0:T(8,128)S(1)}, f32[256,256]{1,0:T(8,128)S(1)}, f32[6,256,256]{2,1,0:T(8,128)S(1)}) custom-call(f32[10,256,256]{2,1,0:T(8,128)S(1)} %collect.1.gram_ref._.refs_7_), custom_call_target="tpu_custom_call" | custom-call | tf_op jit(solution)/shard_map/factor_step/pallas_call | solution.py:201
  110.6 7.0 %factor_step.5 = (f32[256,512]{1,0:T(8,128)S(1)}, f32[256,256]{1,0:T(8,128)S(1)}, f32[3,256,256]{2,1,0:T(8,128)S(1)}) custom-call(f32[6,256,256]{2,1,0:T(8,128)S(1)} %get-tuple-element.58.gram_ref), custom_call_target="tpu_custom_call" | custom-call | tf_op jit(solution)/shard_map/factor_step/pallas_call | solution.py:201
  117.6 5.3 %collective-permute-done.28.right_ref = f32[256,256]{1,0:T(8,128)S(1)} collective-permute-done((f32[256,256]{1,0:T(8,128)S(1)}, f32[256,256]{1,0:T(8,128)S(1)}, u32[]{:S(2)}, u32[]{:S(2)}) %collective-permute-start.28) | collective-permute-done | bytes 262176 | tf_op jit(solution)/shard_map/ppermute | solution.py:365
  123.0 6.7 %factor_step.6 = (f32[256,256]{1,0:T(8,128)S(1)}, f32[256,256]{1,0:T(8,128)S(1)}, f32[1,256,256]{2,1,0:T(8,128)S(1)}) custom-call(f32[3,256,256]{2,1,0:T(8,128)S(1)} %get-tuple-element.60.gram_ref), custom_call_target="tpu_custom_call" | custom-call | tf_op jit(solution)/shard_map/factor_step/pallas_call | solution.py:201
  129.8 2.1 %collective-permute-start.30 = (f32[2,256,256]{2,1,0:T(8,128)S(1)}, f32[2,256,256]{2,1,0:T(8,128)S(1)}, u32[]{:S(2)}, u32[]{:S(2)}) collective-permute-start(f32[2,256,256]{2,1,0:T(8,128)S(1)} %stack.61.refs_8_), channel_id=1, source_target_pairs={{0,1},{1,0},{2,3},{3,2},{4,5},{5,4},{6,7},{7,6},{8,9},{9,8},{10,11... | collective-permute-start | bytes 1572872 | tf_op jit(solution)/shard_map/ppermute | solution.py:361
  131.9 6.4 %factor_step.7.refs_6_ = f32[256,256]{1,0:T(8,128)S(1)} custom-call(f32[1,256,256]{2,1,0:T(8,128)S(1)} %get-tuple-element.65.gram_ref), custom_call_target="tpu_custom_call" | custom-call | tf_op jit(solution)/shard_map/factor_step/pallas_call | solution.py:201
  138.4 4.1 %solve.1 = f32[256,256]{1,0:T(8,128)} custom-call(s32[5]{0:T(128)S(1)} %stack.51.place_ref, f32[256,768]{1,0:T(8,128)S(1)} %get-tuple-element.57.after_ref.refs_0_, f32[256,512]{1,0:T(8,128)S(1)} %get-tuple-element.59.after_ref.refs_1_, f32[256,256]{1,0:T(8,128)S(1)} %get-tuple-element.61._.refs_2_, f32[256,256]{1,0:T(8,128)S(1)} %get-tuple-element.62.refs_3_, ...), custom_call_target="tpu_custom_call" | custom-call | tf_op jit(solution)/shard_map/solve/pallas_call | solution.py:201
  (46 shorter events, 8.2 us)
Async XLA Ops:
  0.8 1.2 copy-start
  2.0 0.9 copy-start.1
  3.8 12.3 %collective-permute-start = (f32[160,256]{1,0:T(8,128)S(1)}, f32[160,256]{1,0:T(8,128)S(1)}, u32[]{:S(2)}, u32[]{:S(2)}) collective-permute-start(f32[160,256]{1,0:T(8,128)S(1)} %get-tuple-element.38), channel_id=1, source_target_pairs={{0,24},{4,28},{8,16},{12,20},{16,8},{20,12},{24,0},{28,4},{1,25},{... | collective-permute-start | bytes 491528 | tf_op jit(solution)/shard_map/ppermute | solution.py:365
  5.1 14.5 %collective-permute-start.1 = (f32[160,256]{1,0:T(8,128)S(1)}, f32[160,256]{1,0:T(8,128)S(1)}, u32[]{:S(2)}, u32[]{:S(2)}) collective-permute-start(f32[160,256]{1,0:T(8,128)S(1)} %get-tuple-element.41), channel_id=1, source_target_pairs={{0,24},{4,28},{8,16},{12,20},{16,8},{20,12},{24,0},{28,4},{1,25},{... | collective-permute-start | bytes 491528 | tf_op jit(solution)/shard_map/ppermute | solution.py:365
  16.7 4.2 %collective-permute-start.3 = (f32[160,256]{1,0:T(8,128)S(1)}, f32[160,256]{1,0:T(8,128)S(1)}, u32[]{:S(2)}, u32[]{:S(2)}) collective-permute-start(f32[160,256]{1,0:T(8,128)S(1)} %get-tuple-element.39.refs_0_), channel_id=1, source_target_pairs={{0,8},{2,10},{4,12},{6,14},{8,0},{10,2},{12,4},{14,6},{1,9},{3,11}... | collective-permute-start | bytes 491528 | tf_op jit(solution)/shard_map/ppermute | solution.py:357
  16.8 4.2 %collective-permute-start.2 = (f32[160,256]{1,0:T(8,128)S(1)}, f32[160,256]{1,0:T(8,128)S(1)}, u32[]{:S(2)}, u32[]{:S(2)}) collective-permute-start(f32[160,256]{1,0:T(8,128)S(1)} %get-tuple-element.39.refs_0_), channel_id=1, source_target_pairs={{0,4},{2,6},{4,0},{6,2},{8,12},{10,14},{12,8},{14,10},{1,5},{3,7},... | collective-permute-start | bytes 491528 | tf_op jit(solution)/shard_map/ppermute | solution.py:357
  21.6 5.4 %collective-permute-start.5 = (f32[160,256]{1,0:T(8,128)S(1)}, f32[160,256]{1,0:T(8,128)S(1)}, u32[]{:S(2)}, u32[]{:S(2)}) collective-permute-start(f32[160,256]{1,0:T(8,128)S(1)} %get-tuple-element.42.refs_1_), channel_id=1, source_target_pairs={{0,8},{2,10},{4,12},{6,14},{8,0},{10,2},{12,4},{14,6},{1,9},{3,11}... | collective-permute-start | bytes 491528 | tf_op jit(solution)/shard_map/ppermute | solution.py:357
  23.3 6.2 %collective-permute-start.4 = (f32[160,256]{1,0:T(8,128)S(1)}, f32[160,256]{1,0:T(8,128)S(1)}, u32[]{:S(2)}, u32[]{:S(2)}) collective-permute-start(f32[160,256]{1,0:T(8,128)S(1)} %get-tuple-element.44), channel_id=1, source_target_pairs={{0,24},{4,28},{8,16},{12,20},{16,8},{20,12},{24,0},{28,4},{1,25},{... | collective-permute-start | bytes 491528 | tf_op jit(solution)/shard_map/ppermute | solution.py:365
  24.4 7.6 %collective-permute-start.7 = (f32[160,256]{1,0:T(8,128)S(1)}, f32[160,256]{1,0:T(8,128)S(1)}, u32[]{:S(2)}, u32[]{:S(2)}) collective-permute-start(f32[160,256]{1,0:T(8,128)S(1)} %collective-permute-done.2.refs_0_.refs_4_), channel_id=1, source_target_pairs={{0,8},{2,10},{4,12},{6,14},{8,0},{10,2},{12,4},{14,6},{1,9},{3,11}... | collective-permute-start | bytes 491528 | tf_op jit(solution)/shard_map/ppermute | solution.py:357
  25.4 6.7 %collective-permute-start.6 = (f32[160,256]{1,0:T(8,128)S(1)}, f32[160,256]{1,0:T(8,128)S(1)}, u32[]{:S(2)}, u32[]{:S(2)}) collective-permute-start(f32[160,256]{1,0:T(8,128)S(1)} %get-tuple-element.42.refs_1_), channel_id=1, source_target_pairs={{0,4},{2,6},{4,0},{6,2},{8,12},{10,14},{12,8},{14,10},{1,5},{3,7},... | collective-permute-start | bytes 491528 | tf_op jit(solution)/shard_map/ppermute | solution.py:357
  26.7 8.2 %collective-permute-start.8 = (f32[160,256]{1,0:T(8,128)S(1)}, f32[160,256]{1,0:T(8,128)S(1)}, u32[]{:S(2)}, u32[]{:S(2)}) collective-permute-start(f32[160,256]{1,0:T(8,128)S(1)} %get-tuple-element.47), channel_id=1, source_target_pairs={{0,24},{4,28},{8,16},{12,20},{16,8},{20,12},{24,0},{28,4},{1,25},{... | collective-permute-start | bytes 491528 | tf_op jit(solution)/shard_map/ppermute | solution.py:365
  27.0 7.8 %collective-permute-start.11 = (f32[160,256]{1,0:T(8,128)S(1)}, f32[160,256]{1,0:T(8,128)S(1)}, u32[]{:S(2)}, u32[]{:S(2)}) collective-permute-start(f32[160,256]{1,0:T(8,128)S(1)} %collective-permute-done.5.refs_0_.refs_9_), channel_id=1, source_target_pairs={{0,4},{2,6},{4,0},{6,2},{8,12},{10,14},{12,8},{14,10},{1,5},{3,7},... | collective-permute-start | bytes 491528 | tf_op jit(solution)/shard_map/ppermute | solution.py:357
  32.7 6.3 %collective-permute-start.10 = (f32[160,256]{1,0:T(8,128)S(1)}, f32[160,256]{1,0:T(8,128)S(1)}, u32[]{:S(2)}, u32[]{:S(2)}) collective-permute-start(f32[160,256]{1,0:T(8,128)S(1)} %get-tuple-element.45.refs_2_), channel_id=1, source_target_pairs={{0,8},{2,10},{4,12},{6,14},{8,0},{10,2},{12,4},{14,6},{1,9},{3,11}... | collective-permute-start | bytes 491528 | tf_op jit(solution)/shard_map/ppermute | solution.py:357
  33.6 5.3 %collective-permute-start.9 = (f32[160,256]{1,0:T(8,128)S(1)}, f32[160,256]{1,0:T(8,128)S(1)}, u32[]{:S(2)}, u32[]{:S(2)}) collective-permute-start(f32[160,256]{1,0:T(8,128)S(1)} %get-tuple-element.45.refs_2_), channel_id=1, source_target_pairs={{0,4},{2,6},{4,0},{6,2},{8,12},{10,14},{12,8},{14,10},{1,5},{3,7},... | collective-permute-start | bytes 491528 | tf_op jit(solution)/shard_map/ppermute | solution.py:357
  39.5 5.5 %collective-permute-start.13 = (f32[160,256]{1,0:T(8,128)S(1)}, f32[160,256]{1,0:T(8,128)S(1)}, u32[]{:S(2)}, u32[]{:S(2)}) collective-permute-start(f32[160,256]{1,0:T(8,128)S(1)} %get-tuple-element.48.refs_3_), channel_id=1, source_target_pairs={{0,8},{2,10},{4,12},{6,14},{8,0},{10,2},{12,4},{14,6},{1,9},{3,11}... | collective-permute-start | bytes 491528 | tf_op jit(solution)/shard_map/ppermute | solution.py:357
  41.1 6.2 %collective-permute-start.12 = (f32[160,256]{1,0:T(8,128)S(1)}, f32[160,256]{1,0:T(8,128)S(1)}, u32[]{:S(2)}, u32[]{:S(2)}) collective-permute-start(f32[160,256]{1,0:T(8,128)S(1)} %get-tuple-element.48.refs_3_), channel_id=1, source_target_pairs={{0,4},{2,6},{4,0},{6,2},{8,12},{10,14},{12,8},{14,10},{1,5},{3,7},... | collective-permute-start | bytes 491528 | tf_op jit(solution)/shard_map/ppermute | solution.py:357
  42.3 5.0 %collective-permute-start.14 = (f32[160,256]{1,0:T(8,128)S(1)}, f32[160,256]{1,0:T(8,128)S(1)}, u32[]{:S(2)}, u32[]{:S(2)}) collective-permute-start(f32[160,256]{1,0:T(8,128)S(1)} %collective-permute-done.9.refs_0_.refs_6_), channel_id=1, source_target_pairs={{0,8},{2,10},{4,12},{6,14},{8,0},{10,2},{12,4},{14,6},{1,9},{3,11}... | collective-permute-start | bytes 491528 | tf_op jit(solution)/shard_map/ppermute | solution.py:357
  45.0 4.2 %collective-permute-start.15 = (f32[160,256]{1,0:T(8,128)S(1)}, f32[160,256]{1,0:T(8,128)S(1)}, u32[]{:S(2)}, u32[]{:S(2)}) collective-permute-start(f32[160,256]{1,0:T(8,128)S(1)} %collective-permute-done.13.refs_11_), channel_id=1, source_target_pairs={{0,4},{2,6},{4,0},{6,2},{8,12},{10,14},{12,8},{14,10},{1,5},{3,7},... | collective-permute-start | bytes 491528 | tf_op jit(solution)/shard_map/ppermute | solution.py:357
  52.8 11.8 %collective-permute-start.16 = (f32[2,416,256]{2,1,0:T(8,128)S(1)}, f32[2,416,256]{2,1,0:T(8,128)S(1)}, u32[]{:S(2)}, u32[]{:S(2)}) collective-permute-start(f32[2,416,256]{2,1,0:T(8,128)S(1)} %get-tuple-element.54._), channel_id=1, source_target_pairs={{0,1},{1,0},{2,3},{3,2},{4,5},{5,4},{6,7},{7,6},{8,9},{9,8},{10,11... | collective-permute-start | bytes 2555912 | tf_op jit(solution)/shard_map/ppermute | solution.py:361
  65.2 5.5 %collective-permute-start.17 = (f32[160,256]{1,0:T(8,128)S(1)}, f32[160,256]{1,0:T(8,128)S(1)}, u32[]{:S(2)}, u32[]{:S(2)}) collective-permute-start(f32[160,256]{1,0:T(8,128)S(1)} %get-tuple-element.56), channel_id=1, source_target_pairs={{0,2},{2,0},{4,6},{6,4},{8,10},{10,8},{12,14},{14,12},{1,3},{3,1},... | collective-permute-start | bytes 491528 | tf_op jit(solution)/shard_map/ppermute | solution.py:357
  70.7 8.6 %collective-permute-start.18 = (f32[160,256]{1,0:T(8,128)S(1)}, f32[160,256]{1,0:T(8,128)S(1)}, u32[]{:S(2)}, u32[]{:S(2)}) collective-permute-start(f32[160,256]{1,0:T(8,128)S(1)} %add.12), channel_id=1, source_target_pairs={{0,24},{4,28},{8,16},{12,20},{16,8},{20,12},{24,0},{28,4},{1,25},{... | collective-permute-start | bytes 491528 | tf_op jit(solution)/shard_map/ppermute | solution.py:365
  79.3 4.2 %collective-permute-start.20 = (f32[160,256]{1,0:T(8,128)S(1)}, f32[160,256]{1,0:T(8,128)S(1)}, u32[]{:S(2)}, u32[]{:S(2)}) collective-permute-start(f32[160,256]{1,0:T(8,128)S(1)} %get-tuple-element.70), channel_id=1, source_target_pairs={{0,8},{2,10},{4,12},{6,14},{8,0},{10,2},{12,4},{14,6},{1,9},{3,11}... | collective-permute-start | bytes 491528 | tf_op jit(solution)/shard_map/ppermute | solution.py:357
  79.4 5.3 %collective-permute-start.19 = (f32[160,256]{1,0:T(8,128)S(1)}, f32[160,256]{1,0:T(8,128)S(1)}, u32[]{:S(2)}, u32[]{:S(2)}) collective-permute-start(f32[160,256]{1,0:T(8,128)S(1)} %get-tuple-element.70), channel_id=1, source_target_pairs={{0,4},{2,6},{4,0},{6,2},{8,12},{10,14},{12,8},{14,10},{1,5},{3,7},... | collective-permute-start | bytes 491528 | tf_op jit(solution)/shard_map/ppermute | solution.py:357
  80.7 5.3 %collective-permute-start.22 = (f32[160,256]{1,0:T(8,128)S(1)}, f32[160,256]{1,0:T(8,128)S(1)}, u32[]{:S(2)}, u32[]{:S(2)}) collective-permute-start(f32[160,256]{1,0:T(8,128)S(1)} %get-tuple-element.70), channel_id=1, source_target_pairs={{0,2},{2,0},{4,6},{6,4},{8,10},{10,8},{12,14},{14,12},{1,3},{3,1},... | collective-permute-start | bytes 491528 | tf_op jit(solution)/shard_map/ppermute | solution.py:357
  83.6 4.2 %collective-permute-start.21 = (f32[160,256]{1,0:T(8,128)S(1)}, f32[160,256]{1,0:T(8,128)S(1)}, u32[]{:S(2)}, u32[]{:S(2)}) collective-permute-start(f32[160,256]{1,0:T(8,128)S(1)} %collective-permute-done.20), channel_id=1, source_target_pairs={{0,4},{2,6},{4,0},{6,2},{8,12},{10,14},{12,8},{14,10},{1,5},{3,7},... | collective-permute-start | bytes 491528 | tf_op jit(solution)/shard_map/ppermute | solution.py:357
  84.8 4.2 %collective-permute-start.23 = (f32[160,256]{1,0:T(8,128)S(1)}, f32[160,256]{1,0:T(8,128)S(1)}, u32[]{:S(2)}, u32[]{:S(2)}) collective-permute-start(f32[160,256]{1,0:T(8,128)S(1)} %collective-permute-done.19), channel_id=1, source_target_pairs={{0,2},{2,0},{4,6},{6,4},{8,10},{10,8},{12,14},{14,12},{1,3},{3,1},... | collective-permute-start | bytes 491528 | tf_op jit(solution)/shard_map/ppermute | solution.py:357
  86.0 4.5 %collective-permute-start.24 = (f32[160,256]{1,0:T(8,128)S(1)}, f32[160,256]{1,0:T(8,128)S(1)}, u32[]{:S(2)}, u32[]{:S(2)}) collective-permute-start(f32[160,256]{1,0:T(8,128)S(1)} %collective-permute-done.22), channel_id=1, source_target_pairs={{0,8},{2,10},{4,12},{6,14},{8,0},{10,2},{12,4},{14,6},{1,9},{3,11}... | collective-permute-start | bytes 491528 | tf_op jit(solution)/shard_map/ppermute | solution.py:357
  87.8 5.8 %collective-permute-start.25 = (f32[160,256]{1,0:T(8,128)S(1)}, f32[160,256]{1,0:T(8,128)S(1)}, u32[]{:S(2)}, u32[]{:S(2)}) collective-permute-start(f32[160,256]{1,0:T(8,128)S(1)} %collective-permute-done.21), channel_id=1, source_target_pairs={{0,2},{2,0},{4,6},{6,4},{8,10},{10,8},{12,14},{14,12},{1,3},{3,1},... | collective-permute-start | bytes 491528 | tf_op jit(solution)/shard_map/ppermute | solution.py:357
  93.6 6.1 %collective-permute-start.26 = (f32[8,160,256]{2,1,0:T(8,128)S(1)}, f32[8,160,256]{2,1,0:T(8,128)S(1)}, u32[]{:S(2)}, u32[]{:S(2)}) collective-permute-start(f32[8,160,256]{2,1,0:T(8,128)S(1)} %bitcast_dynamic-update-slice_fusion.mine_ref), channel_id=1, source_target_pairs={{0,1},{1,0},{2,3},{3,2},{4,5},{5,4},{6,7},{7,6},{8,9},{9,8},{10,11... | collective-permute-start | bytes 3932168 | tf_op jit(solution)/shard_map/ppermute | solution.py:361
  101.4 8.6 %collective-permute-start.27 = (f32[256,256]{1,0:T(8,128)S(1)}, f32[256,256]{1,0:T(8,128)S(1)}, u32[]{:S(2)}, u32[]{:S(2)}) collective-permute-start(f32[256,256]{1,0:T(8,128)S(1)} %get-tuple-element.68), channel_id=1, source_target_pairs={{0,2},{2,0},{4,6},{6,4},{8,10},{10,8},{12,14},{14,12},{1,3},{3,1},... | collective-permute-start | bytes 786440 | tf_op jit(solution)/shard_map/ppermute | solution.py:357
  110.0 12.9 %collective-permute-start.28 = (f32[256,256]{1,0:T(8,128)S(1)}, f32[256,256]{1,0:T(8,128)S(1)}, u32[]{:S(2)}, u32[]{:S(2)}) collective-permute-start(f32[256,256]{1,0:T(8,128)S(1)} %add.15.left_ref), channel_id=1, source_target_pairs={{0,24},{4,28},{8,16},{12,20},{16,8},{20,12},{24,0},{28,4},{1,25},{... | collective-permute-start | bytes 786440 | tf_op jit(solution)/shard_map/ppermute | solution.py:365
  122.9 6.8 %collective-permute-start.29 = (f32[256,256]{1,0:T(8,128)S(1)}, f32[256,256]{1,0:T(8,128)S(1)}, u32[]{:S(2)}, u32[]{:S(2)}) collective-permute-start(f32[256,256]{1,0:T(8,128)S(1)} %add.16.first_ref), channel_id=1, source_target_pairs={{0,2},{2,0},{4,6},{6,4},{8,10},{10,8},{12,14},{14,12},{1,3},{3,1},... | collective-permute-start | bytes 786440 | tf_op jit(solution)/shard_map/ppermute | solution.py:357
  129.8 8.6 %collective-permute-start.30 = (f32[2,256,256]{2,1,0:T(8,128)S(1)}, f32[2,256,256]{2,1,0:T(8,128)S(1)}, u32[]{:S(2)}, u32[]{:S(2)}) collective-permute-start(f32[2,256,256]{2,1,0:T(8,128)S(1)} %stack.61.refs_8_), channel_id=1, source_target_pairs={{0,1},{1,0},{2,3},{3,2},{4,5},{5,4},{6,7},{7,6},{8,9},{9,8},{10,11... | collective-permute-start | bytes 1572872 | tf_op jit(solution)/shard_map/ppermute | solution.py:361

commit v11 on v10

--- a/solution.py
+++ b/solution.py
@@ -144,33 +144,41 @@
 
 
 def products_kernel(place_ref, *refs):
-    panels, right = refs[: P_SIZE * CHUNKS], refs[P_SIZE * CHUNKS : (P_SIZE + 1) * CHUNKS]
-    keep_ref, keep_cross_ref, send_ref, upper, cross = refs[(P_SIZE + 1) * CHUNKS :]
+    n = CHUNKS // 2
+    panels, right = refs[: P_SIZE * n], refs[P_SIZE * n : (P_SIZE + 1) * n]
+    refs = refs[(P_SIZE + 1) * n :]
+    last = len(refs) > 2
+    if last:
+        old_upper, old_cross, keep_ref, keep_cross_ref, send_ref, upper, cross = refs
+    else:
+        upper, cross = refs
     side, own = place_ref[0], place_ref[2]
 
     def whole(chunks):
         return jnp.concatenate([chunk[...] for chunk in chunks], axis=0)
 
-    both = jnp.concatenate(
-        [right_parts(whole(panels[:CHUNKS])), right_parts(whole(right))], axis=1
-    )
+    both = jnp.concatenate([right_parts(whole(panels[:n])), right_parts(whole(right))], axis=1)
     for t in range(P_SIZE):
-        left = left_parts(whole(panels[t * CHUNKS : (t + 1) * CHUNKS]))
+        left = left_parts(whole(panels[t * n : (t + 1) * n]))
         product = parts_dot(left, both)
-        cross[own ^ t] = product[:, B:]
+        spot = own ^ t
+        cross[spot] = product[:, B:] + old_cross[spot] if last else product[:, B:]
+        rows = slice(0, B) if t == 0 else slice(B + (t - 1) * B // 2, B + t * B // 2)
         if t == 0:
-            upper[:B, :] = product[:, :B]
-            continue
-        at = B + (t - 1) * B // 2
-
-        @pl.when(own < (own ^ t))
-        def _(at=at, product=product):
-            upper[at : at + B // 2, :] = product[:, : B // 2].T
-
-        @pl.when(own > (own ^ t))
-        def _(at=at, product=product):
-            upper[at : at + B // 2, :] = product[B // 2 :, :B]
-
+            upper[rows, :] = product[:, :B]
+        else:
+
+            @pl.when(own < spot)
+            def _(rows=rows, product=product):
+                upper[rows, :] = product[:, : B // 2].T
+
+            @pl.when(own > spot)
+            def _(rows=rows, product=product):
+                upper[rows, :] = product[B // 2 :, :B]
+
+    if not last:
+        return
+    upper[...] = upper[...] + old_upper[...]
     count = keep_ref.shape[1]
     for h in range(2):
         here, there = 2 * h + side, 2 * h + 1 - side
@@ -412,8 +420,23 @@
             after=after,
         )
 
+    pair, block = (2, B, B), (B, B)
+    count = len(PAIRS) * B // P_SIZE // P_SIZE
+    sums = [(P_SIZE * count, B), (P_SIZE, B, B)]
     panels, right, before, relayed = [[] for _ in range(P_SIZE)], [], (), ()
     for k in range(CHUNKS):
+        if k == CHUNKS - 1:
+            half = [chunk for chunks_of in panels for chunk in chunks_of[: CHUNKS // 2]]
+            begun = on_chip(
+                products_kernel,
+                sums,
+                "first_products",
+                place,
+                *half,
+                *right[: CHUNKS // 2],
+                scalars=1,
+            )
+            before = (*before, begun[0])
         own, own_right = halves(k, before)
         early, late = (y, z) if k % 2 == 0 else (z, y)
         by_early, by_late = exchange(own, *early), exchange(own, *late)
@@ -424,22 +447,17 @@
         for chunks_of, chunk in zip(panels, (own, by_y, by_z, by_both)):
             chunks_of.append(chunk)
         right.append(own_right)
-    panels = [chunk for chunks_of in panels for chunk in chunks_of]
-
-    pair, block = (2, B, B), (B, B)
-    count = len(PAIRS) * B // P_SIZE // P_SIZE
+    half = [chunk for chunks_of in panels for chunk in chunks_of[CHUNKS // 2 :]]
     keep, keep_cross, send = on_chip(
         products_kernel,
         [(2, count, B), pair, (2, count + B, B)],
         "products",
         place,
-        *panels,
-        *right,
+        *half,
+        *right[CHUNKS // 2 :],
+        *begun,
         scalars=1,
-        scratch=[
-            pltpu.VMEM((P_SIZE * count, B), jnp.float32),
-            pltpu.VMEM((P_SIZE, B, B), jnp.float32),
-        ],
+        scratch=[pltpu.VMEM(shape, jnp.float32) for shape in sums],
     )
     got = swap(send)
 
@@ -457,8 +475,12 @@
 
     mine, other = picked(0, keep, send)
     piece = mine + exchange(other, 1, 0)
+    mine, other = picked(count, keep_cross, piece)
     if in_two:
-        piece = piece + other_group(piece)
+        (piece,) = on_chip(
+            add_kernel, [piece.shape], "add", piece, other_group(piece), after=(other,)
+        )
+    other = exchange(other, 1, 0)
     pieces = spread(piece)
     (gram,) = on_chip(
         collect_kernel,
@@ -475,8 +497,7 @@
         return total
 
     rows, inverses = factor(gram)
-    mine, other = picked(count, keep_cross, gram)
-    mine = added(mine, exchange(other, 1, 0), rows[0])
+    mine = added(mine, other, rows[0])
     if in_two:
         mine = added(mine, other_group(mine), rows[1])
     (own,) = on_chip(stack_kernel, [pair], "stack", mine, exchange(mine, 1, 0), after=(rows[2],))

time: 143 us -> 144 us (level)
  starting transfers between devices: 40.8 us -> 36.8 us
  waiting for transfers between devices: 57.7 us -> 61.1 us
    ppermute x22, starting transfers between devices: 21.3 us -> 15.6 us  [exchange(): lax.ppermute(value, ('lo', 'rh'), [(i, i ^ bits) for i in range(2 * P_SIZ...]
    ppermute x22, waiting for transfers between devices: 25.1 us -> 29.8 us  [exchange(): lax.ppermute(value, ('lo', 'rh'), [(i, i ^ bits) for i in range(2 * P_SIZ...]
    ppermute x6, starting transfers between devices: 4.11 us -> 5.79 us  [other_group(): lax.ppermute(value, ('hi', 'lo'), [(i, i ^ 6) for i in range(2 * P_SIZE)])]
    pallas_call x17 -> x19, Pallas kernels: 40.5 us -> 41.9 us  [on_chip(): pl.pallas_call(kernel, out_shape=[jax.ShapeDtypeStruct(shape, jnp.float32...]
    unnamed x11 -> x12, local copies, waits for them, and re-layouts: 2.98 us -> 2.99 us
  transfers between devices with their start and end apart: 31 -> 31, of which waited for: 19 -> 21; matrix products, arithmetic and copies ran while one was open for 0% -> 0% of each run, Pallas kernels for 20% -> 23%
where the time goes in v11:
time: 144 us; the launch traced here: 143 us
  waiting for transfers between devices  61.1 us (42%)
  Pallas kernels  41.9 us (29%)
  starting transfers between devices  36.8 us (26%)
  local copies, waits for them, and re-layouts  3.08 us (2%)
    pallas_call x19, Pallas kernels, on_chip(): pl.pallas_call(kernel, out_shape=[jax.ShapeDtypeStruct(shape, jnp.float32...  41.9 us
    ppermute x22, waiting for transfers between devices, exchange(): lax.ppermute(value, ('lo', 'rh'), [(i, i ^ bits) for i in range(2 * P_SIZ...  29.8 us
    ppermute x6, waiting for transfers between devices, other_group(): lax.ppermute(value, ('hi', 'lo'), [(i, i ^ 6) for i in range(2 * P_SIZE)])  26.7 us
    ppermute x22, starting transfers between devices, exchange(): lax.ppermute(value, ('lo', 'rh'), [(i, i ^ bits) for i in range(2 * P_SIZ...  15.6 us
    ppermute x3, starting transfers between devices, swap(): return lax.ppermute(value, axis, [(0, 1), (1, 0)])  15.5 us
    ppermute x6, starting transfers between devices, other_group(): lax.ppermute(value, ('hi', 'lo'), [(i, i ^ 6) for i in range(2 * P_SIZE)])  5.79 us
    ppermute x3, waiting for transfers between devices, swap(): return lax.ppermute(value, axis, [(0, 1), (1, 0)])  4.67 us
    unnamed x12, local copies, waits for them, and re-layouts  2.99 us
  transfers between devices with their start and end apart: 31, of which 21 were waited for; matrix products, arithmetic and copies ran while one was open for 0% of the time, Pallas kernels for 23%

profile of v11, /device:TPU:9, one launch (start us, length us, event | category | flops | bytes accessed | tf_op | source)
XLA Modules:
  0.0 143.2 jit_solution(6562310645393920614)
XLA Ops:
  0.0 0.7 copy.4.arcs_ref
  0.8 1.2 copy-done
  2.0 0.9 copy-done.1
  3.0 0.8 mask.1
  3.8 1.4 collective-permute-start.2
  5.3 10.8 %collective-permute-done.2.got_ref = f32[160,256]{1,0:T(8,128)S(1)} collective-permute-done((f32[160,256]{1,0:T(8,128)S(1)}, f32[160,256]{1,0:T(8,128)S(1)}, u32[]{:S(2)}, u32[]{:S(2)}) %collective-permute-start.2) | collective-permute-done | bytes 163872 | tf_op jit(solution)/shard_map/ppermute | solution.py:373
  16.8 1.3 collective-permute-start.3
  18.1 1.5 %collective-permute-done.1.got_ref = f32[160,256]{1,0:T(8,128)S(1)} collective-permute-done((f32[160,256]{1,0:T(8,128)S(1)}, f32[160,256]{1,0:T(8,128)S(1)}, u32[]{:S(2)}, u32[]{:S(2)}) %collective-permute-start.1) | collective-permute-done | bytes 163872 | tf_op jit(solution)/shard_map/ppermute | solution.py:373
  19.6 1.3 collective-permute-done.4.refs_1_.refs_4_
  21.6 1.7 %collective-permute-start.5 = (f32[160,256]{1,0:T(8,128)S(1)}, f32[160,256]{1,0:T(8,128)S(1)}, u32[]{:S(2)}, u32[]{:S(2)}) collective-permute-start(f32[160,256]{1,0:T(8,128)S(1)} %get-tuple-element.46.refs_1_), channel_id=1, source_target_pairs={{0,8},{2,10},{4,12},{6,14},{8,0},{10,2},{12,4},{14,6},{1,9},{3,11}... | collective-permute-start | bytes 491528 | tf_op jit(solution)/shard_map/ppermute | solution.py:365
  23.3 1.1 collective-permute-start
  24.4 1.2 collective-permute-start.6
  25.7 1.0 collective-permute-start.7
  27.3 2.3 %collective-permute-done.got_ref = f32[160,256]{1,0:T(8,128)S(1)} collective-permute-done((f32[160,256]{1,0:T(8,128)S(1)}, f32[160,256]{1,0:T(8,128)S(1)}, u32[]{:S(2)}, u32[]{:S(2)}) %collective-permute-start) | collective-permute-done | bytes 163872 | tf_op jit(solution)/shard_map/ppermute | solution.py:373
  29.6 2.5 %collective-permute-done.7.refs_2_.refs_6_ = f32[160,256]{1,0:T(8,128)S(1)} collective-permute-done((f32[160,256]{1,0:T(8,128)S(1)}, f32[160,256]{1,0:T(8,128)S(1)}, u32[]{:S(2)}, u32[]{:S(2)}) %collective-permute-start.7) | collective-permute-done | bytes 163872 | tf_op jit(solution)/shard_map/ppermute | solution.py:365
  32.7 2.2 %collective-permute-start.10 = (f32[160,256]{1,0:T(8,128)S(1)}, f32[160,256]{1,0:T(8,128)S(1)}, u32[]{:S(2)}, u32[]{:S(2)}) collective-permute-start(f32[160,256]{1,0:T(8,128)S(1)} %get-tuple-element.47.refs_0_), channel_id=1, source_target_pairs={{0,8},{2,10},{4,12},{6,14},{8,0},{10,2},{12,4},{14,6},{1,9},{3,11}... | collective-permute-start | bytes 491528 | tf_op jit(solution)/shard_map/ppermute | solution.py:365
  34.9 0.8 collective-permute-start.9
  35.7 2.3 %first_products.1 = (f32[640,256]{1,0:T(8,128)S(1)}, f32[4,256,256]{2,1,0:T(8,128)S(1)}) custom-call(s32[5]{0:T(128)S(1)} %stack.51.place_ref, f32[160,256]{1,0:T(8,128)S(1)} %get-tuple-element.45.refs_0_, f32[160,256]{1,0:T(8,128)S(1)} %get-tuple-element.46.refs_1_, f32[160,256]{1,0:T(8,128)S(1)} %collective-permute-done.3.refs_0_.refs_2_, ...), custom_call_target="tpu_custom_call" | custom-call | tf_op jit(solution)/shard_map/first_products/pallas_call | solution.py:209
  38.0 1.4 collective-permute-done.10.refs_1_.refs_4_
  40.0 1.6 %collective-permute-start.13 = (f32[160,256]{1,0:T(8,128)S(1)}, f32[160,256]{1,0:T(8,128)S(1)}, u32[]{:S(2)}, u32[]{:S(2)}) collective-permute-start(f32[160,256]{1,0:T(8,128)S(1)} %get-tuple-element.53.refs_1_), channel_id=1, source_target_pairs={{0,8},{2,10},{4,12},{6,14},{8,0},{10,2},{12,4},{14,6},{1,9},{3,11}... | collective-permute-start | bytes 491528 | tf_op jit(solution)/shard_map/ppermute | solution.py:365
  41.6 0.9 collective-permute-start.12
  42.6 3.6 %collective-permute-done.13.refs_5_ = f32[160,256]{1,0:T(8,128)S(1)} collective-permute-done((f32[160,256]{1,0:T(8,128)S(1)}, f32[160,256]{1,0:T(8,128)S(1)}, u32[]{:S(2)}, u32[]{:S(2)}) %collective-permute-start.13) | collective-permute-done | bytes 163872 | tf_op jit(solution)/shard_map/ppermute | solution.py:365
  46.2 0.7 collective-permute-start.15
  46.8 1.0 collective-permute-done.14.refs_6_
  47.9 2.5 %collective-permute-done.15.refs_7_ = f32[160,256]{1,0:T(8,128)S(1)} collective-permute-done((f32[160,256]{1,0:T(8,128)S(1)}, f32[160,256]{1,0:T(8,128)S(1)}, u32[]{:S(2)}, u32[]{:S(2)}) %collective-permute-start.15) | collective-permute-done | bytes 163872 | tf_op jit(solution)/shard_map/ppermute | solution.py:365
  50.4 2.6 %products.1 = (f32[2,160,256]{2,1,0:T(8,128)S(1)}, f32[2,256,256]{2,1,0:T(8,128)S(1)}, f32[2,416,256]{2,1,0:T(8,128)S(1)}) custom-call(s32[5]{0:T(128)S(1)} %stack.51.place_ref, f32[160,256]{1,0:T(8,128)S(1)} %get-tuple-element.47.refs_0_, f32[160,256]{1,0:T(8,128)S(1)} %get-tuple-element.53.refs_1_, f32[160,256]{1,0:T(8,128)S(1)} %collective-permute-done.9.refs_0_.refs_2_, ...), custom_call_target="tpu_custom_call" | custom-call | tf_op jit(solution)/shard_map/products/pallas_call | solution.py:209
  52.9 9.3 %collective-permute-start.16 = (f32[2,416,256]{2,1,0:T(8,128)S(1)}, f32[2,416,256]{2,1,0:T(8,128)S(1)}, u32[]{:S(2)}, u32[]{:S(2)}) collective-permute-start(f32[2,416,256]{2,1,0:T(8,128)S(1)} %get-tuple-element.58._), channel_id=1, source_target_pairs={{0,1},{1,0},{2,3},{3,2},{4,5},{5,4},{6,7},{7,6},{8,9},{9,8},{10,11... | collective-permute-start | bytes 2555912 | tf_op jit(solution)/shard_map/ppermute | solution.py:369
  62.2 2.0 %collective-permute-done.16.got_ref = f32[2,416,256]{2,1,0:T(8,128)S(1)} collective-permute-done((f32[2,416,256]{2,1,0:T(8,128)S(1)}, f32[2,416,256]{2,1,0:T(8,128)S(1)}, u32[]{:S(2)}, u32[]{:S(2)}) %collective-permute-start.16) | collective-permute-done | bytes 852000 | tf_op jit(solution)/shard_map/ppermute | solution.py:369
  64.8 1.3 collective-permute-start.17
  66.0 4.2 %collective-permute-done.17 = f32[160,256]{1,0:T(8,128)S(1)} collective-permute-done((f32[160,256]{1,0:T(8,128)S(1)}, f32[160,256]{1,0:T(8,128)S(1)}, u32[]{:S(2)}, u32[]{:S(2)}) %collective-permute-start.17) | collective-permute-done | bytes 163872 | tf_op jit(solution)/shard_map/ppermute | solution.py:365
  70.3 1.2 collective-permute-start.18
  72.1 7.0 %collective-permute-done.18.right_ref = f32[160,256]{1,0:T(8,128)S(1)} collective-permute-done((f32[160,256]{1,0:T(8,128)S(1)}, f32[160,256]{1,0:T(8,128)S(1)}, u32[]{:S(2)}, u32[]{:S(2)}) %collective-permute-start.18) | collective-permute-done | bytes 163872 | tf_op jit(solution)/shard_map/ppermute | solution.py:373
  79.1 1.3 collective-permute-start.22
  80.9 2.4 %collective-permute-done.22 = f32[160,256]{1,0:T(8,128)S(1)} collective-permute-done((f32[160,256]{1,0:T(8,128)S(1)}, f32[160,256]{1,0:T(8,128)S(1)}, u32[]{:S(2)}, u32[]{:S(2)}) %collective-permute-start.22) | collective-permute-done | bytes 163872 | tf_op jit(solution)/shard_map/ppermute | solution.py:365
  83.3 1.5 %collective-permute-done.20 = f32[160,256]{1,0:T(8,128)S(1)} collective-permute-done((f32[160,256]{1,0:T(8,128)S(1)}, f32[160,256]{1,0:T(8,128)S(1)}, u32[]{:S(2)}, u32[]{:S(2)}) %collective-permute-start.20) | collective-permute-done | bytes 163872 | tf_op jit(solution)/shard_map/ppermute | solution.py:365
  85.4 3.9 %collective-permute-done.21 = f32[160,256]{1,0:T(8,128)S(1)} collective-permute-done((f32[160,256]{1,0:T(8,128)S(1)}, f32[160,256]{1,0:T(8,128)S(1)}, u32[]{:S(2)}, u32[]{:S(2)}) %collective-permute-start.21) | collective-permute-done | bytes 163872 | tf_op jit(solution)/shard_map/ppermute | solution.py:365
  89.9 4.7 %collective-permute-done.25 = f32[160,256]{1,0:T(8,128)S(1)} collective-permute-done((f32[160,256]{1,0:T(8,128)S(1)}, f32[160,256]{1,0:T(8,128)S(1)}, u32[]{:S(2)}, u32[]{:S(2)}) %collective-permute-start.25) | collective-permute-done | bytes 163872 | tf_op jit(solution)/shard_map/ppermute | solution.py:365
  94.7 4.4 %collective-permute-start.26 = (f32[8,160,256]{2,1,0:T(8,128)S(1)}, f32[8,160,256]{2,1,0:T(8,128)S(1)}, u32[]{:S(2)}, u32[]{:S(2)}) collective-permute-start(f32[8,160,256]{2,1,0:T(8,128)S(1)} %bitcast_dynamic-update-slice_fusion.mine_ref), channel_id=1, source_target_pairs={{0,1},{1,0},{2,3},{3,2},{4,5},{5,4},{6,7},{7,6},{8,9},{9,8},{10,11... | collective-permute-start | bytes 3932168 | tf_op jit(solution)/shard_map/ppermute | solution.py:369
  99.0 2.7 %collective-permute-done.26.other_ref = f32[8,160,256]{2,1,0:T(8,128)S(1)} collective-permute-done((f32[8,160,256]{2,1,0:T(8,128)S(1)}, f32[8,160,256]{2,1,0:T(8,128)S(1)}, u32[]{:S(2)}, u32[]{:S(2)}) %collective-permute-start.26) | collective-permute-done | bytes 1310752 | tf_op jit(solution)/shard_map/ppermute | solution.py:369
  101.7 1.1 collect.1.gram_ref.refs_7_
  102.7 7.3 %factor_step.4 = (f32[256,768]{1,0:T(8,128)S(1)}, f32[256,256]{1,0:T(8,128)S(1)}, f32[6,256,256]{2,1,0:T(8,128)S(1)}) custom-call(f32[10,256,256]{2,1,0:T(8,128)S(1)} %collect.1.gram_ref.refs_7_), custom_call_target="tpu_custom_call" | custom-call | tf_op jit(solution)/shard_map/factor_step/pallas_call | solution.py:209
  110.1 1.6 %collective-permute-start.28 = (f32[256,256]{1,0:T(8,128)S(1)}, f32[256,256]{1,0:T(8,128)S(1)}, u32[]{:S(2)}, u32[]{:S(2)}) collective-permute-start(f32[256,256]{1,0:T(8,128)S(1)} %add.12.left_ref), channel_id=1, source_target_pairs={{0,24},{4,28},{8,16},{12,20},{16,8},{20,12},{24,0},{28,4},{1,25},{... | collective-permute-start | bytes 786440 | tf_op jit(solution)/shard_map/ppermute | solution.py:373
  111.7 7.0 %factor_step.5 = (f32[256,512]{1,0:T(8,128)S(1)}, f32[256,256]{1,0:T(8,128)S(1)}, f32[3,256,256]{2,1,0:T(8,128)S(1)}) custom-call(f32[6,256,256]{2,1,0:T(8,128)S(1)} %get-tuple-element.64.gram_ref), custom_call_target="tpu_custom_call" | custom-call | tf_op jit(solution)/shard_map/factor_step/pallas_call | solution.py:209
  118.7 5.0 %collective-permute-done.28.right_ref = f32[256,256]{1,0:T(8,128)S(1)} collective-permute-done((f32[256,256]{1,0:T(8,128)S(1)}, f32[256,256]{1,0:T(8,128)S(1)}, u32[]{:S(2)}, u32[]{:S(2)}) %collective-permute-start.28) | collective-permute-done | bytes 262176 | tf_op jit(solution)/shard_map/ppermute | solution.py:373
  123.8 6.7 %factor_step.6 = (f32[256,256]{1,0:T(8,128)S(1)}, f32[256,256]{1,0:T(8,128)S(1)}, f32[1,256,256]{2,1,0:T(8,128)S(1)}) custom-call(f32[3,256,256]{2,1,0:T(8,128)S(1)} %get-tuple-element.66.gram_ref), custom_call_target="tpu_custom_call" | custom-call | tf_op jit(solution)/shard_map/factor_step/pallas_call | solution.py:209
  130.8 1.9 %collective-permute-start.30 = (f32[2,256,256]{2,1,0:T(8,128)S(1)}, f32[2,256,256]{2,1,0:T(8,128)S(1)}, u32[]{:S(2)}, u32[]{:S(2)}) collective-permute-start(f32[2,256,256]{2,1,0:T(8,128)S(1)} %stack.61.refs_8_), channel_id=1, source_target_pairs={{0,1},{1,0},{2,3},{3,2},{4,5},{5,4},{6,7},{7,6},{8,9},{9,8},{10,11... | collective-permute-start | bytes 1572872 | tf_op jit(solution)/shard_map/ppermute | solution.py:369
  132.6 6.4 %factor_step.7.refs_6_ = f32[256,256]{1,0:T(8,128)S(1)} custom-call(f32[1,256,256]{2,1,0:T(8,128)S(1)} %get-tuple-element.71.gram_ref), custom_call_target="tpu_custom_call" | custom-call | tf_op jit(solution)/shard_map/factor_step/pallas_call | solution.py:209
  139.1 4.1 %solve.1 = f32[256,256]{1,0:T(8,128)} custom-call(s32[5]{0:T(128)S(1)} %stack.51.place_ref, f32[256,768]{1,0:T(8,128)S(1)} %get-tuple-element.63.after_ref.refs_0_, f32[256,512]{1,0:T(8,128)S(1)} %get-tuple-element.65.after_ref.refs_1_, f32[256,256]{1,0:T(8,128)S(1)} %get-tuple-element.67._.refs_2_, f32[256,256]{1,0:T(8,128)S(1)} %get-tuple-element.68.refs_3_, ...), custom_call_target="tpu_custom_call" | custom-call | tf_op jit(solution)/shard_map/solve/pallas_call | solution.py:209
  (48 shorter events, 6.7 us)
Async XLA Ops:
  0.8 1.2 copy-start
  2.0 0.9 copy-start.1
  3.8 12.3 %collective-permute-start.2 = (f32[160,256]{1,0:T(8,128)S(1)}, f32[160,256]{1,0:T(8,128)S(1)}, u32[]{:S(2)}, u32[]{:S(2)}) collective-permute-start(f32[160,256]{1,0:T(8,128)S(1)} %get-tuple-element.44), channel_id=1, source_target_pairs={{0,24},{4,28},{8,16},{12,20},{16,8},{20,12},{24,0},{28,4},{1,25},{... | collective-permute-start | bytes 491528 | tf_op jit(solution)/shard_map/ppermute | solution.py:373
  5.1 14.5 %collective-permute-start.1 = (f32[160,256]{1,0:T(8,128)S(1)}, f32[160,256]{1,0:T(8,128)S(1)}, u32[]{:S(2)}, u32[]{:S(2)}) collective-permute-start(f32[160,256]{1,0:T(8,128)S(1)} %get-tuple-element.42), channel_id=1, source_target_pairs={{0,24},{4,28},{8,16},{12,20},{16,8},{20,12},{24,0},{28,4},{1,25},{... | collective-permute-start | bytes 491528 | tf_op jit(solution)/shard_map/ppermute | solution.py:373
  16.7 4.2 %collective-permute-start.4 = (f32[160,256]{1,0:T(8,128)S(1)}, f32[160,256]{1,0:T(8,128)S(1)}, u32[]{:S(2)}, u32[]{:S(2)}) collective-permute-start(f32[160,256]{1,0:T(8,128)S(1)} %get-tuple-element.45.refs_0_), channel_id=1, source_target_pairs={{0,8},{2,10},{4,12},{6,14},{8,0},{10,2},{12,4},{14,6},{1,9},{3,11}... | collective-permute-start | bytes 491528 | tf_op jit(solution)/shard_map/ppermute | solution.py:365
  16.8 4.2 %collective-permute-start.3 = (f32[160,256]{1,0:T(8,128)S(1)}, f32[160,256]{1,0:T(8,128)S(1)}, u32[]{:S(2)}, u32[]{:S(2)}) collective-permute-start(f32[160,256]{1,0:T(8,128)S(1)} %get-tuple-element.45.refs_0_), channel_id=1, source_target_pairs={{0,4},{2,6},{4,0},{6,2},{8,12},{10,14},{12,8},{14,10},{1,5},{3,7},... | collective-permute-start | bytes 491528 | tf_op jit(solution)/shard_map/ppermute | solution.py:365
  21.6 5.4 %collective-permute-start.5 = (f32[160,256]{1,0:T(8,128)S(1)}, f32[160,256]{1,0:T(8,128)S(1)}, u32[]{:S(2)}, u32[]{:S(2)}) collective-permute-start(f32[160,256]{1,0:T(8,128)S(1)} %get-tuple-element.46.refs_1_), channel_id=1, source_target_pairs={{0,8},{2,10},{4,12},{6,14},{8,0},{10,2},{12,4},{14,6},{1,9},{3,11}... | collective-permute-start | bytes 491528 | tf_op jit(solution)/shard_map/ppermute | solution.py:365
  23.3 6.2 %collective-permute-start = (f32[160,256]{1,0:T(8,128)S(1)}, f32[160,256]{1,0:T(8,128)S(1)}, u32[]{:S(2)}, u32[]{:S(2)}) collective-permute-start(f32[160,256]{1,0:T(8,128)S(1)} %get-tuple-element.40), channel_id=1, source_target_pairs={{0,24},{4,28},{8,16},{12,20},{16,8},{20,12},{24,0},{28,4},{1,25},{... | collective-permute-start | bytes 491528 | tf_op jit(solution)/shard_map/ppermute | solution.py:373
  24.4 5.1 %collective-permute-start.6 = (f32[160,256]{1,0:T(8,128)S(1)}, f32[160,256]{1,0:T(8,128)S(1)}, u32[]{:S(2)}, u32[]{:S(2)}) collective-permute-start(f32[160,256]{1,0:T(8,128)S(1)} %get-tuple-element.46.refs_1_), channel_id=1, source_target_pairs={{0,4},{2,6},{4,0},{6,2},{8,12},{10,14},{12,8},{14,10},{1,5},{3,7},... | collective-permute-start | bytes 491528 | tf_op jit(solution)/shard_map/ppermute | solution.py:365
  25.7 6.4 %collective-permute-start.7 = (f32[160,256]{1,0:T(8,128)S(1)}, f32[160,256]{1,0:T(8,128)S(1)}, u32[]{:S(2)}, u32[]{:S(2)}) collective-permute-start(f32[160,256]{1,0:T(8,128)S(1)} %collective-permute-done.3.refs_0_.refs_2_), channel_id=1, source_target_pairs={{0,8},{2,10},{4,12},{6,14},{8,0},{10,2},{12,4},{14,6},{1,9},{3,11}... | collective-permute-start | bytes 491528 | tf_op jit(solution)/shard_map/ppermute | solution.py:365
  26.7 11.3 %collective-permute-start.8 = (f32[160,256]{1,0:T(8,128)S(1)}, f32[160,256]{1,0:T(8,128)S(1)}, u32[]{:S(2)}, u32[]{:S(2)}) collective-permute-start(f32[160,256]{1,0:T(8,128)S(1)} %get-tuple-element.49), channel_id=1, source_target_pairs={{0,24},{4,28},{8,16},{12,20},{16,8},{20,12},{24,0},{28,4},{1,25},{... | collective-permute-start | bytes 491528 | tf_op jit(solution)/shard_map/ppermute | solution.py:373
  27.0 8.6 %collective-permute-start.11 = (f32[160,256]{1,0:T(8,128)S(1)}, f32[160,256]{1,0:T(8,128)S(1)}, u32[]{:S(2)}, u32[]{:S(2)}) collective-permute-start(f32[160,256]{1,0:T(8,128)S(1)} %collective-permute-done.5.refs_0_.refs_5_), channel_id=1, source_target_pairs={{0,4},{2,6},{4,0},{6,2},{8,12},{10,14},{12,8},{14,10},{1,5},{3,7},... | collective-permute-start | bytes 491528 | tf_op jit(solution)/shard_map/ppermute | solution.py:365
  32.7 6.8 %collective-permute-start.10 = (f32[160,256]{1,0:T(8,128)S(1)}, f32[160,256]{1,0:T(8,128)S(1)}, u32[]{:S(2)}, u32[]{:S(2)}) collective-permute-start(f32[160,256]{1,0:T(8,128)S(1)} %get-tuple-element.47.refs_0_), channel_id=1, source_target_pairs={{0,8},{2,10},{4,12},{6,14},{8,0},{10,2},{12,4},{14,6},{1,9},{3,11}... | collective-permute-start | bytes 491528 | tf_op jit(solution)/shard_map/ppermute | solution.py:365
  34.9 4.5 %collective-permute-start.9 = (f32[160,256]{1,0:T(8,128)S(1)}, f32[160,256]{1,0:T(8,128)S(1)}, u32[]{:S(2)}, u32[]{:S(2)}) collective-permute-start(f32[160,256]{1,0:T(8,128)S(1)} %get-tuple-element.47.refs_0_), channel_id=1, source_target_pairs={{0,4},{2,6},{4,0},{6,2},{8,12},{10,14},{12,8},{14,10},{1,5},{3,7},... | collective-permute-start | bytes 491528 | tf_op jit(solution)/shard_map/ppermute | solution.py:365
  40.0 6.2 %collective-permute-start.13 = (f32[160,256]{1,0:T(8,128)S(1)}, f32[160,256]{1,0:T(8,128)S(1)}, u32[]{:S(2)}, u32[]{:S(2)}) collective-permute-start(f32[160,256]{1,0:T(8,128)S(1)} %get-tuple-element.53.refs_1_), channel_id=1, source_target_pairs={{0,8},{2,10},{4,12},{6,14},{8,0},{10,2},{12,4},{14,6},{1,9},{3,11}... | collective-permute-start | bytes 491528 | tf_op jit(solution)/shard_map/ppermute | solution.py:365
  41.6 6.2 %collective-permute-start.12 = (f32[160,256]{1,0:T(8,128)S(1)}, f32[160,256]{1,0:T(8,128)S(1)}, u32[]{:S(2)}, u32[]{:S(2)}) collective-permute-start(f32[160,256]{1,0:T(8,128)S(1)} %get-tuple-element.53.refs_1_), channel_id=1, source_target_pairs={{0,4},{2,6},{4,0},{6,2},{8,12},{10,14},{12,8},{14,10},{1,5},{3,7},... | collective-permute-start | bytes 491528 | tf_op jit(solution)/shard_map/ppermute | solution.py:365
  42.5 5.3 %collective-permute-start.14 = (f32[160,256]{1,0:T(8,128)S(1)}, f32[160,256]{1,0:T(8,128)S(1)}, u32[]{:S(2)}, u32[]{:S(2)}) collective-permute-start(f32[160,256]{1,0:T(8,128)S(1)} %collective-permute-done.9.refs_0_.refs_2_), channel_id=1, source_target_pairs={{0,8},{2,10},{4,12},{6,14},{8,0},{10,2},{12,4},{14,6},{1,9},{3,11}... | collective-permute-start | bytes 491528 | tf_op jit(solution)/shard_map/ppermute | solution.py:365
  46.2 4.2 %collective-permute-start.15 = (f32[160,256]{1,0:T(8,128)S(1)}, f32[160,256]{1,0:T(8,128)S(1)}, u32[]{:S(2)}, u32[]{:S(2)}) collective-permute-start(f32[160,256]{1,0:T(8,128)S(1)} %collective-permute-done.13.refs_5_), channel_id=1, source_target_pairs={{0,4},{2,6},{4,0},{6,2},{8,12},{10,14},{12,8},{14,10},{1,5},{3,7},... | collective-permute-start | bytes 491528 | tf_op jit(solution)/shard_map/ppermute | solution.py:365
  52.9 11.3 %collective-permute-start.16 = (f32[2,416,256]{2,1,0:T(8,128)S(1)}, f32[2,416,256]{2,1,0:T(8,128)S(1)}, u32[]{:S(2)}, u32[]{:S(2)}) collective-permute-start(f32[2,416,256]{2,1,0:T(8,128)S(1)} %get-tuple-element.58._), channel_id=1, source_target_pairs={{0,1},{1,0},{2,3},{3,2},{4,5},{5,4},{6,7},{7,6},{8,9},{9,8},{10,11... | collective-permute-start | bytes 2555912 | tf_op jit(solution)/shard_map/ppermute | solution.py:369
  64.8 5.5 %collective-permute-start.17 = (f32[160,256]{1,0:T(8,128)S(1)}, f32[160,256]{1,0:T(8,128)S(1)}, u32[]{:S(2)}, u32[]{:S(2)}) collective-permute-start(f32[160,256]{1,0:T(8,128)S(1)} %get-tuple-element.60), channel_id=1, source_target_pairs={{0,2},{2,0},{4,6},{6,4},{8,10},{10,8},{12,14},{14,12},{1,3},{3,1},... | collective-permute-start | bytes 491528 | tf_op jit(solution)/shard_map/ppermute | solution.py:365
  70.3 8.8 %collective-permute-start.18 = (f32[160,256]{1,0:T(8,128)S(1)}, f32[160,256]{1,0:T(8,128)S(1)}, u32[]{:S(2)}, u32[]{:S(2)}) collective-permute-start(f32[160,256]{1,0:T(8,128)S(1)} %add.10._.left_ref), channel_id=1, source_target_pairs={{0,24},{4,28},{8,16},{12,20},{16,8},{20,12},{24,0},{28,4},{1,25},{... | collective-permute-start | bytes 491528 | tf_op jit(solution)/shard_map/ppermute | solution.py:373
  79.1 4.2 %collective-permute-start.22 = (f32[160,256]{1,0:T(8,128)S(1)}, f32[160,256]{1,0:T(8,128)S(1)}, u32[]{:S(2)}, u32[]{:S(2)}) collective-permute-start(f32[160,256]{1,0:T(8,128)S(1)} %add.11), channel_id=1, source_target_pairs={{0,2},{2,0},{4,6},{6,4},{8,10},{10,8},{12,14},{14,12},{1,3},{3,1},... | collective-permute-start | bytes 491528 | tf_op jit(solution)/shard_map/ppermute | solution.py:365
  80.4 4.5 %collective-permute-start.20 = (f32[160,256]{1,0:T(8,128)S(1)}, f32[160,256]{1,0:T(8,128)S(1)}, u32[]{:S(2)}, u32[]{:S(2)}) collective-permute-start(f32[160,256]{1,0:T(8,128)S(1)} %add.11), channel_id=1, source_target_pairs={{0,8},{2,10},{4,12},{6,14},{8,0},{10,2},{12,4},{14,6},{1,9},{3,11}... | collective-permute-start | bytes 491528 | tf_op jit(solution)/shard_map/ppermute | solution.py:365
  80.4 5.0 %collective-permute-start.19 = (f32[160,256]{1,0:T(8,128)S(1)}, f32[160,256]{1,0:T(8,128)S(1)}, u32[]{:S(2)}, u32[]{:S(2)}) collective-permute-start(f32[160,256]{1,0:T(8,128)S(1)} %add.11), channel_id=1, source_target_pairs={{0,4},{2,6},{4,0},{6,2},{8,12},{10,14},{12,8},{14,10},{1,5},{3,7},... | collective-permute-start | bytes 491528 | tf_op jit(solution)/shard_map/ppermute | solution.py:365
  83.3 6.5 %collective-permute-start.24 = (f32[160,256]{1,0:T(8,128)S(1)}, f32[160,256]{1,0:T(8,128)S(1)}, u32[]{:S(2)}, u32[]{:S(2)}) collective-permute-start(f32[160,256]{1,0:T(8,128)S(1)} %collective-permute-done.22), channel_id=1, source_target_pairs={{0,8},{2,10},{4,12},{6,14},{8,0},{10,2},{12,4},{14,6},{1,9},{3,11}... | collective-permute-start | bytes 491528 | tf_op jit(solution)/shard_map/ppermute | solution.py:365
  84.8 4.5 %collective-permute-start.21 = (f32[160,256]{1,0:T(8,128)S(1)}, f32[160,256]{1,0:T(8,128)S(1)}, u32[]{:S(2)}, u32[]{:S(2)}) collective-permute-start(f32[160,256]{1,0:T(8,128)S(1)} %collective-permute-done.20), channel_id=1, source_target_pairs={{0,4},{2,6},{4,0},{6,2},{8,12},{10,14},{12,8},{14,10},{1,5},{3,7},... | collective-permute-start | bytes 491528 | tf_op jit(solution)/shard_map/ppermute | solution.py:365
  85.4 4.5 %collective-permute-start.23 = (f32[160,256]{1,0:T(8,128)S(1)}, f32[160,256]{1,0:T(8,128)S(1)}, u32[]{:S(2)}, u32[]{:S(2)}) collective-permute-start(f32[160,256]{1,0:T(8,128)S(1)} %collective-permute-done.19), channel_id=1, source_target_pairs={{0,2},{2,0},{4,6},{6,4},{8,10},{10,8},{12,14},{14,12},{1,3},{3,1},... | collective-permute-start | bytes 491528 | tf_op jit(solution)/shard_map/ppermute | solution.py:365
  89.3 5.3 %collective-permute-start.25 = (f32[160,256]{1,0:T(8,128)S(1)}, f32[160,256]{1,0:T(8,128)S(1)}, u32[]{:S(2)}, u32[]{:S(2)}) collective-permute-start(f32[160,256]{1,0:T(8,128)S(1)} %collective-permute-done.21), channel_id=1, source_target_pairs={{0,2},{2,0},{4,6},{6,4},{8,10},{10,8},{12,14},{14,12},{1,3},{3,1},... | collective-permute-start | bytes 491528 | tf_op jit(solution)/shard_map/ppermute | solution.py:365
  94.7 7.0 %collective-permute-start.26 = (f32[8,160,256]{2,1,0:T(8,128)S(1)}, f32[8,160,256]{2,1,0:T(8,128)S(1)}, u32[]{:S(2)}, u32[]{:S(2)}) collective-permute-start(f32[8,160,256]{2,1,0:T(8,128)S(1)} %bitcast_dynamic-update-slice_fusion.mine_ref), channel_id=1, source_target_pairs={{0,1},{1,0},{2,3},{3,2},{4,5},{5,4},{6,7},{7,6},{8,9},{9,8},{10,11... | collective-permute-start | bytes 3932168 | tf_op jit(solution)/shard_map/ppermute | solution.py:369
  99.0 11.1 %collective-permute-start.27 = (f32[256,256]{1,0:T(8,128)S(1)}, f32[256,256]{1,0:T(8,128)S(1)}, u32[]{:S(2)}, u32[]{:S(2)}) collective-permute-start(f32[256,256]{1,0:T(8,128)S(1)} %get-tuple-element.62.after_ref), channel_id=1, source_target_pairs={{0,2},{2,0},{4,6},{6,4},{8,10},{10,8},{12,14},{14,12},{1,3},{3,1},... | collective-permute-start | bytes 786440 | tf_op jit(solution)/shard_map/ppermute | solution.py:365
  110.1 13.6 %collective-permute-start.28 = (f32[256,256]{1,0:T(8,128)S(1)}, f32[256,256]{1,0:T(8,128)S(1)}, u32[]{:S(2)}, u32[]{:S(2)}) collective-permute-start(f32[256,256]{1,0:T(8,128)S(1)} %add.12.left_ref), channel_id=1, source_target_pairs={{0,24},{4,28},{8,16},{12,20},{16,8},{20,12},{24,0},{28,4},{1,25},{... | collective-permute-start | bytes 786440 | tf_op jit(solution)/shard_map/ppermute | solution.py:373
  123.8 7.0 %collective-permute-start.29 = (f32[256,256]{1,0:T(8,128)S(1)}, f32[256,256]{1,0:T(8,128)S(1)}, u32[]{:S(2)}, u32[]{:S(2)}) collective-permute-start(f32[256,256]{1,0:T(8,128)S(1)} %add.13.first_ref), channel_id=1, source_target_pairs={{0,2},{2,0},{4,6},{6,4},{8,10},{10,8},{12,14},{14,12},{1,3},{3,1},... | collective-permute-start | bytes 786440 | tf_op jit(solution)/shard_map/ppermute | solution.py:365
  130.8 8.3 %collective-permute-start.30 = (f32[2,256,256]{2,1,0:T(8,128)S(1)}, f32[2,256,256]{2,1,0:T(8,128)S(1)}, u32[]{:S(2)}, u32[]{:S(2)}) collective-permute-start(f32[2,256,256]{2,1,0:T(8,128)S(1)} %stack.61.refs_8_), channel_id=1, source_target_pairs={{0,1},{1,0},{2,3},{3,2},{4,5},{5,4},{6,7},{7,6},{8,9},{9,8},{10,11... | collective-permute-start | bytes 1572872 | tf_op jit(solution)/shard_map/ppermute | solution.py:369

commit v12 on v11

--- a/solution.py
+++ b/solution.py
@@ -375,9 +375,9 @@
 
 def spread(piece):
     y, z, x = (0, 1), (0, 2), (1, 0)
-    by_z, by_y, by_x = exchange(piece, *z), exchange(piece, *y), exchange(piece, *x)
-    by_zy, by_yx, by_xz = exchange(by_z, *y), exchange(by_y, *x), exchange(by_x, *z)
-    by_zyx = exchange(by_zy, *x)
+    by_x, by_z, by_y = exchange(piece, *x), exchange(piece, *z), exchange(piece, *y)
+    by_xz, by_zy, by_yx = exchange(by_x, *z), exchange(by_z, *y), exchange(by_y, *x)
+    by_zyx = exchange(by_xz, *y)
     return jnp.stack([piece, by_y, by_z, by_zy, by_x, by_yx, by_xz, by_zyx])
 
 

time: 144 us -> 141 us (0.979)
  waiting for transfers between devices: 61.1 us -> 59.3 us
    ppermute x22, starting transfers between devices: 15.6 us -> 18.2 us  [exchange(): lax.ppermute(value, ('lo', 'rh'), [(i, i ^ bits) for i in range(2 * P_SIZ...]
    ppermute x3, starting transfers between devices: 15.5 us -> 13 us  [swap(): return lax.ppermute(value, axis, [(0, 1), (1, 0)])]
  transfers between devices with their start and end apart: 31 -> 31, of which waited for: 21 -> 20; matrix products, arithmetic and copies ran while one was open for 0% -> 0% of each run, Pallas kernels for 23% -> 23%
where the time goes in v12:
time: 141 us
  waiting for transfers between devices  59.3 us (42%)
  Pallas kernels  41.9 us (30%)
  starting transfers between devices  36.6 us (26%)
  local copies, waits for them, and re-layouts  3.08 us (2%)
    pallas_call x19, Pallas kernels, on_chip(): pl.pallas_call(kernel, out_shape=[jax.ShapeDtypeStruct(shape, jnp.float32...  41.9 us
    ppermute x22, waiting for transfers between devices, exchange(): lax.ppermute(value, ('lo', 'rh'), [(i, i ^ bits) for i in range(2 * P_SIZ...  28.5 us
    ppermute x6, waiting for transfers between devices, other_group(): lax.ppermute(value, ('hi', 'lo'), [(i, i ^ 6) for i in range(2 * P_SIZE)])  27.1 us
    ppermute x22, starting transfers between devices, exchange(): lax.ppermute(value, ('lo', 'rh'), [(i, i ^ bits) for i in range(2 * P_SIZ...  18.2 us
    ppermute x3, starting transfers between devices, swap(): return lax.ppermute(value, axis, [(0, 1), (1, 0)])  13 us
    ppermute x6, starting transfers between devices, other_group(): lax.ppermute(value, ('hi', 'lo'), [(i, i ^ 6) for i in range(2 * P_SIZE)])  5.37 us
    ppermute x3, waiting for transfers between devices, swap(): return lax.ppermute(value, axis, [(0, 1), (1, 0)])  3.73 us
    unnamed x12, local copies, waits for them, and re-layouts  2.99 us
  transfers between devices with their start and end apart: 31, of which 20 were waited for; matrix products, arithmetic and copies ran while one was open for 0% of the time, Pallas kernels for 23%

profile of v12, /device:TPU:9, one launch (start us, length us, event | category | flops | bytes accessed | tf_op | source)
XLA Modules:
  0.0 141.1 jit_solution(549378601011075222)
XLA Ops:
  0.8 1.2 copy-done
  2.0 0.9 copy-done.1
  3.0 0.8 mask.1
  3.8 1.4 collective-permute-start.2
  5.3 10.8 %collective-permute-done.2.got_ref = f32[160,256]{1,0:T(8,128)S(1)} collective-permute-done((f32[160,256]{1,0:T(8,128)S(1)}, f32[160,256]{1,0:T(8,128)S(1)}, u32[]{:S(2)}, u32[]{:S(2)}) %collective-permute-start.2) | collective-permute-done | bytes 163872 | tf_op jit(solution)/shard_map/ppermute | solution.py:373
  16.8 1.3 collective-permute-start.3
  18.1 1.5 %collective-permute-done.1.got_ref = f32[160,256]{1,0:T(8,128)S(1)} collective-permute-done((f32[160,256]{1,0:T(8,128)S(1)}, f32[160,256]{1,0:T(8,128)S(1)}, u32[]{:S(2)}, u32[]{:S(2)}) %collective-permute-start.1) | collective-permute-done | bytes 163872 | tf_op jit(solution)/shard_map/ppermute | solution.py:373
  19.6 1.3 collective-permute-done.4.refs_1_.refs_4_
  21.6 1.7 %collective-permute-start.5 = (f32[160,256]{1,0:T(8,128)S(1)}, f32[160,256]{1,0:T(8,128)S(1)}, u32[]{:S(2)}, u32[]{:S(2)}) collective-permute-start(f32[160,256]{1,0:T(8,128)S(1)} %get-tuple-element.46.refs_1_), channel_id=1, source_target_pairs={{0,8},{2,10},{4,12},{6,14},{8,0},{10,2},{12,4},{14,6},{1,9},{3,11}... | collective-permute-start | bytes 491528 | tf_op jit(solution)/shard_map/ppermute | solution.py:365
  23.3 1.1 collective-permute-start
  24.4 1.2 collective-permute-start.6
  25.7 1.0 collective-permute-start.7
  27.3 2.3 %collective-permute-done.got_ref = f32[160,256]{1,0:T(8,128)S(1)} collective-permute-done((f32[160,256]{1,0:T(8,128)S(1)}, f32[160,256]{1,0:T(8,128)S(1)}, u32[]{:S(2)}, u32[]{:S(2)}) %collective-permute-start) | collective-permute-done | bytes 163872 | tf_op jit(solution)/shard_map/ppermute | solution.py:373
  29.6 2.5 %collective-permute-done.7.refs_2_.refs_6_ = f32[160,256]{1,0:T(8,128)S(1)} collective-permute-done((f32[160,256]{1,0:T(8,128)S(1)}, f32[160,256]{1,0:T(8,128)S(1)}, u32[]{:S(2)}, u32[]{:S(2)}) %collective-permute-start.7) | collective-permute-done | bytes 163872 | tf_op jit(solution)/shard_map/ppermute | solution.py:365
  32.7 2.2 %collective-permute-start.10 = (f32[160,256]{1,0:T(8,128)S(1)}, f32[160,256]{1,0:T(8,128)S(1)}, u32[]{:S(2)}, u32[]{:S(2)}) collective-permute-start(f32[160,256]{1,0:T(8,128)S(1)} %get-tuple-element.47.refs_0_), channel_id=1, source_target_pairs={{0,8},{2,10},{4,12},{6,14},{8,0},{10,2},{12,4},{14,6},{1,9},{3,11}... | collective-permute-start | bytes 491528 | tf_op jit(solution)/shard_map/ppermute | solution.py:365
  35.7 2.3 %first_products.1 = (f32[640,256]{1,0:T(8,128)S(1)}, f32[4,256,256]{2,1,0:T(8,128)S(1)}) custom-call(s32[5]{0:T(128)S(1)} %stack.51.place_ref, f32[160,256]{1,0:T(8,128)S(1)} %get-tuple-element.45.refs_0_, f32[160,256]{1,0:T(8,128)S(1)} %get-tuple-element.46.refs_1_, f32[160,256]{1,0:T(8,128)S(1)} %collective-permute-done.3.refs_0_.refs_2_, ...), custom_call_target="tpu_custom_call" | custom-call | tf_op jit(solution)/shard_map/first_products/pallas_call | solution.py:209
  38.0 1.4 collective-permute-done.10.refs_1_.refs_4_
  40.0 1.6 %collective-permute-start.13 = (f32[160,256]{1,0:T(8,128)S(1)}, f32[160,256]{1,0:T(8,128)S(1)}, u32[]{:S(2)}, u32[]{:S(2)}) collective-permute-start(f32[160,256]{1,0:T(8,128)S(1)} %get-tuple-element.53.refs_1_), channel_id=1, source_target_pairs={{0,8},{2,10},{4,12},{6,14},{8,0},{10,2},{12,4},{14,6},{1,9},{3,11}... | collective-permute-start | bytes 491528 | tf_op jit(solution)/shard_map/ppermute | solution.py:365
  41.6 0.9 collective-permute-start.12
  42.6 3.6 %collective-permute-done.13.refs_5_ = f32[160,256]{1,0:T(8,128)S(1)} collective-permute-done((f32[160,256]{1,0:T(8,128)S(1)}, f32[160,256]{1,0:T(8,128)S(1)}, u32[]{:S(2)}, u32[]{:S(2)}) %collective-permute-start.13) | collective-permute-done | bytes 163872 | tf_op jit(solution)/shard_map/ppermute | solution.py:365
  46.8 1.0 collective-permute-done.14.refs_6_
  47.9 2.5 %collective-permute-done.15.refs_7_ = f32[160,256]{1,0:T(8,128)S(1)} collective-permute-done((f32[160,256]{1,0:T(8,128)S(1)}, f32[160,256]{1,0:T(8,128)S(1)}, u32[]{:S(2)}, u32[]{:S(2)}) %collective-permute-start.15) | collective-permute-done | bytes 163872 | tf_op jit(solution)/shard_map/ppermute | solution.py:365
  50.4 2.6 %products.1 = (f32[2,160,256]{2,1,0:T(8,128)S(1)}, f32[2,256,256]{2,1,0:T(8,128)S(1)}, f32[2,416,256]{2,1,0:T(8,128)S(1)}) custom-call(s32[5]{0:T(128)S(1)} %stack.51.place_ref, f32[160,256]{1,0:T(8,128)S(1)} %get-tuple-element.47.refs_0_, f32[160,256]{1,0:T(8,128)S(1)} %get-tuple-element.53.refs_1_, f32[160,256]{1,0:T(8,128)S(1)} %collective-permute-done.9.refs_0_.refs_2_, ...), custom_call_target="tpu_custom_call" | custom-call | tf_op jit(solution)/shard_map/products/pallas_call | solution.py:209
  52.9 9.3 %collective-permute-start.16 = (f32[2,416,256]{2,1,0:T(8,128)S(1)}, f32[2,416,256]{2,1,0:T(8,128)S(1)}, u32[]{:S(2)}, u32[]{:S(2)}) collective-permute-start(f32[2,416,256]{2,1,0:T(8,128)S(1)} %get-tuple-element.58._), channel_id=1, source_target_pairs={{0,1},{1,0},{2,3},{3,2},{4,5},{5,4},{6,7},{7,6},{8,9},{9,8},{10,11... | collective-permute-start | bytes 2555912 | tf_op jit(solution)/shard_map/ppermute | solution.py:369
  62.2 2.0 %collective-permute-done.16.got_ref = f32[2,416,256]{2,1,0:T(8,128)S(1)} collective-permute-done((f32[2,416,256]{2,1,0:T(8,128)S(1)}, f32[2,416,256]{2,1,0:T(8,128)S(1)}, u32[]{:S(2)}, u32[]{:S(2)}) %collective-permute-start.16) | collective-permute-done | bytes 852000 | tf_op jit(solution)/shard_map/ppermute | solution.py:369
  64.8 1.3 collective-permute-start.17
  66.0 4.2 %collective-permute-done.17 = f32[160,256]{1,0:T(8,128)S(1)} collective-permute-done((f32[160,256]{1,0:T(8,128)S(1)}, f32[160,256]{1,0:T(8,128)S(1)}, u32[]{:S(2)}, u32[]{:S(2)}) %collective-permute-start.17) | collective-permute-done | bytes 163872 | tf_op jit(solution)/shard_map/ppermute | solution.py:365
  70.3 1.2 collective-permute-start.18
  72.1 7.0 %collective-permute-done.18.right_ref = f32[160,256]{1,0:T(8,128)S(1)} collective-permute-done((f32[160,256]{1,0:T(8,128)S(1)}, f32[160,256]{1,0:T(8,128)S(1)}, u32[]{:S(2)}, u32[]{:S(2)}) %collective-permute-start.18) | collective-permute-done | bytes 163872 | tf_op jit(solution)/shard_map/ppermute | solution.py:373
  79.1 1.3 collective-permute-start.22
  80.9 2.4 %collective-permute-done.22 = f32[160,256]{1,0:T(8,128)S(1)} collective-permute-done((f32[160,256]{1,0:T(8,128)S(1)}, f32[160,256]{1,0:T(8,128)S(1)}, u32[]{:S(2)}, u32[]{:S(2)}) %collective-permute-start.22) | collective-permute-done | bytes 163872 | tf_op jit(solution)/shard_map/ppermute | solution.py:365
  83.3 1.5 %collective-permute-done.20 = f32[160,256]{1,0:T(8,128)S(1)} collective-permute-done((f32[160,256]{1,0:T(8,128)S(1)}, f32[160,256]{1,0:T(8,128)S(1)}, u32[]{:S(2)}, u32[]{:S(2)}) %collective-permute-start.20) | collective-permute-done | bytes 163872 | tf_op jit(solution)/shard_map/ppermute | solution.py:365
  85.4 3.0 %collective-permute-done.24 = f32[160,256]{1,0:T(8,128)S(1)} collective-permute-done((f32[160,256]{1,0:T(8,128)S(1)}, f32[160,256]{1,0:T(8,128)S(1)}, u32[]{:S(2)}, u32[]{:S(2)}) %collective-permute-start.24) | collective-permute-done | bytes 163872 | tf_op jit(solution)/shard_map/ppermute | solution.py:365
  88.4 0.8 collective-permute-start.25
  89.9 4.4 %collective-permute-done.25 = f32[160,256]{1,0:T(8,128)S(1)} collective-permute-done((f32[160,256]{1,0:T(8,128)S(1)}, f32[160,256]{1,0:T(8,128)S(1)}, u32[]{:S(2)}, u32[]{:S(2)}) %collective-permute-start.25) | collective-permute-done | bytes 163872 | tf_op jit(solution)/shard_map/ppermute | solution.py:365
  94.3 2.5 %collective-permute-start.26 = (f32[8,160,256]{2,1,0:T(8,128)S(1)}, f32[8,160,256]{2,1,0:T(8,128)S(1)}, u32[]{:S(2)}, u32[]{:S(2)}) collective-permute-start(f32[8,160,256]{2,1,0:T(8,128)S(1)} %bitcast_dynamic-update-slice_fusion.mine_ref), channel_id=1, source_target_pairs={{0,1},{1,0},{2,3},{3,2},{4,5},{5,4},{6,7},{7,6},{8,9},{9,8},{10,11... | collective-permute-start | bytes 3932168 | tf_op jit(solution)/shard_map/ppermute | solution.py:369
  96.9 0.9 collective-permute-start.27
  97.8 1.7 %collective-permute-done.26.other_ref = f32[8,160,256]{2,1,0:T(8,128)S(1)} collective-permute-done((f32[8,160,256]{2,1,0:T(8,128)S(1)}, f32[8,160,256]{2,1,0:T(8,128)S(1)}, u32[]{:S(2)}, u32[]{:S(2)}) %collective-permute-start.26) | collective-permute-done | bytes 1310752 | tf_op jit(solution)/shard_map/ppermute | solution.py:369
  99.5 1.1 collect.1.gram_ref.refs_7_
  100.6 7.3 %factor_step.4 = (f32[256,768]{1,0:T(8,128)S(1)}, f32[256,256]{1,0:T(8,128)S(1)}, f32[6,256,256]{2,1,0:T(8,128)S(1)}) custom-call(f32[10,256,256]{2,1,0:T(8,128)S(1)} %collect.1.gram_ref.refs_7_), custom_call_target="tpu_custom_call" | custom-call | tf_op jit(solution)/shard_map/factor_step/pallas_call | solution.py:209
  108.0 1.2 collective-permute-start.28
  109.2 7.0 %factor_step.5 = (f32[256,512]{1,0:T(8,128)S(1)}, f32[256,256]{1,0:T(8,128)S(1)}, f32[3,256,256]{2,1,0:T(8,128)S(1)}) custom-call(f32[6,256,256]{2,1,0:T(8,128)S(1)} %get-tuple-element.64.gram_ref), custom_call_target="tpu_custom_call" | custom-call | tf_op jit(solution)/shard_map/factor_step/pallas_call | solution.py:209
  116.2 5.4 %collective-permute-done.28.right_ref = f32[256,256]{1,0:T(8,128)S(1)} collective-permute-done((f32[256,256]{1,0:T(8,128)S(1)}, f32[256,256]{1,0:T(8,128)S(1)}, u32[]{:S(2)}, u32[]{:S(2)}) %collective-permute-start.28) | collective-permute-done | bytes 262176 | tf_op jit(solution)/shard_map/ppermute | solution.py:373
  121.6 0.9 collective-permute-start.29
  122.5 6.7 %factor_step.6 = (f32[256,256]{1,0:T(8,128)S(1)}, f32[256,256]{1,0:T(8,128)S(1)}, f32[1,256,256]{2,1,0:T(8,128)S(1)}) custom-call(f32[3,256,256]{2,1,0:T(8,128)S(1)} %get-tuple-element.66.gram_ref), custom_call_target="tpu_custom_call" | custom-call | tf_op jit(solution)/shard_map/factor_step/pallas_call | solution.py:209
  129.3 1.2 collective-permute-start.30
  130.5 6.4 %factor_step.7.refs_6_ = f32[256,256]{1,0:T(8,128)S(1)} custom-call(f32[1,256,256]{2,1,0:T(8,128)S(1)} %get-tuple-element.71.gram_ref), custom_call_target="tpu_custom_call" | custom-call | tf_op jit(solution)/shard_map/factor_step/pallas_call | solution.py:209
  137.0 4.1 %solve.1 = f32[256,256]{1,0:T(8,128)} custom-call(s32[5]{0:T(128)S(1)} %stack.51.place_ref, f32[256,768]{1,0:T(8,128)S(1)} %get-tuple-element.63.after_ref.refs_0_, f32[256,512]{1,0:T(8,128)S(1)} %get-tuple-element.65.after_ref.refs_1_, f32[256,256]{1,0:T(8,128)S(1)} %get-tuple-element.67._.refs_2_, f32[256,256]{1,0:T(8,128)S(1)} %get-tuple-element.68.refs_3_, ...), custom_call_target="tpu_custom_call" | custom-call | tf_op jit(solution)/shard_map/solve/pallas_call | solution.py:209
  (48 shorter events, 8.6 us)
Async XLA Ops:
  0.8 1.2 copy-start
  2.0 0.9 copy-start.1
  3.8 12.3 %collective-permute-start.2 = (f32[160,256]{1,0:T(8,128)S(1)}, f32[160,256]{1,0:T(8,128)S(1)}, u32[]{:S(2)}, u32[]{:S(2)}) collective-permute-start(f32[160,256]{1,0:T(8,128)S(1)} %get-tuple-element.44), channel_id=1, source_target_pairs={{0,24},{4,28},{8,16},{12,20},{16,8},{20,12},{24,0},{28,4},{1,25},{... | collective-permute-start | bytes 491528 | tf_op jit(solution)/shard_map/ppermute | solution.py:373
  5.1 14.5 %collective-permute-start.1 = (f32[160,256]{1,0:T(8,128)S(1)}, f32[160,256]{1,0:T(8,128)S(1)}, u32[]{:S(2)}, u32[]{:S(2)}) collective-permute-start(f32[160,256]{1,0:T(8,128)S(1)} %get-tuple-element.42), channel_id=1, source_target_pairs={{0,24},{4,28},{8,16},{12,20},{16,8},{20,12},{24,0},{28,4},{1,25},{... | collective-permute-start | bytes 491528 | tf_op jit(solution)/shard_map/ppermute | solution.py:373
  16.7 4.2 %collective-permute-start.4 = (f32[160,256]{1,0:T(8,128)S(1)}, f32[160,256]{1,0:T(8,128)S(1)}, u32[]{:S(2)}, u32[]{:S(2)}) collective-permute-start(f32[160,256]{1,0:T(8,128)S(1)} %get-tuple-element.45.refs_0_), channel_id=1, source_target_pairs={{0,8},{2,10},{4,12},{6,14},{8,0},{10,2},{12,4},{14,6},{1,9},{3,11}... | collective-permute-start | bytes 491528 | tf_op jit(solution)/shard_map/ppermute | solution.py:365
  16.8 4.2 %collective-permute-start.3 = (f32[160,256]{1,0:T(8,128)S(1)}, f32[160,256]{1,0:T(8,128)S(1)}, u32[]{:S(2)}, u32[]{:S(2)}) collective-permute-start(f32[160,256]{1,0:T(8,128)S(1)} %get-tuple-element.45.refs_0_), channel_id=1, source_target_pairs={{0,4},{2,6},{4,0},{6,2},{8,12},{10,14},{12,8},{14,10},{1,5},{3,7},... | collective-permute-start | bytes 491528 | tf_op jit(solution)/shard_map/ppermute | solution.py:365
  21.6 5.4 %collective-permute-start.5 = (f32[160,256]{1,0:T(8,128)S(1)}, f32[160,256]{1,0:T(8,128)S(1)}, u32[]{:S(2)}, u32[]{:S(2)}) collective-permute-start(f32[160,256]{1,0:T(8,128)S(1)} %get-tuple-element.46.refs_1_), channel_id=1, source_target_pairs={{0,8},{2,10},{4,12},{6,14},{8,0},{10,2},{12,4},{14,6},{1,9},{3,11}... | collective-permute-start | bytes 491528 | tf_op jit(solution)/shard_map/ppermute | solution.py:365
  23.3 6.2 %collective-permute-start = (f32[160,256]{1,0:T(8,128)S(1)}, f32[160,256]{1,0:T(8,128)S(1)}, u32[]{:S(2)}, u32[]{:S(2)}) collective-permute-start(f32[160,256]{1,0:T(8,128)S(1)} %get-tuple-element.40), channel_id=1, source_target_pairs={{0,24},{4,28},{8,16},{12,20},{16,8},{20,12},{24,0},{28,4},{1,25},{... | collective-permute-start | bytes 491528 | tf_op jit(solution)/shard_map/ppermute | solution.py:373
  24.4 5.1 %collective-permute-start.6 = (f32[160,256]{1,0:T(8,128)S(1)}, f32[160,256]{1,0:T(8,128)S(1)}, u32[]{:S(2)}, u32[]{:S(2)}) collective-permute-start(f32[160,256]{1,0:T(8,128)S(1)} %get-tuple-element.46.refs_1_), channel_id=1, source_target_pairs={{0,4},{2,6},{4,0},{6,2},{8,12},{10,14},{12,8},{14,10},{1,5},{3,7},... | collective-permute-start | bytes 491528 | tf_op jit(solution)/shard_map/ppermute | solution.py:365
  25.7 6.4 %collective-permute-start.7 = (f32[160,256]{1,0:T(8,128)S(1)}, f32[160,256]{1,0:T(8,128)S(1)}, u32[]{:S(2)}, u32[]{:S(2)}) collective-permute-start(f32[160,256]{1,0:T(8,128)S(1)} %collective-permute-done.3.refs_0_.refs_2_), channel_id=1, source_target_pairs={{0,8},{2,10},{4,12},{6,14},{8,0},{10,2},{12,4},{14,6},{1,9},{3,11}... | collective-permute-start | bytes 491528 | tf_op jit(solution)/shard_map/ppermute | solution.py:365
  26.7 11.3 %collective-permute-start.8 = (f32[160,256]{1,0:T(8,128)S(1)}, f32[160,256]{1,0:T(8,128)S(1)}, u32[]{:S(2)}, u32[]{:S(2)}) collective-permute-start(f32[160,256]{1,0:T(8,128)S(1)} %get-tuple-element.49), channel_id=1, source_target_pairs={{0,24},{4,28},{8,16},{12,20},{16,8},{20,12},{24,0},{28,4},{1,25},{... | collective-permute-start | bytes 491528 | tf_op jit(solution)/shard_map/ppermute | solution.py:373
  27.0 8.6 %collective-permute-start.11 = (f32[160,256]{1,0:T(8,128)S(1)}, f32[160,256]{1,0:T(8,128)S(1)}, u32[]{:S(2)}, u32[]{:S(2)}) collective-permute-start(f32[160,256]{1,0:T(8,128)S(1)} %collective-permute-done.5.refs_0_.refs_5_), channel_id=1, source_target_pairs={{0,4},{2,6},{4,0},{6,2},{8,12},{10,14},{12,8},{14,10},{1,5},{3,7},... | collective-permute-start | bytes 491528 | tf_op jit(solution)/shard_map/ppermute | solution.py:365
  32.7 6.8 %collective-permute-start.10 = (f32[160,256]{1,0:T(8,128)S(1)}, f32[160,256]{1,0:T(8,128)S(1)}, u32[]{:S(2)}, u32[]{:S(2)}) collective-permute-start(f32[160,256]{1,0:T(8,128)S(1)} %get-tuple-element.47.refs_0_), channel_id=1, source_target_pairs={{0,8},{2,10},{4,12},{6,14},{8,0},{10,2},{12,4},{14,6},{1,9},{3,11}... | collective-permute-start | bytes 491528 | tf_op jit(solution)/shard_map/ppermute | solution.py:365
  34.9 4.5 %collective-permute-start.9 = (f32[160,256]{1,0:T(8,128)S(1)}, f32[160,256]{1,0:T(8,128)S(1)}, u32[]{:S(2)}, u32[]{:S(2)}) collective-permute-start(f32[160,256]{1,0:T(8,128)S(1)} %get-tuple-element.47.refs_0_), channel_id=1, source_target_pairs={{0,4},{2,6},{4,0},{6,2},{8,12},{10,14},{12,8},{14,10},{1,5},{3,7},... | collective-permute-start | bytes 491528 | tf_op jit(solution)/shard_map/ppermute | solution.py:365
  40.0 6.2 %collective-permute-start.13 = (f32[160,256]{1,0:T(8,128)S(1)}, f32[160,256]{1,0:T(8,128)S(1)}, u32[]{:S(2)}, u32[]{:S(2)}) collective-permute-start(f32[160,256]{1,0:T(8,128)S(1)} %get-tuple-element.53.refs_1_), channel_id=1, source_target_pairs={{0,8},{2,10},{4,12},{6,14},{8,0},{10,2},{12,4},{14,6},{1,9},{3,11}... | collective-permute-start | bytes 491528 | tf_op jit(solution)/shard_map/ppermute | solution.py:365
  41.6 6.2 %collective-permute-start.12 = (f32[160,256]{1,0:T(8,128)S(1)}, f32[160,256]{1,0:T(8,128)S(1)}, u32[]{:S(2)}, u32[]{:S(2)}) collective-permute-start(f32[160,256]{1,0:T(8,128)S(1)} %get-tuple-element.53.refs_1_), channel_id=1, source_target_pairs={{0,4},{2,6},{4,0},{6,2},{8,12},{10,14},{12,8},{14,10},{1,5},{3,7},... | collective-permute-start | bytes 491528 | tf_op jit(solution)/shard_map/ppermute | solution.py:365
  42.5 5.3 %collective-permute-start.14 = (f32[160,256]{1,0:T(8,128)S(1)}, f32[160,256]{1,0:T(8,128)S(1)}, u32[]{:S(2)}, u32[]{:S(2)}) collective-permute-start(f32[160,256]{1,0:T(8,128)S(1)} %collective-permute-done.9.refs_0_.refs_2_), channel_id=1, source_target_pairs={{0,8},{2,10},{4,12},{6,14},{8,0},{10,2},{12,4},{14,6},{1,9},{3,11}... | collective-permute-start | bytes 491528 | tf_op jit(solution)/shard_map/ppermute | solution.py:365
  46.2 4.2 %collective-permute-start.15 = (f32[160,256]{1,0:T(8,128)S(1)}, f32[160,256]{1,0:T(8,128)S(1)}, u32[]{:S(2)}, u32[]{:S(2)}) collective-permute-start(f32[160,256]{1,0:T(8,128)S(1)} %collective-permute-done.13.refs_5_), channel_id=1, source_target_pairs={{0,4},{2,6},{4,0},{6,2},{8,12},{10,14},{12,8},{14,10},{1,5},{3,7},... | collective-permute-start | bytes 491528 | tf_op jit(solution)/shard_map/ppermute | solution.py:365
  52.9 11.3 %collective-permute-start.16 = (f32[2,416,256]{2,1,0:T(8,128)S(1)}, f32[2,416,256]{2,1,0:T(8,128)S(1)}, u32[]{:S(2)}, u32[]{:S(2)}) collective-permute-start(f32[2,416,256]{2,1,0:T(8,128)S(1)} %get-tuple-element.58._), channel_id=1, source_target_pairs={{0,1},{1,0},{2,3},{3,2},{4,5},{5,4},{6,7},{7,6},{8,9},{9,8},{10,11... | collective-permute-start | bytes 2555912 | tf_op jit(solution)/shard_map/ppermute | solution.py:369
  64.8 5.5 %collective-permute-start.17 = (f32[160,256]{1,0:T(8,128)S(1)}, f32[160,256]{1,0:T(8,128)S(1)}, u32[]{:S(2)}, u32[]{:S(2)}) collective-permute-start(f32[160,256]{1,0:T(8,128)S(1)} %get-tuple-element.60), channel_id=1, source_target_pairs={{0,2},{2,0},{4,6},{6,4},{8,10},{10,8},{12,14},{14,12},{1,3},{3,1},... | collective-permute-start | bytes 491528 | tf_op jit(solution)/shard_map/ppermute | solution.py:365
  70.3 8.8 %collective-permute-start.18 = (f32[160,256]{1,0:T(8,128)S(1)}, f32[160,256]{1,0:T(8,128)S(1)}, u32[]{:S(2)}, u32[]{:S(2)}) collective-permute-start(f32[160,256]{1,0:T(8,128)S(1)} %add.10._.left_ref), channel_id=1, source_target_pairs={{0,24},{4,28},{8,16},{12,20},{16,8},{20,12},{24,0},{28,4},{1,25},{... | collective-permute-start | bytes 491528 | tf_op jit(solution)/shard_map/ppermute | solution.py:373
  79.1 4.2 %collective-permute-start.22 = (f32[160,256]{1,0:T(8,128)S(1)}, f32[160,256]{1,0:T(8,128)S(1)}, u32[]{:S(2)}, u32[]{:S(2)}) collective-permute-start(f32[160,256]{1,0:T(8,128)S(1)} %add.11), channel_id=1, source_target_pairs={{0,2},{2,0},{4,6},{6,4},{8,10},{10,8},{12,14},{14,12},{1,3},{3,1},... | collective-permute-start | bytes 491528 | tf_op jit(solution)/shard_map/ppermute | solution.py:365
  80.4 4.5 %collective-permute-start.20 = (f32[160,256]{1,0:T(8,128)S(1)}, f32[160,256]{1,0:T(8,128)S(1)}, u32[]{:S(2)}, u32[]{:S(2)}) collective-permute-start(f32[160,256]{1,0:T(8,128)S(1)} %add.11), channel_id=1, source_target_pairs={{0,8},{2,10},{4,12},{6,14},{8,0},{10,2},{12,4},{14,6},{1,9},{3,11}... | collective-permute-start | bytes 491528 | tf_op jit(solution)/shard_map/ppermute | solution.py:365
  80.4 5.0 %collective-permute-start.19 = (f32[160,256]{1,0:T(8,128)S(1)}, f32[160,256]{1,0:T(8,128)S(1)}, u32[]{:S(2)}, u32[]{:S(2)}) collective-permute-start(f32[160,256]{1,0:T(8,128)S(1)} %add.11), channel_id=1, source_target_pairs={{0,4},{2,6},{4,0},{6,2},{8,12},{10,14},{12,8},{14,10},{1,5},{3,7},... | collective-permute-start | bytes 491528 | tf_op jit(solution)/shard_map/ppermute | solution.py:365
  83.3 5.1 %collective-permute-start.24 = (f32[160,256]{1,0:T(8,128)S(1)}, f32[160,256]{1,0:T(8,128)S(1)}, u32[]{:S(2)}, u32[]{:S(2)}) collective-permute-start(f32[160,256]{1,0:T(8,128)S(1)} %collective-permute-done.22), channel_id=1, source_target_pairs={{0,8},{2,10},{4,12},{6,14},{8,0},{10,2},{12,4},{14,6},{1,9},{3,11}... | collective-permute-start | bytes 491528 | tf_op jit(solution)/shard_map/ppermute | solution.py:365
  84.8 4.5 %collective-permute-start.21 = (f32[160,256]{1,0:T(8,128)S(1)}, f32[160,256]{1,0:T(8,128)S(1)}, u32[]{:S(2)}, u32[]{:S(2)}) collective-permute-start(f32[160,256]{1,0:T(8,128)S(1)} %collective-permute-done.20), channel_id=1, source_target_pairs={{0,4},{2,6},{4,0},{6,2},{8,12},{10,14},{12,8},{14,10},{1,5},{3,7},... | collective-permute-start | bytes 491528 | tf_op jit(solution)/shard_map/ppermute | solution.py:365
  85.4 4.5 %collective-permute-start.23 = (f32[160,256]{1,0:T(8,128)S(1)}, f32[160,256]{1,0:T(8,128)S(1)}, u32[]{:S(2)}, u32[]{:S(2)}) collective-permute-start(f32[160,256]{1,0:T(8,128)S(1)} %collective-permute-done.19), channel_id=1, source_target_pairs={{0,2},{2,0},{4,6},{6,4},{8,10},{10,8},{12,14},{14,12},{1,3},{3,1},... | collective-permute-start | bytes 491528 | tf_op jit(solution)/shard_map/ppermute | solution.py:365
  88.4 5.9 %collective-permute-start.25 = (f32[160,256]{1,0:T(8,128)S(1)}, f32[160,256]{1,0:T(8,128)S(1)}, u32[]{:S(2)}, u32[]{:S(2)}) collective-permute-start(f32[160,256]{1,0:T(8,128)S(1)} %collective-permute-done.24), channel_id=1, source_target_pairs={{0,4},{2,6},{4,0},{6,2},{8,12},{10,14},{12,8},{14,10},{1,5},{3,7},... | collective-permute-start | bytes 491528 | tf_op jit(solution)/shard_map/ppermute | solution.py:365
  94.3 5.2 %collective-permute-start.26 = (f32[8,160,256]{2,1,0:T(8,128)S(1)}, f32[8,160,256]{2,1,0:T(8,128)S(1)}, u32[]{:S(2)}, u32[]{:S(2)}) collective-permute-start(f32[8,160,256]{2,1,0:T(8,128)S(1)} %bitcast_dynamic-update-slice_fusion.mine_ref), channel_id=1, source_target_pairs={{0,1},{1,0},{2,3},{3,2},{4,5},{5,4},{6,7},{7,6},{8,9},{9,8},{10,11... | collective-permute-start | bytes 3932168 | tf_op jit(solution)/shard_map/ppermute | solution.py:369
  96.9 11.1 %collective-permute-start.27 = (f32[256,256]{1,0:T(8,128)S(1)}, f32[256,256]{1,0:T(8,128)S(1)}, u32[]{:S(2)}, u32[]{:S(2)}) collective-permute-start(f32[256,256]{1,0:T(8,128)S(1)} %get-tuple-element.62.after_ref), channel_id=1, source_target_pairs={{0,2},{2,0},{4,6},{6,4},{8,10},{10,8},{12,14},{14,12},{1,3},{3,1},... | collective-permute-start | bytes 786440 | tf_op jit(solution)/shard_map/ppermute | solution.py:365
  108.0 13.6 %collective-permute-start.28 = (f32[256,256]{1,0:T(8,128)S(1)}, f32[256,256]{1,0:T(8,128)S(1)}, u32[]{:S(2)}, u32[]{:S(2)}) collective-permute-start(f32[256,256]{1,0:T(8,128)S(1)} %add.12.left_ref), channel_id=1, source_target_pairs={{0,24},{4,28},{8,16},{12,20},{16,8},{20,12},{24,0},{28,4},{1,25},{... | collective-permute-start | bytes 786440 | tf_op jit(solution)/shard_map/ppermute | solution.py:373
  121.6 7.6 %collective-permute-start.29 = (f32[256,256]{1,0:T(8,128)S(1)}, f32[256,256]{1,0:T(8,128)S(1)}, u32[]{:S(2)}, u32[]{:S(2)}) collective-permute-start(f32[256,256]{1,0:T(8,128)S(1)} %add.13.first_ref), channel_id=1, source_target_pairs={{0,2},{2,0},{4,6},{6,4},{8,10},{10,8},{12,14},{14,12},{1,3},{3,1},... | collective-permute-start | bytes 786440 | tf_op jit(solution)/shard_map/ppermute | solution.py:365
  129.3 7.7 %collective-permute-start.30 = (f32[2,256,256]{2,1,0:T(8,128)S(1)}, f32[2,256,256]{2,1,0:T(8,128)S(1)}, u32[]{:S(2)}, u32[]{:S(2)}) collective-permute-start(f32[2,256,256]{2,1,0:T(8,128)S(1)} %stack.61.refs_8_), channel_id=1, source_target_pairs={{0,1},{1,0},{2,3},{3,2},{4,5},{5,4},{6,7},{7,6},{8,9},{9,8},{10,11... | collective-permute-start | bytes 1572872 | tf_op jit(solution)/shard_map/ppermute | solution.py:369

commit v13 on v12

--- a/solution.py
+++ b/solution.py
@@ -370,7 +370,7 @@
 
 
 def other_group(value):
-    return lax.ppermute(value, ("hi", "lo"), [(i, i ^ 6) for i in range(2 * P_SIZE)])
+    return lax.ppermute(value, ("hi", "lo"), [(i, i ^ P_SIZE) for i in range(2 * P_SIZE)])
 
 
 def spread(piece):
@@ -388,8 +388,7 @@
     col_index = group * P_SIZE + low
     columns = arc_rows.shape[1]
     in_two = n_hi == 2
-    panel = low ^ (2 * group) if in_two else low
-    place = jnp.stack([side, high_row, panel, col_index, group]).astype(jnp.int32)
+    place = jnp.stack([side, high_row, low, col_index, group]).astype(jnp.int32)
     total = r_slab.shape[0] + arc_rows.shape[0]
     parts = 2 * CHUNKS if in_two else CHUNKS
     chunks = on_chip(

time: 141 us -> 144 us (1.021)
  the two profiles are of different devices: /device:TPU:9 before, /device:TPU:1 now
where the time goes in v13:
time: 144 us
  waiting for transfers between devices  60.9 us (42%)
  Pallas kernels  42.1 us (29%)
  starting transfers between devices  37.7 us (26%)
  local copies, waits for them, and re-layouts  3.08 us (2%)
    pallas_call x19, Pallas kernels, on_chip(): pl.pallas_call(kernel, out_shape=[jax.ShapeDtypeStruct(shape, jnp.float32...  42.1 us
    ppermute x22, waiting for transfers between devices, exchange(): lax.ppermute(value, ('lo', 'rh'), [(i, i ^ bits) for i in range(2 * P_SIZ...  29.4 us
    ppermute x6, waiting for transfers between devices, other_group(): lax.ppermute(value, ('hi', 'lo'), [(i, i ^ P_SIZE) for i in range(2 * P_S...  27.9 us
    ppermute x22, starting transfers between devices, exchange(): lax.ppermute(value, ('lo', 'rh'), [(i, i ^ bits) for i in range(2 * P_SIZ...  19.8 us
    ppermute x6, starting transfers between devices, other_group(): lax.ppermute(value, ('hi', 'lo'), [(i, i ^ P_SIZE) for i in range(2 * P_S...  9.4 us
    ppermute x3, starting transfers between devices, swap(): return lax.ppermute(value, axis, [(0, 1), (1, 0)])  8.49 us
    ppermute x3, waiting for transfers between devices, swap(): return lax.ppermute(value, axis, [(0, 1), (1, 0)])  3.61 us
    unnamed x12, local copies, waits for them, and re-layouts  2.99 us
  transfers between devices with their start and end apart: 31, of which 22 were waited for; matrix products, arithmetic and copies ran while one was open for 0% of the time, Pallas kernels for 23%

profile of v13, /device:TPU:1, one launch (start us, length us, event | category | flops | bytes accessed | tf_op | source)
XLA Modules:
  0.0 144.0 jit_solution(4437654767253122164)
XLA Ops:
  0.0 0.7 copy.4.arcs_ref
  0.8 1.2 copy-done
  2.0 0.9 copy-done.1
  3.0 0.8 mask.1
  3.8 3.2 %collective-permute-start.2 = (f32[160,256]{1,0:T(8,128)S(1)}, f32[160,256]{1,0:T(8,128)S(1)}, u32[]{:S(2)}, u32[]{:S(2)}) collective-permute-start(f32[160,256]{1,0:T(8,128)S(1)} %get-tuple-element.44), channel_id=1, source_target_pairs={{0,16},{4,20},{8,24},{12,28},{16,0},{20,4},{24,8},{28,12},{1,17},{... | collective-permute-start | bytes 491528 | tf_op jit(solution)/shard_map/ppermute | solution.py:373
  7.1 10.9 %collective-permute-done.2.got_ref = f32[160,256]{1,0:T(8,128)S(1)} collective-permute-done((f32[160,256]{1,0:T(8,128)S(1)}, f32[160,256]{1,0:T(8,128)S(1)}, u32[]{:S(2)}, u32[]{:S(2)}) %collective-permute-start.2) | collective-permute-done | bytes 163872 | tf_op jit(solution)/shard_map/ppermute | solution.py:373
  18.5 1.2 collective-permute-start.4
  19.7 1.2 collective-permute-start.3
  21.4 2.7 %collective-permute-done.4.refs_1_.refs_4_ = f32[160,256]{1,0:T(8,128)S(1)} collective-permute-done((f32[160,256]{1,0:T(8,128)S(1)}, f32[160,256]{1,0:T(8,128)S(1)}, u32[]{:S(2)}, u32[]{:S(2)}) %collective-permute-start.4) | collective-permute-done | bytes 163872 | tf_op jit(solution)/shard_map/ppermute | solution.py:365
  25.5 3.6 %collective-permute-start = (f32[160,256]{1,0:T(8,128)S(1)}, f32[160,256]{1,0:T(8,128)S(1)}, u32[]{:S(2)}, u32[]{:S(2)}) collective-permute-start(f32[160,256]{1,0:T(8,128)S(1)} %get-tuple-element.40), channel_id=1, source_target_pairs={{0,16},{4,20},{8,24},{12,28},{16,0},{20,4},{24,8},{28,12},{1,17},{... | collective-permute-start | bytes 491528 | tf_op jit(solution)/shard_map/ppermute | solution.py:373
  29.2 1.2 collective-permute-start.6
  31.3 1.8 %collective-permute-done.got_ref = f32[160,256]{1,0:T(8,128)S(1)} collective-permute-done((f32[160,256]{1,0:T(8,128)S(1)}, f32[160,256]{1,0:T(8,128)S(1)}, u32[]{:S(2)}, u32[]{:S(2)}) %collective-permute-start) | collective-permute-done | bytes 163872 | tf_op jit(solution)/shard_map/ppermute | solution.py:373
  33.6 6.4 %collective-permute-done.7.refs_2_.refs_6_ = f32[160,256]{1,0:T(8,128)S(1)} collective-permute-done((f32[160,256]{1,0:T(8,128)S(1)}, f32[160,256]{1,0:T(8,128)S(1)}, u32[]{:S(2)}, u32[]{:S(2)}) %collective-permute-start.7) | collective-permute-done | bytes 163872 | tf_op jit(solution)/shard_map/ppermute | solution.py:365
  40.7 0.6 collective-permute-start.9
  41.3 2.5 %first_products.1 = (f32[640,256]{1,0:T(8,128)S(1)}, f32[4,256,256]{2,1,0:T(8,128)S(1)}) custom-call(s32[5]{0:T(128)S(1)} %stack.51.place_ref, f32[160,256]{1,0:T(8,128)S(1)} %get-tuple-element.45.refs_0_, f32[160,256]{1,0:T(8,128)S(1)} %get-tuple-element.46.refs_1_, f32[160,256]{1,0:T(8,128)S(1)} %collective-permute-done.3.refs_0_.refs_2_, ...), custom_call_target="tpu_custom_call" | custom-call | tf_op jit(solution)/shard_map/first_products/pallas_call | solution.py:209
  43.8 1.0 collective-permute-done.10.refs_1_.refs_4_
  45.5 1.7 %collective-permute-start.13 = (f32[160,256]{1,0:T(8,128)S(1)}, f32[160,256]{1,0:T(8,128)S(1)}, u32[]{:S(2)}, u32[]{:S(2)}) collective-permute-start(f32[160,256]{1,0:T(8,128)S(1)} %get-tuple-element.53.refs_1_), channel_id=1, source_target_pairs={{0,8},{2,10},{4,12},{6,14},{8,0},{10,2},{12,4},{14,6},{1,9},{3,11}... | collective-permute-start | bytes 491528 | tf_op jit(solution)/shard_map/ppermute | solution.py:365
  48.3 1.6 %collective-permute-done.13.refs_5_ = f32[160,256]{1,0:T(8,128)S(1)} collective-permute-done((f32[160,256]{1,0:T(8,128)S(1)}, f32[160,256]{1,0:T(8,128)S(1)}, u32[]{:S(2)}, u32[]{:S(2)}) %collective-permute-start.13) | collective-permute-done | bytes 163872 | tf_op jit(solution)/shard_map/ppermute | solution.py:365
  49.9 1.1 collective-permute-start.15
  51.0 1.0 collective-permute-done.14.refs_6_
  52.0 3.3 %collective-permute-done.15.refs_7_ = f32[160,256]{1,0:T(8,128)S(1)} collective-permute-done((f32[160,256]{1,0:T(8,128)S(1)}, f32[160,256]{1,0:T(8,128)S(1)}, u32[]{:S(2)}, u32[]{:S(2)}) %collective-permute-start.15) | collective-permute-done | bytes 163872 | tf_op jit(solution)/shard_map/ppermute | solution.py:365
  55.3 2.7 %products.1 = (f32[2,160,256]{2,1,0:T(8,128)S(1)}, f32[2,256,256]{2,1,0:T(8,128)S(1)}, f32[2,416,256]{2,1,0:T(8,128)S(1)}) custom-call(s32[5]{0:T(128)S(1)} %stack.51.place_ref, f32[160,256]{1,0:T(8,128)S(1)} %get-tuple-element.47.refs_0_, f32[160,256]{1,0:T(8,128)S(1)} %get-tuple-element.53.refs_1_, f32[160,256]{1,0:T(8,128)S(1)} %collective-permute-done.9.refs_0_.refs_2_, ...), custom_call_target="tpu_custom_call" | custom-call | tf_op jit(solution)/shard_map/products/pallas_call | solution.py:209
  58.0 4.5 %collective-permute-start.16 = (f32[2,416,256]{2,1,0:T(8,128)S(1)}, f32[2,416,256]{2,1,0:T(8,128)S(1)}, u32[]{:S(2)}, u32[]{:S(2)}) collective-permute-start(f32[2,416,256]{2,1,0:T(8,128)S(1)} %get-tuple-element.58._), channel_id=1, source_target_pairs={{0,1},{1,0},{2,3},{3,2},{4,5},{5,4},{6,7},{7,6},{8,9},{9,8},{10,11... | collective-permute-start | bytes 2555912 | tf_op jit(solution)/shard_map/ppermute | solution.py:369
  62.5 2.0 %collective-permute-done.16.got_ref = f32[2,416,256]{2,1,0:T(8,128)S(1)} collective-permute-done((f32[2,416,256]{2,1,0:T(8,128)S(1)}, f32[2,416,256]{2,1,0:T(8,128)S(1)}, u32[]{:S(2)}, u32[]{:S(2)}) %collective-permute-start.16) | collective-permute-done | bytes 852000 | tf_op jit(solution)/shard_map/ppermute | solution.py:369
  65.1 1.8 %collective-permute-start.17 = (f32[160,256]{1,0:T(8,128)S(1)}, f32[160,256]{1,0:T(8,128)S(1)}, u32[]{:S(2)}, u32[]{:S(2)}) collective-permute-start(f32[160,256]{1,0:T(8,128)S(1)} %get-tuple-element.60), channel_id=1, source_target_pairs={{0,2},{2,0},{4,6},{6,4},{8,10},{10,8},{12,14},{14,12},{1,3},{3,1},... | collective-permute-start | bytes 491528 | tf_op jit(solution)/shard_map/ppermute | solution.py:365
  66.9 4.2 %collective-permute-done.17 = f32[160,256]{1,0:T(8,128)S(1)} collective-permute-done((f32[160,256]{1,0:T(8,128)S(1)}, f32[160,256]{1,0:T(8,128)S(1)}, u32[]{:S(2)}, u32[]{:S(2)}) %collective-permute-start.17) | collective-permute-done | bytes 163872 | tf_op jit(solution)/shard_map/ppermute | solution.py:365
  71.2 2.1 %collective-permute-start.18 = (f32[160,256]{1,0:T(8,128)S(1)}, f32[160,256]{1,0:T(8,128)S(1)}, u32[]{:S(2)}, u32[]{:S(2)}) collective-permute-start(f32[160,256]{1,0:T(8,128)S(1)} %add.10._.left_ref), channel_id=1, source_target_pairs={{0,16},{4,20},{8,24},{12,28},{16,0},{20,4},{24,8},{28,12},{1,17},{... | collective-permute-start | bytes 491528 | tf_op jit(solution)/shard_map/ppermute | solution.py:373
  73.9 7.7 %collective-permute-done.18.right_ref = f32[160,256]{1,0:T(8,128)S(1)} collective-permute-done((f32[160,256]{1,0:T(8,128)S(1)}, f32[160,256]{1,0:T(8,128)S(1)}, u32[]{:S(2)}, u32[]{:S(2)}) %collective-permute-start.18) | collective-permute-done | bytes 163872 | tf_op jit(solution)/shard_map/ppermute | solution.py:373
  81.6 1.1 collective-permute-start.22
  82.7 1.5 %collective-permute-start.19 = (f32[160,256]{1,0:T(8,128)S(1)}, f32[160,256]{1,0:T(8,128)S(1)}, u32[]{:S(2)}, u32[]{:S(2)}) collective-permute-start(f32[160,256]{1,0:T(8,128)S(1)} %add.11), channel_id=1, source_target_pairs={{0,4},{2,6},{4,0},{6,2},{8,12},{10,14},{12,8},{14,10},{1,5},{3,7},... | collective-permute-start | bytes 491528 | tf_op jit(solution)/shard_map/ppermute | solution.py:365
  84.2 2.5 %collective-permute-done.22 = f32[160,256]{1,0:T(8,128)S(1)} collective-permute-done((f32[160,256]{1,0:T(8,128)S(1)}, f32[160,256]{1,0:T(8,128)S(1)}, u32[]{:S(2)}, u32[]{:S(2)}) %collective-permute-start.22) | collective-permute-done | bytes 163872 | tf_op jit(solution)/shard_map/ppermute | solution.py:365
  87.3 1.8 %collective-permute-start.21 = (f32[160,256]{1,0:T(8,128)S(1)}, f32[160,256]{1,0:T(8,128)S(1)}, u32[]{:S(2)}, u32[]{:S(2)}) collective-permute-start(f32[160,256]{1,0:T(8,128)S(1)} %collective-permute-done.20), channel_id=1, source_target_pairs={{0,4},{2,6},{4,0},{6,2},{8,12},{10,14},{12,8},{14,10},{1,5},{3,7},... | collective-permute-start | bytes 491528 | tf_op jit(solution)/shard_map/ppermute | solution.py:365
  89.5 1.4 collective-permute-done.24
  90.9 1.5 %collective-permute-start.25 = (f32[160,256]{1,0:T(8,128)S(1)}, f32[160,256]{1,0:T(8,128)S(1)}, u32[]{:S(2)}, u32[]{:S(2)}) collective-permute-start(f32[160,256]{1,0:T(8,128)S(1)} %collective-permute-done.24), channel_id=1, source_target_pairs={{0,4},{2,6},{4,0},{6,2},{8,12},{10,14},{12,8},{14,10},{1,5},{3,7},... | collective-permute-start | bytes 491528 | tf_op jit(solution)/shard_map/ppermute | solution.py:365
  92.4 1.1 collective-permute-done.23
  93.6 2.4 %collective-permute-done.25 = f32[160,256]{1,0:T(8,128)S(1)} collective-permute-done((f32[160,256]{1,0:T(8,128)S(1)}, f32[160,256]{1,0:T(8,128)S(1)}, u32[]{:S(2)}, u32[]{:S(2)}) %collective-permute-start.25) | collective-permute-done | bytes 163872 | tf_op jit(solution)/shard_map/ppermute | solution.py:365
  96.0 3.0 %collective-permute-start.26 = (f32[8,160,256]{2,1,0:T(8,128)S(1)}, f32[8,160,256]{2,1,0:T(8,128)S(1)}, u32[]{:S(2)}, u32[]{:S(2)}) collective-permute-start(f32[8,160,256]{2,1,0:T(8,128)S(1)} %bitcast_dynamic-update-slice_fusion.mine_ref), channel_id=1, source_target_pairs={{0,1},{1,0},{2,3},{3,2},{4,5},{5,4},{6,7},{7,6},{8,9},{9,8},{10,11... | collective-permute-start | bytes 3932168 | tf_op jit(solution)/shard_map/ppermute | solution.py:369
  99.0 1.1 collective-permute-start.27
  100.0 1.6 %collective-permute-done.26.other_ref = f32[8,160,256]{2,1,0:T(8,128)S(1)} collective-permute-done((f32[8,160,256]{2,1,0:T(8,128)S(1)}, f32[8,160,256]{2,1,0:T(8,128)S(1)}, u32[]{:S(2)}, u32[]{:S(2)}) %collective-permute-start.26) | collective-permute-done | bytes 1310752 | tf_op jit(solution)/shard_map/ppermute | solution.py:369
  101.6 1.1 collect.1.gram_ref.refs_7_
  102.7 7.3 %factor_step.4 = (f32[256,768]{1,0:T(8,128)S(1)}, f32[256,256]{1,0:T(8,128)S(1)}, f32[6,256,256]{2,1,0:T(8,128)S(1)}) custom-call(f32[10,256,256]{2,1,0:T(8,128)S(1)} %collect.1.gram_ref.refs_7_), custom_call_target="tpu_custom_call" | custom-call | tf_op jit(solution)/shard_map/factor_step/pallas_call | solution.py:209
  110.5 7.0 %factor_step.5 = (f32[256,512]{1,0:T(8,128)S(1)}, f32[256,256]{1,0:T(8,128)S(1)}, f32[3,256,256]{2,1,0:T(8,128)S(1)}) custom-call(f32[6,256,256]{2,1,0:T(8,128)S(1)} %get-tuple-element.64.gram_ref), custom_call_target="tpu_custom_call" | custom-call | tf_op jit(solution)/shard_map/factor_step/pallas_call | solution.py:209
  117.5 7.1 %collective-permute-done.28.right_ref = f32[256,256]{1,0:T(8,128)S(1)} collective-permute-done((f32[256,256]{1,0:T(8,128)S(1)}, f32[256,256]{1,0:T(8,128)S(1)}, u32[]{:S(2)}, u32[]{:S(2)}) %collective-permute-start.28) | collective-permute-done | bytes 262176 | tf_op jit(solution)/shard_map/ppermute | solution.py:373
  124.6 1.1 collective-permute-start.29
  125.8 6.7 %factor_step.6 = (f32[256,256]{1,0:T(8,128)S(1)}, f32[256,256]{1,0:T(8,128)S(1)}, f32[1,256,256]{2,1,0:T(8,128)S(1)}) custom-call(f32[3,256,256]{2,1,0:T(8,128)S(1)} %get-tuple-element.66.gram_ref), custom_call_target="tpu_custom_call" | custom-call | tf_op jit(solution)/shard_map/factor_step/pallas_call | solution.py:209
  132.5 1.0 collective-permute-start.30
  133.5 6.4 %factor_step.7.refs_6_ = f32[256,256]{1,0:T(8,128)S(1)} custom-call(f32[1,256,256]{2,1,0:T(8,128)S(1)} %get-tuple-element.71.gram_ref), custom_call_target="tpu_custom_call" | custom-call | tf_op jit(solution)/shard_map/factor_step/pallas_call | solution.py:209
  140.0 4.1 %solve.1 = f32[256,256]{1,0:T(8,128)} custom-call(s32[5]{0:T(128)S(1)} %stack.51.place_ref, f32[256,768]{1,0:T(8,128)S(1)} %get-tuple-element.63.after_ref.refs_0_, f32[256,512]{1,0:T(8,128)S(1)} %get-tuple-element.65.after_ref.refs_1_, f32[256,256]{1,0:T(8,128)S(1)} %get-tuple-element.67._.refs_2_, f32[256,256]{1,0:T(8,128)S(1)} %get-tuple-element.68.refs_3_, ...), custom_call_target="tpu_custom_call" | custom-call | tf_op jit(solution)/shard_map/solve/pallas_call | solution.py:209
  (48 shorter events, 9.0 us)
Async XLA Ops:
  0.8 1.2 copy-start
  2.0 0.9 copy-start.1
  3.8 14.2 %collective-permute-start.2 = (f32[160,256]{1,0:T(8,128)S(1)}, f32[160,256]{1,0:T(8,128)S(1)}, u32[]{:S(2)}, u32[]{:S(2)}) collective-permute-start(f32[160,256]{1,0:T(8,128)S(1)} %get-tuple-element.44), channel_id=1, source_target_pairs={{0,16},{4,20},{8,24},{12,28},{16,0},{20,4},{24,8},{28,12},{1,17},{... | collective-permute-start | bytes 491528 | tf_op jit(solution)/shard_map/ppermute | solution.py:373
  7.0 14.5 %collective-permute-start.1 = (f32[160,256]{1,0:T(8,128)S(1)}, f32[160,256]{1,0:T(8,128)S(1)}, u32[]{:S(2)}, u32[]{:S(2)}) collective-permute-start(f32[160,256]{1,0:T(8,128)S(1)} %get-tuple-element.42), channel_id=1, source_target_pairs={{0,16},{4,20},{8,24},{12,28},{16,0},{20,4},{24,8},{28,12},{1,17},{... | collective-permute-start | bytes 491528 | tf_op jit(solution)/shard_map/ppermute | solution.py:373
  18.5 5.7 %collective-permute-start.4 = (f32[160,256]{1,0:T(8,128)S(1)}, f32[160,256]{1,0:T(8,128)S(1)}, u32[]{:S(2)}, u32[]{:S(2)}) collective-permute-start(f32[160,256]{1,0:T(8,128)S(1)} %get-tuple-element.45.refs_0_), channel_id=1, source_target_pairs={{0,8},{2,10},{4,12},{6,14},{8,0},{10,2},{12,4},{14,6},{1,9},{3,11}... | collective-permute-start | bytes 491528 | tf_op jit(solution)/shard_map/ppermute | solution.py:365
  19.7 4.7 %collective-permute-start.3 = (f32[160,256]{1,0:T(8,128)S(1)}, f32[160,256]{1,0:T(8,128)S(1)}, u32[]{:S(2)}, u32[]{:S(2)}) collective-permute-start(f32[160,256]{1,0:T(8,128)S(1)} %get-tuple-element.45.refs_0_), channel_id=1, source_target_pairs={{0,4},{2,6},{4,0},{6,2},{8,12},{10,14},{12,8},{14,10},{1,5},{3,7},... | collective-permute-start | bytes 491528 | tf_op jit(solution)/shard_map/ppermute | solution.py:365
  25.1 6.0 %collective-permute-start.5 = (f32[160,256]{1,0:T(8,128)S(1)}, f32[160,256]{1,0:T(8,128)S(1)}, u32[]{:S(2)}, u32[]{:S(2)}) collective-permute-start(f32[160,256]{1,0:T(8,128)S(1)} %get-tuple-element.46.refs_1_), channel_id=1, source_target_pairs={{0,8},{2,10},{4,12},{6,14},{8,0},{10,2},{12,4},{14,6},{1,9},{3,11}... | collective-permute-start | bytes 491528 | tf_op jit(solution)/shard_map/ppermute | solution.py:365
  25.5 7.6 %collective-permute-start = (f32[160,256]{1,0:T(8,128)S(1)}, f32[160,256]{1,0:T(8,128)S(1)}, u32[]{:S(2)}, u32[]{:S(2)}) collective-permute-start(f32[160,256]{1,0:T(8,128)S(1)} %get-tuple-element.40), channel_id=1, source_target_pairs={{0,16},{4,20},{8,24},{12,28},{16,0},{20,4},{24,8},{28,12},{1,17},{... | collective-permute-start | bytes 491528 | tf_op jit(solution)/shard_map/ppermute | solution.py:373
  29.2 4.5 %collective-permute-start.6 = (f32[160,256]{1,0:T(8,128)S(1)}, f32[160,256]{1,0:T(8,128)S(1)}, u32[]{:S(2)}, u32[]{:S(2)}) collective-permute-start(f32[160,256]{1,0:T(8,128)S(1)} %get-tuple-element.46.refs_1_), channel_id=1, source_target_pairs={{0,4},{2,6},{4,0},{6,2},{8,12},{10,14},{12,8},{14,10},{1,5},{3,7},... | collective-permute-start | bytes 491528 | tf_op jit(solution)/shard_map/ppermute | solution.py:365
  30.4 9.6 %collective-permute-start.7 = (f32[160,256]{1,0:T(8,128)S(1)}, f32[160,256]{1,0:T(8,128)S(1)}, u32[]{:S(2)}, u32[]{:S(2)}) collective-permute-start(f32[160,256]{1,0:T(8,128)S(1)} %collective-permute-done.3.refs_0_.refs_2_), channel_id=1, source_target_pairs={{0,8},{2,10},{4,12},{6,14},{8,0},{10,2},{12,4},{14,6},{1,9},{3,11}... | collective-permute-start | bytes 491528 | tf_op jit(solution)/shard_map/ppermute | solution.py:365
  31.1 12.7 %collective-permute-start.8 = (f32[160,256]{1,0:T(8,128)S(1)}, f32[160,256]{1,0:T(8,128)S(1)}, u32[]{:S(2)}, u32[]{:S(2)}) collective-permute-start(f32[160,256]{1,0:T(8,128)S(1)} %get-tuple-element.49), channel_id=1, source_target_pairs={{0,16},{4,20},{8,24},{12,28},{16,0},{20,4},{24,8},{28,12},{1,17},{... | collective-permute-start | bytes 491528 | tf_op jit(solution)/shard_map/ppermute | solution.py:373
  31.1 10.3 %collective-permute-start.11 = (f32[160,256]{1,0:T(8,128)S(1)}, f32[160,256]{1,0:T(8,128)S(1)}, u32[]{:S(2)}, u32[]{:S(2)}) collective-permute-start(f32[160,256]{1,0:T(8,128)S(1)} %collective-permute-done.5.refs_0_.refs_5_), channel_id=1, source_target_pairs={{0,4},{2,6},{4,0},{6,2},{8,12},{10,14},{12,8},{14,10},{1,5},{3,7},... | collective-permute-start | bytes 491528 | tf_op jit(solution)/shard_map/ppermute | solution.py:365
  40.6 4.2 %collective-permute-start.10 = (f32[160,256]{1,0:T(8,128)S(1)}, f32[160,256]{1,0:T(8,128)S(1)}, u32[]{:S(2)}, u32[]{:S(2)}) collective-permute-start(f32[160,256]{1,0:T(8,128)S(1)} %get-tuple-element.47.refs_0_), channel_id=1, source_target_pairs={{0,8},{2,10},{4,12},{6,14},{8,0},{10,2},{12,4},{14,6},{1,9},{3,11}... | collective-permute-start | bytes 491528 | tf_op jit(solution)/shard_map/ppermute | solution.py:365
  40.7 4.2 %collective-permute-start.9 = (f32[160,256]{1,0:T(8,128)S(1)}, f32[160,256]{1,0:T(8,128)S(1)}, u32[]{:S(2)}, u32[]{:S(2)}) collective-permute-start(f32[160,256]{1,0:T(8,128)S(1)} %get-tuple-element.47.refs_0_), channel_id=1, source_target_pairs={{0,4},{2,6},{4,0},{6,2},{8,12},{10,14},{12,8},{14,10},{1,5},{3,7},... | collective-permute-start | bytes 491528 | tf_op jit(solution)/shard_map/ppermute | solution.py:365
  45.5 4.5 %collective-permute-start.13 = (f32[160,256]{1,0:T(8,128)S(1)}, f32[160,256]{1,0:T(8,128)S(1)}, u32[]{:S(2)}, u32[]{:S(2)}) collective-permute-start(f32[160,256]{1,0:T(8,128)S(1)} %get-tuple-element.53.refs_1_), channel_id=1, source_target_pairs={{0,8},{2,10},{4,12},{6,14},{8,0},{10,2},{12,4},{14,6},{1,9},{3,11}... | collective-permute-start | bytes 491528 | tf_op jit(solution)/shard_map/ppermute | solution.py:365
  47.2 4.8 %collective-permute-start.12 = (f32[160,256]{1,0:T(8,128)S(1)}, f32[160,256]{1,0:T(8,128)S(1)}, u32[]{:S(2)}, u32[]{:S(2)}) collective-permute-start(f32[160,256]{1,0:T(8,128)S(1)} %get-tuple-element.53.refs_1_), channel_id=1, source_target_pairs={{0,4},{2,6},{4,0},{6,2},{8,12},{10,14},{12,8},{14,10},{1,5},{3,7},... | collective-permute-start | bytes 491528 | tf_op jit(solution)/shard_map/ppermute | solution.py:365
  47.8 4.2 %collective-permute-start.14 = (f32[160,256]{1,0:T(8,128)S(1)}, f32[160,256]{1,0:T(8,128)S(1)}, u32[]{:S(2)}, u32[]{:S(2)}) collective-permute-start(f32[160,256]{1,0:T(8,128)S(1)} %collective-permute-done.9.refs_0_.refs_2_), channel_id=1, source_target_pairs={{0,8},{2,10},{4,12},{6,14},{8,0},{10,2},{12,4},{14,6},{1,9},{3,11}... | collective-permute-start | bytes 491528 | tf_op jit(solution)/shard_map/ppermute | solution.py:365
  49.9 5.4 %collective-permute-start.15 = (f32[160,256]{1,0:T(8,128)S(1)}, f32[160,256]{1,0:T(8,128)S(1)}, u32[]{:S(2)}, u32[]{:S(2)}) collective-permute-start(f32[160,256]{1,0:T(8,128)S(1)} %collective-permute-done.13.refs_5_), channel_id=1, source_target_pairs={{0,4},{2,6},{4,0},{6,2},{8,12},{10,14},{12,8},{14,10},{1,5},{3,7},... | collective-permute-start | bytes 491528 | tf_op jit(solution)/shard_map/ppermute | solution.py:365
  58.0 6.5 %collective-permute-start.16 = (f32[2,416,256]{2,1,0:T(8,128)S(1)}, f32[2,416,256]{2,1,0:T(8,128)S(1)}, u32[]{:S(2)}, u32[]{:S(2)}) collective-permute-start(f32[2,416,256]{2,1,0:T(8,128)S(1)} %get-tuple-element.58._), channel_id=1, source_target_pairs={{0,1},{1,0},{2,3},{3,2},{4,5},{5,4},{6,7},{7,6},{8,9},{9,8},{10,11... | collective-permute-start | bytes 2555912 | tf_op jit(solution)/shard_map/ppermute | solution.py:369
  65.1 6.0 %collective-permute-start.17 = (f32[160,256]{1,0:T(8,128)S(1)}, f32[160,256]{1,0:T(8,128)S(1)}, u32[]{:S(2)}, u32[]{:S(2)}) collective-permute-start(f32[160,256]{1,0:T(8,128)S(1)} %get-tuple-element.60), channel_id=1, source_target_pairs={{0,2},{2,0},{4,6},{6,4},{8,10},{10,8},{12,14},{14,12},{1,3},{3,1},... | collective-permute-start | bytes 491528 | tf_op jit(solution)/shard_map/ppermute | solution.py:365
  71.2 10.4 %collective-permute-start.18 = (f32[160,256]{1,0:T(8,128)S(1)}, f32[160,256]{1,0:T(8,128)S(1)}, u32[]{:S(2)}, u32[]{:S(2)}) collective-permute-start(f32[160,256]{1,0:T(8,128)S(1)} %add.10._.left_ref), channel_id=1, source_target_pairs={{0,16},{4,20},{8,24},{12,28},{16,0},{20,4},{24,8},{28,12},{1,17},{... | collective-permute-start | bytes 491528 | tf_op jit(solution)/shard_map/ppermute | solution.py:373
  81.6 5.1 %collective-permute-start.22 = (f32[160,256]{1,0:T(8,128)S(1)}, f32[160,256]{1,0:T(8,128)S(1)}, u32[]{:S(2)}, u32[]{:S(2)}) collective-permute-start(f32[160,256]{1,0:T(8,128)S(1)} %add.11), channel_id=1, source_target_pairs={{0,2},{2,0},{4,6},{6,4},{8,10},{10,8},{12,14},{14,12},{1,3},{3,1},... | collective-permute-start | bytes 491528 | tf_op jit(solution)/shard_map/ppermute | solution.py:365
  82.7 4.6 %collective-permute-start.20 = (f32[160,256]{1,0:T(8,128)S(1)}, f32[160,256]{1,0:T(8,128)S(1)}, u32[]{:S(2)}, u32[]{:S(2)}) collective-permute-start(f32[160,256]{1,0:T(8,128)S(1)} %add.11), channel_id=1, source_target_pairs={{0,8},{2,10},{4,12},{6,14},{8,0},{10,2},{12,4},{14,6},{1,9},{3,11}... | collective-permute-start | bytes 491528 | tf_op jit(solution)/shard_map/ppermute | solution.py:365
  82.7 6.4 %collective-permute-start.19 = (f32[160,256]{1,0:T(8,128)S(1)}, f32[160,256]{1,0:T(8,128)S(1)}, u32[]{:S(2)}, u32[]{:S(2)}) collective-permute-start(f32[160,256]{1,0:T(8,128)S(1)} %add.11), channel_id=1, source_target_pairs={{0,4},{2,6},{4,0},{6,2},{8,12},{10,14},{12,8},{14,10},{1,5},{3,7},... | collective-permute-start | bytes 491528 | tf_op jit(solution)/shard_map/ppermute | solution.py:365
  86.7 4.2 %collective-permute-start.24 = (f32[160,256]{1,0:T(8,128)S(1)}, f32[160,256]{1,0:T(8,128)S(1)}, u32[]{:S(2)}, u32[]{:S(2)}) collective-permute-start(f32[160,256]{1,0:T(8,128)S(1)} %collective-permute-done.22), channel_id=1, source_target_pairs={{0,8},{2,10},{4,12},{6,14},{8,0},{10,2},{12,4},{14,6},{1,9},{3,11}... | collective-permute-start | bytes 491528 | tf_op jit(solution)/shard_map/ppermute | solution.py:365
  87.3 5.1 %collective-permute-start.21 = (f32[160,256]{1,0:T(8,128)S(1)}, f32[160,256]{1,0:T(8,128)S(1)}, u32[]{:S(2)}, u32[]{:S(2)}) collective-permute-start(f32[160,256]{1,0:T(8,128)S(1)} %collective-permute-done.20), channel_id=1, source_target_pairs={{0,4},{2,6},{4,0},{6,2},{8,12},{10,14},{12,8},{14,10},{1,5},{3,7},... | collective-permute-start | bytes 491528 | tf_op jit(solution)/shard_map/ppermute | solution.py:365
  89.1 4.5 %collective-permute-start.23 = (f32[160,256]{1,0:T(8,128)S(1)}, f32[160,256]{1,0:T(8,128)S(1)}, u32[]{:S(2)}, u32[]{:S(2)}) collective-permute-start(f32[160,256]{1,0:T(8,128)S(1)} %collective-permute-done.19), channel_id=1, source_target_pairs={{0,2},{2,0},{4,6},{6,4},{8,10},{10,8},{12,14},{14,12},{1,3},{3,1},... | collective-permute-start | bytes 491528 | tf_op jit(solution)/shard_map/ppermute | solution.py:365
  90.9 5.1 %collective-permute-start.25 = (f32[160,256]{1,0:T(8,128)S(1)}, f32[160,256]{1,0:T(8,128)S(1)}, u32[]{:S(2)}, u32[]{:S(2)}) collective-permute-start(f32[160,256]{1,0:T(8,128)S(1)} %collective-permute-done.24), channel_id=1, source_target_pairs={{0,4},{2,6},{4,0},{6,2},{8,12},{10,14},{12,8},{14,10},{1,5},{3,7},... | collective-permute-start | bytes 491528 | tf_op jit(solution)/shard_map/ppermute | solution.py:365
  96.0 5.6 %collective-permute-start.26 = (f32[8,160,256]{2,1,0:T(8,128)S(1)}, f32[8,160,256]{2,1,0:T(8,128)S(1)}, u32[]{:S(2)}, u32[]{:S(2)}) collective-permute-start(f32[8,160,256]{2,1,0:T(8,128)S(1)} %bitcast_dynamic-update-slice_fusion.mine_ref), channel_id=1, source_target_pairs={{0,1},{1,0},{2,3},{3,2},{4,5},{5,4},{6,7},{7,6},{8,9},{9,8},{10,11... | collective-permute-start | bytes 3932168 | tf_op jit(solution)/shard_map/ppermute | solution.py:369
  99.0 11.1 %collective-permute-start.27 = (f32[256,256]{1,0:T(8,128)S(1)}, f32[256,256]{1,0:T(8,128)S(1)}, u32[]{:S(2)}, u32[]{:S(2)}) collective-permute-start(f32[256,256]{1,0:T(8,128)S(1)} %get-tuple-element.62.after_ref), channel_id=1, source_target_pairs={{0,2},{2,0},{4,6},{6,4},{8,10},{10,8},{12,14},{14,12},{1,3},{3,1},... | collective-permute-start | bytes 786440 | tf_op jit(solution)/shard_map/ppermute | solution.py:365
  110.1 14.5 %collective-permute-start.28 = (f32[256,256]{1,0:T(8,128)S(1)}, f32[256,256]{1,0:T(8,128)S(1)}, u32[]{:S(2)}, u32[]{:S(2)}) collective-permute-start(f32[256,256]{1,0:T(8,128)S(1)} %add.12.left_ref), channel_id=1, source_target_pairs={{0,16},{4,20},{8,24},{12,28},{16,0},{20,4},{24,8},{28,12},{1,17},{... | collective-permute-start | bytes 786440 | tf_op jit(solution)/shard_map/ppermute | solution.py:373
  124.6 7.8 %collective-permute-start.29 = (f32[256,256]{1,0:T(8,128)S(1)}, f32[256,256]{1,0:T(8,128)S(1)}, u32[]{:S(2)}, u32[]{:S(2)}) collective-permute-start(f32[256,256]{1,0:T(8,128)S(1)} %add.13.first_ref), channel_id=1, source_target_pairs={{0,2},{2,0},{4,6},{6,4},{8,10},{10,8},{12,14},{14,12},{1,3},{3,1},... | collective-permute-start | bytes 786440 | tf_op jit(solution)/shard_map/ppermute | solution.py:365
  132.5 7.5 %collective-permute-start.30 = (f32[2,256,256]{2,1,0:T(8,128)S(1)}, f32[2,256,256]{2,1,0:T(8,128)S(1)}, u32[]{:S(2)}, u32[]{:S(2)}) collective-permute-start(f32[2,256,256]{2,1,0:T(8,128)S(1)} %stack.61.refs_8_), channel_id=1, source_target_pairs={{0,1},{1,0},{2,3},{3,2},{4,5},{5,4},{6,7},{7,6},{8,9},{9,8},{10,11... | collective-permute-start | bytes 1572872 | tf_op jit(solution)/shard_map/ppermute | solution.py:369

commit v14 on v12

--- a/solution.py
+++ b/solution.py
@@ -288,10 +288,12 @@
         row = work[:, B:]
         row_ref[...] = row
         at = n
+        left, right = left_parts(row), right_parts(row)
         for r in range(1, n):
-            left = row[:, (r - 1) * B : r * B]
-            for c in range(r, n):
-                next_ref[at - n] = gram_ref[at] - dot_t(left, row[:, (c - 1) * B : c * B])
+            off = (r - 1) * B
+            update = parts_dot(left[:, off : off + B], right[:, off:])
+            for c in range(n - r):
+                next_ref[at - n] = gram_ref[at] - update[:, c * B : (c + 1) * B]
                 at += 1
 
 
@@ -336,9 +338,9 @@
     done = []
     for i in range(P_SIZE):
         block = own_ref[i]
-        for k in range(i):
-            off = (i - k - 1) * B
-            block = block - dot_t(rows[k][:, off : off + B], done[k])
+        if i:
+            above = [rows[k][:, (i - k - 1) * B : (i - k) * B] for k in range(i)]
+            block = block - dot_t(jnp.concatenate(above, axis=0), jnp.concatenate(done, axis=0))
         block = dot(inverses[i][...], block)
         done.append(block)
 

time: 141 us -> 142 us (level)
  no operation moved by 1% of the time
where the time goes in v14:
time: 142 us; the launch traced here: 141 us
  waiting for transfers between devices  59.3 us (42%)
  Pallas kernels  42.2 us (30%)
  starting transfers between devices  36.6 us (26%)
  local copies, waits for them, and re-layouts  3.08 us (2%)
    pallas_call x19, Pallas kernels, on_chip(): pl.pallas_call(kernel, out_shape=[jax.ShapeDtypeStruct(shape, jnp.float32...  42.2 us
    ppermute x22, waiting for transfers between devices, exchange(): lax.ppermute(value, ('lo', 'rh'), [(i, i ^ bits) for i in range(2 * P_SIZ...  28.5 us
    ppermute x6, waiting for transfers between devices, other_group(): lax.ppermute(value, ('hi', 'lo'), [(i, i ^ 6) for i in range(2 * P_SIZE)])  27.1 us
    ppermute x22, starting transfers between devices, exchange(): lax.ppermute(value, ('lo', 'rh'), [(i, i ^ bits) for i in range(2 * P_SIZ...  18.2 us
    ppermute x3, starting transfers between devices, swap(): return lax.ppermute(value, axis, [(0, 1), (1, 0)])  13 us
    ppermute x6, starting transfers between devices, other_group(): lax.ppermute(value, ('hi', 'lo'), [(i, i ^ 6) for i in range(2 * P_SIZE)])  5.37 us
    ppermute x3, waiting for transfers between devices, swap(): return lax.ppermute(value, axis, [(0, 1), (1, 0)])  3.73 us
    unnamed x12, local copies, waits for them, and re-layouts  2.99 us
  transfers between devices with their start and end apart: 31, of which 20 were waited for; matrix products, arithmetic and copies ran while one was open for 0% of the time, Pallas kernels for 23%

profile of v14, /device:TPU:9, one launch (start us, length us, event | category | flops | bytes accessed | tf_op | source)
XLA Modules:
  0.0 141.4 jit_solution(11816428142047009547)
XLA Ops:
  0.8 1.2 copy-done
  2.0 0.9 copy-done.1
  3.0 0.8 mask.1
  3.8 1.4 collective-permute-start.2
  5.3 10.8 %collective-permute-done.2.got_ref = f32[160,256]{1,0:T(8,128)S(1)} collective-permute-done((f32[160,256]{1,0:T(8,128)S(1)}, f32[160,256]{1,0:T(8,128)S(1)}, u32[]{:S(2)}, u32[]{:S(2)}) %collective-permute-start.2) | collective-permute-done | bytes 163872 | tf_op jit(solution)/shard_map/ppermute | solution.py:375
  16.8 1.3 collective-permute-start.3
  18.1 1.5 %collective-permute-done.1.got_ref = f32[160,256]{1,0:T(8,128)S(1)} collective-permute-done((f32[160,256]{1,0:T(8,128)S(1)}, f32[160,256]{1,0:T(8,128)S(1)}, u32[]{:S(2)}, u32[]{:S(2)}) %collective-permute-start.1) | collective-permute-done | bytes 163872 | tf_op jit(solution)/shard_map/ppermute | solution.py:375
  19.6 1.3 collective-permute-done.4.refs_1_.refs_4_
  21.6 1.7 %collective-permute-start.5 = (f32[160,256]{1,0:T(8,128)S(1)}, f32[160,256]{1,0:T(8,128)S(1)}, u32[]{:S(2)}, u32[]{:S(2)}) collective-permute-start(f32[160,256]{1,0:T(8,128)S(1)} %get-tuple-element.46.refs_1_), channel_id=1, source_target_pairs={{0,8},{2,10},{4,12},{6,14},{8,0},{10,2},{12,4},{14,6},{1,9},{3,11}... | collective-permute-start | bytes 491528 | tf_op jit(solution)/shard_map/ppermute | solution.py:367
  23.3 1.1 collective-permute-start
  24.4 1.2 collective-permute-start.6
  25.7 1.0 collective-permute-start.7
  27.3 2.3 %collective-permute-done.got_ref = f32[160,256]{1,0:T(8,128)S(1)} collective-permute-done((f32[160,256]{1,0:T(8,128)S(1)}, f32[160,256]{1,0:T(8,128)S(1)}, u32[]{:S(2)}, u32[]{:S(2)}) %collective-permute-start) | collective-permute-done | bytes 163872 | tf_op jit(solution)/shard_map/ppermute | solution.py:375
  29.6 2.5 %collective-permute-done.7.refs_2_.refs_6_ = f32[160,256]{1,0:T(8,128)S(1)} collective-permute-done((f32[160,256]{1,0:T(8,128)S(1)}, f32[160,256]{1,0:T(8,128)S(1)}, u32[]{:S(2)}, u32[]{:S(2)}) %collective-permute-start.7) | collective-permute-done | bytes 163872 | tf_op jit(solution)/shard_map/ppermute | solution.py:367
  32.7 2.2 %collective-permute-start.10 = (f32[160,256]{1,0:T(8,128)S(1)}, f32[160,256]{1,0:T(8,128)S(1)}, u32[]{:S(2)}, u32[]{:S(2)}) collective-permute-start(f32[160,256]{1,0:T(8,128)S(1)} %get-tuple-element.47.refs_0_), channel_id=1, source_target_pairs={{0,8},{2,10},{4,12},{6,14},{8,0},{10,2},{12,4},{14,6},{1,9},{3,11}... | collective-permute-start | bytes 491528 | tf_op jit(solution)/shard_map/ppermute | solution.py:367
  35.7 2.3 %first_products.1 = (f32[640,256]{1,0:T(8,128)S(1)}, f32[4,256,256]{2,1,0:T(8,128)S(1)}) custom-call(s32[5]{0:T(128)S(1)} %stack.51.place_ref, f32[160,256]{1,0:T(8,128)S(1)} %get-tuple-element.45.refs_0_, f32[160,256]{1,0:T(8,128)S(1)} %get-tuple-element.46.refs_1_, f32[160,256]{1,0:T(8,128)S(1)} %collective-permute-done.3.refs_0_.refs_2_, ...), custom_call_target="tpu_custom_call" | custom-call | tf_op jit(solution)/shard_map/first_products/pallas_call | solution.py:209
  38.0 1.4 collective-permute-done.10.refs_1_.refs_4_
  40.0 1.6 %collective-permute-start.13 = (f32[160,256]{1,0:T(8,128)S(1)}, f32[160,256]{1,0:T(8,128)S(1)}, u32[]{:S(2)}, u32[]{:S(2)}) collective-permute-start(f32[160,256]{1,0:T(8,128)S(1)} %get-tuple-element.53.refs_1_), channel_id=1, source_target_pairs={{0,8},{2,10},{4,12},{6,14},{8,0},{10,2},{12,4},{14,6},{1,9},{3,11}... | collective-permute-start | bytes 491528 | tf_op jit(solution)/shard_map/ppermute | solution.py:367
  41.6 0.9 collective-permute-start.12
  42.6 3.6 %collective-permute-done.13.refs_5_ = f32[160,256]{1,0:T(8,128)S(1)} collective-permute-done((f32[160,256]{1,0:T(8,128)S(1)}, f32[160,256]{1,0:T(8,128)S(1)}, u32[]{:S(2)}, u32[]{:S(2)}) %collective-permute-start.13) | collective-permute-done | bytes 163872 | tf_op jit(solution)/shard_map/ppermute | solution.py:367
  46.8 1.0 collective-permute-done.14.refs_6_
  47.9 2.5 %collective-permute-done.15.refs_7_ = f32[160,256]{1,0:T(8,128)S(1)} collective-permute-done((f32[160,256]{1,0:T(8,128)S(1)}, f32[160,256]{1,0:T(8,128)S(1)}, u32[]{:S(2)}, u32[]{:S(2)}) %collective-permute-start.15) | collective-permute-done | bytes 163872 | tf_op jit(solution)/shard_map/ppermute | solution.py:367
  50.4 2.6 %products.1 = (f32[2,160,256]{2,1,0:T(8,128)S(1)}, f32[2,256,256]{2,1,0:T(8,128)S(1)}, f32[2,416,256]{2,1,0:T(8,128)S(1)}) custom-call(s32[5]{0:T(128)S(1)} %stack.51.place_ref, f32[160,256]{1,0:T(8,128)S(1)} %get-tuple-element.47.refs_0_, f32[160,256]{1,0:T(8,128)S(1)} %get-tuple-element.53.refs_1_, f32[160,256]{1,0:T(8,128)S(1)} %collective-permute-done.9.refs_0_.refs_2_, ...), custom_call_target="tpu_custom_call" | custom-call | tf_op jit(solution)/shard_map/products/pallas_call | solution.py:209
  52.9 9.3 %collective-permute-start.16 = (f32[2,416,256]{2,1,0:T(8,128)S(1)}, f32[2,416,256]{2,1,0:T(8,128)S(1)}, u32[]{:S(2)}, u32[]{:S(2)}) collective-permute-start(f32[2,416,256]{2,1,0:T(8,128)S(1)} %get-tuple-element.58._), channel_id=1, source_target_pairs={{0,1},{1,0},{2,3},{3,2},{4,5},{5,4},{6,7},{7,6},{8,9},{9,8},{10,11... | collective-permute-start | bytes 2555912 | tf_op jit(solution)/shard_map/ppermute | solution.py:371
  62.2 2.0 %collective-permute-done.16.got_ref = f32[2,416,256]{2,1,0:T(8,128)S(1)} collective-permute-done((f32[2,416,256]{2,1,0:T(8,128)S(1)}, f32[2,416,256]{2,1,0:T(8,128)S(1)}, u32[]{:S(2)}, u32[]{:S(2)}) %collective-permute-start.16) | collective-permute-done | bytes 852000 | tf_op jit(solution)/shard_map/ppermute | solution.py:371
  64.8 1.3 collective-permute-start.17
  66.0 4.2 %collective-permute-done.17 = f32[160,256]{1,0:T(8,128)S(1)} collective-permute-done((f32[160,256]{1,0:T(8,128)S(1)}, f32[160,256]{1,0:T(8,128)S(1)}, u32[]{:S(2)}, u32[]{:S(2)}) %collective-permute-start.17) | collective-permute-done | bytes 163872 | tf_op jit(solution)/shard_map/ppermute | solution.py:367
  70.3 1.2 collective-permute-start.18
  72.1 7.0 %collective-permute-done.18.right_ref = f32[160,256]{1,0:T(8,128)S(1)} collective-permute-done((f32[160,256]{1,0:T(8,128)S(1)}, f32[160,256]{1,0:T(8,128)S(1)}, u32[]{:S(2)}, u32[]{:S(2)}) %collective-permute-start.18) | collective-permute-done | bytes 163872 | tf_op jit(solution)/shard_map/ppermute | solution.py:375
  79.1 1.3 collective-permute-start.22
  80.9 2.4 %collective-permute-done.22 = f32[160,256]{1,0:T(8,128)S(1)} collective-permute-done((f32[160,256]{1,0:T(8,128)S(1)}, f32[160,256]{1,0:T(8,128)S(1)}, u32[]{:S(2)}, u32[]{:S(2)}) %collective-permute-start.22) | collective-permute-done | bytes 163872 | tf_op jit(solution)/shard_map/ppermute | solution.py:367
  83.3 1.5 %collective-permute-done.20 = f32[160,256]{1,0:T(8,128)S(1)} collective-permute-done((f32[160,256]{1,0:T(8,128)S(1)}, f32[160,256]{1,0:T(8,128)S(1)}, u32[]{:S(2)}, u32[]{:S(2)}) %collective-permute-start.20) | collective-permute-done | bytes 163872 | tf_op jit(solution)/shard_map/ppermute | solution.py:367
  85.4 3.0 %collective-permute-done.24 = f32[160,256]{1,0:T(8,128)S(1)} collective-permute-done((f32[160,256]{1,0:T(8,128)S(1)}, f32[160,256]{1,0:T(8,128)S(1)}, u32[]{:S(2)}, u32[]{:S(2)}) %collective-permute-start.24) | collective-permute-done | bytes 163872 | tf_op jit(solution)/shard_map/ppermute | solution.py:367
  88.4 0.8 collective-permute-start.25
  89.9 4.4 %collective-permute-done.25 = f32[160,256]{1,0:T(8,128)S(1)} collective-permute-done((f32[160,256]{1,0:T(8,128)S(1)}, f32[160,256]{1,0:T(8,128)S(1)}, u32[]{:S(2)}, u32[]{:S(2)}) %collective-permute-start.25) | collective-permute-done | bytes 163872 | tf_op jit(solution)/shard_map/ppermute | solution.py:367
  94.3 2.5 %collective-permute-start.26 = (f32[8,160,256]{2,1,0:T(8,128)S(1)}, f32[8,160,256]{2,1,0:T(8,128)S(1)}, u32[]{:S(2)}, u32[]{:S(2)}) collective-permute-start(f32[8,160,256]{2,1,0:T(8,128)S(1)} %bitcast_dynamic-update-slice_fusion.mine_ref), channel_id=1, source_target_pairs={{0,1},{1,0},{2,3},{3,2},{4,5},{5,4},{6,7},{7,6},{8,9},{9,8},{10,11... | collective-permute-start | bytes 3932168 | tf_op jit(solution)/shard_map/ppermute | solution.py:371
  96.9 0.9 collective-permute-start.27
  97.8 1.7 %collective-permute-done.26.other_ref = f32[8,160,256]{2,1,0:T(8,128)S(1)} collective-permute-done((f32[8,160,256]{2,1,0:T(8,128)S(1)}, f32[8,160,256]{2,1,0:T(8,128)S(1)}, u32[]{:S(2)}, u32[]{:S(2)}) %collective-permute-start.26) | collective-permute-done | bytes 1310752 | tf_op jit(solution)/shard_map/ppermute | solution.py:371
  99.5 1.1 collect.1.gram_ref.refs_7_
  100.6 7.3 %factor_step.4 = (f32[256,768]{1,0:T(8,128)S(1)}, f32[256,256]{1,0:T(8,128)S(1)}, f32[6,256,256]{2,1,0:T(8,128)S(1)}) custom-call(f32[10,256,256]{2,1,0:T(8,128)S(1)} %collect.1.gram_ref.refs_7_), custom_call_target="tpu_custom_call" | custom-call | tf_op jit(solution)/shard_map/factor_step/pallas_call | solution.py:209
  108.0 1.2 collective-permute-start.28
  109.2 7.0 %factor_step.5 = (f32[256,512]{1,0:T(8,128)S(1)}, f32[256,256]{1,0:T(8,128)S(1)}, f32[3,256,256]{2,1,0:T(8,128)S(1)}) custom-call(f32[6,256,256]{2,1,0:T(8,128)S(1)} %get-tuple-element.64.gram_ref), custom_call_target="tpu_custom_call" | custom-call | tf_op jit(solution)/shard_map/factor_step/pallas_call | solution.py:209
  116.2 5.4 %collective-permute-done.28.right_ref = f32[256,256]{1,0:T(8,128)S(1)} collective-permute-done((f32[256,256]{1,0:T(8,128)S(1)}, f32[256,256]{1,0:T(8,128)S(1)}, u32[]{:S(2)}, u32[]{:S(2)}) %collective-permute-start.28) | collective-permute-done | bytes 262176 | tf_op jit(solution)/shard_map/ppermute | solution.py:375
  121.6 0.9 collective-permute-start.29
  122.5 6.7 %factor_step.6 = (f32[256,256]{1,0:T(8,128)S(1)}, f32[256,256]{1,0:T(8,128)S(1)}, f32[1,256,256]{2,1,0:T(8,128)S(1)}) custom-call(f32[3,256,256]{2,1,0:T(8,128)S(1)} %get-tuple-element.66.gram_ref), custom_call_target="tpu_custom_call" | custom-call | tf_op jit(solution)/shard_map/factor_step/pallas_call | solution.py:209
  129.3 1.2 collective-permute-start.30
  130.5 6.4 %factor_step.7.refs_6_ = f32[256,256]{1,0:T(8,128)S(1)} custom-call(f32[1,256,256]{2,1,0:T(8,128)S(1)} %get-tuple-element.71.gram_ref), custom_call_target="tpu_custom_call" | custom-call | tf_op jit(solution)/shard_map/factor_step/pallas_call | solution.py:209
  137.0 4.4 %solve.1 = f32[256,256]{1,0:T(8,128)} custom-call(s32[5]{0:T(128)S(1)} %stack.51.place_ref, f32[256,768]{1,0:T(8,128)S(1)} %get-tuple-element.63.after_ref.refs_0_, f32[256,512]{1,0:T(8,128)S(1)} %get-tuple-element.65.after_ref.refs_1_, f32[256,256]{1,0:T(8,128)S(1)} %get-tuple-element.67._.refs_2_, f32[256,256]{1,0:T(8,128)S(1)} %get-tuple-element.68.refs_3_, ...), custom_call_target="tpu_custom_call" | custom-call | tf_op jit(solution)/shard_map/solve/pallas_call | solution.py:209
  (48 shorter events, 8.6 us)
Async XLA Ops:
  0.8 1.2 copy-start
  2.0 0.9 copy-start.1
  3.8 12.3 %collective-permute-start.2 = (f32[160,256]{1,0:T(8,128)S(1)}, f32[160,256]{1,0:T(8,128)S(1)}, u32[]{:S(2)}, u32[]{:S(2)}) collective-permute-start(f32[160,256]{1,0:T(8,128)S(1)} %get-tuple-element.44), channel_id=1, source_target_pairs={{0,24},{4,28},{8,16},{12,20},{16,8},{20,12},{24,0},{28,4},{1,25},{... | collective-permute-start | bytes 491528 | tf_op jit(solution)/shard_map/ppermute | solution.py:375
  5.1 14.5 %collective-permute-start.1 = (f32[160,256]{1,0:T(8,128)S(1)}, f32[160,256]{1,0:T(8,128)S(1)}, u32[]{:S(2)}, u32[]{:S(2)}) collective-permute-start(f32[160,256]{1,0:T(8,128)S(1)} %get-tuple-element.42), channel_id=1, source_target_pairs={{0,24},{4,28},{8,16},{12,20},{16,8},{20,12},{24,0},{28,4},{1,25},{... | collective-permute-start | bytes 491528 | tf_op jit(solution)/shard_map/ppermute | solution.py:375
  16.7 4.2 %collective-permute-start.4 = (f32[160,256]{1,0:T(8,128)S(1)}, f32[160,256]{1,0:T(8,128)S(1)}, u32[]{:S(2)}, u32[]{:S(2)}) collective-permute-start(f32[160,256]{1,0:T(8,128)S(1)} %get-tuple-element.45.refs_0_), channel_id=1, source_target_pairs={{0,8},{2,10},{4,12},{6,14},{8,0},{10,2},{12,4},{14,6},{1,9},{3,11}... | collective-permute-start | bytes 491528 | tf_op jit(solution)/shard_map/ppermute | solution.py:367
  16.8 4.2 %collective-permute-start.3 = (f32[160,256]{1,0:T(8,128)S(1)}, f32[160,256]{1,0:T(8,128)S(1)}, u32[]{:S(2)}, u32[]{:S(2)}) collective-permute-start(f32[160,256]{1,0:T(8,128)S(1)} %get-tuple-element.45.refs_0_), channel_id=1, source_target_pairs={{0,4},{2,6},{4,0},{6,2},{8,12},{10,14},{12,8},{14,10},{1,5},{3,7},... | collective-permute-start | bytes 491528 | tf_op jit(solution)/shard_map/ppermute | solution.py:367
  21.6 5.4 %collective-permute-start.5 = (f32[160,256]{1,0:T(8,128)S(1)}, f32[160,256]{1,0:T(8,128)S(1)}, u32[]{:S(2)}, u32[]{:S(2)}) collective-permute-start(f32[160,256]{1,0:T(8,128)S(1)} %get-tuple-element.46.refs_1_), channel_id=1, source_target_pairs={{0,8},{2,10},{4,12},{6,14},{8,0},{10,2},{12,4},{14,6},{1,9},{3,11}... | collective-permute-start | bytes 491528 | tf_op jit(solution)/shard_map/ppermute | solution.py:367
  23.3 6.2 %collective-permute-start = (f32[160,256]{1,0:T(8,128)S(1)}, f32[160,256]{1,0:T(8,128)S(1)}, u32[]{:S(2)}, u32[]{:S(2)}) collective-permute-start(f32[160,256]{1,0:T(8,128)S(1)} %get-tuple-element.40), channel_id=1, source_target_pairs={{0,24},{4,28},{8,16},{12,20},{16,8},{20,12},{24,0},{28,4},{1,25},{... | collective-permute-start | bytes 491528 | tf_op jit(solution)/shard_map/ppermute | solution.py:375
  24.4 5.1 %collective-permute-start.6 = (f32[160,256]{1,0:T(8,128)S(1)}, f32[160,256]{1,0:T(8,128)S(1)}, u32[]{:S(2)}, u32[]{:S(2)}) collective-permute-start(f32[160,256]{1,0:T(8,128)S(1)} %get-tuple-element.46.refs_1_), channel_id=1, source_target_pairs={{0,4},{2,6},{4,0},{6,2},{8,12},{10,14},{12,8},{14,10},{1,5},{3,7},... | collective-permute-start | bytes 491528 | tf_op jit(solution)/shard_map/ppermute | solution.py:367
  25.7 6.4 %collective-permute-start.7 = (f32[160,256]{1,0:T(8,128)S(1)}, f32[160,256]{1,0:T(8,128)S(1)}, u32[]{:S(2)}, u32[]{:S(2)}) collective-permute-start(f32[160,256]{1,0:T(8,128)S(1)} %collective-permute-done.3.refs_0_.refs_2_), channel_id=1, source_target_pairs={{0,8},{2,10},{4,12},{6,14},{8,0},{10,2},{12,4},{14,6},{1,9},{3,11}... | collective-permute-start | bytes 491528 | tf_op jit(solution)/shard_map/ppermute | solution.py:367
  26.7 11.3 %collective-permute-start.8 = (f32[160,256]{1,0:T(8,128)S(1)}, f32[160,256]{1,0:T(8,128)S(1)}, u32[]{:S(2)}, u32[]{:S(2)}) collective-permute-start(f32[160,256]{1,0:T(8,128)S(1)} %get-tuple-element.49), channel_id=1, source_target_pairs={{0,24},{4,28},{8,16},{12,20},{16,8},{20,12},{24,0},{28,4},{1,25},{... | collective-permute-start | bytes 491528 | tf_op jit(solution)/shard_map/ppermute | solution.py:375
  27.0 8.6 %collective-permute-start.11 = (f32[160,256]{1,0:T(8,128)S(1)}, f32[160,256]{1,0:T(8,128)S(1)}, u32[]{:S(2)}, u32[]{:S(2)}) collective-permute-start(f32[160,256]{1,0:T(8,128)S(1)} %collective-permute-done.5.refs_0_.refs_5_), channel_id=1, source_target_pairs={{0,4},{2,6},{4,0},{6,2},{8,12},{10,14},{12,8},{14,10},{1,5},{3,7},... | collective-permute-start | bytes 491528 | tf_op jit(solution)/shard_map/ppermute | solution.py:367
  32.7 6.8 %collective-permute-start.10 = (f32[160,256]{1,0:T(8,128)S(1)}, f32[160,256]{1,0:T(8,128)S(1)}, u32[]{:S(2)}, u32[]{:S(2)}) collective-permute-start(f32[160,256]{1,0:T(8,128)S(1)} %get-tuple-element.47.refs_0_), channel_id=1, source_target_pairs={{0,8},{2,10},{4,12},{6,14},{8,0},{10,2},{12,4},{14,6},{1,9},{3,11}... | collective-permute-start | bytes 491528 | tf_op jit(solution)/shard_map/ppermute | solution.py:367
  34.9 4.5 %collective-permute-start.9 = (f32[160,256]{1,0:T(8,128)S(1)}, f32[160,256]{1,0:T(8,128)S(1)}, u32[]{:S(2)}, u32[]{:S(2)}) collective-permute-start(f32[160,256]{1,0:T(8,128)S(1)} %get-tuple-element.47.refs_0_), channel_id=1, source_target_pairs={{0,4},{2,6},{4,0},{6,2},{8,12},{10,14},{12,8},{14,10},{1,5},{3,7},... | collective-permute-start | bytes 491528 | tf_op jit(solution)/shard_map/ppermute | solution.py:367
  40.0 6.2 %collective-permute-start.13 = (f32[160,256]{1,0:T(8,128)S(1)}, f32[160,256]{1,0:T(8,128)S(1)}, u32[]{:S(2)}, u32[]{:S(2)}) collective-permute-start(f32[160,256]{1,0:T(8,128)S(1)} %get-tuple-element.53.refs_1_), channel_id=1, source_target_pairs={{0,8},{2,10},{4,12},{6,14},{8,0},{10,2},{12,4},{14,6},{1,9},{3,11}... | collective-permute-start | bytes 491528 | tf_op jit(solution)/shard_map/ppermute | solution.py:367
  41.6 6.2 %collective-permute-start.12 = (f32[160,256]{1,0:T(8,128)S(1)}, f32[160,256]{1,0:T(8,128)S(1)}, u32[]{:S(2)}, u32[]{:S(2)}) collective-permute-start(f32[160,256]{1,0:T(8,128)S(1)} %get-tuple-element.53.refs_1_), channel_id=1, source_target_pairs={{0,4},{2,6},{4,0},{6,2},{8,12},{10,14},{12,8},{14,10},{1,5},{3,7},... | collective-permute-start | bytes 491528 | tf_op jit(solution)/shard_map/ppermute | solution.py:367
  42.5 5.3 %collective-permute-start.14 = (f32[160,256]{1,0:T(8,128)S(1)}, f32[160,256]{1,0:T(8,128)S(1)}, u32[]{:S(2)}, u32[]{:S(2)}) collective-permute-start(f32[160,256]{1,0:T(8,128)S(1)} %collective-permute-done.9.refs_0_.refs_2_), channel_id=1, source_target_pairs={{0,8},{2,10},{4,12},{6,14},{8,0},{10,2},{12,4},{14,6},{1,9},{3,11}... | collective-permute-start | bytes 491528 | tf_op jit(solution)/shard_map/ppermute | solution.py:367
  46.2 4.2 %collective-permute-start.15 = (f32[160,256]{1,0:T(8,128)S(1)}, f32[160,256]{1,0:T(8,128)S(1)}, u32[]{:S(2)}, u32[]{:S(2)}) collective-permute-start(f32[160,256]{1,0:T(8,128)S(1)} %collective-permute-done.13.refs_5_), channel_id=1, source_target_pairs={{0,4},{2,6},{4,0},{6,2},{8,12},{10,14},{12,8},{14,10},{1,5},{3,7},... | collective-permute-start | bytes 491528 | tf_op jit(solution)/shard_map/ppermute | solution.py:367
  52.9 11.3 %collective-permute-start.16 = (f32[2,416,256]{2,1,0:T(8,128)S(1)}, f32[2,416,256]{2,1,0:T(8,128)S(1)}, u32[]{:S(2)}, u32[]{:S(2)}) collective-permute-start(f32[2,416,256]{2,1,0:T(8,128)S(1)} %get-tuple-element.58._), channel_id=1, source_target_pairs={{0,1},{1,0},{2,3},{3,2},{4,5},{5,4},{6,7},{7,6},{8,9},{9,8},{10,11... | collective-permute-start | bytes 2555912 | tf_op jit(solution)/shard_map/ppermute | solution.py:371
  64.8 5.5 %collective-permute-start.17 = (f32[160,256]{1,0:T(8,128)S(1)}, f32[160,256]{1,0:T(8,128)S(1)}, u32[]{:S(2)}, u32[]{:S(2)}) collective-permute-start(f32[160,256]{1,0:T(8,128)S(1)} %get-tuple-element.60), channel_id=1, source_target_pairs={{0,2},{2,0},{4,6},{6,4},{8,10},{10,8},{12,14},{14,12},{1,3},{3,1},... | collective-permute-start | bytes 491528 | tf_op jit(solution)/shard_map/ppermute | solution.py:367
  70.3 8.8 %collective-permute-start.18 = (f32[160,256]{1,0:T(8,128)S(1)}, f32[160,256]{1,0:T(8,128)S(1)}, u32[]{:S(2)}, u32[]{:S(2)}) collective-permute-start(f32[160,256]{1,0:T(8,128)S(1)} %add.10._.left_ref), channel_id=1, source_target_pairs={{0,24},{4,28},{8,16},{12,20},{16,8},{20,12},{24,0},{28,4},{1,25},{... | collective-permute-start | bytes 491528 | tf_op jit(solution)/shard_map/ppermute | solution.py:375
  79.1 4.2 %collective-permute-start.22 = (f32[160,256]{1,0:T(8,128)S(1)}, f32[160,256]{1,0:T(8,128)S(1)}, u32[]{:S(2)}, u32[]{:S(2)}) collective-permute-start(f32[160,256]{1,0:T(8,128)S(1)} %add.11), channel_id=1, source_target_pairs={{0,2},{2,0},{4,6},{6,4},{8,10},{10,8},{12,14},{14,12},{1,3},{3,1},... | collective-permute-start | bytes 491528 | tf_op jit(solution)/shard_map/ppermute | solution.py:367
  80.4 4.5 %collective-permute-start.20 = (f32[160,256]{1,0:T(8,128)S(1)}, f32[160,256]{1,0:T(8,128)S(1)}, u32[]{:S(2)}, u32[]{:S(2)}) collective-permute-start(f32[160,256]{1,0:T(8,128)S(1)} %add.11), channel_id=1, source_target_pairs={{0,8},{2,10},{4,12},{6,14},{8,0},{10,2},{12,4},{14,6},{1,9},{3,11}... | collective-permute-start | bytes 491528 | tf_op jit(solution)/shard_map/ppermute | solution.py:367
  80.4 5.0 %collective-permute-start.19 = (f32[160,256]{1,0:T(8,128)S(1)}, f32[160,256]{1,0:T(8,128)S(1)}, u32[]{:S(2)}, u32[]{:S(2)}) collective-permute-start(f32[160,256]{1,0:T(8,128)S(1)} %add.11), channel_id=1, source_target_pairs={{0,4},{2,6},{4,0},{6,2},{8,12},{10,14},{12,8},{14,10},{1,5},{3,7},... | collective-permute-start | bytes 491528 | tf_op jit(solution)/shard_map/ppermute | solution.py:367
  83.3 5.1 %collective-permute-start.24 = (f32[160,256]{1,0:T(8,128)S(1)}, f32[160,256]{1,0:T(8,128)S(1)}, u32[]{:S(2)}, u32[]{:S(2)}) collective-permute-start(f32[160,256]{1,0:T(8,128)S(1)} %collective-permute-done.22), channel_id=1, source_target_pairs={{0,8},{2,10},{4,12},{6,14},{8,0},{10,2},{12,4},{14,6},{1,9},{3,11}... | collective-permute-start | bytes 491528 | tf_op jit(solution)/shard_map/ppermute | solution.py:367
  84.8 4.5 %collective-permute-start.21 = (f32[160,256]{1,0:T(8,128)S(1)}, f32[160,256]{1,0:T(8,128)S(1)}, u32[]{:S(2)}, u32[]{:S(2)}) collective-permute-start(f32[160,256]{1,0:T(8,128)S(1)} %collective-permute-done.20), channel_id=1, source_target_pairs={{0,4},{2,6},{4,0},{6,2},{8,12},{10,14},{12,8},{14,10},{1,5},{3,7},... | collective-permute-start | bytes 491528 | tf_op jit(solution)/shard_map/ppermute | solution.py:367
  85.4 4.5 %collective-permute-start.23 = (f32[160,256]{1,0:T(8,128)S(1)}, f32[160,256]{1,0:T(8,128)S(1)}, u32[]{:S(2)}, u32[]{:S(2)}) collective-permute-start(f32[160,256]{1,0:T(8,128)S(1)} %collective-permute-done.19), channel_id=1, source_target_pairs={{0,2},{2,0},{4,6},{6,4},{8,10},{10,8},{12,14},{14,12},{1,3},{3,1},... | collective-permute-start | bytes 491528 | tf_op jit(solution)/shard_map/ppermute | solution.py:367
  88.4 5.9 %collective-permute-start.25 = (f32[160,256]{1,0:T(8,128)S(1)}, f32[160,256]{1,0:T(8,128)S(1)}, u32[]{:S(2)}, u32[]{:S(2)}) collective-permute-start(f32[160,256]{1,0:T(8,128)S(1)} %collective-permute-done.24), channel_id=1, source_target_pairs={{0,4},{2,6},{4,0},{6,2},{8,12},{10,14},{12,8},{14,10},{1,5},{3,7},... | collective-permute-start | bytes 491528 | tf_op jit(solution)/shard_map/ppermute | solution.py:367
  94.3 5.2 %collective-permute-start.26 = (f32[8,160,256]{2,1,0:T(8,128)S(1)}, f32[8,160,256]{2,1,0:T(8,128)S(1)}, u32[]{:S(2)}, u32[]{:S(2)}) collective-permute-start(f32[8,160,256]{2,1,0:T(8,128)S(1)} %bitcast_dynamic-update-slice_fusion.mine_ref), channel_id=1, source_target_pairs={{0,1},{1,0},{2,3},{3,2},{4,5},{5,4},{6,7},{7,6},{8,9},{9,8},{10,11... | collective-permute-start | bytes 3932168 | tf_op jit(solution)/shard_map/ppermute | solution.py:371
  96.9 11.1 %collective-permute-start.27 = (f32[256,256]{1,0:T(8,128)S(1)}, f32[256,256]{1,0:T(8,128)S(1)}, u32[]{:S(2)}, u32[]{:S(2)}) collective-permute-start(f32[256,256]{1,0:T(8,128)S(1)} %get-tuple-element.62.after_ref), channel_id=1, source_target_pairs={{0,2},{2,0},{4,6},{6,4},{8,10},{10,8},{12,14},{14,12},{1,3},{3,1},... | collective-permute-start | bytes 786440 | tf_op jit(solution)/shard_map/ppermute | solution.py:367
  108.0 13.6 %collective-permute-start.28 = (f32[256,256]{1,0:T(8,128)S(1)}, f32[256,256]{1,0:T(8,128)S(1)}, u32[]{:S(2)}, u32[]{:S(2)}) collective-permute-start(f32[256,256]{1,0:T(8,128)S(1)} %add.12.left_ref), channel_id=1, source_target_pairs={{0,24},{4,28},{8,16},{12,20},{16,8},{20,12},{24,0},{28,4},{1,25},{... | collective-permute-start | bytes 786440 | tf_op jit(solution)/shard_map/ppermute | solution.py:375
  121.6 7.6 %collective-permute-start.29 = (f32[256,256]{1,0:T(8,128)S(1)}, f32[256,256]{1,0:T(8,128)S(1)}, u32[]{:S(2)}, u32[]{:S(2)}) collective-permute-start(f32[256,256]{1,0:T(8,128)S(1)} %add.13.first_ref), channel_id=1, source_target_pairs={{0,2},{2,0},{4,6},{6,4},{8,10},{10,8},{12,14},{14,12},{1,3},{3,1},... | collective-permute-start | bytes 786440 | tf_op jit(solution)/shard_map/ppermute | solution.py:367
  129.3 7.7 %collective-permute-start.30 = (f32[2,256,256]{2,1,0:T(8,128)S(1)}, f32[2,256,256]{2,1,0:T(8,128)S(1)}, u32[]{:S(2)}, u32[]{:S(2)}) collective-permute-start(f32[2,256,256]{2,1,0:T(8,128)S(1)} %stack.61.refs_8_), channel_id=1, source_target_pairs={{0,1},{1,0},{2,3},{3,2},{4,5},{5,4},{6,7},{7,6},{8,9},{9,8},{10,11... | collective-permute-start | bytes 1572872 | tf_op jit(solution)/shard_map/ppermute | solution.py:371
